TPU v7x, 32 devices: a whole 2x2x4 slice. The times are simulated.
32 devices in a mesh: req: 8 (over z, y), tp: 4 (over x, core).
Axes of the slice: x: 2, y: 2, z: 4, core: 2. Of those that a mesh axis runs over, the one named last changes fastest.
Arguments:
- patches: bfloat16 [2048, 1280], P('req'), may hold values from -6 to 6
- half_grid: int32 [8, 2], P('req'), may hold values from 6 to 8
- text_embed: bfloat16 [1536, 1280], P('req'), may hold values from -6 to 6
- dest_dev: int32 [512], P('req'), may hold values from 0 to 7, as said below
- dest_pos: int32 [512], P('req'), may hold values from 0 to 191, as said below
- text_len: int32 [8], P('req'), may hold values from 1 to 128, as said below
- enc_qkv: bfloat16 [1280, 3840], P('req', 'tp')
- enc_out_t: bfloat16 [1280, 1280], P('req', 'tp'), may hold values from -0.15625 to 0.15625
- enc_up: bfloat16 [1280, 5120], P('req', 'tp'), may hold values from -0.15625 to 0.15625
- enc_down_t: bfloat16 [1280, 5120], P('req', 'tp'), may hold values from -0.078125 to 0.078125
- merge_t: bfloat16 [1280, 5120], P('req', 'tp'), may hold values from -0.078125 to 0.078125
- dec_qkv: bfloat16 [1280, 3840], P('req', 'tp')
- dec_out_t: bfloat16 [1280, 1280], P('req', 'tp'), may hold values from -0.15625 to 0.15625
- dec_up: bfloat16 [1280, 5120], P('req', 'tp'), may hold values from -0.15625 to 0.15625
- dec_down_t: bfloat16 [1280, 5120], P('req', 'tp'), may hold values from -0.078125 to 0.078125
Outputs:
- decoded: bfloat16 [1536, 1280], P('req')
Inputs may be any that keep to these rules, and one draw needn't show every extreme that they name: `dest_dev`: the slots of one device go in runs to destination devices; at most 12 slots of one device name one destination device, exactly 12 for some pairs; every device is named by exactly 64 slots in all. `dest_pos`: positions named for one destination device are distinct and below 64 plus its text_len. `text_len`: some request has exactly 128.
All inputs are finite; a program needn't handle non-finite values.
Results may differ from a plain program's by a relative error of at most 0.024.
Values may be sent and summed in bfloat16 or wider, within the bound.
No kernel may reach another device: no remote copies, remote signals or barrier semaphores. Data moves between devices by JAX's collectives and lax.ppermute only.
A program may use at most 64 MiB of HBM per device.

v0:
```python
import jax
import jax.numpy as jnp
from jax import lax
from jax.sharding import PartitionSpec as P

HEAD_DIM = 80
GRID = 16


EPS = 1e-06


def for_sending(shard):

    def short(part):
        return part.astype(jnp.bfloat16) if part.dtype == jnp.float32 else part

    return jax.tree.map(short, shard)


def normalize(stream):
    values_f = stream.astype(jnp.float32)
    center = values_f - jnp.mean(values_f, axis=-1, keepdims=True)
    spread = jnp.mean(center * center, axis=-1, keepdims=True)
    return (center * lax.rsqrt(spread + EPS)).astype(jnp.bfloat16)


def fetch_weights(weights):
    return jax.tree.map(
        lambda part, own: part.astype(own.dtype),
        lax.all_gather(for_sending(weights), "req", axis=0, tiled=True),
        weights,
    )


def tensor_total(partial_value):
    return lax.psum(partial_value.astype(jnp.bfloat16), "tp").astype(jnp.float32)


def attention(normed, w_qkv, w_out_t, allowed, sample_count):
    total_rows = normed.shape[0]
    length = total_rows // sample_count
    projected = jnp.dot(normed, w_qkv, preferred_element_type=jnp.float32).astype(jnp.bfloat16)
    projected = projected.reshape(sample_count, length, -1, 3, HEAD_DIM)
    queries = projected[:, :, :, 0]
    key_part = projected[:, :, :, 1]
    value_part = projected[:, :, :, 2]
    scores = jnp.einsum(
        "bqhd,bkhd->bhqk", queries, key_part, preferred_element_type=jnp.float32
    ) * HEAD_DIM ** (-0.5)
    scores = jnp.where(allowed, scores, -1e30)
    highest = jnp.max(scores, axis=-1, keepdims=True)
    exponent = jnp.exp(scores - highest)
    weights_soft = (exponent / jnp.sum(exponent, axis=-1, keepdims=True)).astype(jnp.bfloat16)
    heads_out = jnp.einsum(
        "bhqk,bkhd->bqhd", weights_soft, value_part, preferred_element_type=jnp.float32
    )
    heads_out = heads_out.astype(jnp.bfloat16).reshape(total_rows, -1)
    return lax.dot_general(
        heads_out, w_out_t, (((1,), (1,)), ((), ())), preferred_element_type=jnp.float32
    )


def feed_forward(normed, w_up, w_down_t):
    hidden = jax.nn.gelu(
        jnp.dot(normed, w_up, preferred_element_type=jnp.float32), approximate=False
    )
    hidden = hidden.astype(jnp.bfloat16)
    return lax.dot_general(
        hidden, w_down_t, (((1,), (1,)), ((), ())), preferred_element_type=jnp.float32
    )


def transformer_layer(stream, weights, allowed, sample_count):
    w_qkv, w_out_t, w_up, w_down_t = weights
    attended = attention(normalize(stream), w_qkv, w_out_t, allowed, sample_count)
    middle = (stream.astype(jnp.float32) + tensor_total(attended)).astype(jnp.bfloat16)
    result_rows = middle.astype(jnp.float32) + tensor_total(
        feed_forward(normalize(middle), w_up, w_down_t)
    )
    result_rows = result_rows.astype(jnp.bfloat16)
    return result_rows


def on_device(
    patches,
    half_grid,
    text_embed,
    dest_dev,
    dest_pos,
    text_len,
    enc_qkv,
    enc_out_t,
    enc_up,
    enc_down_t,
    merge_t,
    dec_qkv,
    dec_out_t,
    dec_up,
    dec_down_t,
):
    image_count = half_grid.shape[0]
    model_width = patches.shape[1]
    per_image = GRID * GRID
    patch_index = jnp.arange(per_image, dtype=jnp.int32)
    key_valid = ((patch_index // GRID)[None, :] < 2 * half_grid[:, 0:1]) & (
        (patch_index % GRID)[None, :] < 2 * half_grid[:, 1:2]
    )
    enc_weights = fetch_weights((enc_qkv, enc_out_t, enc_up, enc_down_t))
    encoded = transformer_layer(patches, enc_weights, key_valid[:, None, None, :], image_count)
    merge_local, qkv_dec, out_dec, up_dec, down_dec = fetch_weights(
        (merge_t, dec_qkv, dec_out_t, dec_up, dec_down_t)
    )
    half_side = GRID // 2
    blocks = encoded.reshape(image_count, half_side, 2, half_side, 2, model_width).transpose(
        0, 1, 3, 2, 4, 5
    )
    blocks = blocks.reshape(image_count * half_side * half_side, 4 * model_width)
    span_width = merge_local.shape[1]
    feature_part = lax.dynamic_slice_in_dim(
        blocks, lax.axis_index("tp") * span_width, span_width, 1
    )
    merge_partial = lax.dot_general(
        feature_part, merge_local, (((1,), (1,)), ((), ())), preferred_element_type=jnp.float32
    )
    merged = tensor_total(merge_partial).astype(jnp.bfloat16)
    slot_count = merged.shape[0]
    senders = lax.axis_size("req")
    even_share = slot_count // senders
    capacity = even_share + max(even_share // 2, 1)
    cell_index = jnp.arange(half_side * half_side, dtype=jnp.int32)
    slot_valid = ((cell_index // half_side)[None, :] < half_grid[:, 0:1]) & (
        (cell_index % half_side)[None, :] < half_grid[:, 1:2]
    )
    slot_valid = slot_valid.reshape(slot_count)
    one_hot = (dest_dev[:, None] == jnp.arange(senders, dtype=jnp.int32)[None, :]).astype(jnp.int32)
    earlier = jnp.cumsum(one_hot, axis=0) - one_hot
    slot_rank = jnp.sum(earlier * one_hot, axis=1)
    outgoing = (
        jnp.zeros((senders, capacity, model_width), jnp.bfloat16)
        .at[dest_dev, slot_rank]
        .set(merged)
    )
    out_pos = (
        jnp.full((senders, capacity), -1, jnp.int32)
        .at[dest_dev, slot_rank]
        .set(jnp.where(slot_valid, dest_pos, -1))
    )
    incoming, in_pos = (
        lax.all_to_all(outgoing, "req", split_axis=0, concat_axis=0, tiled=True),
        lax.all_to_all(out_pos, "req", split_axis=0, concat_axis=0, tiled=True),
    )
    seq_len = text_embed.shape[0]
    target = jnp.where(in_pos >= 0, in_pos, seq_len).astype(jnp.int32).reshape(-1)
    dec_input = text_embed.at[target].set(incoming.reshape(-1, model_width), mode="drop")
    positions = jnp.arange(seq_len, dtype=jnp.int32)
    causal = (positions[:, None] >= positions[None, :])[None, None]
    decoded = transformer_layer(dec_input, (qkv_dec, out_dec, up_dec, down_dec), causal, 1)
    keep_mask = positions < slot_count + text_len[0]
    return jnp.where(keep_mask[:, None], decoded, jnp.zeros_like(decoded))


def solution(mesh):
    return jax.shard_map(
        on_device,
        mesh=mesh,
        in_specs=(
            P("req", None),
            P("req", None),
            P("req", None),
            P("req"),
            P("req"),
            P("req"),
            P("req", "tp"),
            P("req", "tp"),
            P("req", "tp"),
            P("req", "tp"),
            P("req", "tp"),
            P("req", "tp"),
            P("req", "tp"),
            P("req", "tp"),
            P("req", "tp"),
        ),
        out_specs=P("req", None),
        check_vma=False,
    )
```

profile of v0, /device:TPU:0, one launch (start us, length us, event | category | flops | bytes accessed | tf_op | source)
XLA Modules:
  0.0 662.7 jit_solution(5399131302444200287)
XLA Ops:
  6.5 0.7 all-gather.8.cloned.1.call-update
  7.3 0.6 fusion.214
  9.2 0.2 convert_reduce_fusion.1
  9.4 0.3 fusion.12
  9.7 36.6 %all_gather.28 = bf16[1280,320]{1,0:T(8,128)(2,1)S(1)} all-gather(bf16[160,320]{1,0:T(8,128)(2,1)S(1)} %copy-done.2), channel_id=1, replica_groups=mesh['req'=8,'tp'=4] {'req'}, dimensions={0}, use_global_device_ids=true | all-gather | bytes 921600 | tf_op jit(solution)/shard_map/all_gather | solution.py:31
  46.3 26.4 %all-gather.8.cloned.1.call-done = bf16[1280,960]{1,0:T(8,128)(2,1)} async-done(((bf16[160,960]{1,0:T(8,128)(2,1)}), bf16[1280,960]{1,0:T(8,128)(2,1)}) %all-gather.8.cloned.1.call-update) | async-done | bytes 2457616 | tf_op jit(solution)/shard_map/all_gather | solution.py:31
  72.7 2.9 convolution_convert_fusion.5
  75.6 0.3 fusion.9
  75.9 0.5 fusion.215
  76.5 0.4 convolution_convert_fusion.8
  76.9 1.4 convolution_convert_fusion
  78.3 0.7 all-gather.10.cloned.1.call-update
  79.1 0.5 all-gather.12.cloned.1.call-update
  79.6 31.3 %all-reduce.6.cloned.1.call-done = bf16[256,1280]{1,0:T(8,128)(2,1)} async-done(((bf16[256,1280]{1,0:T(8,128)(2,1)}), bf16[256,1280]{1,0:T(8,128)(2,1)}) %all-reduce.6.cloned.1.call-update) | async-done | bytes 655376 | tf_op jit(solution)/shard_map/psum | solution.py:37
  111.0 1.4 convert_reduce_fusion
  112.3 0.3 fusion.10
  112.7 62.5 %all-gather.10.cloned.1.call-done = bf16[1280,1280]{1,0:T(8,128)(2,1)} async-done(((bf16[160,1280]{1,0:T(8,128)(2,1)}), bf16[1280,1280]{1,0:T(8,128)(2,1)}) %all-gather.10.cloned.1.call-update) | async-done | bytes 3276816 | tf_op jit(solution)/shard_map/all_gather | solution.py:31
  175.2 62.6 %all-gather.12.cloned.1.call-done = bf16[1280,1280]{1,0:T(8,128)(2,1)} async-done(((bf16[160,1280]{1,0:T(8,128)(2,1)}), bf16[1280,1280]{1,0:T(8,128)(2,1)}) %all-gather.12.cloned.1.call-update) | async-done | bytes 3276816 | tf_op jit(solution)/shard_map/all_gather | solution.py:31
  237.8 8.2 %convolution_convert_fusion.1 = bf16[256,1280]{1,0:T(8,128)(2,1)} fusion(bf16[1280,1280]{1,0:T(8,128)(2,1)} %all-gather.12.cloned.1.call-done, bf16[1280,1280]{1,0:T(8,128)(2,1)} %all-gather.10.cloned.1.call-done, bf16[256,1280]{1,0:T(8,128)(2,1)S(1)} %get-tuple-element.8, f32[256]{0:T(256)S(1)} %add_rsqrt_fusion.2, f32[256]{0:T(256)S(1)} %broadcast_multiply_fusion.2), kind=kOutput, calls=%fused_computation.6 | convolution fusion | flops 1700659200 | bytes 7866368 | tf_op jit(solution)/shard_map/dot_general | solution.py:69
  246.1 0.5 all-gather.14.cloned.1.call-update
  246.7 31.9 %all-reduce.8.cloned.1.call-done = bf16[256,1280]{1,0:T(8,128)(2,1)} async-done(((bf16[256,1280]{1,0:T(8,128)(2,1)}), bf16[256,1280]{1,0:T(8,128)(2,1)}) %all-reduce.8.cloned.1.call-update) | async-done | bytes 655376 | tf_op jit(solution)/shard_map/psum | solution.py:37
  278.6 1.2 fusion.15
  279.8 0.2 reshape.248
  280.1 0.5 copy.56
  280.5 0.5 reshape.249
  281.0 61.6 %all-gather.14.cloned.1.call-done = bf16[1280,1280]{1,0:T(8,128)(2,1)} async-done(((bf16[160,1280]{1,0:T(8,128)(2,1)}), bf16[1280,1280]{1,0:T(8,128)(2,1)}) %all-gather.14.cloned.1.call-update) | async-done | bytes 3276816 | tf_op jit(solution)/shard_map/all_gather | solution.py:31
  342.6 3.7 convolution_convert_fusion.4
  346.4 0.7 all-gather.16.cloned.1.call-update
  347.1 0.1 fusion.138
  347.2 0.1 reduce_window_sum.11
  347.3 0.2 select_reduce_fusion
  347.5 1.3 and_select_fusion.2
  348.8 0.6 broadcast_in_dim.40
  349.4 10.2 %scatter_fusion = s32[8,12]{1,0:T(8,128)} fusion(s32[8,12]{1,0:T(8,128)} %broadcast_in_dim.40, s32[64]{0:T(128)S(1)} %fusion.146, s32[64]{0:T(128)S(1)} %and_select_fusion.2), kind=kCustom, calls=%fused_computation | custom fusion | bytes 1280 | tf_op jit(solution)/shard_map/scatter | solution.py:147
  359.6 3.5 all-to-all-start
  363.1 13.6 %all-reduce.10.cloned.1.call-done = bf16[64,1280]{1,0:T(8,128)(2,1)} async-done(((bf16[64,1280]{1,0:T(8,128)(2,1)}), bf16[64,1280]{1,0:T(8,128)(2,1)}) %all-reduce.10.cloned.1.call-update) | async-done | bytes 163856 | tf_op jit(solution)/shard_map/psum | solution.py:37
  376.7 7.5 %scatter_fusion.1 = bf16[8,12,1280]{2,0,1:T(8,128)(2,1)S(1)} fusion(bf16[8,12,1280]{2,0,1:T(8,128)(2,1)S(1)} %broadcast_in_dim.47, s32[64]{0:T(128)S(1)} %fusion.146, bf16[64,1280]{1,0:T(8,128)(2,1)} %all-reduce.10.cloned.1.call-done), kind=kCustom, calls=%fused_computation.1 | custom fusion | bytes 492032 | tf_op jit(solution)/shard_map/scatter | solution.py:142
  384.2 0.8 copy.41
  385.0 5.6 all-to-all-start.1
  390.7 45.0 %all_gather.33 = bf16[1280,320]{1,0:T(8,128)(2,1)S(1)} all-gather(bf16[160,320]{1,0:T(8,128)(2,1)S(1)} %copy-done.3), channel_id=1, replica_groups=mesh['req'=8,'tp'=4] {'req'}, dimensions={0}, use_global_device_ids=true | all-gather | bytes 921600 | tf_op jit(solution)/shard_map/all_gather | solution.py:31
  435.7 0.5 broadcast.368
  436.2 0.6 reduce.11
  436.9 0.1 all_to_all.13
  437.0 0.1 reshape.272
  437.1 1.3 scatter_fusion.2
  438.4 0.1 convert_reduce_fusion.3
  438.5 0.3 fusion.34
  438.8 12.4 %all-gather.16.cloned.1.call-done = bf16[1280,960]{1,0:T(8,128)(2,1)} async-done(((bf16[160,960]{1,0:T(8,128)(2,1)}), bf16[1280,960]{1,0:T(8,128)(2,1)}) %all-gather.16.cloned.1.call-update) | async-done | bytes 2457616 | tf_op jit(solution)/shard_map/all_gather | solution.py:31
  451.2 2.5 convolution_convert_fusion.6
  453.6 0.2 copy.42
  453.9 0.3 fusion.27
  454.2 0.5 fusion.216
  454.6 0.3 convolution_convert_fusion.7
  455.0 1.3 convolution_convert_fusion.3
  456.3 0.5 all-gather.18.cloned.1.call-update
  456.9 0.7 all-gather.20.cloned.1.call-update
  457.7 30.2 %all-reduce.12.cloned.1.call-done = bf16[192,1280]{1,0:T(8,128)(2,1)} async-done(((bf16[192,1280]{1,0:T(8,128)(2,1)}), bf16[192,1280]{1,0:T(8,128)(2,1)}) %all-reduce.12.cloned.1.call-update) | async-done | bytes 491536 | tf_op jit(solution)/shard_map/psum | solution.py:37
  487.9 1.3 convert_reduce_fusion.2
  489.1 0.3 fusion.32
  489.4 62.6 %all-gather.18.cloned.1.call-done = bf16[1280,1280]{1,0:T(8,128)(2,1)} async-done(((bf16[160,1280]{1,0:T(8,128)(2,1)}), bf16[1280,1280]{1,0:T(8,128)(2,1)}) %all-gather.18.cloned.1.call-update) | async-done | bytes 3276816 | tf_op jit(solution)/shard_map/all_gather | solution.py:31
  552.0 62.8 %all-gather.20.cloned.1.call-done = bf16[1280,1280]{1,0:T(8,128)(2,1)} async-done(((bf16[160,1280]{1,0:T(8,128)(2,1)}), bf16[1280,1280]{1,0:T(8,128)(2,1)}) %all-gather.20.cloned.1.call-update) | async-done | bytes 3276816 | tf_op jit(solution)/shard_map/all_gather | solution.py:31
  614.8 7.4 %convolution_convert_fusion.2 = bf16[192,1280]{1,0:T(8,128)(2,1)} fusion(bf16[1280,1280]{1,0:T(8,128)(2,1)} %all-gather.20.cloned.1.call-done, bf16[1280,1280]{1,0:T(8,128)(2,1)} %all-gather.18.cloned.1.call-done, bf16[192,1280]{1,0:T(8,128)(2,1)S(1)} %get-tuple-element.6, f32[192]{0:T(256)S(1)} %add_rsqrt_fusion, f32[192]{0:T(256)S(1)} %broadcast_multiply_fusion), kind=kOutput, calls=%fused_computation.7 | convolution fusion | flops 1275494400 | bytes 7538176 | tf_op jit(solution)/shard_map/dot_general | solution.py:69
  622.9 31.0 %all-reduce.14.cloned.1.call-done = bf16[192,1280]{1,0:T(8,128)(2,1)} async-done(((bf16[192,1280]{1,0:T(8,128)(2,1)}), bf16[192,1280]{1,0:T(8,128)(2,1)}) %all-reduce.14.cloned.1.call-update) | async-done | bytes 491536 | tf_op jit(solution)/shard_map/psum | solution.py:37
  653.9 2.0 fusion.93
  (47 shorter events, 0.7 us)
Async XLA Ops:
  6.5 2.7 copy-start.1
  6.5 0.8 copy-start.5
  6.5 66.1 %all-gather.8.cloned.1.call-start = ((), (), s32[]{:S(2)}) async-start(), calls=%async_computation.2 | async-start | bytes 2949120 | tf_op jit(solution)/shard_map/all_gather | solution.py:31
  6.5 3.2 copy-start.2
  7.3 103.7 %all-reduce.6.cloned.1.call-start = ((), (), s32[]{:S(2)}) async-start(), calls=%async_computation.3 | async-start | bytes 1310720 | tf_op jit(solution)/shard_map/psum | solution.py:37
  78.3 96.9 %all-gather.10.cloned.1.call-start = ((), (), s32[]{:S(2)}) async-start(), calls=%async_computation.4 | async-start | bytes 3686400 | tf_op jit(solution)/shard_map/all_gather | solution.py:31
  79.0 158.8 %all-gather.12.cloned.1.call-start = ((), (), s32[]{:S(2)}) async-start(), calls=%async_computation.5 | async-start | bytes 3686400 | tf_op jit(solution)/shard_map/all_gather | solution.py:31
  79.6 199.0 %all-reduce.8.cloned.1.call-start = ((), (), s32[]{:S(2)}) async-start(), calls=%async_computation.6 | async-start | bytes 1310720 | tf_op jit(solution)/shard_map/psum | solution.py:37
  246.1 96.6 %all-gather.14.cloned.1.call-start = ((), (), s32[]{:S(2)}) async-start(), calls=%async_computation.7 | async-start | bytes 3686400 | tf_op jit(solution)/shard_map/all_gather | solution.py:31
  246.6 130.0 %all-reduce.10.cloned.1.call-start = ((), (), s32[]{:S(2)}) async-start(), calls=%async_computation.8 | async-start | bytes 327680 | tf_op jit(solution)/shard_map/psum | solution.py:37
  281.0 66.1 %copy-start.4 = (s32[64]{0:T(128)S(1)}, s32[64]{0:T(128)}, u32[]{:S(2)}) copy-start(s32[64]{0:T(128)} %param.18) | copy-start | bytes 772
  281.0 66.4 %copy-start.6 = (s32[64]{0:T(128)S(1)}, s32[64]{0:T(128)}, u32[]{:S(2)}) copy-start(s32[64]{0:T(128)} %param.19) | copy-start | bytes 772
  346.4 104.8 %all-gather.16.cloned.1.call-start = ((), (), s32[]{:S(2)}) async-start(), calls=%async_computation.9 | async-start | bytes 2949120 | tf_op jit(solution)/shard_map/all_gather | solution.py:31
  359.6 25.4 %all-to-all-start = ((s32[8,1,12]{2,1,0:T(1,128)}), s32[8,1,12]{2,1,0:T(1,128)S(1)}, u32[]{:S(2)}, u32[]{:S(2)}) async-start(s32[8,1,12]{2,1,0:T(1,128)} %bitcast.7), calls=%async_computation | async-start | bytes 8192 | tf_op jit(solution)/shard_map/all_to_all | solution.py:151
  384.2 6.5 copy-start.3
  385.0 52.1 %copy-start = (bf16[192,1280]{1,0:T(8,128)(2,1)S(1)}, bf16[192,1280]{1,0:T(8,128)(2,1)}, u32[]{:S(2)}) copy-start(bf16[192,1280]{1,0:T(8,128)(2,1)} %param.17) | copy-start | bytes 1474564
  385.0 52.0 %all-to-all-start.1 = ((bf16[8,12,1280]{2,1,0:T(8,128)(2,1)}), bf16[8,12,1280]{2,1,0:T(8,128)(2,1)S(1)}, u32[]{:S(2)}, u32[]{:S(2)}) async-start(bf16[8,12,1280]{2,1,0:T(8,128)(2,1)} %copy.41), calls=%async_computation.1 | async-start | bytes 655360 | tf_op jit(solution)/shard_map/all_to_all | solution.py:150
  390.6 97.2 %all-reduce.12.cloned.1.call-start = ((), (), s32[]{:S(2)}) async-start(), calls=%async_computation.10 | async-start | bytes 983040 | tf_op jit(solution)/shard_map/psum | solution.py:37
  456.3 95.7 %all-gather.18.cloned.1.call-start = ((), (), s32[]{:S(2)}) async-start(), calls=%async_computation.11 | async-start | bytes 3686400 | tf_op jit(solution)/shard_map/all_gather | solution.py:31
  456.9 157.9 %all-gather.20.cloned.1.call-start = ((), (), s32[]{:S(2)}) async-start(), calls=%async_computation.12 | async-start | bytes 3686400 | tf_op jit(solution)/shard_map/all_gather | solution.py:31
  457.6 196.3 %all-reduce.14.cloned.1.call-start = ((), (), s32[]{:S(2)}) async-start(), calls=%async_computation.13 | async-start | bytes 983040 | tf_op jit(solution)/shard_map/psum | solution.py:37
Sparse Core Ops, SparseCore 0:
  9.5 63.0 all-gather.7
  78.4 32.5 all-reduce.5
  113.2 61.9 all-gather.9
  177.2 60.5 all-gather.11
  246.2 32.3 all-reduce.7
  280.6 61.9 all-gather.13
  346.5 30.1 all-reduce.9
  379.1 72.0 all-gather.15
  456.4 31.4 all-reduce.11
  489.9 62.0 all-gather.17
  554.2 60.5 all-gather.19
  622.3 31.4 all-reduce.13
where the time goes:
time: 664 us; the launch traced here: 663 us
  waiting for transfers between devices  493 us (74%)
  blocking collectives  81.6 us (12%)
  matrix products  29.8 us (4%)
  local copies, waits for them, and re-layouts  23 us (3%)
  between operations  15.7 us (2%)
  other arithmetic  9.66 us (1%)
  starting transfers between devices  9.6 us (1%)
    all_gather x7, waiting for transfers between devices, fetch_weights(): lax.all_gather(for_sending(weights), 'req', axis=0, tiled=True)  351 us
    psum x5, waiting for transfers between devices, tensor_total(): lax.psum(partial_value.astype(jnp.bfloat16), 'tp').astype(jnp.float32)  138 us
    all_gather x2, blocking collectives, fetch_weights(): lax.all_gather(for_sending(weights), 'req', axis=0, tiled=True)  81.6 us
    dot_general x2, matrix products, feed_forward(): lax.dot_general(hidden, w_down_t, (((1,), (1,)), ((), ())), preferred_ele...  15.6 us
  transfers between devices with their start and end apart: 14, of which 12 were waited for; matrix products, arithmetic and copies ran while one was open for 5% of the time, Pallas kernels for 0%

commit v1 on v0

v1 whole, which is shorter than its diff:
```python
import jax
import jax.numpy as jnp
from jax import lax
from jax.sharding import PartitionSpec as P

HEAD_DIM = 80
GRID = 16
HALF = GRID // 2
EPS = 1e-06
AXES = ("req", "tp")


def routes(move):
    groups = lax.axis_size("req") // 8
    pairs = []
    for z in range(4):
        for y in range(2):
            for x in range(2):
                for c in range(2):
                    z2, y2, x2, c2 = move(z, y, x, c)
                    for g in range(groups):
                        source = ((z * 2 + y) * groups + g) * 4 + x * 2 + c
                        target = ((z2 * 2 + y2) * groups + g) * 4 + x2 * 2 + c2
                        pairs.append((source, target))
    return pairs


def swap_core(part):
    return lax.ppermute(part, AXES, routes(lambda z, y, x, c: (z, y, x, 1 - c)))


def swap_x(part):
    return lax.ppermute(part, AXES, routes(lambda z, y, x, c: (z, y, 1 - x, c)))


def swap_y(part):
    return lax.ppermute(part, AXES, routes(lambda z, y, x, c: (z, 1 - y, x, c)))


def swap_z(part, k):
    return lax.ppermute(part, AXES, routes(lambda z, y, x, c: (z ^ k, y, x, c)))


def place():
    index = lax.axis_index("req") // (lax.axis_size("req") // 8)
    tensor = lax.axis_index("tp")
    return index // 2, index % 2, tensor // 2, tensor % 2


def normalize(stream):
    values_f = stream.astype(jnp.float32)
    center = values_f - jnp.mean(values_f, axis=-1, keepdims=True)
    spread = jnp.mean(center * center, axis=-1, keepdims=True)
    return (center * lax.rsqrt(spread + EPS)).astype(jnp.bfloat16)


def to_received_order(rows):
    z, y, _, _ = place()
    width = rows.shape[1] // 8
    return jnp.concatenate(
        [
            lax.dynamic_slice_in_dim(rows, ((z ^ k) * 2 + (y ^ v)) * width, width, 1)
            for v in range(2)
            for k in range(4)
        ],
        axis=1,
    )


def to_plain_order(rows):
    z, y, _, _ = place()
    width = rows.shape[1] // 8
    return jnp.concatenate(
        [
            lax.dynamic_slice_in_dim(rows, ((y ^ b) * 4 + (z ^ a)) * width, width, 1)
            for a in range(4)
            for b in range(2)
        ],
        axis=1,
    )


def from_pair_order(rows):
    lead = rows.shape[:-1]
    width = rows.shape[-1] // 8
    blocks = rows.reshape(lead + (4, 2, width))
    return jnp.concatenate([blocks[..., 1:, :], blocks[..., :1, :]], axis=-2).reshape(rows.shape)


def own_rows(weight):
    groups = lax.axis_size("req") // 8
    if groups == 1:
        return weight
    members = [[i * groups + g for g in range(groups)] for i in range(8)]
    return lax.all_gather(weight, "req", axis=0, tiled=True, axis_index_groups=members)


def gather_blocks(parts):
    column = [parts[0]] + [swap_z(parts[k], k) for k in (1, 2, 3)]
    other_own = swap_y(column[0])
    other_rest = swap_y(jnp.concatenate(column[1:], axis=0))
    return jnp.concatenate(column + [other_own, other_rest], axis=0)


def gather_same(weight):
    return gather_blocks([weight] * 4)


def gather_halved(w_up, w_down_t):
    z, _, _, _ = place()
    half = w_up.shape[1] // 2
    parts = []
    for bit in (0, 1):
        start = ((z % 2) ^ bit) * half
        parts.append(
            jnp.concatenate(
                [
                    lax.dynamic_slice_in_dim(w_up, start, half, 1),
                    lax.dynamic_slice_in_dim(w_down_t, start, half, 1),
                ],
                axis=1,
            )
        )
    both = gather_blocks([parts[0], parts[1], parts[0], parts[1]])
    return both[:, :half], both[:, half:]


def pick(rows, which, axis):
    return lax.dynamic_index_in_dim(rows, which, axis, keepdims=False)


def join_core(half, axis):
    _, _, _, c = place()
    other = swap_core(half)
    first = jnp.where(c == 0, half, other)
    second = jnp.where(c == 0, other, half)
    return jnp.concatenate([first, second], axis=axis)


def add_short(left, right):
    return left.astype(jnp.float32) + right.astype(jnp.float32)


def attention(normed, w_qkv, w_out_t, allowed, split, join):
    total_rows = normed.shape[0]
    projected = jnp.dot(normed, w_qkv, preferred_element_type=jnp.float32).astype(jnp.bfloat16)
    projected = split(projected)
    sample_count, length = projected.shape[:2]
    projected = projected.reshape(sample_count, length, -1, 3, HEAD_DIM)
    queries = projected[:, :, :, 0]
    key_part = projected[:, :, :, 1]
    value_part = projected[:, :, :, 2]
    scores = jnp.einsum(
        "bqhd,bkhd->bhqk", queries, key_part, preferred_element_type=jnp.float32
    ) * HEAD_DIM ** (-0.5)
    scores = jnp.where(allowed, scores, -1e30)
    highest = jnp.max(scores, axis=-1, keepdims=True)
    exponent = jnp.exp(scores - highest)
    weights_soft = (exponent / jnp.sum(exponent, axis=-1, keepdims=True)).astype(jnp.bfloat16)
    heads_out = jnp.einsum(
        "bhqk,bkhd->bqhd", weights_soft, value_part, preferred_element_type=jnp.float32
    )
    heads_out = join(heads_out.astype(jnp.bfloat16).reshape(sample_count, length, -1))
    return lax.dot_general(
        heads_out.reshape(total_rows, -1),
        w_out_t,
        (((1,), (1,)), ((), ())),
        preferred_element_type=jnp.float32,
    )


def middle_half(stream, partial_value):
    _, _, _, c = place()
    rows = stream.shape[0]
    split = partial_value.astype(jnp.bfloat16).reshape(2, rows // 2, -1)
    mine = add_short(pick(split, c, 0), swap_core(pick(split, 1 - c, 0))).astype(jnp.bfloat16)
    total = add_short(mine, swap_x(mine))
    kept = pick(stream.reshape(2, rows // 2, -1), c, 0)
    return (kept.astype(jnp.float32) + total).astype(jnp.bfloat16)


def feed_forward(normed, w_up, w_down_t):
    hidden = jax.nn.gelu(
        jnp.dot(normed, w_up, preferred_element_type=jnp.float32), approximate=False
    ).astype(jnp.bfloat16)
    return lax.dot_general(
        hidden, w_down_t, (((1,), (1,)), ((), ())), preferred_element_type=jnp.float32
    ).astype(jnp.bfloat16)


def paired_feed_forward(mid_half, w_up, w_down_t):
    normed_half = normalize(mid_half)
    pair_half = from_pair_order(swap_z(normed_half, 1))
    own = feed_forward(join_core(normed_half, 0), w_up, w_down_t)
    pair = feed_forward(join_core(pair_half, 0), w_up, w_down_t)
    return own, pair


def sum_pair(own, pair):
    _, _, _, c = place()
    pair_mine = add_short(pick(pair, c, 0), swap_core(pick(pair, 1 - c, 0))).astype(jnp.bfloat16)
    arrived = from_pair_order(swap_z(pair_mine, 1))
    own_mine = add_short(pick(own, c, 0), swap_core(pick(own, 1 - c, 0)))
    return (own_mine + arrived.astype(jnp.float32)).astype(jnp.bfloat16)


def on_device(
    patches,
    half_grid,
    text_embed,
    dest_dev,
    dest_pos,
    text_len,
    enc_qkv,
    enc_out_t,
    enc_up,
    enc_down_t,
    merge_t,
    dec_qkv,
    dec_out_t,
    dec_up,
    dec_down_t,
):
    z, y, x, c = place()
    senders = lax.axis_size("req")
    image_count = half_grid.shape[0]
    model_width = patches.shape[1]
    cells = HALF * HALF
    slot_count = image_count * cells
    qkv_width = enc_qkv.shape[1]

    enc_attn = gather_same(own_rows(jnp.concatenate([enc_qkv, enc_out_t], axis=1)))
    enc_ff = gather_halved(own_rows(enc_up), own_rows(enc_down_t))
    merge_all = gather_same(own_rows(merge_t))
    dec_attn = gather_same(own_rows(jnp.concatenate([dec_qkv, dec_out_t], axis=1)))
    dec_ff = gather_halved(own_rows(dec_up), own_rows(dec_down_t))

    cell_index = jnp.arange(cells, dtype=jnp.int32)
    slot_valid = ((cell_index // HALF)[None, :] < half_grid[:, 0:1]) & (
        (cell_index % HALF)[None, :] < half_grid[:, 1:2]
    )

    rows = patches.reshape(image_count, HALF, 2, HALF, 2, model_width)
    rows = rows.transpose(2, 4, 0, 1, 3, 5).reshape(4 * slot_count, model_width)
    rows = to_received_order(rows)
    key_valid = jnp.tile(slot_valid, (1, 4))

    def by_image(value):
        value = value.reshape(4, image_count, cells, -1).transpose(1, 0, 2, 3)
        return value.reshape(image_count, 4 * cells, -1)

    def by_place(value):
        value = value.reshape(image_count, 4, cells, -1).transpose(1, 0, 2, 3)
        return value.reshape(4 * slot_count, -1)

    def halves(value):
        width = value.shape[1]
        return value.reshape(2, 2, slot_count, width).transpose(1, 0, 2, 3).reshape(-1, width)

    attended = attention(
        normalize(rows),
        enc_attn[:, :qkv_width],
        enc_attn[:, qkv_width:],
        key_valid[:, None, None, :],
        by_image,
        by_place,
    )
    mid_half = middle_half(halves(rows), halves(attended))
    own, pair = paired_feed_forward(mid_half, *enc_ff)
    total = sum_pair(
        own.reshape(2, 2 * slot_count, model_width), pair.reshape(2, 2 * slot_count, model_width)
    ).reshape(2, slot_count, model_width)
    total = add_short(pick(total, x, 0), swap_x(pick(total, 1 - x, 0)))
    kept = pick(mid_half.reshape(2, slot_count, model_width), x, 0)
    encoded = (kept.astype(jnp.float32) + total).astype(jnp.bfloat16)

    partial_merge = lax.dot_general(
        to_plain_order(encoded),
        merge_all,
        (((1,), (1,)), ((), ())),
        preferred_element_type=jnp.float32,
    )
    partial_merge = to_plain_order(partial_merge.astype(jnp.bfloat16))
    half_width = model_width // 2
    partial_merge = partial_merge.reshape(slot_count, 2, half_width)
    merged = add_short(pick(partial_merge, c, 1), swap_core(pick(partial_merge, 1 - c, 1)))
    merged = merged.astype(jnp.bfloat16)
    merged = add_short(merged, swap_x(merged)).astype(jnp.bfloat16)

    even_share = slot_count // senders
    capacity = even_share + max(even_share // 2, 1)
    one_hot = (dest_dev[:, None] == jnp.arange(senders, dtype=jnp.int32)[None, :]).astype(jnp.int32)
    earlier = jnp.cumsum(one_hot, axis=0) - one_hot
    slot_rank = jnp.sum(earlier * one_hot, axis=1)
    bucket = dest_dev * capacity + slot_rank
    chosen = jnp.arange(senders * capacity, dtype=jnp.int32)[:, None] == bucket[None, :]
    digits = jnp.stack([slot_valid.reshape(-1).astype(jnp.int32), dest_pos // 128, dest_pos % 128], 1)
    digits = jnp.pad(digits, ((0, 0), (0, 125))).astype(jnp.bfloat16)
    outgoing = jnp.dot(
        chosen.astype(jnp.bfloat16),
        jnp.concatenate([merged, digits], axis=1),
        preferred_element_type=jnp.float32,
    ).astype(jnp.bfloat16)
    incoming = lax.all_to_all(
        outgoing.reshape(senders, capacity, -1), "req", split_axis=0, concat_axis=0, tiled=True
    ).reshape(senders * capacity, -1)

    seq_len = text_embed.shape[0]
    positions = jnp.arange(seq_len, dtype=jnp.int32)
    marks = incoming[:, half_width:].astype(jnp.int32)
    target = jnp.where(marks[:, 0] > 0, marks[:, 1] * 128 + marks[:, 2], -1)
    hits = positions[:, None] == target[None, :]
    placed = jnp.dot(
        hits.astype(jnp.bfloat16), incoming[:, :half_width], preferred_element_type=jnp.float32
    ).astype(jnp.bfloat16)
    text_half = lax.dynamic_slice_in_dim(text_embed, c * half_width, half_width, 1)
    dec_half = jnp.where(jnp.any(hits, axis=1)[:, None], placed, text_half)
    dec_rows = to_received_order(join_core(dec_half, 1))

    causal = (positions[:, None] >= positions[None, :])[None, None]
    attended = attention(
        normalize(dec_rows),
        dec_attn[:, :qkv_width],
        dec_attn[:, qkv_width:],
        causal,
        lambda value: value[None],
        lambda value: value[0],
    )
    mid_half = middle_half(dec_rows, attended)
    own, pair = paired_feed_forward(mid_half, *dec_ff)
    half_rows = seq_len // 2
    total = sum_pair(
        own.reshape(2, half_rows, model_width), pair.reshape(2, half_rows, model_width)
    )
    total = add_short(total, swap_x(total))
    decoded = (mid_half.astype(jnp.float32) + total).astype(jnp.bfloat16)
    keep_mask = positions < slot_count + text_len[0]
    keep_half = pick(keep_mask.reshape(2, half_rows), c, 0)
    decoded = jnp.where(keep_half[:, None], decoded, jnp.zeros_like(decoded))
    return join_core(to_plain_order(decoded), 0)


def solution(mesh):
    return jax.shard_map(
        on_device,
        mesh=mesh,
        in_specs=(
            P("req", None),
            P("req", None),
            P("req", None),
            P("req"),
            P("req"),
            P("req"),
            P("req", "tp"),
            P("req", "tp"),
            P("req", "tp"),
            P("req", "tp"),
            P("req", "tp"),
            P("req", "tp"),
            P("req", "tp"),
            P("req", "tp"),
            P("req", "tp"),
        ),
        out_specs=P("req", None),
        check_vma=False,
    )
```

time: 664 us -> 339 us (0.51)
  waiting for transfers between devices: 493 us -> 127 us
  blocking collectives: 81.6 us -> 0 us
  starting transfers between devices: 9.6 us -> 82.9 us
  local copies, waits for them, and re-layouts: 23 us -> 67 us
  other arithmetic: 9.66 us -> 26.3 us
  between operations: 15.7 us -> 1.71 us
    all_gather x7 -> x0, waiting for transfers between devices: 351 us -> none  [fetch_weights(): lax.all_gather(for_sending(weights), 'req', axis=0, tiled=True)]
    psum x5 -> x0, waiting for transfers between devices: 138 us -> none  [tensor_total(): lax.psum(partial_value.astype(jnp.bfloat16), 'tp').astype(jnp.float32)]
    ppermute x0 -> x47, waiting for transfers between devices: none -> 105 us  [the longest x19 60.5 us: swap_z(): return lax.ppermute(part, AXES, routes(lambda z, y, x, c: (z ^ k, y, x, c)))]
    all_gather x2 -> x0, blocking collectives: 81.6 us -> none  [fetch_weights(): lax.all_gather(for_sending(weights), 'req', axis=0, tiled=True)]
    ppermute x0 -> x47, starting transfers between devices: none -> 78.8 us  [the longest x19 60.6 us: swap_z(): return lax.ppermute(part, AXES, routes(lambda z, y, x, c: (z ^ k, y, x, c)))]
    unnamed x14 -> x59, local copies, waits for them, and re-layouts: 0.03 us -> 27.1 us
    all_to_all x2 -> x1, waiting for transfers between devices: 0.01 us -> 22 us  [on_device(): lax.all_to_all(outgoing.reshape(senders, capacity, -1), 'req', split_axis...]
    concatenate x0 -> x12, local copies, waits for them, and re-layouts: none -> 20.6 us  [the longest x5 16.5 us: gather_blocks(): return jnp.concatenate(column + [other_own, other_rest], axis=0)]
  transfers between devices with their start and end apart: 14 -> 48, of which waited for: 12 -> 18; matrix products, arithmetic and copies ran while one was open for 5% -> 35% of each run, Pallas kernels for 0% -> 0%
where the time goes in v1:
time: 339 us; the launch traced here: 337 us
  waiting for transfers between devices  127 us (37%)
  starting transfers between devices  82.9 us (24%)
  local copies, waits for them, and re-layouts  67 us (20%)
  matrix products  32.6 us (10%)
  other arithmetic  26.3 us (8%)
    ppermute x19, starting transfers between devices, swap_z(): return lax.ppermute(part, AXES, routes(lambda z, y, x, c: (z ^ k, y, x, c)))  60.6 us
    ppermute x19, waiting for transfers between devices, swap_z(): return lax.ppermute(part, AXES, routes(lambda z, y, x, c: (z ^ k, y, x, c)))  60.5 us
    unnamed x59, local copies, waits for them, and re-layouts  27.1 us
    ppermute x5, waiting for transfers between devices, swap_x(): return lax.ppermute(part, AXES, routes(lambda z, y, x, c: (z, y, 1 - x, c)))  22.3 us
    all_to_all x1, waiting for transfers between devices, on_device(): lax.all_to_all(outgoing.reshape(senders, capacity, -1), 'req', split_axis...  22 us
    ppermute x10, waiting for transfers between devices, swap_y(): return lax.ppermute(part, AXES, routes(lambda z, y, x, c: (z, 1 - y, x, c)))  19.1 us
    dot_general x4, matrix products, feed_forward(): lax.dot_general(hidden, w_down_t, (((1,), (1,)), ((), ())), preferred_ele...  17.9 us
    concatenate x5, local copies, waits for them, and re-layouts, gather_blocks(): return jnp.concatenate(column + [other_own, other_rest], axis=0)  16.5 us
  transfers between devices with their start and end apart: 48, of which 18 were waited for; matrix products, arithmetic and copies ran while one was open for 35% of the time, Pallas kernels for 0%

profile of v1, /device:TPU:0, one launch (start us, length us, event | category | flops | bytes accessed | tf_op | source)
XLA Modules:
  0.0 337.4 jit_solution(909696115145325183)
XLA Ops:
  3.4 3.0 collective-permute-start
  6.4 2.6 collective-permute-start.1
  9.0 1.7 collective-permute-start.3
  12.3 2.0 reshape.355
  17.4 1.8 constant_dynamic-update-slice_fusion.11
  25.3 4.3 %collective-permute-start.10 = (bf16[160,1280]{1,0:T(8,128)(2,1)}, bf16[160,1280]{1,0:T(8,128)(2,1)S(1)}, u32[]{:S(2)}, u32[]{:S(2)}) collective-permute-start(bf16[160,1280]{1,0:T(8,128)(2,1)} %pad_maximum_fusion.7), channel_id=1, source_target_pairs={{0,24},{1,25},{2,26},{3,27},{4,28},{5,29},{6,30},{7,31},{8,16},{9,... | collective-permute-start | bytes 1228808 | tf_op jit(solution)/shard_map/ppermute | solution.py:41
  29.6 7.9 %collective-permute-done.1 = bf16[160,1280]{1,0:T(8,128)(2,1)S(1)} collective-permute-done((bf16[160,1280]{1,0:T(8,128)(2,1)}, bf16[160,1280]{1,0:T(8,128)(2,1)S(1)}, u32[]{:S(2)}, u32[]{:S(2)}) %collective-permute-start.1) | collective-permute-done | bytes 409632 | tf_op jit(solution)/shard_map/ppermute | solution.py:41
  38.3 2.4 pad_maximum_fusion
  40.7 1.5 collective-permute-start.4
  46.0 2.1 copy.153
  48.1 2.1 copy.154
  50.6 2.1 copy.155
  52.7 26.2 %collective-permute-start.19 = (bf16[160,1280]{1,0:T(8,128)(2,1)}, bf16[160,1280]{1,0:T(8,128)(2,1)}, u32[]{:S(2)}, u32[]{:S(2)}) collective-permute-start(bf16[160,1280]{1,0:T(8,128)(2,1)} %param.25), channel_id=1, source_target_pairs={{0,8},{1,9},{2,10},{3,11},{4,12},{5,13},{6,14},{7,15},{8,0},{9,1},... | collective-permute-start | bytes 1228808 | tf_op jit(solution)/shard_map/ppermute | solution.py:41
  81.5 1.7 collective-permute-start.21
  86.2 1.6 copy.156
  87.8 6.8 %concatenate.99 = bf16[1280,1280]{0,1:T(8,128)(2,1)} concatenate(bf16[160,1280]{0,1:T(8,128)(2,1)S(1)} %pad_maximum_fusion.5, bf16[160,1280]{0,1:T(8,128)(2,1)S(1)} %copy.152, bf16[160,1280]{0,1:T(8,128)(2,1)} %copy.153, bf16[160,1280]{0,1:T(8,128)(2,1)} %copy.154, bf16[160,1280]{0,1:T(8,128)(2,1)} %copy.155, bf16[480,1280]{0,1:T(8,128)(2,1)S(1)} %copy.156), dimensions={0} | concatenate | bytes 6553600 | tf_op jit(solution)/shard_map/concatenate | solution.py:102
  94.6 2.6 fusion.29
  98.8 1.6 fusion.4
  100.7 1.8 constant_dynamic-update-slice_fusion.10
  102.5 8.0 %collective-permute-done.20 = bf16[160,1280]{1,0:T(8,128)(2,1)} collective-permute-done((bf16[160,1280]{1,0:T(8,128)(2,1)}, bf16[160,1280]{1,0:T(8,128)(2,1)}, u32[]{:S(2)}, u32[]{:S(2)}) %collective-permute-start.20) | collective-permute-done | bytes 409632 | tf_op jit(solution)/shard_map/ppermute | solution.py:41
  111.6 2.4 pad_maximum_fusion.2
  114.0 1.6 collective-permute-start.6
  115.6 1.8 constant_dynamic-update-slice_fusion.9
  117.4 1.5 collective-permute-start.22
  118.9 25.6 %collective-permute-done.28 = bf16[160,1280]{1,0:T(8,128)(2,1)S(1)} collective-permute-done((bf16[160,1280]{1,0:T(8,128)(2,1)}, bf16[160,1280]{1,0:T(8,128)(2,1)S(1)}, u32[]{:S(2)}, u32[]{:S(2)}) %collective-permute-start.28) | collective-permute-done | bytes 409632 | tf_op jit(solution)/shard_map/ppermute | solution.py:41
  144.5 1.5 collective-permute-start.30
  146.5 2.1 pad_maximum_fusion.3
  150.0 8.0 %collective-permute-start.14 = (bf16[128,1280]{1,0:T(8,128)(2,1)}, bf16[128,1280]{1,0:T(8,128)(2,1)S(1)}, u32[]{:S(2)}, u32[]{:S(2)}) collective-permute-start(bf16[128,1280]{1,0:T(8,128)(2,1)} %fusion.49), channel_id=1, source_target_pairs={{0,8},{1,9},{2,10},{3,11},{4,12},{5,13},{6,14},{7,15},{8,0},{9,1},... | collective-permute-start | bytes 983048 | tf_op jit(solution)/shard_map/ppermute | solution.py:41
  158.1 1.8 constant_dynamic-update-slice_fusion.8
  159.9 1.8 constant_dynamic-update-slice_fusion.1
  161.7 5.2 %collective-permute-done.14 = bf16[128,1280]{1,0:T(8,128)(2,1)S(1)} collective-permute-done((bf16[128,1280]{1,0:T(8,128)(2,1)}, bf16[128,1280]{1,0:T(8,128)(2,1)S(1)}, u32[]{:S(2)}, u32[]{:S(2)}) %collective-permute-start.14) | collective-permute-done | bytes 327712 | tf_op jit(solution)/shard_map/ppermute | solution.py:41
  166.9 1.5 collective-permute-start.37
  169.0 1.8 constant_dynamic-update-slice_fusion.7
  170.8 10.2 %collective-permute-done.12 = bf16[480,1280]{1,0:T(8,128)(2,1)} collective-permute-done((bf16[480,1280]{1,0:T(8,128)(2,1)}, bf16[480,1280]{1,0:T(8,128)(2,1)}, u32[]{:S(2)}, u32[]{:S(2)}) %collective-permute-start.12) | collective-permute-done | bytes 1228832 | tf_op jit(solution)/shard_map/ppermute | solution.py:37
  181.0 1.5 collective-permute-start.23
  182.5 2.5 constant_dynamic-update-slice_fusion
  185.9 4.7 %convolution_convert_fusion = bf16[256,1280]{1,0:T(8,128)(2,1)S(1)} fusion(bf16[1280,1280]{1,0:T(8,128)(2,1)} %constant_dynamic-update-slice_fusion, bf16[128,1280]{1,0:T(8,128)(2,1)} %get-tuple-element.22, bf16[128,1280]{1,0:T(8,128)(2,1)} %get-tuple-element.21), kind=kOutput, calls=%fused_computation.4 | convolution fusion | flops 851148800 | bytes 4587520 | tf_op jit(solution)/shard_map/dot_general | solution.py:186
  191.4 2.1 broadcast_select_fusion.3
  194.6 6.8 %collective-permute-start.17 = (bf16[128,1280]{0,1:T(8,128)(2,1)}, bf16[128,1280]{0,1:T(8,128)(2,1)}, u32[]{:S(2)}, u32[]{:S(2)}) collective-permute-start(bf16[128,1280]{0,1:T(8,128)(2,1)} %fusion.75), channel_id=1, source_target_pairs={{0,8},{1,9},{2,10},{3,11},{4,12},{5,13},{6,14},{7,15},{8,0},{9,1},... | collective-permute-start | bytes 983048 | tf_op jit(solution)/shard_map/ppermute | solution.py:41
  201.4 4.7 %convolution_convert_fusion.1 = bf16[256,1280]{1,0:T(8,128)(2,1)S(1)} fusion(bf16[1280,1280]{1,0:T(8,128)(2,1)} %constant_dynamic-update-slice_fusion, bf16[128,1280]{1,0:T(8,128)(2,1)} %get-tuple-element.24, bf16[128,1280]{1,0:T(8,128)(2,1)} %get-tuple-element.23), kind=kOutput, calls=%fused_computation.5 | convolution fusion | flops 851148800 | bytes 4587520 | tf_op jit(solution)/shard_map/dot_general | solution.py:186
  206.6 3.0 collective-permute-done.17
  211.2 2.2 collective-permute-start.36
  214.4 2.4 constant_dynamic-update-slice_fusion.6
  216.8 3.0 collective-permute-done.18
  220.2 3.3 convolution_convert_fusion.6
  224.3 1.8 constant_dynamic-update-slice_fusion.16
  227.5 3.5 %collective-permute-done.25 = bf16[64,640]{1,0:T(8,128)(2,1)S(1)} collective-permute-done((bf16[64,640]{1,0:T(8,128)(2,1)S(1)}, bf16[64,640]{1,0:T(8,128)(2,1)S(1)}, u32[]{:S(2)}, u32[]{:S(2)}) %collective-permute-start.25) | collective-permute-done | bytes 81952 | tf_op jit(solution)/shard_map/ppermute | solution.py:33
  232.5 4.2 %all-to-all-start = ((bf16[8,12,768]{2,1,0:T(8,128)(2,1)}), bf16[8,12,768]{2,1,0:T(8,128)(2,1)S(1)}, u32[]{:S(2)}, u32[]{:S(2)}) async-start(bf16[8,12,768]{2,1,0:T(8,128)(2,1)} %reshape.369), calls=%async_computation | async-start | bytes 393216 | tf_op jit(solution)/shard_map/all_to_all | solution.py:304
  237.4 2.0 collective-permute-start.38
  239.5 1.8 constant_dynamic-update-slice_fusion.13
  241.3 22.0 %all-to-all-done = bf16[8,12,768]{2,1,0:T(8,128)(2,1)S(1)} async-done(((bf16[8,12,768]{2,1,0:T(8,128)(2,1)}), bf16[8,12,768]{2,1,0:T(8,128)(2,1)S(1)}, u32[]{:S(2)}, u32[]{:S(2)}) %all-to-all-start) | async-done | bytes 147488 | tf_op jit(solution)/shard_map/all_to_all | solution.py:304
  264.0 2.4 constant_dynamic-update-slice_fusion.12
  268.4 2.5 fusion.32
  272.2 2.0 convolution_convert_fusion.5
  279.5 7.8 %collective-permute-done.33 = bf16[96,1280]{0,1:T(8,128)(2,1)S(1)} collective-permute-done((bf16[96,1280]{0,1:T(8,128)(2,1)S(1)}, bf16[96,1280]{0,1:T(8,128)(2,1)S(1)}, u32[]{:S(2)}, u32[]{:S(2)}) %collective-permute-start.33) | collective-permute-done | bytes 245792 | tf_op jit(solution)/shard_map/ppermute | solution.py:33
  288.9 1.8 constant_dynamic-update-slice_fusion.19
  290.7 5.7 %collective-permute-done.41 = bf16[96,1280]{0,1:T(8,128)(2,1)S(1)} collective-permute-done((bf16[96,1280]{0,1:T(8,128)(2,1)S(1)}, bf16[96,1280]{0,1:T(8,128)(2,1)S(1)}, u32[]{:S(2)}, u32[]{:S(2)}) %collective-permute-start.41) | collective-permute-done | bytes 245792 | tf_op jit(solution)/shard_map/ppermute | solution.py:41
  296.6 8.9 %collective-permute-done.39 = bf16[480,1280]{1,0:T(8,128)(2,1)} collective-permute-done((bf16[480,1280]{1,0:T(8,128)(2,1)}, bf16[480,1280]{1,0:T(8,128)(2,1)}, u32[]{:S(2)}, u32[]{:S(2)}) %collective-permute-start.39) | collective-permute-done | bytes 1228832 | tf_op jit(solution)/shard_map/ppermute | solution.py:37
  305.5 2.4 constant_dynamic-update-slice_fusion.18
  308.0 4.2 %convolution_convert_fusion.3 = bf16[192,1280]{1,0:T(8,128)(2,1)S(1)} fusion(bf16[1280,1280]{1,0:T(8,128)(2,1)} %constant_dynamic-update-slice_fusion.18, bf16[96,1280]{0,1:T(8,128)(2,1)S(1)} %get-tuple-element.14, bf16[96,1280]{0,1:T(8,128)(2,1)S(1)} %get-tuple-element.13), kind=kOutput, calls=%fused_computation.7 | convolution fusion | flops 638361600 | bytes 4259840 | tf_op jit(solution)/shard_map/dot_general | solution.py:186
  314.8 4.2 %convolution_convert_fusion.4 = bf16[192,1280]{1,0:T(8,128)(2,1)S(1)} fusion(bf16[1280,1280]{1,0:T(8,128)(2,1)} %constant_dynamic-update-slice_fusion.18, bf16[96,1280]{0,1:T(8,128)(2,1)S(1)} %get-tuple-element.16, bf16[96,1280]{0,1:T(8,128)(2,1)S(1)} %get-tuple-element.15), kind=kOutput, calls=%fused_computation.8 | convolution fusion | flops 638361600 | bytes 4259840 | tf_op jit(solution)/shard_map/dot_general | solution.py:186
  319.7 4.8 %collective-permute-done.44 = bf16[96,1280]{0,1:T(8,128)(2,1)S(1)} collective-permute-done((bf16[96,1280]{0,1:T(8,128)(2,1)S(1)}, bf16[96,1280]{0,1:T(8,128)(2,1)S(1)}, u32[]{:S(2)}, u32[]{:S(2)}) %collective-permute-start.44) | collective-permute-done | bytes 245792 | tf_op jit(solution)/shard_map/ppermute | solution.py:41
  326.1 7.9 %collective-permute-done.45 = bf16[96,1280]{0,1:T(8,128)(2,1)S(1)} collective-permute-done((bf16[96,1280]{0,1:T(8,128)(2,1)S(1)}, bf16[96,1280]{0,1:T(8,128)(2,1)S(1)}, u32[]{:S(2)}, u32[]{:S(2)}) %collective-permute-start.45) | collective-permute-done | bytes 245792 | tf_op jit(solution)/shard_map/ppermute | solution.py:33
  334.4 1.6 collective-permute-done.46
  (230 shorter events, 57.1 us)
Async XLA Ops:
  0.0 10.7 %copy-start.3 = (bf16[160,1280]{1,0:T(8,128)(2,1)S(1)}, bf16[160,1280]{1,0:T(8,128)(2,1)}, u32[]{:S(2)}) copy-start(bf16[160,1280]{1,0:T(8,128)(2,1)} %param.23) | copy-start | bytes 1228804
  0.0 10.7 %copy-start.2 = (bf16[160,1280]{1,0:T(8,128)(2,1)S(1)}, bf16[160,1280]{1,0:T(8,128)(2,1)}, u32[]{:S(2)}) copy-start(bf16[160,1280]{1,0:T(8,128)(2,1)} %param.24) | copy-start | bytes 1228804
  3.4 21.9 %collective-permute-start = (bf16[160,1280]{1,0:T(8,128)(2,1)}, bf16[160,1280]{1,0:T(8,128)(2,1)}, u32[]{:S(2)}, u32[]{:S(2)}) collective-permute-start(bf16[160,1280]{1,0:T(8,128)(2,1)} %copy.148), channel_id=1, source_target_pairs={{0,8},{1,9},{2,10},{3,11},{4,12},{5,13},{6,14},{7,15},{8,0},{9,1},... | collective-permute-start | bytes 1228808 | tf_op jit(solution)/shard_map/ppermute | solution.py:41
  6.4 31.1 %collective-permute-start.1 = (bf16[160,1280]{1,0:T(8,128)(2,1)}, bf16[160,1280]{1,0:T(8,128)(2,1)S(1)}, u32[]{:S(2)}, u32[]{:S(2)}) collective-permute-start(bf16[160,1280]{1,0:T(8,128)(2,1)} %copy.148), channel_id=1, source_target_pairs={{0,16},{1,17},{2,18},{3,19},{4,20},{5,21},{6,22},{7,23},{8,24},{9,... | collective-permute-start | bytes 1228808 | tf_op jit(solution)/shard_map/ppermute | solution.py:41
  9.0 29.3 %collective-permute-start.2 = (bf16[160,1280]{1,0:T(8,128)(2,1)}, bf16[160,1280]{1,0:T(8,128)(2,1)}, u32[]{:S(2)}, u32[]{:S(2)}) collective-permute-start(bf16[160,1280]{1,0:T(8,128)(2,1)} %copy.148), channel_id=1, source_target_pairs={{0,24},{1,25},{2,26},{3,27},{4,28},{5,29},{6,30},{7,31},{8,16},{9,... | collective-permute-start | bytes 1228808 | tf_op jit(solution)/shard_map/ppermute | solution.py:41
  9.0 41.1 %collective-permute-start.3 = (bf16[160,1280]{1,0:T(8,128)(2,1)}, bf16[160,1280]{1,0:T(8,128)(2,1)}, u32[]{:S(2)}, u32[]{:S(2)}) collective-permute-start(bf16[160,1280]{1,0:T(8,128)(2,1)} %copy.148), channel_id=1, source_target_pairs={{0,4},{1,5},{2,6},{3,7},{4,0},{5,1},{6,2},{7,3},{8,12},{9,13},{10,... | collective-permute-start | bytes 1228808 | tf_op jit(solution)/shard_map/ppermute | solution.py:37
  11.6 41.1 %collective-permute-start.8 = (bf16[160,1280]{1,0:T(8,128)(2,1)}, bf16[160,1280]{1,0:T(8,128)(2,1)S(1)}, u32[]{:S(2)}, u32[]{:S(2)}) collective-permute-start(bf16[160,1280]{1,0:T(8,128)(2,1)} %pad_maximum_fusion.7), channel_id=1, source_target_pairs={{0,8},{1,9},{2,10},{3,11},{4,12},{5,13},{6,14},{7,15},{8,0},{9,1},... | collective-permute-start | bytes 1228808 | tf_op jit(solution)/shard_map/ppermute | solution.py:41
  14.4 4.8 %copy-start.12 = (s32[64]{0:T(128)S(1)}, s32[64]{0:T(128)}, u32[]{:S(2)}) copy-start(s32[64]{0:T(128)} %param.19) | copy-start | bytes 772
  14.4 4.8 %copy-start.10 = (s32[64]{0:T(128)S(1)}, s32[64]{0:T(128)}, u32[]{:S(2)}) copy-start(s32[64]{0:T(128)} %param.18) | copy-start | bytes 772
  16.9 3.7 %copy-start.7 = (bf16[160,960]{1,0:T(8,128)(2,1)S(1)}, bf16[160,960]{1,0:T(8,128)(2,1)}, u32[]{:S(2)}) copy-start(bf16[160,960]{1,0:T(8,128)(2,1)} %param.26) | copy-start | bytes 921604
  16.9 3.7 %copy-start.9 = (bf16[160,320]{1,0:T(8,128)(2,1)S(1)}, bf16[160,320]{1,0:T(8,128)(2,1)}, u32[]{:S(2)}) copy-start(bf16[160,320]{1,0:T(8,128)(2,1)} %param.27) | copy-start | bytes 307204
  19.4 2.2 copy-start.4
  19.4 2.2 copy-start.5
  19.6 2.9 copy-start.11
  25.3 56.3 %collective-permute-start.10 = (bf16[160,1280]{1,0:T(8,128)(2,1)}, bf16[160,1280]{1,0:T(8,128)(2,1)S(1)}, u32[]{:S(2)}, u32[]{:S(2)}) collective-permute-start(bf16[160,1280]{1,0:T(8,128)(2,1)} %pad_maximum_fusion.7), channel_id=1, source_target_pairs={{0,24},{1,25},{2,26},{3,27},{4,28},{5,29},{6,30},{7,31},{8,16},{9,... | collective-permute-start | bytes 1228808 | tf_op jit(solution)/shard_map/ppermute | solution.py:41
  37.5 0.8 copy-start
  38.3 41.7 %collective-permute-start.9 = (bf16[160,1280]{1,0:T(8,128)(2,1)}, bf16[160,1280]{1,0:T(8,128)(2,1)S(1)}, u32[]{:S(2)}, u32[]{:S(2)}) collective-permute-start(bf16[160,1280]{1,0:T(8,128)(2,1)} %get-tuple-element.49), channel_id=1, source_target_pairs={{0,16},{1,17},{2,18},{3,19},{4,20},{5,21},{6,22},{7,23},{8,24},{9,... | collective-permute-start | bytes 1228808 | tf_op jit(solution)/shard_map/ppermute | solution.py:41
  40.7 44.5 %collective-permute-start.4 = (bf16[480,1280]{1,0:T(8,128)(2,1)}, bf16[480,1280]{1,0:T(8,128)(2,1)}, u32[]{:S(2)}, u32[]{:S(2)}) collective-permute-start(bf16[480,1280]{1,0:T(8,128)(2,1)} %pad_maximum_fusion), channel_id=1, source_target_pairs={{0,4},{1,5},{2,6},{3,7},{4,0},{5,1},{6,2},{7,3},{8,12},{9,13},{10,... | collective-permute-start | bytes 3686408 | tf_op jit(solution)/shard_map/ppermute | solution.py:37
  50.1 109.8 %collective-permute-start.11 = (bf16[160,1280]{1,0:T(8,128)(2,1)}, bf16[160,1280]{1,0:T(8,128)(2,1)}, u32[]{:S(2)}, u32[]{:S(2)}) collective-permute-start(bf16[160,1280]{1,0:T(8,128)(2,1)} %get-tuple-element.49), channel_id=1, source_target_pairs={{0,4},{1,5},{2,6},{3,7},{4,0},{5,1},{6,2},{7,3},{8,12},{9,13},{10,... | collective-permute-start | bytes 1228808 | tf_op jit(solution)/shard_map/ppermute | solution.py:37
  52.7 47.9 %collective-permute-start.19 = (bf16[160,1280]{1,0:T(8,128)(2,1)}, bf16[160,1280]{1,0:T(8,128)(2,1)}, u32[]{:S(2)}, u32[]{:S(2)}) collective-permute-start(bf16[160,1280]{1,0:T(8,128)(2,1)} %param.25), channel_id=1, source_target_pairs={{0,8},{1,9},{2,10},{3,11},{4,12},{5,13},{6,14},{7,15},{8,0},{9,1},... | collective-permute-start | bytes 1228808 | tf_op jit(solution)/shard_map/ppermute | solution.py:41
  80.0 30.5 %collective-permute-start.20 = (bf16[160,1280]{1,0:T(8,128)(2,1)}, bf16[160,1280]{1,0:T(8,128)(2,1)}, u32[]{:S(2)}, u32[]{:S(2)}) collective-permute-start(bf16[160,1280]{1,0:T(8,128)(2,1)} %param.25), channel_id=1, source_target_pairs={{0,16},{1,17},{2,18},{3,19},{4,20},{5,21},{6,22},{7,23},{8,24},{9,... | collective-permute-start | bytes 1228808 | tf_op jit(solution)/shard_map/ppermute | solution.py:41
  81.5 29.0 %collective-permute-start.21 = (bf16[160,1280]{1,0:T(8,128)(2,1)}, bf16[160,1280]{1,0:T(8,128)(2,1)}, u32[]{:S(2)}, u32[]{:S(2)}) collective-permute-start(bf16[160,1280]{1,0:T(8,128)(2,1)} %param.25), channel_id=1, source_target_pairs={{0,24},{1,25},{2,26},{3,27},{4,28},{5,29},{6,30},{7,31},{8,16},{9,... | collective-permute-start | bytes 1228808 | tf_op jit(solution)/shard_map/ppermute | solution.py:41
  85.2 32.3 %collective-permute-start.27 = (bf16[160,1280]{1,0:T(8,128)(2,1)}, bf16[160,1280]{1,0:T(8,128)(2,1)}, u32[]{:S(2)}, u32[]{:S(2)}) collective-permute-start(bf16[160,1280]{1,0:T(8,128)(2,1)} %get-tuple-element.10), channel_id=1, source_target_pairs={{0,8},{1,9},{2,10},{3,11},{4,12},{5,13},{6,14},{7,15},{8,0},{9,1},... | collective-permute-start | bytes 1228808 | tf_op jit(solution)/shard_map/ppermute | solution.py:41
  100.6 16.8 %copy-start.6 = (bf16[160,1280]{1,0:T(8,128)(2,1)S(1)}, bf16[160,1280]{1,0:T(8,128)(2,1)}, u32[]{:S(2)}) copy-start(bf16[160,1280]{1,0:T(8,128)(2,1)} %param.25) | copy-start | bytes 1228804
  100.6 13.4 %collective-permute-start.5 = (bf16[128,1280]{1,0:T(8,128)(2,1)S(1)}, bf16[128,1280]{1,0:T(8,128)(2,1)S(1)}, u32[]{:S(2)}, u32[]{:S(2)}) collective-permute-start(bf16[128,1280]{1,0:T(8,128)(2,1)S(1)} %dynamic-slice_bitcast_fusion), channel_id=1, source_target_pairs={{0,1},{1,0},{2,3},{3,2},{4,5},{5,4},{6,7},{7,6},{8,9},{9,8},{10,11... | collective-permute-start | bytes 983048 | tf_op jit(solution)/shard_map/ppermute | solution.py:29
  110.5 34.0 %collective-permute-start.28 = (bf16[160,1280]{1,0:T(8,128)(2,1)}, bf16[160,1280]{1,0:T(8,128)(2,1)S(1)}, u32[]{:S(2)}, u32[]{:S(2)}) collective-permute-start(bf16[160,1280]{1,0:T(8,128)(2,1)} %get-tuple-element.10), channel_id=1, source_target_pairs={{0,16},{1,17},{2,18},{3,19},{4,20},{5,21},{6,22},{7,23},{8,24},{9,... | collective-permute-start | bytes 1228808 | tf_op jit(solution)/shard_map/ppermute | solution.py:41
  110.5 35.5 %collective-permute-start.29 = (bf16[160,1280]{1,0:T(8,128)(2,1)}, bf16[160,1280]{1,0:T(8,128)(2,1)S(1)}, u32[]{:S(2)}, u32[]{:S(2)}) collective-permute-start(bf16[160,1280]{1,0:T(8,128)(2,1)} %get-tuple-element.10), channel_id=1, source_target_pairs={{0,24},{1,25},{2,26},{3,27},{4,28},{5,29},{6,30},{7,31},{8,16},{9,... | collective-permute-start | bytes 1228808 | tf_op jit(solution)/shard_map/ppermute | solution.py:41
  114.0 34.7 %copy-start.1 = (bf16[2,2,64,1280]{3,2,1,0:T(8,128)(2,1)S(1)}, bf16[2,2,64,1280]{3,2,1,0:T(8,128)(2,1)}, u32[]{:S(2)}) copy-start(bf16[2,2,64,1280]{3,2,1,0:T(8,128)(2,1)} %copy.145) | copy-start | bytes 1966084
  114.0 34.6 %collective-permute-start.6 = (bf16[128,1280]{1,0:T(8,128)(2,1)S(1)}, bf16[128,1280]{1,0:T(8,128)(2,1)S(1)}, u32[]{:S(2)}, u32[]{:S(2)}) collective-permute-start(bf16[128,1280]{1,0:T(8,128)(2,1)S(1)} %fusion.76), channel_id=1, source_target_pairs={{0,2},{1,3},{2,0},{3,1},{4,6},{5,7},{6,4},{7,5},{8,10},{9,11},{10,... | collective-permute-start | bytes 983048 | tf_op jit(solution)/shard_map/ppermute | solution.py:33
  117.4 51.5 %collective-permute-start.22 = (bf16[160,1280]{1,0:T(8,128)(2,1)S(1)}, bf16[160,1280]{1,0:T(8,128)(2,1)}, u32[]{:S(2)}, u32[]{:S(2)}) collective-permute-start(bf16[160,1280]{1,0:T(8,128)(2,1)S(1)} %copy-done.6), channel_id=1, source_target_pairs={{0,4},{1,5},{2,6},{3,7},{4,0},{5,1},{6,2},{7,3},{8,12},{9,13},{10,... | collective-permute-start | bytes 1228808 | tf_op jit(solution)/shard_map/ppermute | solution.py:37
  144.5 93.0 %collective-permute-start.30 = (bf16[160,1280]{1,0:T(8,128)(2,1)}, bf16[160,1280]{1,0:T(8,128)(2,1)}, u32[]{:S(2)}, u32[]{:S(2)}) collective-permute-start(bf16[160,1280]{1,0:T(8,128)(2,1)} %get-tuple-element.10), channel_id=1, source_target_pairs={{0,4},{1,5},{2,6},{3,7},{4,0},{5,1},{6,2},{7,3},{8,12},{9,13},{10,... | collective-permute-start | bytes 1228808 | tf_op jit(solution)/shard_map/ppermute | solution.py:37
  146.0 35.0 %collective-permute-start.12 = (bf16[480,1280]{1,0:T(8,128)(2,1)}, bf16[480,1280]{1,0:T(8,128)(2,1)}, u32[]{:S(2)}, u32[]{:S(2)}) collective-permute-start(bf16[480,1280]{1,0:T(8,128)(2,1)} %pad_maximum_fusion.1), channel_id=1, source_target_pairs={{0,4},{1,5},{2,6},{3,7},{4,0},{5,1},{6,2},{7,3},{8,12},{9,13},{10,... | collective-permute-start | bytes 3686408 | tf_op jit(solution)/shard_map/ppermute | solution.py:37
  150.0 16.9 %collective-permute-start.14 = (bf16[128,1280]{1,0:T(8,128)(2,1)}, bf16[128,1280]{1,0:T(8,128)(2,1)S(1)}, u32[]{:S(2)}, u32[]{:S(2)}) collective-permute-start(bf16[128,1280]{1,0:T(8,128)(2,1)} %fusion.49), channel_id=1, source_target_pairs={{0,8},{1,9},{2,10},{3,11},{4,12},{5,13},{6,14},{7,15},{8,0},{9,1},... | collective-permute-start | bytes 983048 | tf_op jit(solution)/shard_map/ppermute | solution.py:41
  159.9 115.1 %collective-permute-start.35 = (bf16[160,1280]{1,0:T(8,128)(2,1)}, bf16[160,1280]{1,0:T(8,128)(2,1)S(1)}, u32[]{:S(2)}, u32[]{:S(2)}) collective-permute-start(bf16[160,1280]{1,0:T(8,128)(2,1)} %pad_maximum_fusion.10), channel_id=1, source_target_pairs={{0,8},{1,9},{2,10},{3,11},{4,12},{5,13},{6,14},{7,15},{8,0},{9,1},... | collective-permute-start | bytes 1228808 | tf_op jit(solution)/shard_map/ppermute | solution.py:41
  166.9 108.2 %collective-permute-start.37 = (bf16[160,1280]{1,0:T(8,128)(2,1)}, bf16[160,1280]{1,0:T(8,128)(2,1)S(1)}, u32[]{:S(2)}, u32[]{:S(2)}) collective-permute-start(bf16[160,1280]{1,0:T(8,128)(2,1)} %pad_maximum_fusion.10), channel_id=1, source_target_pairs={{0,24},{1,25},{2,26},{3,27},{4,28},{5,29},{6,30},{7,31},{8,16},{9,... | collective-permute-start | bytes 1228808 | tf_op jit(solution)/shard_map/ppermute | solution.py:41
  168.9 16.1 %collective-permute-start.15 = (bf16[128,1280]{1,0:T(8,128)(2,1)S(1)}, bf16[128,1280]{1,0:T(8,128)(2,1)S(1)}, u32[]{:S(2)}, u32[]{:S(2)}) collective-permute-start(bf16[128,1280]{1,0:T(8,128)(2,1)S(1)} %copy.167), channel_id=1, source_target_pairs={{0,1},{1,0},{2,3},{3,2},{4,5},{5,4},{6,7},{7,6},{8,9},{9,8},{10,11... | collective-permute-start | bytes 983048 | tf_op jit(solution)/shard_map/ppermute | solution.py:29
  181.0 32.7 %collective-permute-start.23 = (bf16[480,1280]{1,0:T(8,128)(2,1)}, bf16[480,1280]{1,0:T(8,128)(2,1)}, u32[]{:S(2)}, u32[]{:S(2)}) collective-permute-start(bf16[480,1280]{1,0:T(8,128)(2,1)} %pad_maximum_fusion.2), channel_id=1, source_target_pairs={{0,4},{1,5},{2,6},{3,7},{4,0},{5,1},{6,2},{7,3},{8,12},{9,13},{10,... | collective-permute-start | bytes 3686408 | tf_op jit(solution)/shard_map/ppermute | solution.py:37
  185.0 5.9 %collective-permute-start.7 = (bf16[128,1280]{1,0:T(8,128)(2,1)}, bf16[128,1280]{1,0:T(8,128)(2,1)}, u32[]{:S(2)}, u32[]{:S(2)}) collective-permute-start(bf16[128,1280]{1,0:T(8,128)(2,1)} %fusion.49), channel_id=1, source_target_pairs={{0,1},{1,0},{2,3},{3,2},{4,5},{5,4},{6,7},{7,6},{8,9},{9,8},{10,11... | collective-permute-start | bytes 983048 | tf_op jit(solution)/shard_map/ppermute | solution.py:29
  190.9 2.9 collective-permute-start.16
  194.6 15.0 %collective-permute-start.17 = (bf16[128,1280]{0,1:T(8,128)(2,1)}, bf16[128,1280]{0,1:T(8,128)(2,1)}, u32[]{:S(2)}, u32[]{:S(2)}) collective-permute-start(bf16[128,1280]{0,1:T(8,128)(2,1)} %fusion.75), channel_id=1, source_target_pairs={{0,8},{1,9},{2,10},{3,11},{4,12},{5,13},{6,14},{7,15},{8,0},{9,1},... | collective-permute-start | bytes 983048 | tf_op jit(solution)/shard_map/ppermute | solution.py:41
  209.6 1.6 collective-permute-start.13
  211.2 63.9 %collective-permute-start.36 = (bf16[160,1280]{1,0:T(8,128)(2,1)}, bf16[160,1280]{1,0:T(8,128)(2,1)S(1)}, u32[]{:S(2)}, u32[]{:S(2)}) collective-permute-start(bf16[160,1280]{1,0:T(8,128)(2,1)} %get-tuple-element.55), channel_id=1, source_target_pairs={{0,16},{1,17},{2,18},{3,19},{4,20},{5,21},{6,22},{7,23},{8,24},{9,... | collective-permute-start | bytes 1228808 | tf_op jit(solution)/shard_map/ppermute | solution.py:41
  213.8 6.0 %collective-permute-start.18 = (bf16[64,1280]{1,0:T(8,128)(2,1)S(1)}, bf16[64,1280]{1,0:T(8,128)(2,1)S(1)}, u32[]{:S(2)}, u32[]{:S(2)}) collective-permute-start(bf16[64,1280]{1,0:T(8,128)(2,1)S(1)} %dynamic-slice_bitcast_fusion.1), channel_id=1, source_target_pairs={{0,2},{1,3},{2,0},{3,1},{4,6},{5,7},{6,4},{7,5},{8,10},{9,11},{10,... | collective-permute-start | bytes 491528 | tf_op jit(solution)/shard_map/ppermute | solution.py:33
  224.3 1.9 collective-permute-start.24
  226.1 37.5 %copy-start.8 = (bf16[192,1280]{1,0:T(8,128)(2,1)S(1)}, bf16[192,1280]{1,0:T(8,128)(2,1)}, u32[]{:S(2)}) copy-start(bf16[192,1280]{1,0:T(8,128)(2,1)} %param.17) | copy-start | bytes 1474564
  226.2 4.9 %collective-permute-start.25 = (bf16[64,640]{1,0:T(8,128)(2,1)S(1)}, bf16[64,640]{1,0:T(8,128)(2,1)S(1)}, u32[]{:S(2)}, u32[]{:S(2)}) collective-permute-start(bf16[64,640]{1,0:T(8,128)(2,1)S(1)} %fusion.273), channel_id=1, source_target_pairs={{0,2},{1,3},{2,0},{3,1},{4,6},{5,7},{6,4},{7,5},{8,10},{9,11},{10,... | collective-permute-start | bytes 245768 | tf_op jit(solution)/shard_map/ppermute | solution.py:33
  231.1 32.8 %collective-permute-start.31 = (bf16[480,1280]{1,0:T(8,128)(2,1)}, bf16[480,1280]{1,0:T(8,128)(2,1)}, u32[]{:S(2)}, u32[]{:S(2)}) collective-permute-start(bf16[480,1280]{1,0:T(8,128)(2,1)} %pad_maximum_fusion.3), channel_id=1, source_target_pairs={{0,4},{1,5},{2,6},{3,7},{4,0},{5,1},{6,2},{7,3},{8,12},{9,13},{10,... | collective-permute-start | bytes 3686408 | tf_op jit(solution)/shard_map/ppermute | solution.py:37
  232.5 30.8 %all-to-all-start = ((bf16[8,12,768]{2,1,0:T(8,128)(2,1)}), bf16[8,12,768]{2,1,0:T(8,128)(2,1)S(1)}, u32[]{:S(2)}, u32[]{:S(2)}) async-start(bf16[8,12,768]{2,1,0:T(8,128)(2,1)} %reshape.369), calls=%async_computation | async-start | bytes 393216 | tf_op jit(solution)/shard_map/all_to_all | solution.py:304
  237.4 51.5 %collective-permute-start.38 = (bf16[160,1280]{1,0:T(8,128)(2,1)}, bf16[160,1280]{1,0:T(8,128)(2,1)}, u32[]{:S(2)}, u32[]{:S(2)}) collective-permute-start(bf16[160,1280]{1,0:T(8,128)(2,1)} %get-tuple-element.55), channel_id=1, source_target_pairs={{0,4},{1,5},{2,6},{3,7},{4,0},{5,1},{6,2},{7,3},{8,12},{9,13},{10,... | collective-permute-start | bytes 1228808 | tf_op jit(solution)/shard_map/ppermute | solution.py:37
  263.9 2.5 collective-permute-start.26
  274.5 3.3 collective-permute-start.32
  276.2 29.3 %collective-permute-start.39 = (bf16[480,1280]{1,0:T(8,128)(2,1)}, bf16[480,1280]{1,0:T(8,128)(2,1)}, u32[]{:S(2)}, u32[]{:S(2)}) collective-permute-start(bf16[480,1280]{1,0:T(8,128)(2,1)} %pad_maximum_fusion.4), channel_id=1, source_target_pairs={{0,4},{1,5},{2,6},{3,7},{4,0},{5,1},{6,2},{7,3},{8,12},{9,13},{10,... | collective-permute-start | bytes 3686408 | tf_op jit(solution)/shard_map/ppermute | solution.py:37
  277.9 9.4 %collective-permute-start.33 = (bf16[96,1280]{0,1:T(8,128)(2,1)S(1)}, bf16[96,1280]{0,1:T(8,128)(2,1)S(1)}, u32[]{:S(2)}, u32[]{:S(2)}) collective-permute-start(bf16[96,1280]{0,1:T(8,128)(2,1)S(1)} %fusion.72), channel_id=1, source_target_pairs={{0,2},{1,3},{2,0},{3,1},{4,6},{5,7},{6,4},{7,5},{8,10},{9,11},{10,... | collective-permute-start | bytes 737288 | tf_op jit(solution)/shard_map/ppermute | solution.py:33
  287.8 8.7 %collective-permute-start.41 = (bf16[96,1280]{0,1:T(8,128)(2,1)S(1)}, bf16[96,1280]{0,1:T(8,128)(2,1)S(1)}, u32[]{:S(2)}, u32[]{:S(2)}) collective-permute-start(bf16[96,1280]{0,1:T(8,128)(2,1)S(1)} %fusion.47), channel_id=1, source_target_pairs={{0,8},{1,9},{2,10},{3,11},{4,12},{5,13},{6,14},{7,15},{8,0},{9,1},... | collective-permute-start | bytes 737288 | tf_op jit(solution)/shard_map/ppermute | solution.py:41
  296.5 11.4 %collective-permute-start.42 = (bf16[96,1280]{0,1:T(8,128)(2,1)S(1)}, bf16[96,1280]{0,1:T(8,128)(2,1)S(1)}, u32[]{:S(2)}, u32[]{:S(2)}) collective-permute-start(bf16[96,1280]{0,1:T(8,128)(2,1)S(1)} %bitcast.184), channel_id=1, source_target_pairs={{0,1},{1,0},{2,3},{3,2},{4,5},{5,4},{6,7},{7,6},{8,9},{9,8},{10,11... | collective-permute-start | bytes 737288 | tf_op jit(solution)/shard_map/ppermute | solution.py:29
  307.9 5.2 %collective-permute-start.34 = (bf16[96,1280]{0,1:T(8,128)(2,1)S(1)}, bf16[96,1280]{0,1:T(8,128)(2,1)S(1)}, u32[]{:S(2)}, u32[]{:S(2)}) collective-permute-start(bf16[96,1280]{0,1:T(8,128)(2,1)S(1)} %fusion.47), channel_id=1, source_target_pairs={{0,1},{1,0},{2,3},{3,2},{4,5},{5,4},{6,7},{7,6},{8,9},{9,8},{10,11... | collective-permute-start | bytes 737288 | tf_op jit(solution)/shard_map/ppermute | solution.py:29
  312.5 1.8 collective-permute-start.43
  314.4 10.1 %collective-permute-start.44 = (bf16[96,1280]{0,1:T(8,128)(2,1)S(1)}, bf16[96,1280]{0,1:T(8,128)(2,1)S(1)}, u32[]{:S(2)}, u32[]{:S(2)}) collective-permute-start(bf16[96,1280]{0,1:T(8,128)(2,1)S(1)} %fusion.71), channel_id=1, source_target_pairs={{0,8},{1,9},{2,10},{3,11},{4,12},{5,13},{6,14},{7,15},{8,0},{9,1},... | collective-permute-start | bytes 737288 | tf_op jit(solution)/shard_map/ppermute | solution.py:41
  319.3 5.3 %collective-permute-start.40 = (bf16[96,1280]{0,1:T(8,128)(2,1)S(1)}, bf16[96,1280]{0,1:T(8,128)(2,1)S(1)}, u32[]{:S(2)}, u32[]{:S(2)}) collective-permute-start(bf16[96,1280]{0,1:T(8,128)(2,1)S(1)} %bitcast.192), channel_id=1, source_target_pairs={{0,1},{1,0},{2,3},{3,2},{4,5},{5,4},{6,7},{7,6},{8,9},{9,8},{10,11... | collective-permute-start | bytes 737288 | tf_op jit(solution)/shard_map/ppermute | solution.py:29
  324.8 9.2 %collective-permute-start.45 = (bf16[96,1280]{0,1:T(8,128)(2,1)S(1)}, bf16[96,1280]{0,1:T(8,128)(2,1)S(1)}, u32[]{:S(2)}, u32[]{:S(2)}) collective-permute-start(bf16[96,1280]{0,1:T(8,128)(2,1)S(1)} %fusion.70), channel_id=1, source_target_pairs={{0,2},{1,3},{2,0},{3,1},{4,6},{5,7},{6,4},{7,5},{8,10},{9,11},{10,... | collective-permute-start | bytes 737288 | tf_op jit(solution)/shard_map/ppermute | solution.py:33
  334.3 1.7 collective-permute-start.46

commit v2 on v1

--- a/solution.py
+++ b/solution.py
@@ -95,34 +95,60 @@
     return lax.all_gather(weight, "req", axis=0, tiled=True, axis_index_groups=members)
 
 
-def gather_blocks(parts):
-    column = [parts[0]] + [swap_z(parts[k], k) for k in (1, 2, 3)]
-    other_own = swap_y(column[0])
-    other_rest = swap_y(jnp.concatenate(column[1:], axis=0))
-    return jnp.concatenate(column + [other_own, other_rest], axis=0)
-
-
-def gather_same(weight):
-    return gather_blocks([weight] * 4)
-
-
-def gather_halved(w_up, w_down_t):
-    z, _, _, _ = place()
-    half = w_up.shape[1] // 2
-    parts = []
-    for bit in (0, 1):
-        start = ((z % 2) ^ bit) * half
-        parts.append(
-            jnp.concatenate(
-                [
-                    lax.dynamic_slice_in_dim(w_up, start, half, 1),
-                    lax.dynamic_slice_in_dim(w_down_t, start, half, 1),
-                ],
-                axis=1,
+def together(*values):
+    return lax.optimization_barrier(values)
+
+
+class Same:
+    def __init__(self, weight):
+        self.own = weight
+        self.first = swap_z(weight, 1)
+        self.second = swap_z(weight, 2)
+        self.y_own = swap_y(weight)
+
+    def forward(self):
+        self.third = swap_z(self.second, 1)
+        self.y_early = swap_y(jnp.concatenate([self.first, self.second], axis=0))
+
+    def finish(self):
+        y_third = swap_y(self.third)
+        return jnp.concatenate(
+            [self.own, self.first, self.second, self.third, self.y_own, self.y_early, y_third], axis=0
+        )
+
+
+class Halved:
+    def __init__(self, w_up, w_down_t):
+        z, _, _, _ = place()
+        half = w_up.shape[1] // 2
+        parts = []
+        for bit in (0, 1):
+            start = ((z % 2) ^ bit) * half
+            parts.append(
+                jnp.concatenate(
+                    [
+                        lax.dynamic_slice_in_dim(w_up, start, half, 1),
+                        lax.dynamic_slice_in_dim(w_down_t, start, half, 1),
+                    ],
+                    axis=1,
+                )
             )
+        self.half = half
+        self.own = parts[0]
+        self.first = swap_z(parts[1], 1)
+        self.second = swap_z(parts[0], 2)
+        self.third = swap_z(parts[1], 3)
+        self.y_own = swap_y(parts[0])
+
+    def forward(self):
+        self.y_early = swap_y(jnp.concatenate([self.first, self.second], axis=0))
+
+    def finish(self):
+        y_third = swap_y(self.third)
+        both = jnp.concatenate(
+            [self.own, self.first, self.second, self.third, self.y_own, self.y_early, y_third], axis=0
         )
-    both = gather_blocks([parts[0], parts[1], parts[0], parts[1]])
-    return both[:, :half], both[:, half:]
+        return both[:, : self.half], both[:, self.half :]
 
 
 def pick(rows, which, axis):
@@ -188,20 +214,25 @@
     ).astype(jnp.bfloat16)
 
 
-def paired_feed_forward(mid_half, w_up, w_down_t):
-    normed_half = normalize(mid_half)
-    pair_half = from_pair_order(swap_z(normed_half, 1))
-    own = feed_forward(join_core(normed_half, 0), w_up, w_down_t)
-    pair = feed_forward(join_core(pair_half, 0), w_up, w_down_t)
-    return own, pair
-
-
-def sum_pair(own, pair):
+def sum_core(values):
     _, _, _, c = place()
-    pair_mine = add_short(pick(pair, c, 0), swap_core(pick(pair, 1 - c, 0))).astype(jnp.bfloat16)
-    arrived = from_pair_order(swap_z(pair_mine, 1))
-    own_mine = add_short(pick(own, c, 0), swap_core(pick(own, 1 - c, 0)))
-    return (own_mine + arrived.astype(jnp.float32)).astype(jnp.bfloat16)
+    return add_short(pick(values, c, 0), swap_core(pick(values, 1 - c, 0)))
+
+
+def exchange_blocks(blocks):
+    z, y, _, _ = place()
+    groups = blocks.shape[1]
+    if groups > 1:
+        members = [[i * groups + g for g in range(groups)] for i in range(8)]
+        blocks = lax.all_to_all(
+            blocks, "req", split_axis=1, concat_axis=1, tiled=True, axis_index_groups=members
+        )
+    blocks = blocks.reshape((4, 2) + blocks.shape[1:])
+    kept = pick(blocks, y, 1)
+    other = swap_y(pick(blocks, 1 - y, 1))
+    both = jnp.stack([kept, other], axis=1)
+    mixed = [pick(both, z, 0)] + [swap_z(pick(both, z ^ k, 0), k) for k in (1, 2, 3)]
+    return jnp.concatenate(mixed, axis=0)
 
 
 def on_device(
@@ -229,11 +260,16 @@
     slot_count = image_count * cells
     qkv_width = enc_qkv.shape[1]
 
-    enc_attn = gather_same(own_rows(jnp.concatenate([enc_qkv, enc_out_t], axis=1)))
-    enc_ff = gather_halved(own_rows(enc_up), own_rows(enc_down_t))
-    merge_all = gather_same(own_rows(merge_t))
-    dec_attn = gather_same(own_rows(jnp.concatenate([dec_qkv, dec_out_t], axis=1)))
-    dec_ff = gather_halved(own_rows(dec_up), own_rows(dec_down_t))
+    enc_attn = Same(own_rows(jnp.concatenate([enc_qkv, enc_out_t], axis=1)))
+    enc_up, enc_down_t = own_rows(enc_up), own_rows(enc_down_t)
+    merge_t = own_rows(merge_t)
+    dec_attn = own_rows(jnp.concatenate([dec_qkv, dec_out_t], axis=1))
+    dec_up, dec_down_t = own_rows(dec_up), own_rows(dec_down_t)
+
+    enc_attn.second, enc_up, enc_down_t = together(enc_attn.second, enc_up, enc_down_t)
+    enc_attn.forward()
+    enc_ff = Halved(enc_up, enc_down_t)
+    w_enc_attn = enc_attn.finish()
 
     cell_index = jnp.arange(cells, dtype=jnp.int32)
     slot_valid = ((cell_index // HALF)[None, :] < half_grid[:, 0:1]) & (
@@ -259,24 +295,49 @@
 
     attended = attention(
         normalize(rows),
-        enc_attn[:, :qkv_width],
-        enc_attn[:, qkv_width:],
+        w_enc_attn[:, :qkv_width],
+        w_enc_attn[:, qkv_width:],
         key_valid[:, None, None, :],
         by_image,
         by_place,
     )
     mid_half = middle_half(halves(rows), halves(attended))
-    own, pair = paired_feed_forward(mid_half, *enc_ff)
-    total = sum_pair(
-        own.reshape(2, 2 * slot_count, model_width), pair.reshape(2, 2 * slot_count, model_width)
-    ).reshape(2, slot_count, model_width)
+    normed_half = normalize(mid_half)
+    normed_half, enc_ff.first, enc_ff.second, enc_ff.third, merge_t = together(
+        normed_half, enc_ff.first, enc_ff.second, enc_ff.third, merge_t
+    )
+    pair_half = swap_z(normed_half, 1)
+    enc_ff.forward()
+    w_enc_ff = enc_ff.finish()
+    merge_all = Same(merge_t)
+    own = feed_forward(join_core(normed_half, 0), *w_enc_ff)
+    pair_rows = join_core(from_pair_order(pair_half), 0)
+    pair_rows, merge_all.first, merge_all.second = together(
+        pair_rows, merge_all.first, merge_all.second
+    )
+    merge_all.forward()
+    pair = feed_forward(pair_rows, *w_enc_ff)
+    pair = pair.reshape(2, 2 * slot_count, model_width)
+    pair_mine = sum_core(pair).astype(jnp.bfloat16)
+    pair_mine, dec_attn = together(pair_mine, dec_attn)
+    arrived = swap_z(pair_mine, 1)
+    dec_attn = Same(dec_attn)
+    own_mine = sum_core(own.reshape(2, 2 * slot_count, model_width))
+    arrived, merge_all.third = together(arrived, merge_all.third)
+    w_merge = merge_all.finish()
+    total = own_mine + from_pair_order(arrived).astype(jnp.float32)
+    total = total.astype(jnp.bfloat16).reshape(2, slot_count, model_width)
     total = add_short(pick(total, x, 0), swap_x(pick(total, 1 - x, 0)))
     kept = pick(mid_half.reshape(2, slot_count, model_width), x, 0)
     encoded = (kept.astype(jnp.float32) + total).astype(jnp.bfloat16)
 
+    encoded, dec_attn.first, dec_attn.second = together(
+        encoded, dec_attn.first, dec_attn.second
+    )
+    dec_attn.forward()
     partial_merge = lax.dot_general(
         to_plain_order(encoded),
-        merge_all,
+        w_merge,
         (((1,), (1,)), ((), ())),
         preferred_element_type=jnp.float32,
     )
@@ -301,9 +362,12 @@
         jnp.concatenate([merged, digits], axis=1),
         preferred_element_type=jnp.float32,
     ).astype(jnp.bfloat16)
-    incoming = lax.all_to_all(
-        outgoing.reshape(senders, capacity, -1), "req", split_axis=0, concat_axis=0, tiled=True
-    ).reshape(senders * capacity, -1)
+    outgoing, dec_up, dec_down_t = together(outgoing, dec_up, dec_down_t)
+    incoming = exchange_blocks(outgoing.reshape(8, senders // 8, capacity, -1))
+    dec_ff = Halved(dec_up, dec_down_t)
+    incoming, dec_attn.third = together(incoming, dec_attn.third)
+    w_dec_attn = dec_attn.finish()
+    incoming = incoming.reshape(senders * capacity, -1)
 
     seq_len = text_embed.shape[0]
     positions = jnp.arange(seq_len, dtype=jnp.int32)
@@ -320,18 +384,27 @@
     causal = (positions[:, None] >= positions[None, :])[None, None]
     attended = attention(
         normalize(dec_rows),
-        dec_attn[:, :qkv_width],
-        dec_attn[:, qkv_width:],
+        w_dec_attn[:, :qkv_width],
+        w_dec_attn[:, qkv_width:],
         causal,
         lambda value: value[None],
         lambda value: value[0],
     )
     mid_half = middle_half(dec_rows, attended)
-    own, pair = paired_feed_forward(mid_half, *dec_ff)
+    normed_half = normalize(mid_half)
+    normed_half, dec_ff.first, dec_ff.second, dec_ff.third = together(
+        normed_half, dec_ff.first, dec_ff.second, dec_ff.third
+    )
+    pair_half = swap_z(normed_half, 1)
+    dec_ff.forward()
+    w_dec_ff = dec_ff.finish()
     half_rows = seq_len // 2
-    total = sum_pair(
-        own.reshape(2, half_rows, model_width), pair.reshape(2, half_rows, model_width)
-    )
+    own = feed_forward(join_core(normed_half, 0), *w_dec_ff)
+    pair = feed_forward(join_core(from_pair_order(pair_half), 0), *w_dec_ff)
+    pair_mine = sum_core(pair.reshape(2, half_rows, model_width)).astype(jnp.bfloat16)
+    arrived = swap_z(pair_mine, 1)
+    own_mine = sum_core(own.reshape(2, half_rows, model_width))
+    total = (own_mine + from_pair_order(arrived).astype(jnp.float32)).astype(jnp.bfloat16)
     total = add_short(total, swap_x(total))
     decoded = (mid_half.astype(jnp.float32) + total).astype(jnp.bfloat16)
     keep_mask = positions < slot_count + text_len[0]

time: 339 us -> 376 us (1.11)
  waiting for transfers between devices: 127 us -> 175 us
  starting transfers between devices: 82.9 us -> 56.9 us
  local copies, waits for them, and re-layouts: 67 us -> 77.9 us
    ppermute x10 -> x16, waiting for transfers between devices: 19.1 us -> 55 us  [swap_y(): return lax.ppermute(part, AXES, routes(lambda z, y, x, c: (z, 1 - y, x, c)))]
    ppermute x19 -> x22, starting transfers between devices: 60.6 us -> 27 us  [swap_z(): return lax.ppermute(part, AXES, routes(lambda z, y, x, c: (z ^ k, y, x, c)))]
    ppermute x19 -> x22, waiting for transfers between devices: 60.5 us -> 93.3 us  [swap_z(): return lax.ppermute(part, AXES, routes(lambda z, y, x, c: (z ^ k, y, x, c)))]
    all_to_all x1 -> x0, waiting for transfers between devices: 22 us -> none  [on_device(): lax.all_to_all(outgoing.reshape(senders, capacity, -1), 'req', split_axis...]
    ppermute x10 -> x16, starting transfers between devices: 11.9 us -> 24.9 us  [swap_y(): return lax.ppermute(part, AXES, routes(lambda z, y, x, c: (z, 1 - y, x, c)))]
    dynamic_slice x12 -> x16, local copies, waits for them, and re-layouts: 1.67 us -> 9.65 us  [pick(): return lax.dynamic_index_in_dim(rows, which, axis, keepdims=False)]
    concatenate x6, local copies, waits for them, and re-layouts: 17.5 us -> 11.5 us  [the longest x5 10.6 us: finish(): jnp.concatenate([self.own, self.first, self.second, self.third, self.y_ow...]
    unnamed x59 -> x66, local copies, waits for them, and re-layouts: 27.1 us -> 31.3 us
  transfers between devices with their start and end apart: 48 -> 56, of which waited for: 18 -> 31; matrix products, arithmetic and copies ran while one was open for 35% -> 30% of each run, Pallas kernels for 0% -> 0%
where the time goes in v2:
time: 376 us; the launch traced here: 373 us
  waiting for transfers between devices  175 us (47%)
  local copies, waits for them, and re-layouts  77.9 us (21%)
  starting transfers between devices  56.9 us (15%)
  matrix products  33.1 us (9%)
  other arithmetic  28.9 us (8%)
    ppermute x22, waiting for transfers between devices, swap_z(): return lax.ppermute(part, AXES, routes(lambda z, y, x, c: (z ^ k, y, x, c)))  93.3 us
    ppermute x16, waiting for transfers between devices, swap_y(): return lax.ppermute(part, AXES, routes(lambda z, y, x, c: (z, 1 - y, x, c)))  55 us
    unnamed x66, local copies, waits for them, and re-layouts  31.3 us
    ppermute x22, starting transfers between devices, swap_z(): return lax.ppermute(part, AXES, routes(lambda z, y, x, c: (z ^ k, y, x, c)))  27 us
    ppermute x16, starting transfers between devices, swap_y(): return lax.ppermute(part, AXES, routes(lambda z, y, x, c: (z, 1 - y, x, c)))  24.9 us
    ppermute x5, waiting for transfers between devices, swap_x(): return lax.ppermute(part, AXES, routes(lambda z, y, x, c: (z, y, 1 - x, c)))  21.3 us
    dot_general x4, matrix products, feed_forward(): lax.dot_general(hidden, w_down_t, (((1,), (1,)), ((), ())), preferred_ele...  19.6 us
    concatenate x5, local copies, waits for them, and re-layouts, finish(): jnp.concatenate([self.own, self.first, self.second, self.third, self.y_ow...  10.6 us
  transfers between devices with their start and end apart: 56, of which 31 were waited for; matrix products, arithmetic and copies ran while one was open for 30% of the time, Pallas kernels for 0%

profile of v2, /device:TPU:0, one launch (start us, length us, event | category | flops | bytes accessed | tf_op | source)
XLA Modules:
  0.0 373.5 jit_solution(9473582099280803043)
XLA Ops:
  3.4 4.0 %collective-permute-start.1 = (bf16[160,1280]{1,0:T(8,128)(2,1)}, bf16[160,1280]{1,0:T(8,128)(2,1)S(1)}, u32[]{:S(2)}, u32[]{:S(2)}) collective-permute-start(bf16[160,1280]{1,0:T(8,128)(2,1)} %copy.162), channel_id=1, source_target_pairs={{0,16},{1,17},{2,18},{3,19},{4,20},{5,21},{6,22},{7,23},{8,24},{9,... | collective-permute-start | bytes 1228808 | tf_op jit(solution)/shard_map/ppermute | solution.py:41
  14.3 11.7 %collective-permute-done.1 = bf16[160,1280]{1,0:T(8,128)(2,1)S(1)} collective-permute-done((bf16[160,1280]{1,0:T(8,128)(2,1)}, bf16[160,1280]{1,0:T(8,128)(2,1)S(1)}, u32[]{:S(2)}, u32[]{:S(2)}) %collective-permute-start.1) | collective-permute-done | bytes 409632 | tf_op jit(solution)/shard_map/ppermute | solution.py:41
  29.3 7.3 %collective-permute-done.2 = bf16[160,1280]{1,0:T(8,128)(2,1)S(1)} collective-permute-done((bf16[160,1280]{1,0:T(8,128)(2,1)S(1)}, bf16[160,1280]{1,0:T(8,128)(2,1)S(1)}, u32[]{:S(2)}, u32[]{:S(2)}) %collective-permute-start.2) | collective-permute-done | bytes 409632 | tf_op jit(solution)/shard_map/ppermute | solution.py:41
  40.7 1.9 pad_maximum_fusion.10
  43.9 2.1 copy.168
  47.1 2.0 collective-permute-done.4
  50.7 6.0 %collective-permute-done.5 = bf16[160,1280]{1,0:T(8,128)(2,1)} collective-permute-done((bf16[160,1280]{1,0:T(8,128)(2,1)S(1)}, bf16[160,1280]{1,0:T(8,128)(2,1)}, u32[]{:S(2)}, u32[]{:S(2)}) %collective-permute-start.5) | collective-permute-done | bytes 409632 | tf_op jit(solution)/shard_map/ppermute | solution.py:37
  56.6 2.1 copy.170
  58.7 7.0 %concatenate.102 = bf16[1280,1280]{0,1:T(8,128)(2,1)} concatenate(bf16[160,1280]{0,1:T(8,128)(2,1)S(1)} %pad_maximum_fusion.5, bf16[160,1280]{0,1:T(8,128)(2,1)} %copy.165, bf16[160,1280]{0,1:T(8,128)(2,1)S(1)} %copy.166, bf16[160,1280]{0,1:T(8,128)(2,1)} %copy.167, bf16[160,1280]{0,1:T(8,128)(2,1)} %copy.168, bf16[320,1280]{0,1:T(8,128)(2,1)S(1)} %copy.169, bf16[160,1280]{0,1:T(8,128)(2,1)} %copy.170), dimensions={0} | concatenate | bytes 6553600 | tf_op jit(solution)/shard_map/concatenate | solution.py:115
  65.7 2.6 fusion.29
  70.0 1.6 fusion.4
  75.4 4.5 %collective-permute-start.10 = (bf16[160,1280]{1,0:T(8,128)(2,1)S(1)}, bf16[160,1280]{1,0:T(8,128)(2,1)}, u32[]{:S(2)}, u32[]{:S(2)}) collective-permute-start(bf16[160,1280]{1,0:T(8,128)(2,1)S(1)} %pad_maximum_fusion.8), channel_id=1, source_target_pairs={{0,24},{1,25},{2,26},{3,27},{4,28},{5,29},{6,30},{7,31},{8,16},{9,... | collective-permute-start | bytes 1228808 | tf_op jit(solution)/shard_map/ppermute | solution.py:41
  84.8 1.6 collective-permute-done.8
  86.4 27.9 %collective-permute-done.9 = bf16[160,1280]{1,0:T(8,128)(2,1)S(1)} collective-permute-done((bf16[160,1280]{1,0:T(8,128)(2,1)S(1)}, bf16[160,1280]{1,0:T(8,128)(2,1)S(1)}, u32[]{:S(2)}, u32[]{:S(2)}) %collective-permute-start.9) | collective-permute-done | bytes 409632 | tf_op jit(solution)/shard_map/ppermute | solution.py:41
  114.4 2.0 collective-permute-start.18
  120.6 1.8 constant_dynamic-update-slice_fusion.3
  125.4 10.0 %collective-permute-start.26 = (bf16[160,1280]{1,0:T(8,128)(2,1)}, bf16[160,1280]{1,0:T(8,128)(2,1)}, u32[]{:S(2)}, u32[]{:S(2)}) collective-permute-start(bf16[160,1280]{1,0:T(8,128)(2,1)} %param.25), channel_id=1, source_target_pairs={{0,4},{1,5},{2,6},{3,7},{4,0},{5,1},{6,2},{7,3},{8,12},{9,13},{10,... | collective-permute-start | bytes 1228808 | tf_op jit(solution)/shard_map/ppermute | solution.py:37
  135.5 1.9 copy.179
  139.1 1.9 copy.181
  141.0 2.0 broadcast_select_fusion.3
  144.9 2.1 pad_maximum_fusion.2
  147.0 2.0 collective-permute-start.27
  151.0 13.1 %collective-permute-done.13 = bf16[320,1280]{1,0:T(8,128)(2,1)S(1)} collective-permute-done((bf16[320,1280]{1,0:T(8,128)(2,1)}, bf16[320,1280]{1,0:T(8,128)(2,1)S(1)}, u32[]{:S(2)}, u32[]{:S(2)}) %collective-permute-start.13) | collective-permute-done | bytes 819232 | tf_op jit(solution)/shard_map/ppermute | solution.py:37
  165.1 1.8 constant_dynamic-update-slice_fusion
  166.9 5.5 %convolution_convert_fusion = bf16[256,1280]{1,0:T(8,128)(2,1)} fusion(bf16[1280,1280]{1,0:T(8,128)(2,1)} %constant_dynamic-update-slice_fusion, bf16[256,1280]{1,0:T(8,128)(2,1)} %pad_maximum_fusion.6), kind=kOutput, calls=%fused_computation.4 | convolution fusion | flops 849838080 | bytes 4587520 | tf_op jit(solution)/shard_map/dot_general | solution.py:212
  172.4 2.0 constant_dynamic-slice_fusion.31
  174.4 1.9 copy.184
  176.3 5.6 %convolution_convert_fusion.1 = bf16[256,1280]{1,0:T(8,128)(2,1)} fusion(bf16[1280,1280]{1,0:T(8,128)(2,1)} %constant_dynamic-update-slice_fusion, bf16[128,1280]{1,0:T(8,128)(2,1)} %get-tuple-element.76, bf16[128,1280]{1,0:T(8,128)(2,1)} %get-tuple-element.75), kind=kOutput, calls=%fused_computation.5 | convolution fusion | flops 851148800 | bytes 4587520 | tf_op jit(solution)/shard_map/dot_general | solution.py:212
  181.9 1.9 copy.214
  183.7 1.9 fusion.72
  185.6 2.0 constant_dynamic-slice_fusion.33
  187.6 1.9 copy.178
  190.0 1.9 copy.213
  191.9 1.8 constant_dynamic-update-slice_fusion.20
  193.6 1.7 collective-permute-start.24
  198.1 2.0 fusion.71
  200.1 1.9 copy.185
  204.0 2.0 collective-permute-start.28
  208.9 3.6 collective-permute-done.23
  213.5 3.7 collective-permute-done.25
  224.0 1.8 constant_dynamic-update-slice_fusion.19
  225.8 2.4 collective-permute-done.30
  228.6 1.8 constant_dynamic-update-slice_fusion.18
  230.4 2.7 collective-permute-done.31
  233.2 2.1 collective-permute-start.34
  243.2 1.8 constant_dynamic-update-slice_fusion.17
  245.0 1.8 constant_dynamic-update-slice_fusion.16
  250.9 9.5 %collective-permute-done.38 = bf16[320,1280]{1,0:T(8,128)(2,1)S(1)} collective-permute-done((bf16[320,1280]{1,0:T(8,128)(2,1)S(1)}, bf16[320,1280]{1,0:T(8,128)(2,1)S(1)}, u32[]{:S(2)}, u32[]{:S(2)}) %collective-permute-start.38) | collective-permute-done | bytes 819232 | tf_op jit(solution)/shard_map/ppermute | solution.py:37
  261.4 4.0 %collective-permute-done.39 = bf16[160,1280]{1,0:T(8,128)(2,1)S(1)} collective-permute-done((bf16[160,1280]{1,0:T(8,128)(2,1)}, bf16[160,1280]{1,0:T(8,128)(2,1)S(1)}, u32[]{:S(2)}, u32[]{:S(2)}) %collective-permute-start.39) | collective-permute-done | bytes 409632 | tf_op jit(solution)/shard_map/ppermute | solution.py:37
  266.2 2.5 fusion.32
  270.0 2.0 convolution_convert_fusion.5
  274.1 2.1 collective-permute-start.44
  280.6 6.6 %collective-permute-done.41 = bf16[96,1280]{0,1:T(8,128)(2,1)S(1)} collective-permute-done((bf16[96,1280]{0,1:T(8,128)(2,1)S(1)}, bf16[96,1280]{0,1:T(8,128)(2,1)S(1)}, u32[]{:S(2)}, u32[]{:S(2)}) %collective-permute-start.41) | collective-permute-done | bytes 245792 | tf_op jit(solution)/shard_map/ppermute | solution.py:33
  287.6 25.7 %collective-permute-done.43 = bf16[160,1280]{1,0:T(8,128)(2,1)S(1)} collective-permute-done((bf16[160,1280]{1,0:T(8,128)(2,1)S(1)}, bf16[160,1280]{1,0:T(8,128)(2,1)S(1)}, u32[]{:S(2)}, u32[]{:S(2)}) %collective-permute-start.43) | collective-permute-done | bytes 409632 | tf_op jit(solution)/shard_map/ppermute | solution.py:41
  313.9 1.7 collective-permute-start.48
  315.6 7.9 %collective-permute-done.50 = bf16[96,1280]{0,1:T(8,128)(2,1)S(1)} collective-permute-done((bf16[96,1280]{0,1:T(8,128)(2,1)S(1)}, bf16[96,1280]{0,1:T(8,128)(2,1)S(1)}, u32[]{:S(2)}, u32[]{:S(2)}) %collective-permute-start.50) | collective-permute-done | bytes 245792 | tf_op jit(solution)/shard_map/ppermute | solution.py:41
  325.4 9.2 %collective-permute-done.47 = bf16[320,1280]{1,0:T(8,128)(2,1)S(1)} collective-permute-done((bf16[320,1280]{1,0:T(8,128)(2,1)S(1)}, bf16[320,1280]{1,0:T(8,128)(2,1)S(1)}, u32[]{:S(2)}, u32[]{:S(2)}) %collective-permute-start.47) | collective-permute-done | bytes 819232 | tf_op jit(solution)/shard_map/ppermute | solution.py:37
  334.7 8.3 %collective-permute-done.48 = bf16[160,1280]{1,0:T(8,128)(2,1)S(1)} collective-permute-done((bf16[160,1280]{1,0:T(8,128)(2,1)S(1)}, bf16[160,1280]{1,0:T(8,128)(2,1)S(1)}, u32[]{:S(2)}, u32[]{:S(2)}) %collective-permute-start.48) | collective-permute-done | bytes 409632 | tf_op jit(solution)/shard_map/ppermute | solution.py:37
  343.0 1.7 copy-done.10
  344.7 4.2 %convolution_convert_fusion.3 = bf16[192,1280]{1,0:T(8,128)(2,1)S(1)} fusion(bf16[1280,1280]{1,0:T(8,128)(2,1)} %copy-done.10, bf16[96,1280]{0,1:T(8,128)(2,1)S(1)} %get-tuple-element.66, bf16[96,1280]{0,1:T(8,128)(2,1)S(1)} %get-tuple-element.65), kind=kOutput, calls=%fused_computation.7 | convolution fusion | flops 638361600 | bytes 4259840 | tf_op jit(solution)/shard_map/dot_general | solution.py:212
  351.0 1.8 collective-permute-start.53
  352.8 4.2 %convolution_convert_fusion.4 = bf16[192,1280]{1,0:T(8,128)(2,1)S(1)} fusion(bf16[1280,1280]{1,0:T(8,128)(2,1)} %copy-done.10, bf16[96,1280]{0,1:T(8,128)(2,1)S(1)} %get-tuple-element.68, bf16[96,1280]{0,1:T(8,128)(2,1)S(1)} %get-tuple-element.67), kind=kOutput, calls=%fused_computation.8 | convolution fusion | flops 638361600 | bytes 4259840 | tf_op jit(solution)/shard_map/dot_general | solution.py:212
  357.6 3.2 collective-permute-done.53
  362.4 7.6 %collective-permute-done.54 = bf16[96,1280]{0,1:T(8,128)(2,1)S(1)} collective-permute-done((bf16[96,1280]{0,1:T(8,128)(2,1)S(1)}, bf16[96,1280]{0,1:T(8,128)(2,1)S(1)}, u32[]{:S(2)}, u32[]{:S(2)}) %collective-permute-start.54) | collective-permute-done | bytes 245792 | tf_op jit(solution)/shard_map/ppermute | solution.py:33
  (264 shorter events, 92.7 us)
Async XLA Ops:
  0.0 10.5 %copy-start.13 = (s32[64]{0:T(128)S(1)}, s32[64]{0:T(128)}, u32[]{:S(2)}) copy-start(s32[64]{0:T(128)} %param.19) | copy-start | bytes 772
  0.0 10.5 %copy-start.12 = (s32[1,2]{1,0:T(1,128)S(1)}, s32[1,2]{1,0:T(1,128)}, u32[]{:S(2)}) copy-start(s32[1,2]{1,0:T(1,128)} %param.16) | copy-start | bytes 28
  0.0 11.1 %copy-start.4 = (bf16[256,1280]{1,0:T(8,128)(2,1)S(1)}, bf16[256,1280]{1,0:T(8,128)(2,1)}, u32[]{:S(2)}) copy-start(bf16[256,1280]{1,0:T(8,128)(2,1)} %param.15) | copy-start | bytes 1966084
  3.4 22.6 %collective-permute-start.1 = (bf16[160,1280]{1,0:T(8,128)(2,1)}, bf16[160,1280]{1,0:T(8,128)(2,1)S(1)}, u32[]{:S(2)}, u32[]{:S(2)}) collective-permute-start(bf16[160,1280]{1,0:T(8,128)(2,1)} %copy.162), channel_id=1, source_target_pairs={{0,16},{1,17},{2,18},{3,19},{4,20},{5,21},{6,22},{7,23},{8,24},{9,... | collective-permute-start | bytes 1228808 | tf_op jit(solution)/shard_map/ppermute | solution.py:41
  7.4 19.3 %collective-permute-start = (bf16[160,1280]{1,0:T(8,128)(2,1)}, bf16[160,1280]{1,0:T(8,128)(2,1)S(1)}, u32[]{:S(2)}, u32[]{:S(2)}) collective-permute-start(bf16[160,1280]{1,0:T(8,128)(2,1)} %copy.162), channel_id=1, source_target_pairs={{0,8},{1,9},{2,10},{3,11},{4,12},{5,13},{6,14},{7,15},{8,0},{9,1},... | collective-permute-start | bytes 1228808 | tf_op jit(solution)/shard_map/ppermute | solution.py:41
  9.0 34.9 %collective-permute-start.3 = (bf16[160,1280]{1,0:T(8,128)(2,1)}, bf16[160,1280]{1,0:T(8,128)(2,1)}, u32[]{:S(2)}, u32[]{:S(2)}) collective-permute-start(bf16[160,1280]{1,0:T(8,128)(2,1)} %copy.162), channel_id=1, source_target_pairs={{0,4},{1,5},{2,6},{3,7},{4,0},{5,1},{6,2},{7,3},{8,12},{9,13},{10,... | collective-permute-start | bytes 1228808 | tf_op jit(solution)/shard_map/ppermute | solution.py:37
  11.5 17.7 %copy-start.11 = (s32[64]{0:T(128)S(1)}, s32[64]{0:T(128)}, u32[]{:S(2)}) copy-start(s32[64]{0:T(128)} %param.18) | copy-start | bytes 772
  26.0 10.6 %collective-permute-start.2 = (bf16[160,1280]{1,0:T(8,128)(2,1)S(1)}, bf16[160,1280]{1,0:T(8,128)(2,1)S(1)}, u32[]{:S(2)}, u32[]{:S(2)}) collective-permute-start(bf16[160,1280]{1,0:T(8,128)(2,1)S(1)} %collective-permute-done.1), channel_id=1, source_target_pairs={{0,8},{1,9},{2,10},{3,11},{4,12},{5,13},{6,14},{7,15},{8,0},{9,1},... | collective-permute-start | bytes 1228808 | tf_op jit(solution)/shard_map/ppermute | solution.py:41
  27.7 21.5 %collective-permute-start.4 = (bf16[320,1280]{1,0:T(8,128)(2,1)}, bf16[320,1280]{1,0:T(8,128)(2,1)}, u32[]{:S(2)}, u32[]{:S(2)}) collective-permute-start(bf16[320,1280]{1,0:T(8,128)(2,1)} %pad_maximum_fusion), channel_id=1, source_target_pairs={{0,4},{1,5},{2,6},{3,7},{4,0},{5,1},{6,2},{7,3},{8,12},{9,13},{10,... | collective-permute-start | bytes 2457608 | tf_op jit(solution)/shard_map/ppermute | solution.py:37
  36.6 20.1 %collective-permute-start.5 = (bf16[160,1280]{1,0:T(8,128)(2,1)S(1)}, bf16[160,1280]{1,0:T(8,128)(2,1)}, u32[]{:S(2)}, u32[]{:S(2)}) collective-permute-start(bf16[160,1280]{1,0:T(8,128)(2,1)S(1)} %collective-permute-done.2), channel_id=1, source_target_pairs={{0,4},{1,5},{2,6},{3,7},{4,0},{5,1},{6,2},{7,3},{8,12},{9,13},{10,... | collective-permute-start | bytes 1228808 | tf_op jit(solution)/shard_map/ppermute | solution.py:37
  71.6 11.7 %copy-start.2 = (bf16[2,2,64,1280]{3,2,1,0:T(8,128)(2,1)S(1)}, bf16[2,2,64,1280]{3,2,1,0:T(8,128)(2,1)}, u32[]{:S(2)}) copy-start(bf16[2,2,64,1280]{3,2,1,0:T(8,128)(2,1)} %copy.159) | copy-start | bytes 1966084
  71.7 1.7 collective-permute-start.6
  73.5 9.8 %collective-permute-start.7 = (bf16[128,1280]{1,0:T(8,128)(2,1)S(1)}, bf16[128,1280]{1,0:T(8,128)(2,1)S(1)}, u32[]{:S(2)}, u32[]{:S(2)}) collective-permute-start(bf16[128,1280]{1,0:T(8,128)(2,1)S(1)} %fusion.73), channel_id=1, source_target_pairs={{0,2},{1,3},{2,0},{3,1},{4,6},{5,7},{6,4},{7,5},{8,10},{9,11},{10,... | collective-permute-start | bytes 983048 | tf_op jit(solution)/shard_map/ppermute | solution.py:33
  75.1 11.3 %collective-permute-start.8 = (bf16[160,1280]{1,0:T(8,128)(2,1)S(1)}, bf16[160,1280]{1,0:T(8,128)(2,1)S(1)}, u32[]{:S(2)}, u32[]{:S(2)}) collective-permute-start(bf16[160,1280]{1,0:T(8,128)(2,1)S(1)} %pad_maximum_fusion.8), channel_id=1, source_target_pairs={{0,8},{1,9},{2,10},{3,11},{4,12},{5,13},{6,14},{7,15},{8,0},{9,1},... | collective-permute-start | bytes 1228808 | tf_op jit(solution)/shard_map/ppermute | solution.py:41
  75.4 38.9 %collective-permute-start.10 = (bf16[160,1280]{1,0:T(8,128)(2,1)S(1)}, bf16[160,1280]{1,0:T(8,128)(2,1)}, u32[]{:S(2)}, u32[]{:S(2)}) collective-permute-start(bf16[160,1280]{1,0:T(8,128)(2,1)S(1)} %pad_maximum_fusion.8), channel_id=1, source_target_pairs={{0,24},{1,25},{2,26},{3,27},{4,28},{5,29},{6,30},{7,31},{8,16},{9,... | collective-permute-start | bytes 1228808 | tf_op jit(solution)/shard_map/ppermute | solution.py:41
  80.7 33.6 %collective-permute-start.9 = (bf16[160,1280]{1,0:T(8,128)(2,1)S(1)}, bf16[160,1280]{1,0:T(8,128)(2,1)S(1)}, u32[]{:S(2)}, u32[]{:S(2)}) collective-permute-start(bf16[160,1280]{1,0:T(8,128)(2,1)S(1)} %get-tuple-element.107), channel_id=1, source_target_pairs={{0,16},{1,17},{2,18},{3,19},{4,20},{5,21},{6,22},{7,23},{8,24},{9,... | collective-permute-start | bytes 1228808 | tf_op jit(solution)/shard_map/ppermute | solution.py:41
  80.7 41.7 %collective-permute-start.12 = (bf16[160,1280]{1,0:T(8,128)(2,1)S(1)}, bf16[160,1280]{1,0:T(8,128)(2,1)S(1)}, u32[]{:S(2)}, u32[]{:S(2)}) collective-permute-start(bf16[160,1280]{1,0:T(8,128)(2,1)S(1)} %get-tuple-element.107), channel_id=1, source_target_pairs={{0,4},{1,5},{2,6},{3,7},{4,0},{5,1},{6,2},{7,3},{8,12},{9,13},{10,... | collective-permute-start | bytes 1228808 | tf_op jit(solution)/shard_map/ppermute | solution.py:37
  83.5 30.8 %copy-start = (bf16[128,1280]{1,0:T(8,128)(2,1)}, bf16[128,1280]{1,0:T(8,128)(2,1)S(1)}, u32[]{:S(2)}) copy-start(bf16[128,1280]{1,0:T(8,128)(2,1)S(1)} %get-tuple-element.62) | copy-start | bytes 983044
  114.3 26.6 %collective-permute-start.11 = (bf16[128,1280]{1,0:T(8,128)(2,1)}, bf16[128,1280]{1,0:T(8,128)(2,1)}, u32[]{:S(2)}, u32[]{:S(2)}) collective-permute-start(bf16[128,1280]{1,0:T(8,128)(2,1)} %fusion.49), channel_id=1, source_target_pairs={{0,1},{1,0},{2,3},{3,2},{4,5},{5,4},{6,7},{7,6},{8,9},{9,8},{10,11... | collective-permute-start | bytes 983048 | tf_op jit(solution)/shard_map/ppermute | solution.py:29
  114.3 11.1 %collective-permute-start.16 = (bf16[128,1280]{1,0:T(8,128)(2,1)}, bf16[128,1280]{1,0:T(8,128)(2,1)}, u32[]{:S(2)}, u32[]{:S(2)}) collective-permute-start(bf16[128,1280]{1,0:T(8,128)(2,1)} %fusion.49), channel_id=1, source_target_pairs={{0,8},{1,9},{2,10},{3,11},{4,12},{5,13},{6,14},{7,15},{8,0},{9,1},... | collective-permute-start | bytes 983048 | tf_op jit(solution)/shard_map/ppermute | solution.py:41
  114.4 30.5 %collective-permute-start.18 = (bf16[160,1280]{1,0:T(8,128)(2,1)}, bf16[160,1280]{1,0:T(8,128)(2,1)}, u32[]{:S(2)}, u32[]{:S(2)}) collective-permute-start(bf16[160,1280]{1,0:T(8,128)(2,1)} %param.25), channel_id=1, source_target_pairs={{0,8},{1,9},{2,10},{3,11},{4,12},{5,13},{6,14},{7,15},{8,0},{9,1},... | collective-permute-start | bytes 1228808 | tf_op jit(solution)/shard_map/ppermute | solution.py:41
  117.4 47.7 %collective-permute-start.14 = (bf16[160,1280]{1,0:T(8,128)(2,1)}, bf16[160,1280]{1,0:T(8,128)(2,1)}, u32[]{:S(2)}, u32[]{:S(2)}) collective-permute-start(bf16[160,1280]{1,0:T(8,128)(2,1)} %collective-permute-done.10), channel_id=1, source_target_pairs={{0,4},{1,5},{2,6},{3,7},{4,0},{5,1},{6,2},{7,3},{8,12},{9,13},{10,... | collective-permute-start | bytes 1228808 | tf_op jit(solution)/shard_map/ppermute | solution.py:37
  122.4 22.4 %collective-permute-start.19 = (bf16[160,1280]{1,0:T(8,128)(2,1)}, bf16[160,1280]{1,0:T(8,128)(2,1)}, u32[]{:S(2)}, u32[]{:S(2)}) collective-permute-start(bf16[160,1280]{1,0:T(8,128)(2,1)} %param.25), channel_id=1, source_target_pairs={{0,16},{1,17},{2,18},{3,19},{4,20},{5,21},{6,22},{7,23},{8,24},{9,... | collective-permute-start | bytes 1228808 | tf_op jit(solution)/shard_map/ppermute | solution.py:41
  125.4 78.6 %collective-permute-start.26 = (bf16[160,1280]{1,0:T(8,128)(2,1)}, bf16[160,1280]{1,0:T(8,128)(2,1)}, u32[]{:S(2)}, u32[]{:S(2)}) collective-permute-start(bf16[160,1280]{1,0:T(8,128)(2,1)} %param.25), channel_id=1, source_target_pairs={{0,4},{1,5},{2,6},{3,7},{4,0},{5,1},{6,2},{7,3},{8,12},{9,13},{10,... | collective-permute-start | bytes 1228808 | tf_op jit(solution)/shard_map/ppermute | solution.py:37
  141.0 2.0 collective-permute-start.17
  142.9 21.2 %collective-permute-start.13 = (bf16[320,1280]{1,0:T(8,128)(2,1)}, bf16[320,1280]{1,0:T(8,128)(2,1)S(1)}, u32[]{:S(2)}, u32[]{:S(2)}) collective-permute-start(bf16[320,1280]{1,0:T(8,128)(2,1)} %pad_maximum_fusion.1), channel_id=1, source_target_pairs={{0,4},{1,5},{2,6},{3,7},{4,0},{5,1},{6,2},{7,3},{8,12},{9,13},{10,... | collective-permute-start | bytes 2457608 | tf_op jit(solution)/shard_map/ppermute | solution.py:37
  144.9 48.8 %collective-permute-start.22 = (bf16[160,1280]{1,0:T(8,128)(2,1)}, bf16[160,1280]{1,0:T(8,128)(2,1)}, u32[]{:S(2)}, u32[]{:S(2)}) collective-permute-start(bf16[160,1280]{1,0:T(8,128)(2,1)} %collective-permute-done.19), channel_id=1, source_target_pairs={{0,8},{1,9},{2,10},{3,11},{4,12},{5,13},{6,14},{7,15},{8,0},{9,1},... | collective-permute-start | bytes 1228808 | tf_op jit(solution)/shard_map/ppermute | solution.py:41
  147.0 60.1 %collective-permute-start.27 = (bf16[320,1280]{1,0:T(8,128)(2,1)}, bf16[320,1280]{1,0:T(8,128)(2,1)}, u32[]{:S(2)}, u32[]{:S(2)}) collective-permute-start(bf16[320,1280]{1,0:T(8,128)(2,1)} %pad_maximum_fusion.2), channel_id=1, source_target_pairs={{0,4},{1,5},{2,6},{3,7},{4,0},{5,1},{6,2},{7,3},{8,12},{9,13},{10,... | collective-permute-start | bytes 2457608 | tf_op jit(solution)/shard_map/ppermute | solution.py:37
  176.3 7.4 %collective-permute-start.20 = (bf16[128,1280]{0,1:T(8,128)(2,1)}, bf16[128,1280]{0,1:T(8,128)(2,1)}, u32[]{:S(2)}, u32[]{:S(2)}) collective-permute-start(bf16[128,1280]{0,1:T(8,128)(2,1)} %bitcast.212), channel_id=1, source_target_pairs={{0,1},{1,0},{2,3},{3,2},{4,5},{5,4},{6,7},{7,6},{8,9},{9,8},{10,11... | collective-permute-start | bytes 983048 | tf_op jit(solution)/shard_map/ppermute | solution.py:29
  185.6 10.4 %collective-permute-start.21 = (bf16[128,1280]{0,1:T(8,128)(2,1)}, bf16[128,1280]{0,1:T(8,128)(2,1)}, u32[]{:S(2)}, u32[]{:S(2)}) collective-permute-start(bf16[128,1280]{0,1:T(8,128)(2,1)} %fusion.72), channel_id=1, source_target_pairs={{0,8},{1,9},{2,10},{3,11},{4,12},{5,13},{6,14},{7,15},{8,0},{9,1},... | collective-permute-start | bytes 983048 | tf_op jit(solution)/shard_map/ppermute | solution.py:41
  189.5 8.5 %collective-permute-start.15 = (bf16[128,1280]{0,1:T(8,128)(2,1)}, bf16[128,1280]{0,1:T(8,128)(2,1)}, u32[]{:S(2)}, u32[]{:S(2)}) collective-permute-start(bf16[128,1280]{0,1:T(8,128)(2,1)} %bitcast.207), channel_id=1, source_target_pairs={{0,1},{1,0},{2,3},{3,2},{4,5},{5,4},{6,7},{7,6},{8,9},{9,8},{10,11... | collective-permute-start | bytes 983048 | tf_op jit(solution)/shard_map/ppermute | solution.py:29
  193.6 19.8 %collective-permute-start.24 = (bf16[160,1280]{1,0:T(8,128)(2,1)}, bf16[160,1280]{1,0:T(8,128)(2,1)}, u32[]{:S(2)}, u32[]{:S(2)}) collective-permute-start(bf16[160,1280]{1,0:T(8,128)(2,1)} %pad_maximum_fusion.10), channel_id=1, source_target_pairs={{0,8},{1,9},{2,10},{3,11},{4,12},{5,13},{6,14},{7,15},{8,0},{9,1},... | collective-permute-start | bytes 1228808 | tf_op jit(solution)/shard_map/ppermute | solution.py:41
  196.0 21.1 %collective-permute-start.25 = (bf16[160,1280]{1,0:T(8,128)(2,1)}, bf16[160,1280]{1,0:T(8,128)(2,1)}, u32[]{:S(2)}, u32[]{:S(2)}) collective-permute-start(bf16[160,1280]{1,0:T(8,128)(2,1)} %pad_maximum_fusion.10), channel_id=1, source_target_pairs={{0,16},{1,17},{2,18},{3,19},{4,20},{5,21},{6,22},{7,23},{8,24},{9,... | collective-permute-start | bytes 1228808 | tf_op jit(solution)/shard_map/ppermute | solution.py:41
  198.0 47.0 %collective-permute-start.37 = (bf16[160,1280]{1,0:T(8,128)(2,1)}, bf16[160,1280]{1,0:T(8,128)(2,1)}, u32[]{:S(2)}, u32[]{:S(2)}) collective-permute-start(bf16[160,1280]{1,0:T(8,128)(2,1)} %pad_maximum_fusion.10), channel_id=1, source_target_pairs={{0,4},{1,5},{2,6},{3,7},{4,0},{5,1},{6,2},{7,3},{8,12},{9,13},{10,... | collective-permute-start | bytes 1228808 | tf_op jit(solution)/shard_map/ppermute | solution.py:37
  204.0 15.0 %collective-permute-start.28 = (bf16[160,1280]{1,0:T(8,128)(2,1)}, bf16[160,1280]{1,0:T(8,128)(2,1)}, u32[]{:S(2)}, u32[]{:S(2)}) collective-permute-start(bf16[160,1280]{1,0:T(8,128)(2,1)} %collective-permute-done.22), channel_id=1, source_target_pairs={{0,4},{1,5},{2,6},{3,7},{4,0},{5,1},{6,2},{7,3},{8,12},{9,13},{10,... | collective-permute-start | bytes 1228808 | tf_op jit(solution)/shard_map/ppermute | solution.py:37
  207.1 5.4 %collective-permute-start.23 = (bf16[64,1280]{1,0:T(8,128)(2,1)S(1)}, bf16[64,1280]{1,0:T(8,128)(2,1)S(1)}, u32[]{:S(2)}, u32[]{:S(2)}) collective-permute-start(bf16[64,1280]{1,0:T(8,128)(2,1)S(1)} %dynamic-slice_bitcast_fusion.1), channel_id=1, source_target_pairs={{0,2},{1,3},{2,0},{3,1},{4,6},{5,7},{6,4},{7,5},{8,10},{9,11},{10,... | collective-permute-start | bytes 491528 | tf_op jit(solution)/shard_map/ppermute | solution.py:33
  217.2 24.0 %collective-permute-start.35 = (bf16[160,1280]{1,0:T(8,128)(2,1)}, bf16[160,1280]{1,0:T(8,128)(2,1)}, u32[]{:S(2)}, u32[]{:S(2)}) collective-permute-start(bf16[160,1280]{1,0:T(8,128)(2,1)} %collective-permute-done.25), channel_id=1, source_target_pairs={{0,8},{1,9},{2,10},{3,11},{4,12},{5,13},{6,14},{7,15},{8,0},{9,1},... | collective-permute-start | bytes 1228808 | tf_op jit(solution)/shard_map/ppermute | solution.py:41
  221.6 16.3 %copy-start.7 = (bf16[160,1280]{1,0:T(8,128)(2,1)S(1)}, bf16[160,1280]{1,0:T(8,128)(2,1)}, u32[]{:S(2)}) copy-start(bf16[160,1280]{1,0:T(8,128)(2,1)} %param.29) | copy-start | bytes 1228804
  222.0 1.3 collective-permute-start.29
  223.3 4.9 %collective-permute-start.30 = (bf16[64,640]{1,0:T(8,128)(2,1)S(1)}, bf16[64,640]{1,0:T(8,128)(2,1)S(1)}, u32[]{:S(2)}, u32[]{:S(2)}) collective-permute-start(bf16[64,640]{1,0:T(8,128)(2,1)S(1)} %fusion.266), channel_id=1, source_target_pairs={{0,2},{1,3},{2,0},{3,1},{4,6},{5,7},{6,4},{7,5},{8,10},{9,11},{10,... | collective-permute-start | bytes 245768 | tf_op jit(solution)/shard_map/ppermute | solution.py:33
  228.5 4.7 %collective-permute-start.31 = (bf16[4,1,12,768]{3,2,0,1:T(8,128)(2,1)S(1)}, bf16[4,1,12,768]{3,2,0,1:T(8,128)(2,1)S(1)}, u32[]{:S(2)}, u32[]{:S(2)}) collective-permute-start(bf16[4,1,12,768]{3,2,0,1:T(8,128)(2,1)S(1)} %get-tuple-element.125), channel_id=1, source_target_pairs={{0,4},{1,5},{2,6},{3,7},{4,0},{5,1},{6,2},{7,3},{8,12},{9,13},{10,... | collective-permute-start | bytes 221192 | tf_op jit(solution)/shard_map/ppermute | solution.py:37
  233.2 6.0 %collective-permute-start.34 = (bf16[2,1,12,768]{3,0,2,1:T(2,128)(2,1)S(1)}, bf16[2,1,12,768]{3,0,2,1:T(2,128)(2,1)S(1)}, u32[]{:S(2)}, u32[]{:S(2)}) collective-permute-start(bf16[2,1,12,768]{3,0,2,1:T(2,128)(2,1)S(1)} %bitcast.218), channel_id=1, source_target_pairs={{0,24},{1,25},{2,26},{3,27},{4,28},{5,29},{6,30},{7,31},{8,16},{9,... | collective-permute-start | bytes 110600 | tf_op jit(solution)/shard_map/ppermute | solution.py:41
  235.4 4.9 %collective-permute-start.33 = (bf16[2,1,12,768]{3,0,2,1:T(2,128)(2,1)S(1)}, bf16[2,1,12,768]{3,0,2,1:T(2,128)(2,1)S(1)}, u32[]{:S(2)}, u32[]{:S(2)}) collective-permute-start(bf16[2,1,12,768]{3,0,2,1:T(2,128)(2,1)S(1)} %bitcast.217), channel_id=1, source_target_pairs={{0,16},{1,17},{2,18},{3,19},{4,20},{5,21},{6,22},{7,23},{8,24},{9,... | collective-permute-start | bytes 110600 | tf_op jit(solution)/shard_map/ppermute | solution.py:41
  236.9 4.0 %collective-permute-start.32 = (bf16[2,1,12,768]{3,0,2,1:T(2,128)(2,1)S(1)}, bf16[2,1,12,768]{3,0,2,1:T(2,128)(2,1)S(1)}, u32[]{:S(2)}, u32[]{:S(2)}) collective-permute-start(bf16[2,1,12,768]{3,0,2,1:T(2,128)(2,1)S(1)} %bitcast.219), channel_id=1, source_target_pairs={{0,8},{1,9},{2,10},{3,11},{4,12},{5,13},{6,14},{7,15},{8,0},{9,1},... | collective-permute-start | bytes 110600 | tf_op jit(solution)/shard_map/ppermute | solution.py:41
  239.3 21.2 %collective-permute-start.38 = (bf16[320,1280]{1,0:T(8,128)(2,1)S(1)}, bf16[320,1280]{1,0:T(8,128)(2,1)S(1)}, u32[]{:S(2)}, u32[]{:S(2)}) collective-permute-start(bf16[320,1280]{1,0:T(8,128)(2,1)S(1)} %pad_maximum_fusion.3), channel_id=1, source_target_pairs={{0,4},{1,5},{2,6},{3,7},{4,0},{5,1},{6,2},{7,3},{8,12},{9,13},{10,... | collective-permute-start | bytes 2457608 | tf_op jit(solution)/shard_map/ppermute | solution.py:37
  241.1 24.3 %collective-permute-start.39 = (bf16[160,1280]{1,0:T(8,128)(2,1)}, bf16[160,1280]{1,0:T(8,128)(2,1)S(1)}, u32[]{:S(2)}, u32[]{:S(2)}) collective-permute-start(bf16[160,1280]{1,0:T(8,128)(2,1)} %collective-permute-done.35), channel_id=1, source_target_pairs={{0,4},{1,5},{2,6},{3,7},{4,0},{5,1},{6,2},{7,3},{8,12},{9,13},{10,... | collective-permute-start | bytes 1228808 | tf_op jit(solution)/shard_map/ppermute | solution.py:37
  243.1 3.7 collective-permute-start.36
  272.9 3.5 collective-permute-start.40
  273.8 13.9 %collective-permute-start.42 = (bf16[160,1280]{1,0:T(8,128)(2,1)}, bf16[160,1280]{1,0:T(8,128)(2,1)S(1)}, u32[]{:S(2)}, u32[]{:S(2)}) collective-permute-start(bf16[160,1280]{1,0:T(8,128)(2,1)} %pad_maximum_fusion.11), channel_id=1, source_target_pairs={{0,8},{1,9},{2,10},{3,11},{4,12},{5,13},{6,14},{7,15},{8,0},{9,1},... | collective-permute-start | bytes 1228808 | tf_op jit(solution)/shard_map/ppermute | solution.py:41
  274.1 39.3 %collective-permute-start.44 = (bf16[160,1280]{1,0:T(8,128)(2,1)}, bf16[160,1280]{1,0:T(8,128)(2,1)S(1)}, u32[]{:S(2)}, u32[]{:S(2)}) collective-permute-start(bf16[160,1280]{1,0:T(8,128)(2,1)} %pad_maximum_fusion.11), channel_id=1, source_target_pairs={{0,24},{1,25},{2,26},{3,27},{4,28},{5,29},{6,30},{7,31},{8,16},{9,... | collective-permute-start | bytes 1228808 | tf_op jit(solution)/shard_map/ppermute | solution.py:41
  277.5 9.6 %collective-permute-start.41 = (bf16[96,1280]{0,1:T(8,128)(2,1)S(1)}, bf16[96,1280]{0,1:T(8,128)(2,1)S(1)}, u32[]{:S(2)}, u32[]{:S(2)}) collective-permute-start(bf16[96,1280]{0,1:T(8,128)(2,1)S(1)} %fusion.69), channel_id=1, source_target_pairs={{0,2},{1,3},{2,0},{3,1},{4,6},{5,7},{6,4},{7,5},{8,10},{9,11},{10,... | collective-permute-start | bytes 737288 | tf_op jit(solution)/shard_map/ppermute | solution.py:33
  278.9 34.5 %collective-permute-start.43 = (bf16[160,1280]{1,0:T(8,128)(2,1)S(1)}, bf16[160,1280]{1,0:T(8,128)(2,1)S(1)}, u32[]{:S(2)}, u32[]{:S(2)}) collective-permute-start(bf16[160,1280]{1,0:T(8,128)(2,1)S(1)} %get-tuple-element.101), channel_id=1, source_target_pairs={{0,16},{1,17},{2,18},{3,19},{4,20},{5,21},{6,22},{7,23},{8,24},{9,... | collective-permute-start | bytes 1228808 | tf_op jit(solution)/shard_map/ppermute | solution.py:41
  280.0 43.7 %collective-permute-start.46 = (bf16[160,1280]{1,0:T(8,128)(2,1)S(1)}, bf16[160,1280]{1,0:T(8,128)(2,1)}, u32[]{:S(2)}, u32[]{:S(2)}) collective-permute-start(bf16[160,1280]{1,0:T(8,128)(2,1)S(1)} %get-tuple-element.101), channel_id=1, source_target_pairs={{0,4},{1,5},{2,6},{3,7},{4,0},{5,1},{6,2},{7,3},{8,12},{9,13},{10,... | collective-permute-start | bytes 1228808 | tf_op jit(solution)/shard_map/ppermute | solution.py:37
  280.6 32.9 %copy-start.9 = (bf16[1280,1280]{1,0:T(8,128)(2,1)S(1)}, bf16[1280,1280]{1,0:T(8,128)(2,1)}, u32[]{:S(2)}) copy-start(bf16[1280,1280]{1,0:T(8,128)(2,1)} %get-tuple-element.102) | copy-start | bytes 9830404
  313.4 35.9 %collective-permute-start.45 = (bf16[96,1280]{0,1:T(8,128)(2,1)S(1)}, bf16[96,1280]{0,1:T(8,128)(2,1)S(1)}, u32[]{:S(2)}, u32[]{:S(2)}) collective-permute-start(bf16[96,1280]{0,1:T(8,128)(2,1)S(1)} %fusion.47), channel_id=1, source_target_pairs={{0,1},{1,0},{2,3},{3,2},{4,5},{5,4},{6,7},{7,6},{8,9},{9,8},{10,11... | collective-permute-start | bytes 737288 | tf_op jit(solution)/shard_map/ppermute | solution.py:29
  313.4 10.1 %collective-permute-start.50 = (bf16[96,1280]{0,1:T(8,128)(2,1)S(1)}, bf16[96,1280]{0,1:T(8,128)(2,1)S(1)}, u32[]{:S(2)}, u32[]{:S(2)}) collective-permute-start(bf16[96,1280]{0,1:T(8,128)(2,1)S(1)} %fusion.47), channel_id=1, source_target_pairs={{0,8},{1,9},{2,10},{3,11},{4,12},{5,13},{6,14},{7,15},{8,0},{9,1},... | collective-permute-start | bytes 737288 | tf_op jit(solution)/shard_map/ppermute | solution.py:41
  313.5 21.1 %collective-permute-start.47 = (bf16[320,1280]{1,0:T(8,128)(2,1)S(1)}, bf16[320,1280]{1,0:T(8,128)(2,1)S(1)}, u32[]{:S(2)}, u32[]{:S(2)}) collective-permute-start(bf16[320,1280]{1,0:T(8,128)(2,1)S(1)} %pad_maximum_fusion.4), channel_id=1, source_target_pairs={{0,4},{1,5},{2,6},{3,7},{4,0},{5,1},{6,2},{7,3},{8,12},{9,13},{10,... | collective-permute-start | bytes 2457608 | tf_op jit(solution)/shard_map/ppermute | solution.py:37
  313.9 29.1 %collective-permute-start.48 = (bf16[160,1280]{1,0:T(8,128)(2,1)S(1)}, bf16[160,1280]{1,0:T(8,128)(2,1)S(1)}, u32[]{:S(2)}, u32[]{:S(2)}) collective-permute-start(bf16[160,1280]{1,0:T(8,128)(2,1)S(1)} %collective-permute-done.44), channel_id=1, source_target_pairs={{0,4},{1,5},{2,6},{3,7},{4,0},{5,1},{6,2},{7,3},{8,12},{9,13},{10,... | collective-permute-start | bytes 1228808 | tf_op jit(solution)/shard_map/ppermute | solution.py:37
  323.6 1.7 collective-permute-start.51
  349.2 1.7 collective-permute-start.52
  351.0 9.8 %collective-permute-start.53 = (bf16[96,1280]{0,1:T(8,128)(2,1)S(1)}, bf16[96,1280]{0,1:T(8,128)(2,1)S(1)}, u32[]{:S(2)}, u32[]{:S(2)}) collective-permute-start(bf16[96,1280]{0,1:T(8,128)(2,1)S(1)} %fusion.68), channel_id=1, source_target_pairs={{0,8},{1,9},{2,10},{3,11},{4,12},{5,13},{6,14},{7,15},{8,0},{9,1},... | collective-permute-start | bytes 737288 | tf_op jit(solution)/shard_map/ppermute | solution.py:41
  357.3 3.6 collective-permute-start.49
  361.1 9.0 %collective-permute-start.54 = (bf16[96,1280]{0,1:T(8,128)(2,1)S(1)}, bf16[96,1280]{0,1:T(8,128)(2,1)S(1)}, u32[]{:S(2)}, u32[]{:S(2)}) collective-permute-start(bf16[96,1280]{0,1:T(8,128)(2,1)S(1)} %fusion.67), channel_id=1, source_target_pairs={{0,2},{1,3},{2,0},{3,1},{4,6},{5,7},{6,4},{7,5},{8,10},{9,11},{10,... | collective-permute-start | bytes 737288 | tf_op jit(solution)/shard_map/ppermute | solution.py:33
  370.4 1.7 collective-permute-start.55
  (6 other events, 30.4 us)

commit v3 on v2

v3 whole, which is shorter than its diff:
```python
import jax
import jax.numpy as jnp
from jax import lax
from jax.experimental import pallas as pl
from jax.experimental.pallas import tpu as pltpu
from jax.sharding import PartitionSpec as P

HEAD_DIM = 80
GRID = 16
HALF = GRID // 2
EPS = 1e-06
AXES = ("req", "tp")


def routes(move):
    groups = lax.axis_size("req") // 8
    pairs = []
    for z in range(4):
        for y in range(2):
            for x in range(2):
                for c in range(2):
                    z2, y2, x2, c2 = move(z, y, x, c)
                    for g in range(groups):
                        source = ((z * 2 + y) * groups + g) * 4 + x * 2 + c
                        target = ((z2 * 2 + y2) * groups + g) * 4 + x2 * 2 + c2
                        pairs.append((source, target))
    return pairs


def swap_core(part):
    return lax.ppermute(part, AXES, routes(lambda z, y, x, c: (z, y, x, 1 - c)))


def swap_x(part):
    return lax.ppermute(part, AXES, routes(lambda z, y, x, c: (z, y, 1 - x, c)))


def swap_y(part):
    return lax.ppermute(part, AXES, routes(lambda z, y, x, c: (z, 1 - y, x, c)))


def swap_z(part, k):
    return lax.ppermute(part, AXES, routes(lambda z, y, x, c: (z ^ k, y, x, c)))


def place():
    index = lax.axis_index("req") // (lax.axis_size("req") // 8)
    tensor = lax.axis_index("tp")
    return index // 2, index % 2, tensor // 2, tensor % 2


def own_rows(weight):
    groups = lax.axis_size("req") // 8
    if groups == 1:
        return weight
    members = [[i * groups + g for g in range(groups)] for i in range(8)]
    return lax.all_gather(weight, "req", axis=0, tiled=True, axis_index_groups=members)


def all_rows(weight):
    return lax.all_gather(weight, "req", axis=0, tiled=True)


def together(*values):
    return lax.optimization_barrier(values)


class Same:
    def __init__(self, weight):
        self.own = weight
        self.first = swap_z(weight, 1)
        self.second = swap_z(weight, 2)
        self.y_own = swap_y(weight)

    def forward(self):
        self.third = swap_z(self.second, 1)
        self.y_early = swap_y(jnp.concatenate([self.first, self.second], axis=0))

    def pieces(self):
        y_third = swap_y(self.third)
        return [self.own, self.first, self.second, self.third, self.y_own, self.y_early, y_third]


class Halved:
    def __init__(self, w_up, w_down_t):
        z, _, _, _ = place()
        half = w_up.shape[1] // 2
        parts = []
        for bit in (0, 1):
            start = ((z % 2) ^ bit) * half
            parts.append(
                jnp.concatenate(
                    [
                        lax.dynamic_slice_in_dim(w_up, start, half, 1),
                        lax.dynamic_slice_in_dim(w_down_t, start, half, 1),
                    ],
                    axis=1,
                )
            )
        self.own = parts[0]
        self.first = swap_z(parts[1], 1)
        self.second = swap_z(parts[0], 2)
        self.third = swap_z(parts[1], 3)
        self.y_own = swap_y(parts[0])

    def forward(self):
        self.y_early = swap_y(jnp.concatenate([self.first, self.second], axis=0))

    def pieces(self):
        y_third = swap_y(self.third)
        return [self.own, self.first, self.second, self.third, self.y_own, self.y_early, y_third]


def block_places():
    z, y, _, c = place()
    spots = [(z ^ k) * 2 + (y ^ v) for v in range(2) for k in range(4)]
    return jnp.stack(spots + [c]).astype(jnp.int32)


def load_weight(spots, pieces, weight, sems):
    if len(pieces) == 1:
        copies = [pltpu.make_async_copy(pieces[0], weight, sems.at[0])]
    else:
        height = weight.shape[0] // 8
        copies = []
        for piece in pieces:
            for block in range(piece.shape[0] // height):
                at = len(copies)
                start = pl.multiple_of(spots[at] * height, 16)
                copies.append(
                    pltpu.make_async_copy(
                        piece.at[pl.ds(block * height, height)],
                        weight.at[pl.ds(start, height)],
                        sems.at[at],
                    )
                )
    for copy in copies:
        copy.start()
    return copies


def norm(values_f):
    center = values_f - jnp.mean(values_f, axis=-1, keepdims=True)
    spread = jnp.mean(center * center, axis=-1, keepdims=True)
    return (center * lax.rsqrt(spread + EPS)).astype(jnp.bfloat16)


def dot_t(left, right):
    return lax.dot_general(left, right, (((1,), (1,)), ((), ())), preferred_element_type=jnp.float32)


VMEM = pl.BlockSpec(memory_space=pltpu.VMEM)
SMEM = pl.BlockSpec(memory_space=pltpu.SMEM)
ANY = pl.BlockSpec(memory_space=pl.ANY)


def local_call(kernel, ins, in_specs, outs, scratch):
    return pl.pallas_call(
        kernel,
        in_specs=in_specs,
        out_specs=[VMEM] * len(outs),
        out_shape=[jax.ShapeDtypeStruct(shape, jnp.bfloat16) for shape in outs],
        scratch_shapes=scratch,
        cost_estimate=pl.CostEstimate(flops=0, bytes_accessed=0, transcendentals=0),
        compiler_params=pltpu.CompilerParams(vmem_limit_bytes=32 * 2**20),
    )(*ins)


def attention(spots, rows, allowed, pieces, qkv_width):
    length, width = rows.shape
    heads = qkv_width // (3 * HEAD_DIM)
    half = length // 2

    def kernel(spots_ref, rows_ref, allowed_ref, *refs):
        piece_refs = refs[: len(pieces)]
        keep, send, weight, projected, mixed, sems = refs[len(pieces) :]
        copies = load_weight(spots_ref, piece_refs, weight, sems)
        normed = norm(rows_ref[...].astype(jnp.float32))
        mixed[...] = jnp.zeros_like(mixed)
        for copy in copies:
            copy.wait()
        projected[...] = (
            jnp.dot(normed, weight[...], preferred_element_type=jnp.float32)
            .astype(jnp.bfloat16)
            .astype(jnp.float32)
        )
        for head in range(heads):
            at = head * 3 * HEAD_DIM
            query = projected[:, at : at + HEAD_DIM].astype(jnp.bfloat16)
            key = projected[:, at + HEAD_DIM : at + 2 * HEAD_DIM].astype(jnp.bfloat16)
            value = projected[:, at + 2 * HEAD_DIM : at + 3 * HEAD_DIM].astype(jnp.bfloat16)
            scores = dot_t(query, key) * HEAD_DIM ** (-0.5)
            scores = jnp.where(allowed_ref[...] > 0, scores, -1e30)
            exponent = jnp.exp(scores - jnp.max(scores, axis=-1, keepdims=True))
            soft = (exponent / jnp.sum(exponent, axis=-1, keepdims=True)).astype(jnp.bfloat16)
            out_at = qkv_width + head * HEAD_DIM
            mixed[:, out_at : out_at + HEAD_DIM] = jnp.dot(
                soft, value, preferred_element_type=jnp.float32
            )
        projected[...] = dot_t(mixed[...].astype(jnp.bfloat16), weight[...])
        core = spots_ref[8]
        keep[...] = projected[pl.ds(pl.multiple_of(core * half, 16), half), :].astype(jnp.bfloat16)
        send[...] = projected[pl.ds(pl.multiple_of((1 - core) * half, 16), half), :].astype(
            jnp.bfloat16
        )

    return local_call(
        kernel,
        [spots, rows, allowed] + pieces,
        [SMEM, VMEM, VMEM] + [ANY] * len(pieces),
        [(half, width)] * 2,
        [
            pltpu.VMEM((width, width), jnp.bfloat16),
            pltpu.VMEM((length, width), jnp.float32),
            pltpu.VMEM((length, width), jnp.float32),
            pltpu.SemaphoreType.DMA((8,)),
        ],
    )


def middle(spots, rows, left, right):
    half, width = left.shape

    def kernel(spots_ref, rows_ref, left_ref, right_ref, mid, normed):
        base = rows_ref[pl.ds(pl.multiple_of(spots_ref[8] * half, 16), half), :]
        total = left_ref[...].astype(jnp.float32) + right_ref[...].astype(jnp.float32)
        value = (base.astype(jnp.float32) + total).astype(jnp.bfloat16)
        mid[...] = value
        normed[...] = norm(value.astype(jnp.float32))

    return local_call(
        kernel, [spots, rows, left, right], [SMEM, VMEM, VMEM, VMEM], [(half, width)] * 2, []
    )


def feed_forward(spots, mine, others, pieces):
    half, width = mine.shape
    units = width // 2

    def kernel(spots_ref, mine_ref, others_ref, *refs):
        piece_refs = refs[: len(pieces)]
        keep, send, weight, sems = refs[len(pieces) :]
        for copy in load_weight(spots_ref, piece_refs, weight, sems):
            copy.wait()
        for source, target in ((others_ref, send), (mine_ref, keep)):
            hidden = jnp.dot(
                source[...], weight[:, :units], preferred_element_type=jnp.float32
            )
            hidden = 0.5 * hidden * (1.0 + lax.erf(hidden * 0.5**0.5))
            target[...] = dot_t(hidden.astype(jnp.bfloat16), weight[:, units:]).astype(jnp.bfloat16)

    return local_call(
        kernel,
        [spots, mine, others] + pieces,
        [SMEM, VMEM, VMEM] + [ANY] * len(pieces),
        [(half, width)] * 2,
        [pltpu.VMEM((width, width), jnp.bfloat16), pltpu.SemaphoreType.DMA((8,))],
    )


def pick(rows, which, axis):
    return lax.dynamic_index_in_dim(rows, which, axis, keepdims=False)


def add_short(left, right):
    return left.astype(jnp.float32) + right.astype(jnp.float32)


def join_core(half, axis):
    _, _, _, c = place()
    other = swap_core(half)
    first = jnp.where(c == 0, half, other)
    second = jnp.where(c == 0, other, half)
    return jnp.concatenate([first, second], axis=axis)


def exchange_blocks(blocks):
    z, y, _, _ = place()
    groups = blocks.shape[1]
    if groups > 1:
        members = [[i * groups + g for g in range(groups)] for i in range(8)]
        blocks = lax.all_to_all(
            blocks, "req", split_axis=1, concat_axis=1, tiled=True, axis_index_groups=members
        )
    blocks = blocks.reshape((4, 2) + blocks.shape[1:])
    kept = pick(blocks, y, 1)
    other = swap_y(pick(blocks, 1 - y, 1))
    both = jnp.stack([kept, other], axis=1)
    mixed = [pick(both, z, 0)] + [swap_z(pick(both, z ^ k, 0), k) for k in (1, 2, 3)]
    return jnp.concatenate(mixed, axis=0)


def on_device(
    patches,
    half_grid,
    text_embed,
    dest_dev,
    dest_pos,
    text_len,
    enc_qkv,
    enc_out_t,
    enc_up,
    enc_down_t,
    merge_t,
    dec_qkv,
    dec_out_t,
    dec_up,
    dec_down_t,
):
    _, _, x, c = place()
    senders = lax.axis_size("req")
    image_count = half_grid.shape[0]
    model_width = patches.shape[1]
    cells = HALF * HALF
    slot_count = image_count * cells
    qkv_width = enc_qkv.shape[1]
    half_width = model_width // 2
    spots = block_places()

    enc_attn = Same(own_rows(jnp.concatenate([enc_qkv, enc_out_t], axis=1)))
    enc_up, enc_down_t = own_rows(enc_up), own_rows(enc_down_t)
    dec_up, dec_down_t = own_rows(dec_up), own_rows(dec_down_t)
    enc_attn.second, enc_up, enc_down_t = together(enc_attn.second, enc_up, enc_down_t)
    enc_attn.forward()
    enc_ff = Halved(enc_up, enc_down_t)
    enc_attn_pieces = enc_attn.pieces()

    cell_index = jnp.arange(cells, dtype=jnp.int32)
    slot_valid = ((cell_index // HALF)[None, :] < half_grid[:, 0:1]) & (
        (cell_index % HALF)[None, :] < half_grid[:, 1:2]
    )
    slot_valid = slot_valid.reshape(-1)

    rows = patches.reshape(image_count, HALF, 2, HALF, 2, model_width)
    rows = rows.transpose(4, 2, 0, 1, 3, 5).reshape(4 * slot_count, model_width)
    image_of = jnp.tile(jnp.arange(slot_count, dtype=jnp.int32) // cells, 4)
    allowed = (image_of[:, None] == image_of[None, :]) & jnp.tile(slot_valid, 4)[None, :]
    allowed = allowed.astype(jnp.float32)

    rows, enc_ff.first, merge_t, dec_qkv, dec_out_t = together(
        rows, enc_ff.first, merge_t, dec_qkv, dec_out_t
    )
    w_merge = all_rows(merge_t)
    w_dec_attn = all_rows(jnp.concatenate([dec_qkv, dec_out_t], axis=1))
    keep, send = attention(spots, rows, allowed, enc_attn_pieces, qkv_width)
    mine = add_short(keep, swap_core(send)).astype(jnp.bfloat16)
    mine, enc_ff.second = together(mine, enc_ff.second)
    enc_ff.forward()
    mid, normed = middle(spots, rows, mine, swap_x(mine))
    normed, enc_ff.third = together(normed, enc_ff.third)
    enc_ff_pieces = enc_ff.pieces()
    normed_pair = swap_z(normed, 1)
    own_keep, own_send = feed_forward(spots, normed, swap_core(normed), enc_ff_pieces)
    pair_keep, pair_send = feed_forward(spots, normed_pair, swap_core(normed_pair), enc_ff_pieces)
    pair_sum = add_short(pair_keep, swap_core(pair_send)).astype(jnp.bfloat16)
    arrived = swap_z(pair_sum, 1)
    own_sum = add_short(own_keep, swap_core(own_send))
    arrived, dec_up, dec_down_t = together(arrived, dec_up, dec_down_t)
    dec_ff = Halved(dec_up, dec_down_t)
    total = (own_sum + arrived.astype(jnp.float32)).astype(jnp.bfloat16)
    total = total.reshape(2, slot_count, model_width)
    total = add_short(pick(total, x, 0), swap_x(pick(total, 1 - x, 0)))
    kept = pick(mid.reshape(2, slot_count, model_width), x, 0)
    encoded = (kept.astype(jnp.float32) + total).astype(jnp.bfloat16)

    encoded, dec_ff.first = together(encoded, dec_ff.first)
    partial_merge = dot_t(encoded, w_merge).astype(jnp.bfloat16)
    partial_merge = partial_merge.reshape(slot_count, 2, half_width)
    merged = add_short(pick(partial_merge, c, 1), swap_core(pick(partial_merge, 1 - c, 1)))
    merged = merged.astype(jnp.bfloat16)
    merged, dec_ff.second = together(merged, dec_ff.second)
    dec_ff.forward()
    merged = add_short(merged, swap_x(merged)).astype(jnp.bfloat16)

    even_share = slot_count // senders
    capacity = even_share + max(even_share // 2, 1)
    padded = -(-capacity // 16) * 16
    one_hot = (dest_dev[:, None] == jnp.arange(senders, dtype=jnp.int32)[None, :]).astype(jnp.int32)
    earlier = jnp.cumsum(one_hot, axis=0) - one_hot
    slot_rank = jnp.sum(earlier * one_hot, axis=1)
    bucket = dest_dev * padded + slot_rank
    chosen = jnp.arange(senders * padded, dtype=jnp.int32)[:, None] == bucket[None, :]
    digits = jnp.stack([slot_valid.astype(jnp.int32), dest_pos // 128, dest_pos % 128], 1)
    digits = jnp.pad(digits, ((0, 0), (0, 125))).astype(jnp.bfloat16)
    outgoing = jnp.dot(
        chosen.astype(jnp.bfloat16),
        jnp.concatenate([merged, digits], axis=1),
        preferred_element_type=jnp.float32,
    ).astype(jnp.bfloat16)
    outgoing, dec_ff.third = together(outgoing, dec_ff.third)
    dec_ff_pieces = dec_ff.pieces()
    incoming = exchange_blocks(outgoing.reshape(8, senders // 8, padded, -1))
    incoming = incoming.reshape(senders * padded, -1)

    seq_len = text_embed.shape[0]
    half_rows = seq_len // 2
    positions = jnp.arange(seq_len, dtype=jnp.int32)
    marks = incoming[:, half_width:].astype(jnp.int32)
    target = jnp.where(marks[:, 0] > 0, marks[:, 1] * 128 + marks[:, 2], -1)
    hits = positions[:, None] == target[None, :]
    placed = jnp.dot(
        hits.astype(jnp.bfloat16), incoming[:, :half_width], preferred_element_type=jnp.float32
    ).astype(jnp.bfloat16)
    text_half = lax.dynamic_slice_in_dim(text_embed, c * half_width, half_width, 1)
    dec_half = jnp.where(jnp.any(hits, axis=1)[:, None], placed, text_half)
    rows = join_core(dec_half, 1)

    causal = (positions[:, None] >= positions[None, :]).astype(jnp.float32)
    keep, send = attention(spots, rows, causal, [w_dec_attn], qkv_width)
    mine = add_short(keep, swap_core(send)).astype(jnp.bfloat16)
    mid, normed = middle(spots, rows, mine, swap_x(mine))
    normed_pair = swap_z(normed, 1)
    own_keep, own_send = feed_forward(spots, normed, swap_core(normed), dec_ff_pieces)
    pair_keep, pair_send = feed_forward(spots, normed_pair, swap_core(normed_pair), dec_ff_pieces)
    pair_sum = add_short(pair_keep, swap_core(pair_send)).astype(jnp.bfloat16)
    arrived = swap_z(pair_sum, 1)
    own_sum = add_short(own_keep, swap_core(own_send))
    total = (own_sum + arrived.astype(jnp.float32)).astype(jnp.bfloat16)
    total = add_short(total, swap_x(total))
    decoded = (mid.astype(jnp.float32) + total).astype(jnp.bfloat16)
    keep_mask = positions < slot_count + text_len[0]
    keep_half = pick(keep_mask.reshape(2, half_rows), c, 0)
    decoded = jnp.where(keep_half[:, None], decoded, jnp.zeros_like(decoded))
    return join_core(decoded, 0)


def solution(mesh):
    return jax.shard_map(
        on_device,
        mesh=mesh,
        in_specs=(
            P("req", None),
            P("req", None),
            P("req", None),
            P("req"),
            P("req"),
            P("req"),
            P("req", "tp"),
            P("req", "tp"),
            P("req", "tp"),
            P("req", "tp"),
            P("req", "tp"),
            P("req", "tp"),
            P("req", "tp"),
            P("req", "tp"),
            P("req", "tp"),
        ),
        out_specs=P("req", None),
        check_vma=False,
    )
```

time: 376 us -> 395 us (1.051)
  waiting for transfers between devices: 175 us -> 280 us
  local copies, waits for them, and re-layouts: 77.9 us -> 7.38 us
  Pallas kernels: 0 us -> 29.8 us
  matrix products: 33.1 us -> 3.45 us
  other arithmetic: 28.9 us -> 10.2 us
  between operations: 1.93 us -> 14.7 us
  starting transfers between devices: 56.9 us -> 48.9 us
    ppermute x22 -> x16, waiting for transfers between devices: 93.3 us -> 175 us  [swap_z(): return lax.ppermute(part, AXES, routes(lambda z, y, x, c: (z ^ k, y, x, c)))]
    pallas_call x0 -> x8, Pallas kernels: none -> 29.8 us  [local_call(): pl.pallas_call(kernel, in_specs=in_specs, out_specs=[VMEM] * len(outs), o...]
    unnamed x66 -> x35, local copies, waits for them, and re-layouts: 31.3 us -> 3.48 us
    dot_general x12 -> x1, matrix products: 30.7 us -> 3.05 us  [dot_t(): lax.dot_general(left, right, (((1,), (1,)), ((), ())), preferred_element_...]
    ppermute x16 -> x10, waiting for transfers between devices: 55 us -> 71.1 us  [swap_y(): return lax.ppermute(part, AXES, routes(lambda z, y, x, c: (z, 1 - y, x, c)))]
    concatenate x12 -> x0, local copies, waits for them, and re-layouts: 15.6 us -> none  [the longest x5 10.6 us: finish(): jnp.concatenate([self.own, self.first, self.second, self.third, self.y_ow...]
    ppermute x16 -> x10, starting transfers between devices: 24.9 us -> 12 us  [swap_y(): return lax.ppermute(part, AXES, routes(lambda z, y, x, c: (z, 1 - y, x, c)))]
    ppermute x6 -> x0, local copies, waits for them, and re-layouts: 9.79 us -> none  [the longest x3 5.76 us: swap_y(): return lax.ppermute(part, AXES, routes(lambda z, y, x, c: (z, 1 - y, x, c)))]
  transfers between devices with their start and end apart: 56 -> 46, of which waited for: 31 -> 31; matrix products, arithmetic and copies ran while one was open for 30% -> 3% of each run, Pallas kernels for 0% -> 6%
where the time goes in v3:
time: 395 us; the launch traced here: 394 us
  waiting for transfers between devices  280 us (71%)
  starting transfers between devices  48.9 us (12%)
  Pallas kernels  29.8 us (8%)
  between operations  14.7 us (4%)
  other arithmetic  10.2 us (3%)
  local copies, waits for them, and re-layouts  7.38 us (2%)
    ppermute x16, waiting for transfers between devices, swap_z(): return lax.ppermute(part, AXES, routes(lambda z, y, x, c: (z ^ k, y, x, c)))  175 us
    ppermute x10, waiting for transfers between devices, swap_y(): return lax.ppermute(part, AXES, routes(lambda z, y, x, c: (z, 1 - y, x, c)))  71.1 us
    ppermute x16, starting transfers between devices, swap_z(): return lax.ppermute(part, AXES, routes(lambda z, y, x, c: (z ^ k, y, x, c)))  30.4 us
    pallas_call x8, Pallas kernels, local_call(): pl.pallas_call(kernel, in_specs=in_specs, out_specs=[VMEM] * len(outs), o...  29.8 us
    ppermute x5, waiting for transfers between devices, swap_x(): return lax.ppermute(part, AXES, routes(lambda z, y, x, c: (z, y, 1 - x, c)))  28.4 us
    ppermute x10, starting transfers between devices, swap_y(): return lax.ppermute(part, AXES, routes(lambda z, y, x, c: (z, 1 - y, x, c)))  12 us
  transfers between devices with their start and end apart: 46, of which 31 were waited for; matrix products, arithmetic and copies ran while one was open for 3% of the time, Pallas kernels for 6%

profile of v3, /device:TPU:0, one launch (start us, length us, event | category | flops | bytes accessed | tf_op | source)
XLA Modules:
  0.0 394.2 jit_solution(5052186723057594567)
XLA Ops:
  6.5 1.2 pad_maximum_fusion.5.refs_0_
  7.7 4.1 %collective-permute-start = (bf16[160,1280]{1,0:T(8,128)(2,1)S(1)}, bf16[160,1280]{1,0:T(8,128)(2,1)S(1)}, u32[]{:S(2)}, u32[]{:S(2)}) collective-permute-start(bf16[160,1280]{1,0:T(8,128)(2,1)S(1)} %pad_maximum_fusion.5.refs_0_), channel_id=1, source_target_pairs={{0,16},{1,17},{2,18},{3,19},{4,20},{5,21},{6,22},{7,23},{8,24},{9,... | collective-permute-start | bytes 1228808 | tf_op jit(solution)/shard_map/ppermute | solution.py:43
  11.8 18.2 %collective-permute-done.refs_2_ = bf16[160,1280]{1,0:T(8,128)(2,1)S(1)} collective-permute-done((bf16[160,1280]{1,0:T(8,128)(2,1)S(1)}, bf16[160,1280]{1,0:T(8,128)(2,1)S(1)}, u32[]{:S(2)}, u32[]{:S(2)}) %collective-permute-start) | collective-permute-done | bytes 409632 | tf_op jit(solution)/shard_map/ppermute | solution.py:43
  30.1 2.1 constant_dynamic-slice_fusion.7
  32.2 0.8 collective-permute-start.1
  33.4 9.6 %collective-permute-done.1.refs_1_ = bf16[160,1280]{1,0:T(8,128)(2,1)S(1)} collective-permute-done((bf16[160,1280]{1,0:T(8,128)(2,1)S(1)}, bf16[160,1280]{1,0:T(8,128)(2,1)S(1)}, u32[]{:S(2)}, u32[]{:S(2)}) %collective-permute-start.1) | collective-permute-done | bytes 409632 | tf_op jit(solution)/shard_map/ppermute | solution.py:43
  43.0 1.5 collective-permute-start.2
  45.1 10.4 %collective-permute-done.2.refs_1_ = bf16[160,1280]{1,0:T(8,128)(2,1)S(1)} collective-permute-done((bf16[160,1280]{1,0:T(8,128)(2,1)S(1)}, bf16[160,1280]{1,0:T(8,128)(2,1)S(1)}, u32[]{:S(2)}, u32[]{:S(2)}) %collective-permute-start.2) | collective-permute-done | bytes 409632 | tf_op jit(solution)/shard_map/ppermute | solution.py:43
  55.5 1.0 pad_maximum_fusion
  56.5 1.3 collective-permute-start.5
  57.7 0.8 collective-permute-start.4
  58.6 13.5 %collective-permute-done.3.refs_3_ = bf16[160,1280]{1,0:T(8,128)(2,1)S(1)} collective-permute-done((bf16[160,1280]{1,0:T(8,128)(2,1)S(1)}, bf16[160,1280]{1,0:T(8,128)(2,1)S(1)}, u32[]{:S(2)}, u32[]{:S(2)}) %collective-permute-start.3) | collective-permute-done | bytes 409632 | tf_op jit(solution)/shard_map/ppermute | solution.py:43
  72.1 1.5 collective-permute-start.6
  74.2 1.2 compare_and_fusion
  75.7 15.7 %collective-permute-done.4.refs_4_ = bf16[160,1280]{1,0:T(8,128)(2,1)} collective-permute-done((bf16[160,1280]{1,0:T(8,128)(2,1)S(1)}, bf16[160,1280]{1,0:T(8,128)(2,1)}, u32[]{:S(2)}, u32[]{:S(2)}) %collective-permute-start.4) | collective-permute-done | bytes 409632 | tf_op jit(solution)/shard_map/ppermute | solution.py:39
  91.4 15.4 %collective-permute-done.6.refs_6_ = bf16[160,1280]{1,0:T(8,128)(2,1)} collective-permute-done((bf16[160,1280]{1,0:T(8,128)(2,1)S(1)}, bf16[160,1280]{1,0:T(8,128)(2,1)}, u32[]{:S(2)}, u32[]{:S(2)}) %collective-permute-start.6) | collective-permute-done | bytes 409632 | tf_op jit(solution)/shard_map/ppermute | solution.py:39
  106.9 6.0 %shard_map.145 = (bf16[128,1280]{1,0:T(8,128)(2,1)S(1)}, bf16[128,1280]{1,0:T(8,128)(2,1)S(1)}) custom-call(s32[9]{0:T(128)S(1)} %stack.59.spots_ref, bf16[256,1280]{1,0:T(8,128)(2,1)S(1)} %bitcast.56, f32[256,256]{1,0:T(8,128)S(1)} %and_convert_fusion.allowed_ref, bf16[160,1280]{1,0:T(8,128)(2,1)S(1)} %pad_maximum_fusion.5.refs_0_, ...), custom_call_target="tpu_custom_call" | custom-call | tf_op jit(solution)/shard_map/pallas_call | solution.py:158
  113.0 7.1 %collective-permute-start.10 = (bf16[160,1280]{1,0:T(8,128)(2,1)S(1)}, bf16[160,1280]{1,0:T(8,128)(2,1)S(1)}, u32[]{:S(2)}, u32[]{:S(2)}) collective-permute-start(bf16[160,1280]{1,0:T(8,128)(2,1)S(1)} %copy-done.11), channel_id=1, source_target_pairs={{0,24},{1,25},{2,26},{3,27},{4,28},{5,29},{6,30},{7,31},{8,16},{9,... | collective-permute-start | bytes 1228808 | tf_op jit(solution)/shard_map/ppermute | solution.py:43
  120.3 40.2 %collective-permute-done.8.refs_2_ = bf16[160,1280]{1,0:T(8,128)(2,1)S(1)} collective-permute-done((bf16[160,1280]{1,0:T(8,128)(2,1)S(1)}, bf16[160,1280]{1,0:T(8,128)(2,1)S(1)}, u32[]{:S(2)}, u32[]{:S(2)}) %collective-permute-start.8) | collective-permute-done | bytes 409632 | tf_op jit(solution)/shard_map/ppermute | solution.py:43
  160.5 1.5 collective-permute-start.9
  162.6 7.5 %collective-permute-done.9.right_ref = bf16[128,1280]{1,0:T(8,128)(2,1)S(1)} collective-permute-done((bf16[128,1280]{1,0:T(8,128)(2,1)S(1)}, bf16[128,1280]{1,0:T(8,128)(2,1)S(1)}, u32[]{:S(2)}, u32[]{:S(2)}) %collective-permute-start.9) | collective-permute-done | bytes 327712 | tf_op jit(solution)/shard_map/ppermute | solution.py:35
  170.2 1.7 shard_map.146
  173.1 1.5 collective-permute-start.14
  174.6 7.0 %collective-permute-done.16.mine_ref = bf16[128,1280]{1,0:T(8,128)(2,1)S(1)} collective-permute-done((bf16[128,1280]{1,0:T(8,128)(2,1)}, bf16[128,1280]{1,0:T(8,128)(2,1)S(1)}, u32[]{:S(2)}, u32[]{:S(2)}) %collective-permute-start.16) | collective-permute-done | bytes 327712 | tf_op jit(solution)/shard_map/ppermute | solution.py:43
  182.3 9.7 %collective-permute-done.12.refs_4_ = bf16[160,1280]{1,0:T(8,128)(2,1)S(1)} collective-permute-done((bf16[160,1280]{1,0:T(8,128)(2,1)S(1)}, bf16[160,1280]{1,0:T(8,128)(2,1)S(1)}, u32[]{:S(2)}, u32[]{:S(2)}) %collective-permute-start.12) | collective-permute-done | bytes 409632 | tf_op jit(solution)/shard_map/ppermute | solution.py:39
  192.0 7.6 %collective-permute-done.14.refs_6_ = bf16[160,1280]{1,0:T(8,128)(2,1)S(1)} collective-permute-done((bf16[160,1280]{1,0:T(8,128)(2,1)S(1)}, bf16[160,1280]{1,0:T(8,128)(2,1)S(1)}, u32[]{:S(2)}, u32[]{:S(2)}) %collective-permute-start.14) | collective-permute-done | bytes 409632 | tf_op jit(solution)/shard_map/ppermute | solution.py:39
  199.6 4.1 %shard_map.148 = (bf16[128,1280]{1,0:T(8,128)(2,1)S(1)}, bf16[128,1280]{1,0:T(8,128)(2,1)}) custom-call(s32[9]{0:T(128)S(1)} %stack.59.spots_ref, bf16[128,1280]{1,0:T(8,128)(2,1)S(1)} %collective-permute-done.16.mine_ref, bf16[128,1280]{1,0:T(8,128)(2,1)S(1)} %collective-permute-done.17.others_ref, bf16[160,1280]{1,0:T(8,128)(2,1)S(1)} %pad_maximum_fusion.7.refs_0_, ...), custom_call_target="tpu_custom_call" | custom-call | tf_op jit(solution)/shard_map/pallas_call | solution.py:158
  203.7 0.7 copy-done.1
  204.6 1.8 pad_maximum_fusion.10
  206.5 4.6 %shard_map.147 = (bf16[128,1280]{1,0:T(8,128)(2,1)S(1)}, bf16[128,1280]{1,0:T(8,128)(2,1)S(1)}) custom-call(s32[9]{0:T(128)S(1)} %stack.59.spots_ref, bf16[128,1280]{1,0:T(8,128)(2,1)} %get-tuple-element.51.mine_ref, bf16[128,1280]{1,0:T(8,128)(2,1)} %collective-permute-done.11.others_ref, bf16[160,1280]{1,0:T(8,128)(2,1)S(1)} %pad_maximum_fusion.7.refs_0_, ...), custom_call_target="tpu_custom_call" | custom-call | tf_op jit(solution)/shard_map/pallas_call | solution.py:158
  211.7 1.1 add_convert_fusion.1
  213.1 21.9 %collective-permute-done.19 = bf16[128,1280]{1,0:T(8,128)(2,1)S(1)} collective-permute-done((bf16[128,1280]{1,0:T(8,128)(2,1)S(1)}, bf16[128,1280]{1,0:T(8,128)(2,1)S(1)}, u32[]{:S(2)}, u32[]{:S(2)}) %collective-permute-start.19) | collective-permute-done | bytes 327712 | tf_op jit(solution)/shard_map/ppermute | solution.py:43
  235.2 1.4 collective-permute-start.20
  236.8 1.1 collective-permute-start.23
  237.9 3.2 collective-permute-done.20
  241.2 27.2 %collective-permute-done.21.refs_1_ = bf16[160,1280]{1,0:T(8,128)(2,1)S(1)} collective-permute-done((bf16[160,1280]{1,0:T(8,128)(2,1)S(1)}, bf16[160,1280]{1,0:T(8,128)(2,1)S(1)}, u32[]{:S(2)}, u32[]{:S(2)}) %collective-permute-start.21) | collective-permute-done | bytes 409632 | tf_op jit(solution)/shard_map/ppermute | solution.py:43
  268.4 3.0 convolution_convert_fusion
  272.0 1.2 fusion.29
  273.3 6.5 %collective-permute-done.23.refs_2_ = bf16[160,1280]{1,0:T(8,128)(2,1)S(1)} collective-permute-done((bf16[160,1280]{1,0:T(8,128)(2,1)S(1)}, bf16[160,1280]{1,0:T(8,128)(2,1)S(1)}, u32[]{:S(2)}, u32[]{:S(2)}) %collective-permute-start.23) | collective-permute-done | bytes 409632 | tf_op jit(solution)/shard_map/ppermute | solution.py:43
  280.0 4.2 %collective-permute-done.24 = bf16[64,640]{1,0:T(8,128)(2,1)S(1)} collective-permute-done((bf16[64,640]{1,0:T(8,128)(2,1)S(1)}, bf16[64,640]{1,0:T(8,128)(2,1)S(1)}, u32[]{:S(2)}, u32[]{:S(2)}) %collective-permute-start.24) | collective-permute-done | bytes 81952 | tf_op jit(solution)/shard_map/ppermute | solution.py:35
  284.4 5.3 %collective-permute-done.25.refs_3_ = bf16[160,1280]{1,0:T(8,128)(2,1)S(1)} collective-permute-done((bf16[160,1280]{1,0:T(8,128)(2,1)S(1)}, bf16[160,1280]{1,0:T(8,128)(2,1)S(1)}, u32[]{:S(2)}, u32[]{:S(2)}) %collective-permute-start.25) | collective-permute-done | bytes 409632 | tf_op jit(solution)/shard_map/ppermute | solution.py:43
  289.8 3.5 collective-permute-start.26
  293.3 2.6 collective-permute-done.26
  295.9 2.8 collective-permute-start.29
  298.7 10.9 %collective-permute-start.28 = (bf16[2,1,16,768]{3,2,0,1:T(8,128)(2,1)S(1)}, bf16[2,1,16,768]{3,2,0,1:T(8,128)(2,1)S(1)}, u32[]{:S(2)}, u32[]{:S(2)}) collective-permute-start(bf16[2,1,16,768]{3,2,0,1:T(8,128)(2,1)S(1)} %get-tuple-element.93), channel_id=1, source_target_pairs={{0,16},{1,17},{2,18},{3,19},{4,20},{5,21},{6,22},{7,23},{8,24},{9,... | collective-permute-start | bytes 147464 | tf_op jit(solution)/shard_map/ppermute | solution.py:43
  309.6 2.6 collective-permute-done.28
  312.2 1.5 collective-permute-done.27
  314.4 1.5 collective-permute-done.30
  316.0 1.9 copy-done
  317.9 4.5 %shard_map.149 = (bf16[96,1280]{1,0:T(8,128)(2,1)S(1)}, bf16[96,1280]{1,0:T(8,128)(2,1)S(1)}) custom-call(s32[9]{0:T(128)S(1)} %stack.59.spots_ref, bf16[192,1280]{1,0:T(8,128)(2,1)S(1)} %pad_maximum_fusion.3.rows_ref, f32[192,192]{1,0:T(8,128)S(1)} %fusion.4.allowed_ref, bf16[1280,1280]{1,0:T(8,128)(2,1)S(1)} %copy-done), custom_call_target="tpu_custom_call" | custom-call | tf_op jit(solution)/shard_map/pallas_call | solution.py:158
  322.9 1.1 collective-permute-done.31
  324.5 7.6 %collective-permute-done.32.right_ref = bf16[96,1280]{1,0:T(8,128)(2,1)S(1)} collective-permute-done((bf16[96,1280]{1,0:T(8,128)(2,1)S(1)}, bf16[96,1280]{1,0:T(8,128)(2,1)S(1)}, u32[]{:S(2)}, u32[]{:S(2)}) %collective-permute-start.32) | collective-permute-done | bytes 245792 | tf_op jit(solution)/shard_map/ppermute | solution.py:35
  332.1 0.8 shard_map.150
  333.6 0.7 collective-permute-start.34
  334.3 1.3 collective-permute-start.36
  335.6 4.6 %collective-permute-done.38.mine_ref = bf16[96,1280]{1,0:T(8,128)(2,1)S(1)} collective-permute-done((bf16[96,1280]{1,0:T(8,128)(2,1)S(1)}, bf16[96,1280]{1,0:T(8,128)(2,1)S(1)}, u32[]{:S(2)}, u32[]{:S(2)}) %collective-permute-start.38) | collective-permute-done | bytes 245792 | tf_op jit(solution)/shard_map/ppermute | solution.py:43
  340.7 11.9 %collective-permute-done.34.refs_4_ = bf16[160,1280]{1,0:T(8,128)(2,1)S(1)} collective-permute-done((bf16[160,1280]{1,0:T(8,128)(2,1)S(1)}, bf16[160,1280]{1,0:T(8,128)(2,1)S(1)}, u32[]{:S(2)}, u32[]{:S(2)}) %collective-permute-start.34) | collective-permute-done | bytes 409632 | tf_op jit(solution)/shard_map/ppermute | solution.py:39
  352.6 8.2 %collective-permute-done.36.refs_6_ = bf16[160,1280]{1,0:T(8,128)(2,1)S(1)} collective-permute-done((bf16[160,1280]{1,0:T(8,128)(2,1)S(1)}, bf16[160,1280]{1,0:T(8,128)(2,1)S(1)}, u32[]{:S(2)}, u32[]{:S(2)}) %collective-permute-start.36) | collective-permute-done | bytes 409632 | tf_op jit(solution)/shard_map/ppermute | solution.py:39
  360.8 4.1 %shard_map.152 = (bf16[96,1280]{1,0:T(8,128)(2,1)S(1)}, bf16[96,1280]{1,0:T(8,128)(2,1)S(1)}) custom-call(s32[9]{0:T(128)S(1)} %stack.59.spots_ref, bf16[96,1280]{1,0:T(8,128)(2,1)S(1)} %collective-permute-done.38.mine_ref, bf16[96,1280]{1,0:T(8,128)(2,1)S(1)} %collective-permute-done.39.others_ref, bf16[160,1280]{1,0:T(8,128)(2,1)S(1)} %pad_maximum_fusion.9.refs_0_, ...), custom_call_target="tpu_custom_call" | custom-call | tf_op jit(solution)/shard_map/pallas_call | solution.py:158
  365.0 4.1 %shard_map.151 = (bf16[96,1280]{1,0:T(8,128)(2,1)S(1)}, bf16[96,1280]{1,0:T(8,128)(2,1)S(1)}) custom-call(s32[9]{0:T(128)S(1)} %stack.59.spots_ref, bf16[96,1280]{1,0:T(8,128)(2,1)S(1)} %get-tuple-element.71.mine_ref, bf16[96,1280]{1,0:T(8,128)(2,1)S(1)} %collective-permute-done.33.others_ref, bf16[160,1280]{1,0:T(8,128)(2,1)S(1)} %pad_maximum_fusion.9.refs_0_, ...), custom_call_target="tpu_custom_call" | custom-call | tf_op jit(solution)/shard_map/pallas_call | solution.py:158
  370.7 6.9 %collective-permute-done.41 = bf16[96,1280]{1,0:T(8,128)(2,1)S(1)} collective-permute-done((bf16[96,1280]{1,0:T(8,128)(2,1)S(1)}, bf16[96,1280]{1,0:T(8,128)(2,1)S(1)}, u32[]{:S(2)}, u32[]{:S(2)}) %collective-permute-start.41) | collective-permute-done | bytes 245792 | tf_op jit(solution)/shard_map/ppermute | solution.py:43
  378.9 5.9 %collective-permute-done.42 = bf16[96,1280]{1,0:T(8,128)(2,1)S(1)} collective-permute-done((bf16[96,1280]{1,0:T(8,128)(2,1)S(1)}, bf16[96,1280]{1,0:T(8,128)(2,1)S(1)}, u32[]{:S(2)}, u32[]{:S(2)}) %collective-permute-start.42) | collective-permute-done | bytes 245792 | tf_op jit(solution)/shard_map/ppermute | solution.py:35
  385.0 1.5 collective-permute-done.43
  386.6 0.8 pad_maximum_fusion.4
  (134 shorter events, 12.8 us)
Async XLA Ops:
  6.5 26.5 %copy-start.7 = (bf16[256,1280]{1,0:T(8,128)(2,1)S(1)}, bf16[256,1280]{1,0:T(8,128)(2,1)}, u32[]{:S(2)}) copy-start(bf16[256,1280]{1,0:T(8,128)(2,1)} %param.15) | copy-start | bytes 1966084
  6.5 261.9 %all-gather.3.cloned.1.call-start = ((), (), s32[]{:S(2)}) async-start(), calls=%async_computation | async-start | bytes 3686400 | tf_op jit(solution)/shard_map/all_gather | solution.py:61
  7.7 22.3 %collective-permute-start = (bf16[160,1280]{1,0:T(8,128)(2,1)S(1)}, bf16[160,1280]{1,0:T(8,128)(2,1)S(1)}, u32[]{:S(2)}, u32[]{:S(2)}) collective-permute-start(bf16[160,1280]{1,0:T(8,128)(2,1)S(1)} %pad_maximum_fusion.5.refs_0_), channel_id=1, source_target_pairs={{0,16},{1,17},{2,18},{3,19},{4,20},{5,21},{6,22},{7,23},{8,24},{9,... | collective-permute-start | bytes 1228808 | tf_op jit(solution)/shard_map/ppermute | solution.py:43
  32.2 10.8 %copy-start.10 = (bf16[160,1280]{1,0:T(8,128)(2,1)}, bf16[160,1280]{1,0:T(8,128)(2,1)S(1)}, u32[]{:S(2)}) copy-start(bf16[160,1280]{1,0:T(8,128)(2,1)S(1)} %pad_maximum_fusion.6) | copy-start | bytes 1228804
  32.2 10.7 %collective-permute-start.1 = (bf16[160,1280]{1,0:T(8,128)(2,1)S(1)}, bf16[160,1280]{1,0:T(8,128)(2,1)S(1)}, u32[]{:S(2)}, u32[]{:S(2)}) collective-permute-start(bf16[160,1280]{1,0:T(8,128)(2,1)S(1)} %pad_maximum_fusion.6), channel_id=1, source_target_pairs={{0,8},{1,9},{2,10},{3,11},{4,12},{5,13},{6,14},{7,15},{8,0},{9,1},... | collective-permute-start | bytes 1228808 | tf_op jit(solution)/shard_map/ppermute | solution.py:43
  33.3 40.3 %copy-start.15 = (s32[1,2]{1,0:T(1,128)S(1)}, s32[1,2]{1,0:T(1,128)}, u32[]{:S(2)}) copy-start(s32[1,2]{1,0:T(1,128)} %param.16) | copy-start | bytes 28
  43.0 273.0 %all-gather.5.cloned.1.call-start = ((), (), s32[]{:S(2)}) async-start(), calls=%async_computation.1 | async-start | bytes 3686400 | tf_op jit(solution)/shard_map/all_gather | solution.py:61
  43.0 12.5 %collective-permute-start.2 = (bf16[160,1280]{1,0:T(8,128)(2,1)S(1)}, bf16[160,1280]{1,0:T(8,128)(2,1)S(1)}, u32[]{:S(2)}, u32[]{:S(2)}) collective-permute-start(bf16[160,1280]{1,0:T(8,128)(2,1)S(1)} %pad_maximum_fusion.5.refs_0_), channel_id=1, source_target_pairs={{0,8},{1,9},{2,10},{3,11},{4,12},{5,13},{6,14},{7,15},{8,0},{9,1},... | collective-permute-start | bytes 1228808 | tf_op jit(solution)/shard_map/ppermute | solution.py:43
  44.6 27.5 %collective-permute-start.3 = (bf16[160,1280]{1,0:T(8,128)(2,1)S(1)}, bf16[160,1280]{1,0:T(8,128)(2,1)S(1)}, u32[]{:S(2)}, u32[]{:S(2)}) collective-permute-start(bf16[160,1280]{1,0:T(8,128)(2,1)S(1)} %collective-permute-done.refs_2_), channel_id=1, source_target_pairs={{0,8},{1,9},{2,10},{3,11},{4,12},{5,13},{6,14},{7,15},{8,0},{9,1},... | collective-permute-start | bytes 1228808 | tf_op jit(solution)/shard_map/ppermute | solution.py:43
  56.5 35.0 %collective-permute-start.5 = (bf16[320,1280]{1,0:T(8,128)(2,1)}, bf16[320,1280]{1,0:T(8,128)(2,1)S(1)}, u32[]{:S(2)}, u32[]{:S(2)}) collective-permute-start(bf16[320,1280]{1,0:T(8,128)(2,1)} %pad_maximum_fusion), channel_id=1, source_target_pairs={{0,4},{1,5},{2,6},{3,7},{4,0},{5,1},{6,2},{7,3},{8,12},{9,13},{10,... | collective-permute-start | bytes 2457608 | tf_op jit(solution)/shard_map/ppermute | solution.py:39
  57.7 33.7 %collective-permute-start.4 = (bf16[160,1280]{1,0:T(8,128)(2,1)S(1)}, bf16[160,1280]{1,0:T(8,128)(2,1)}, u32[]{:S(2)}, u32[]{:S(2)}) collective-permute-start(bf16[160,1280]{1,0:T(8,128)(2,1)S(1)} %pad_maximum_fusion.5.refs_0_), channel_id=1, source_target_pairs={{0,4},{1,5},{2,6},{3,7},{4,0},{5,1},{6,2},{7,3},{8,12},{9,13},{10,... | collective-permute-start | bytes 1228808 | tf_op jit(solution)/shard_map/ppermute | solution.py:39
  72.1 34.8 %collective-permute-start.6 = (bf16[160,1280]{1,0:T(8,128)(2,1)S(1)}, bf16[160,1280]{1,0:T(8,128)(2,1)}, u32[]{:S(2)}, u32[]{:S(2)}) collective-permute-start(bf16[160,1280]{1,0:T(8,128)(2,1)S(1)} %collective-permute-done.3.refs_3_), channel_id=1, source_target_pairs={{0,4},{1,5},{2,6},{3,7},{4,0},{5,1},{6,2},{7,3},{8,12},{9,13},{10,... | collective-permute-start | bytes 1228808 | tf_op jit(solution)/shard_map/ppermute | solution.py:39
  75.7 37.3 %copy-start.11 = (bf16[160,1280]{1,0:T(8,128)(2,1)S(1)}, bf16[160,1280]{1,0:T(8,128)(2,1)}, u32[]{:S(2)}) copy-start(bf16[160,1280]{1,0:T(8,128)(2,1)} %copy-done.10) | copy-start | bytes 1228804
  75.7 44.4 %copy-start.5 = (bf16[160,640]{1,0:T(8,128)(2,1)S(1)}, bf16[160,640]{1,0:T(8,128)(2,1)}, u32[]{:S(2)}) copy-start(bf16[160,640]{1,0:T(8,128)(2,1)} %get-tuple-element.89) | copy-start | bytes 614404
  75.7 44.4 %copy-start.6 = (bf16[160,640]{1,0:T(8,128)(2,1)S(1)}, bf16[160,640]{1,0:T(8,128)(2,1)}, u32[]{:S(2)}) copy-start(bf16[160,640]{1,0:T(8,128)(2,1)} %get-tuple-element.102) | copy-start | bytes 614404
  112.9 7.3 %collective-permute-start.7 = (bf16[128,1280]{1,0:T(8,128)(2,1)S(1)}, bf16[128,1280]{1,0:T(8,128)(2,1)S(1)}, u32[]{:S(2)}, u32[]{:S(2)}) collective-permute-start(bf16[128,1280]{1,0:T(8,128)(2,1)S(1)} %get-tuple-element.47), channel_id=1, source_target_pairs={{0,1},{1,0},{2,3},{3,2},{4,5},{5,4},{6,7},{7,6},{8,9},{9,8},{10,11... | collective-permute-start | bytes 983048 | tf_op jit(solution)/shard_map/ppermute | solution.py:31
  113.0 59.6 %collective-permute-start.10 = (bf16[160,1280]{1,0:T(8,128)(2,1)S(1)}, bf16[160,1280]{1,0:T(8,128)(2,1)S(1)}, u32[]{:S(2)}, u32[]{:S(2)}) collective-permute-start(bf16[160,1280]{1,0:T(8,128)(2,1)S(1)} %copy-done.11), channel_id=1, source_target_pairs={{0,24},{1,25},{2,26},{3,27},{4,28},{5,29},{6,30},{7,31},{8,16},{9,... | collective-permute-start | bytes 1228808 | tf_op jit(solution)/shard_map/ppermute | solution.py:43
  120.1 40.4 %collective-permute-start.8 = (bf16[160,1280]{1,0:T(8,128)(2,1)S(1)}, bf16[160,1280]{1,0:T(8,128)(2,1)S(1)}, u32[]{:S(2)}, u32[]{:S(2)}) collective-permute-start(bf16[160,1280]{1,0:T(8,128)(2,1)S(1)} %pad_maximum_fusion.7.refs_0_), channel_id=1, source_target_pairs={{0,16},{1,17},{2,18},{3,19},{4,20},{5,21},{6,22},{7,23},{8,24},{9,... | collective-permute-start | bytes 1228808 | tf_op jit(solution)/shard_map/ppermute | solution.py:43
  120.3 61.3 %copy-start.14 = (s32[64]{0:T(128)S(1)}, s32[64]{0:T(128)}, u32[]{:S(2)}) copy-start(s32[64]{0:T(128)} %param.18) | copy-start | bytes 772
  160.5 9.7 %collective-permute-start.9 = (bf16[128,1280]{1,0:T(8,128)(2,1)S(1)}, bf16[128,1280]{1,0:T(8,128)(2,1)S(1)}, u32[]{:S(2)}, u32[]{:S(2)}) collective-permute-start(bf16[128,1280]{1,0:T(8,128)(2,1)S(1)} %add_convert_fusion.2.left_ref), channel_id=1, source_target_pairs={{0,2},{1,3},{2,0},{3,1},{4,6},{5,7},{6,4},{7,5},{8,10},{9,11},{10,... | collective-permute-start | bytes 983048 | tf_op jit(solution)/shard_map/ppermute | solution.py:35
  162.0 37.6 %collective-permute-start.13 = (bf16[320,1280]{1,0:T(8,128)(2,1)S(1)}, bf16[320,1280]{1,0:T(8,128)(2,1)S(1)}, u32[]{:S(2)}, u32[]{:S(2)}) collective-permute-start(bf16[320,1280]{1,0:T(8,128)(2,1)S(1)} %pad_maximum_fusion.1), channel_id=1, source_target_pairs={{0,4},{1,5},{2,6},{3,7},{4,0},{5,1},{6,2},{7,3},{8,12},{9,13},{10,... | collective-permute-start | bytes 2457608 | tf_op jit(solution)/shard_map/ppermute | solution.py:39
  171.8 0.7 copy-start.3
  172.6 9.1 %collective-permute-start.16 = (bf16[128,1280]{1,0:T(8,128)(2,1)}, bf16[128,1280]{1,0:T(8,128)(2,1)S(1)}, u32[]{:S(2)}, u32[]{:S(2)}) collective-permute-start(bf16[128,1280]{1,0:T(8,128)(2,1)} %get-tuple-element.51.mine_ref), channel_id=1, source_target_pairs={{0,8},{1,9},{2,10},{3,11},{4,12},{5,13},{6,14},{7,15},{8,0},{9,1},... | collective-permute-start | bytes 983048 | tf_op jit(solution)/shard_map/ppermute | solution.py:43
  172.6 19.4 %collective-permute-start.12 = (bf16[160,1280]{1,0:T(8,128)(2,1)S(1)}, bf16[160,1280]{1,0:T(8,128)(2,1)S(1)}, u32[]{:S(2)}, u32[]{:S(2)}) collective-permute-start(bf16[160,1280]{1,0:T(8,128)(2,1)S(1)} %pad_maximum_fusion.7.refs_0_), channel_id=1, source_target_pairs={{0,4},{1,5},{2,6},{3,7},{4,0},{5,1},{6,2},{7,3},{8,12},{9,13},{10,... | collective-permute-start | bytes 1228808 | tf_op jit(solution)/shard_map/ppermute | solution.py:39
  173.1 26.5 %collective-permute-start.14 = (bf16[160,1280]{1,0:T(8,128)(2,1)S(1)}, bf16[160,1280]{1,0:T(8,128)(2,1)S(1)}, u32[]{:S(2)}, u32[]{:S(2)}) collective-permute-start(bf16[160,1280]{1,0:T(8,128)(2,1)S(1)} %collective-permute-done.10.refs_3_), channel_id=1, source_target_pairs={{0,4},{1,5},{2,6},{3,7},{4,0},{5,1},{6,2},{7,3},{8,12},{9,13},{10,... | collective-permute-start | bytes 1228808 | tf_op jit(solution)/shard_map/ppermute | solution.py:39
  181.6 18.0 %collective-permute-start.17 = (bf16[128,1280]{1,0:T(8,128)(2,1)S(1)}, bf16[128,1280]{1,0:T(8,128)(2,1)S(1)}, u32[]{:S(2)}, u32[]{:S(2)}) collective-permute-start(bf16[128,1280]{1,0:T(8,128)(2,1)S(1)} %collective-permute-done.16.mine_ref), channel_id=1, source_target_pairs={{0,1},{1,0},{2,3},{3,2},{4,5},{5,4},{6,7},{7,6},{8,9},{9,8},{10,11... | collective-permute-start | bytes 983048 | tf_op jit(solution)/shard_map/ppermute | solution.py:31
  181.7 22.7 %copy-start.16 = (s32[64]{0:T(128)S(1)}, s32[64]{0:T(128)}, u32[]{:S(2)}) copy-start(s32[64]{0:T(128)} %param.19) | copy-start | bytes 772
  181.7 22.9 %copy-start.13 = (bf16[160,320]{1,0:T(8,128)(2,1)S(1)}, bf16[160,320]{1,0:T(8,128)(2,1)}, u32[]{:S(2)}) copy-start(bf16[160,320]{1,0:T(8,128)(2,1)} %param.27) | copy-start | bytes 307204
  181.7 24.8 %collective-permute-start.11 = (bf16[128,1280]{1,0:T(8,128)(2,1)}, bf16[128,1280]{1,0:T(8,128)(2,1)}, u32[]{:S(2)}, u32[]{:S(2)}) collective-permute-start(bf16[128,1280]{1,0:T(8,128)(2,1)} %get-tuple-element.51.mine_ref), channel_id=1, source_target_pairs={{0,1},{1,0},{2,3},{3,2},{4,5},{5,4},{6,7},{7,6},{8,9},{9,8},{10,11... | collective-permute-start | bytes 983048 | tf_op jit(solution)/shard_map/ppermute | solution.py:31
  203.7 0.8 copy-start.1
  204.4 7.3 %collective-permute-start.18 = (bf16[128,1280]{1,0:T(8,128)(2,1)}, bf16[128,1280]{1,0:T(8,128)(2,1)}, u32[]{:S(2)}, u32[]{:S(2)}) collective-permute-start(bf16[128,1280]{1,0:T(8,128)(2,1)} %get-tuple-element.58), channel_id=1, source_target_pairs={{0,1},{1,0},{2,3},{3,2},{4,5},{5,4},{6,7},{7,6},{8,9},{9,8},{10,11... | collective-permute-start | bytes 983048 | tf_op jit(solution)/shard_map/ppermute | solution.py:31
  206.5 5.3 %copy-start.2 = (bf16[128,1280]{1,0:T(8,128)(2,1)S(1)}, bf16[128,1280]{1,0:T(8,128)(2,1)}, u32[]{:S(2)}) copy-start(bf16[128,1280]{1,0:T(8,128)(2,1)} %copy-done.1) | copy-start | bytes 983044
  211.1 25.4 %copy-start.8 = (bf16[160,1280]{1,0:T(8,128)(2,1)S(1)}, bf16[160,1280]{1,0:T(8,128)(2,1)}, u32[]{:S(2)}) copy-start(bf16[160,1280]{1,0:T(8,128)(2,1)} %param.29) | copy-start | bytes 1228804
  211.2 23.9 %collective-permute-start.15 = (bf16[128,1280]{1,0:T(8,128)(2,1)S(1)}, bf16[128,1280]{1,0:T(8,128)(2,1)S(1)}, u32[]{:S(2)}, u32[]{:S(2)}) collective-permute-start(bf16[128,1280]{1,0:T(8,128)(2,1)S(1)} %get-tuple-element.56), channel_id=1, source_target_pairs={{0,1},{1,0},{2,3},{3,2},{4,5},{5,4},{6,7},{7,6},{8,9},{9,8},{10,11... | collective-permute-start | bytes 983048 | tf_op jit(solution)/shard_map/ppermute | solution.py:31
  211.7 24.9 %copy-start.9 = (bf16[160,1280]{1,0:T(8,128)(2,1)S(1)}, bf16[160,1280]{1,0:T(8,128)(2,1)}, u32[]{:S(2)}) copy-start(bf16[160,1280]{1,0:T(8,128)(2,1)} %param.28) | copy-start | bytes 1228804
  212.9 22.2 %collective-permute-start.19 = (bf16[128,1280]{1,0:T(8,128)(2,1)S(1)}, bf16[128,1280]{1,0:T(8,128)(2,1)S(1)}, u32[]{:S(2)}, u32[]{:S(2)}) collective-permute-start(bf16[128,1280]{1,0:T(8,128)(2,1)S(1)} %add_convert_fusion.1), channel_id=1, source_target_pairs={{0,8},{1,9},{2,10},{3,11},{4,12},{5,13},{6,14},{7,15},{8,0},{9,1},... | collective-permute-start | bytes 983048 | tf_op jit(solution)/shard_map/ppermute | solution.py:43
  235.2 5.9 %copy-start.4 = (bf16[128,1280]{1,0:T(8,128)(2,1)S(1)}, bf16[128,1280]{1,0:T(8,128)(2,1)}, u32[]{:S(2)}) copy-start(bf16[128,1280]{1,0:T(8,128)(2,1)} %copy-done.3) | copy-start | bytes 983044
  235.2 5.9 %collective-permute-start.20 = (bf16[64,1280]{1,0:T(8,128)(2,1)S(1)}, bf16[64,1280]{1,0:T(8,128)(2,1)S(1)}, u32[]{:S(2)}, u32[]{:S(2)}) collective-permute-start(bf16[64,1280]{1,0:T(8,128)(2,1)S(1)} %dynamic-slice_bitcast_fusion), channel_id=1, source_target_pairs={{0,2},{1,3},{2,0},{3,1},{4,6},{5,7},{6,4},{7,5},{8,10},{9,11},{10,... | collective-permute-start | bytes 491528 | tf_op jit(solution)/shard_map/ppermute | solution.py:35
  236.7 31.7 %collective-permute-start.21 = (bf16[160,1280]{1,0:T(8,128)(2,1)S(1)}, bf16[160,1280]{1,0:T(8,128)(2,1)S(1)}, u32[]{:S(2)}, u32[]{:S(2)}) collective-permute-start(bf16[160,1280]{1,0:T(8,128)(2,1)S(1)} %pad_maximum_fusion.8), channel_id=1, source_target_pairs={{0,8},{1,9},{2,10},{3,11},{4,12},{5,13},{6,14},{7,15},{8,0},{9,1},... | collective-permute-start | bytes 1228808 | tf_op jit(solution)/shard_map/ppermute | solution.py:43
  236.8 42.9 %collective-permute-start.23 = (bf16[160,1280]{1,0:T(8,128)(2,1)S(1)}, bf16[160,1280]{1,0:T(8,128)(2,1)S(1)}, u32[]{:S(2)}, u32[]{:S(2)}) collective-permute-start(bf16[160,1280]{1,0:T(8,128)(2,1)S(1)} %pad_maximum_fusion.9.refs_0_), channel_id=1, source_target_pairs={{0,16},{1,17},{2,18},{3,19},{4,20},{5,21},{6,22},{7,23},{8,24},{9,... | collective-permute-start | bytes 1228808 | tf_op jit(solution)/shard_map/ppermute | solution.py:43
  271.5 42.6 %copy-start.12 = (bf16[192,1280]{1,0:T(8,128)(2,1)S(1)}, bf16[192,1280]{1,0:T(8,128)(2,1)}, u32[]{:S(2)}) copy-start(bf16[192,1280]{1,0:T(8,128)(2,1)} %param.17) | copy-start | bytes 1474564
  271.9 1.3 collective-permute-start.22
  279.8 4.4 %collective-permute-start.24 = (bf16[64,640]{1,0:T(8,128)(2,1)S(1)}, bf16[64,640]{1,0:T(8,128)(2,1)S(1)}, u32[]{:S(2)}, u32[]{:S(2)}) collective-permute-start(bf16[64,640]{1,0:T(8,128)(2,1)S(1)} %fusion.7), channel_id=1, source_target_pairs={{0,2},{1,3},{2,0},{3,1},{4,6},{5,7},{6,4},{7,5},{8,10},{9,11},{10,... | collective-permute-start | bytes 245768 | tf_op jit(solution)/shard_map/ppermute | solution.py:35
  279.9 9.8 %collective-permute-start.25 = (bf16[160,1280]{1,0:T(8,128)(2,1)S(1)}, bf16[160,1280]{1,0:T(8,128)(2,1)S(1)}, u32[]{:S(2)}, u32[]{:S(2)}) collective-permute-start(bf16[160,1280]{1,0:T(8,128)(2,1)S(1)} %pad_maximum_fusion.8), channel_id=1, source_target_pairs={{0,24},{1,25},{2,26},{3,27},{4,28},{5,29},{6,30},{7,31},{8,16},{9,... | collective-permute-start | bytes 1228808 | tf_op jit(solution)/shard_map/ppermute | solution.py:43
  289.8 6.1 %collective-permute-start.26 = (bf16[4,1,16,768]{3,2,0,1:T(8,128)(2,1)S(1)}, bf16[4,1,16,768]{3,2,0,1:T(8,128)(2,1)S(1)}, u32[]{:S(2)}, u32[]{:S(2)}) collective-permute-start(bf16[4,1,16,768]{3,2,0,1:T(8,128)(2,1)S(1)} %dynamic-slice_bitcast_fusion.1), channel_id=1, source_target_pairs={{0,4},{1,5},{2,6},{3,7},{4,0},{5,1},{6,2},{7,3},{8,12},{9,13},{10,... | collective-permute-start | bytes 294920 | tf_op jit(solution)/shard_map/ppermute | solution.py:39
  295.9 13.7 %collective-permute-start.29 = (bf16[2,1,16,768]{3,2,0,1:T(8,128)(2,1)S(1)}, bf16[2,1,16,768]{3,2,0,1:T(8,128)(2,1)S(1)}, u32[]{:S(2)}, u32[]{:S(2)}) collective-permute-start(bf16[2,1,16,768]{3,2,0,1:T(8,128)(2,1)S(1)} %get-tuple-element.94), channel_id=1, source_target_pairs={{0,24},{1,25},{2,26},{3,27},{4,28},{5,29},{6,30},{7,31},{8,16},{9,... | collective-permute-start | bytes 147464 | tf_op jit(solution)/shard_map/ppermute | solution.py:43
  298.7 13.5 %collective-permute-start.28 = (bf16[2,1,16,768]{3,2,0,1:T(8,128)(2,1)S(1)}, bf16[2,1,16,768]{3,2,0,1:T(8,128)(2,1)S(1)}, u32[]{:S(2)}, u32[]{:S(2)}) collective-permute-start(bf16[2,1,16,768]{3,2,0,1:T(8,128)(2,1)S(1)} %get-tuple-element.93), channel_id=1, source_target_pairs={{0,16},{1,17},{2,18},{3,19},{4,20},{5,21},{6,22},{7,23},{8,24},{9,... | collective-permute-start | bytes 147464 | tf_op jit(solution)/shard_map/ppermute | solution.py:43
  309.6 4.1 %collective-permute-start.27 = (bf16[2,1,16,768]{3,2,0,1:T(8,128)(2,1)S(1)}, bf16[2,1,16,768]{3,2,0,1:T(8,128)(2,1)S(1)}, u32[]{:S(2)}, u32[]{:S(2)}) collective-permute-start(bf16[2,1,16,768]{3,2,0,1:T(8,128)(2,1)S(1)} %get-tuple-element.92), channel_id=1, source_target_pairs={{0,8},{1,9},{2,10},{3,11},{4,12},{5,13},{6,14},{7,15},{8,0},{9,1},... | collective-permute-start | bytes 147464 | tf_op jit(solution)/shard_map/ppermute | solution.py:43
  314.3 1.6 collective-permute-start.30
  316.0 1.9 copy-start
  322.4 1.6 collective-permute-start.31
  322.7 38.1 %collective-permute-start.35 = (bf16[320,1280]{1,0:T(8,128)(2,1)S(1)}, bf16[320,1280]{1,0:T(8,128)(2,1)S(1)}, u32[]{:S(2)}, u32[]{:S(2)}) collective-permute-start(bf16[320,1280]{1,0:T(8,128)(2,1)S(1)} %pad_maximum_fusion.2), channel_id=1, source_target_pairs={{0,4},{1,5},{2,6},{3,7},{4,0},{5,1},{6,2},{7,3},{8,12},{9,13},{10,... | collective-permute-start | bytes 2457608 | tf_op jit(solution)/shard_map/ppermute | solution.py:39
  324.1 8.1 %collective-permute-start.32 = (bf16[96,1280]{1,0:T(8,128)(2,1)S(1)}, bf16[96,1280]{1,0:T(8,128)(2,1)S(1)}, u32[]{:S(2)}, u32[]{:S(2)}) collective-permute-start(bf16[96,1280]{1,0:T(8,128)(2,1)S(1)} %add_convert_fusion.6.left_ref), channel_id=1, source_target_pairs={{0,2},{1,3},{2,0},{3,1},{4,6},{5,7},{6,4},{7,5},{8,10},{9,11},{10,... | collective-permute-start | bytes 737288 | tf_op jit(solution)/shard_map/ppermute | solution.py:35
  333.0 7.2 %collective-permute-start.38 = (bf16[96,1280]{1,0:T(8,128)(2,1)S(1)}, bf16[96,1280]{1,0:T(8,128)(2,1)S(1)}, u32[]{:S(2)}, u32[]{:S(2)}) collective-permute-start(bf16[96,1280]{1,0:T(8,128)(2,1)S(1)} %get-tuple-element.71.mine_ref), channel_id=1, source_target_pairs={{0,8},{1,9},{2,10},{3,11},{4,12},{5,13},{6,14},{7,15},{8,0},{9,1},... | collective-permute-start | bytes 737288 | tf_op jit(solution)/shard_map/ppermute | solution.py:43
  333.6 19.0 %collective-permute-start.34 = (bf16[160,1280]{1,0:T(8,128)(2,1)S(1)}, bf16[160,1280]{1,0:T(8,128)(2,1)S(1)}, u32[]{:S(2)}, u32[]{:S(2)}) collective-permute-start(bf16[160,1280]{1,0:T(8,128)(2,1)S(1)} %pad_maximum_fusion.9.refs_0_), channel_id=1, source_target_pairs={{0,4},{1,5},{2,6},{3,7},{4,0},{5,1},{6,2},{7,3},{8,12},{9,13},{10,... | collective-permute-start | bytes 1228808 | tf_op jit(solution)/shard_map/ppermute | solution.py:39
  334.3 26.5 %collective-permute-start.36 = (bf16[160,1280]{1,0:T(8,128)(2,1)S(1)}, bf16[160,1280]{1,0:T(8,128)(2,1)S(1)}, u32[]{:S(2)}, u32[]{:S(2)}) collective-permute-start(bf16[160,1280]{1,0:T(8,128)(2,1)S(1)} %collective-permute-done.25.refs_3_), channel_id=1, source_target_pairs={{0,4},{1,5},{2,6},{3,7},{4,0},{5,1},{6,2},{7,3},{8,12},{9,13},{10,... | collective-permute-start | bytes 1228808 | tf_op jit(solution)/shard_map/ppermute | solution.py:39
  340.2 20.6 %collective-permute-start.39 = (bf16[96,1280]{1,0:T(8,128)(2,1)S(1)}, bf16[96,1280]{1,0:T(8,128)(2,1)S(1)}, u32[]{:S(2)}, u32[]{:S(2)}) collective-permute-start(bf16[96,1280]{1,0:T(8,128)(2,1)S(1)} %collective-permute-done.38.mine_ref), channel_id=1, source_target_pairs={{0,1},{1,0},{2,3},{3,2},{4,5},{5,4},{6,7},{7,6},{8,9},{9,8},{10,11... | collective-permute-start | bytes 737288 | tf_op jit(solution)/shard_map/ppermute | solution.py:31
  340.2 24.8 %collective-permute-start.33 = (bf16[96,1280]{1,0:T(8,128)(2,1)S(1)}, bf16[96,1280]{1,0:T(8,128)(2,1)S(1)}, u32[]{:S(2)}, u32[]{:S(2)}) collective-permute-start(bf16[96,1280]{1,0:T(8,128)(2,1)S(1)} %get-tuple-element.71.mine_ref), channel_id=1, source_target_pairs={{0,1},{1,0},{2,3},{3,2},{4,5},{5,4},{6,7},{7,6},{8,9},{9,8},{10,11... | collective-permute-start | bytes 737288 | tf_op jit(solution)/shard_map/ppermute | solution.py:31
  364.9 4.7 %collective-permute-start.40 = (bf16[96,1280]{1,0:T(8,128)(2,1)S(1)}, bf16[96,1280]{1,0:T(8,128)(2,1)S(1)}, u32[]{:S(2)}, u32[]{:S(2)}) collective-permute-start(bf16[96,1280]{1,0:T(8,128)(2,1)S(1)} %get-tuple-element.78), channel_id=1, source_target_pairs={{0,1},{1,0},{2,3},{3,2},{4,5},{5,4},{6,7},{7,6},{8,9},{9,8},{10,11... | collective-permute-start | bytes 737288 | tf_op jit(solution)/shard_map/ppermute | solution.py:31
  369.0 1.7 collective-permute-start.37
  369.7 8.0 %collective-permute-start.41 = (bf16[96,1280]{1,0:T(8,128)(2,1)S(1)}, bf16[96,1280]{1,0:T(8,128)(2,1)S(1)}, u32[]{:S(2)}, u32[]{:S(2)}) collective-permute-start(bf16[96,1280]{1,0:T(8,128)(2,1)S(1)} %add_convert_fusion.5), channel_id=1, source_target_pairs={{0,8},{1,9},{2,10},{3,11},{4,12},{5,13},{6,14},{7,15},{8,0},{9,1},... | collective-permute-start | bytes 737288 | tf_op jit(solution)/shard_map/ppermute | solution.py:43
  377.7 7.1 %collective-permute-start.42 = (bf16[96,1280]{1,0:T(8,128)(2,1)S(1)}, bf16[96,1280]{1,0:T(8,128)(2,1)S(1)}, u32[]{:S(2)}, u32[]{:S(2)}) collective-permute-start(bf16[96,1280]{1,0:T(8,128)(2,1)S(1)} %add_convert_fusion.4), channel_id=1, source_target_pairs={{0,2},{1,3},{2,0},{3,1},{4,6},{5,7},{6,4},{7,5},{8,10},{9,11},{10,... | collective-permute-start | bytes 737288 | tf_op jit(solution)/shard_map/ppermute | solution.py:35
  384.9 1.6 collective-permute-start.43
Sparse Core Ops, SparseCore 0:
  43.1 103.3 all-gather.2
  206.6 92.4 all-gather.4

commit v4 on v3

--- a/solution.py
+++ b/solution.py
@@ -57,83 +57,71 @@
     return lax.all_gather(weight, "req", axis=0, tiled=True, axis_index_groups=members)
 
 
-def all_rows(weight):
-    return lax.all_gather(weight, "req", axis=0, tiled=True)
-
-
 def together(*values):
     return lax.optimization_barrier(values)
 
 
-class Same:
-    def __init__(self, weight):
-        self.own = weight
-        self.first = swap_z(weight, 1)
-        self.second = swap_z(weight, 2)
-        self.y_own = swap_y(weight)
-
-    def forward(self):
-        self.third = swap_z(self.second, 1)
-        self.y_early = swap_y(jnp.concatenate([self.first, self.second], axis=0))
+def halves_by_z(weight):
+    z, _, _, _ = place()
+    half = weight.shape[1] // 2
+    return [
+        lax.dynamic_slice_in_dim(weight, ((z % 2) ^ bit) * half, half, 1) for bit in (0, 1)
+    ]
+
+
+class Halved:
+    def __init__(self, mine, others, near):
+        self.own = mine
+        self.first = swap_z(near, 1)
+        self.second = swap_z(mine, 2)
+        self.third = swap_z(others, 3)
+        self.y_own = swap_y(mine)
 
     def pieces(self):
-        y_third = swap_y(self.third)
-        return [self.own, self.first, self.second, self.third, self.y_own, self.y_early, y_third]
-
-
-class Halved:
-    def __init__(self, w_up, w_down_t):
-        z, _, _, _ = place()
-        half = w_up.shape[1] // 2
-        parts = []
-        for bit in (0, 1):
-            start = ((z % 2) ^ bit) * half
-            parts.append(
-                jnp.concatenate(
-                    [
-                        lax.dynamic_slice_in_dim(w_up, start, half, 1),
-                        lax.dynamic_slice_in_dim(w_down_t, start, half, 1),
-                    ],
-                    axis=1,
+        column = jnp.concatenate([self.first, self.second, self.third], axis=0)
+        column, self.y_own = together(column, self.y_own)
+        return [self.own, column, self.y_own, swap_y(column)]
+
+
+def halved_column(weight):
+    groups = lax.axis_size("req") // 8
+    half = weight.shape[1] // 2
+    members = [
+        [(z * 2 + y) * groups + g for z in range(4)] for y in range(2) for g in range(groups)
+    ]
+    column = lax.all_to_all(
+        jnp.stack([weight[:, :half], weight[:, half:]] * 2),
+        "req",
+        split_axis=0,
+        concat_axis=0,
+        tiled=True,
+        axis_index_groups=members,
+    ).reshape(-1, half)
+    return [column, swap_y(column)]
+
+
+def block_places():
+    z, y, _, c = place()
+    direct = [(z ^ k) * 2 + (y ^ v) for v in range(2) for k in range(4)]
+    whole = [(z ^ k) * 2 + (y ^ v) for ks in ((0, 2), (1, 3)) for v in range(2) for k in ks]
+    columns = [k * 2 + (y ^ v) for v in range(2) for k in range(4)]
+    return jnp.stack(direct + whole + columns + [c]).astype(jnp.int32)
+
+
+def load_weight(spots, base, pieces, weight, sems):
+    height = weight.shape[0] // 8
+    copies = []
+    for piece in pieces:
+        for block in range(piece.shape[0] // height):
+            at = len(copies)
+            start = pl.multiple_of(spots[base + at] * height, 16)
+            copies.append(
+                pltpu.make_async_copy(
+                    piece.at[pl.ds(block * height, height)],
+                    weight.at[pl.ds(start, height)],
+                    sems.at[at],
                 )
             )
-        self.own = parts[0]
-        self.first = swap_z(parts[1], 1)
-        self.second = swap_z(parts[0], 2)
-        self.third = swap_z(parts[1], 3)
-        self.y_own = swap_y(parts[0])
-
-    def forward(self):
-        self.y_early = swap_y(jnp.concatenate([self.first, self.second], axis=0))
-
-    def pieces(self):
-        y_third = swap_y(self.third)
-        return [self.own, self.first, self.second, self.third, self.y_own, self.y_early, y_third]
-
-
-def block_places():
-    z, y, _, c = place()
-    spots = [(z ^ k) * 2 + (y ^ v) for v in range(2) for k in range(4)]
-    return jnp.stack(spots + [c]).astype(jnp.int32)
-
-
-def load_weight(spots, pieces, weight, sems):
-    if len(pieces) == 1:
-        copies = [pltpu.make_async_copy(pieces[0], weight, sems.at[0])]
-    else:
-        height = weight.shape[0] // 8
-        copies = []
-        for piece in pieces:
-            for block in range(piece.shape[0] // height):
-                at = len(copies)
-                start = pl.multiple_of(spots[at] * height, 16)
-                copies.append(
-                    pltpu.make_async_copy(
-                        piece.at[pl.ds(block * height, height)],
-                        weight.at[pl.ds(start, height)],
-                        sems.at[at],
-                    )
-                )
     for copy in copies:
         copy.start()
     return copies
@@ -149,12 +137,13 @@
     return lax.dot_general(left, right, (((1,), (1,)), ((), ())), preferred_element_type=jnp.float32)
 
 
+DIRECT, WHOLE, COLUMNS = 0, 8, 16
 VMEM = pl.BlockSpec(memory_space=pltpu.VMEM)
 SMEM = pl.BlockSpec(memory_space=pltpu.SMEM)
 ANY = pl.BlockSpec(memory_space=pl.ANY)
 
 
-def local_call(kernel, ins, in_specs, outs, scratch):
+def local_call(kernel, ins, in_specs, outs, scratch, limit=56):
     return pl.pallas_call(
         kernel,
         in_specs=in_specs,
@@ -162,11 +151,11 @@
         out_shape=[jax.ShapeDtypeStruct(shape, jnp.bfloat16) for shape in outs],
         scratch_shapes=scratch,
         cost_estimate=pl.CostEstimate(flops=0, bytes_accessed=0, transcendentals=0),
-        compiler_params=pltpu.CompilerParams(vmem_limit_bytes=32 * 2**20),
+        compiler_params=pltpu.CompilerParams(vmem_limit_bytes=limit * 2**20),
     )(*ins)
 
 
-def attention(spots, rows, allowed, pieces, qkv_width):
+def attention(spots, base, rows, allowed, pieces, qkv_width):
     length, width = rows.shape
     heads = qkv_width // (3 * HEAD_DIM)
     half = length // 2
@@ -174,7 +163,7 @@
     def kernel(spots_ref, rows_ref, allowed_ref, *refs):
         piece_refs = refs[: len(pieces)]
         keep, send, weight, projected, mixed, sems = refs[len(pieces) :]
-        copies = load_weight(spots_ref, piece_refs, weight, sems)
+        copies = load_weight(spots_ref, base, piece_refs, weight, sems)
         normed = norm(rows_ref[...].astype(jnp.float32))
         mixed[...] = jnp.zeros_like(mixed)
         for copy in copies:
@@ -198,7 +187,7 @@
                 soft, value, preferred_element_type=jnp.float32
             )
         projected[...] = dot_t(mixed[...].astype(jnp.bfloat16), weight[...])
-        core = spots_ref[8]
+        core = spots_ref[24]
         keep[...] = projected[pl.ds(pl.multiple_of(core * half, 16), half), :].astype(jnp.bfloat16)
         send[...] = projected[pl.ds(pl.multiple_of((1 - core) * half, 16), half), :].astype(
             jnp.bfloat16
@@ -222,38 +211,77 @@
     half, width = left.shape
 
     def kernel(spots_ref, rows_ref, left_ref, right_ref, mid, normed):
-        base = rows_ref[pl.ds(pl.multiple_of(spots_ref[8] * half, 16), half), :]
+        base = rows_ref[pl.ds(pl.multiple_of(spots_ref[24] * half, 16), half), :]
         total = left_ref[...].astype(jnp.float32) + right_ref[...].astype(jnp.float32)
         value = (base.astype(jnp.float32) + total).astype(jnp.bfloat16)
         mid[...] = value
         normed[...] = norm(value.astype(jnp.float32))
 
     return local_call(
-        kernel, [spots, rows, left, right], [SMEM, VMEM, VMEM, VMEM], [(half, width)] * 2, []
-    )
-
-
-def feed_forward(spots, mine, others, pieces):
-    half, width = mine.shape
+        kernel, [spots, rows, left, right], [SMEM, VMEM, VMEM, VMEM], [(half, width)] * 2, [], 16
+    )
+
+
+def feed_forward(spots, sources, weights, bases):
+    half, width = sources[0].shape
     units = width // 2
-
-    def kernel(spots_ref, mine_ref, others_ref, *refs):
+    pieces = [piece for weight in weights for piece in weight]
+    parts = len(weights)
+    rows = len(sources)
+
+    def kernel(spots_ref, *refs):
+        source_refs, piece_refs, refs = (
+            refs[:rows],
+            refs[rows : rows + len(pieces)],
+            refs[rows + len(pieces) :],
+        )
+        targets, scratch = refs[:rows], refs[rows:]
+        copies, at = [], 0
+        for part in range(parts):
+            mine = piece_refs[at : at + len(weights[part])]
+            at += len(mine)
+            copies += load_weight(spots_ref, bases[part], mine, scratch[part], scratch[parts + part])
+        for copy in copies:
+            copy.wait()
+        if parts == 1:
+            up, down = scratch[0][:, :units], scratch[0][:, units:]
+        else:
+            up, down = scratch[0][...], scratch[1][...]
+        for source, target in zip(source_refs, targets):
+            hidden = jnp.dot(source[...], up, preferred_element_type=jnp.float32)
+            hidden = 0.5 * hidden * (1.0 + lax.erf(hidden * 0.5**0.5))
+            target[...] = dot_t(hidden.astype(jnp.bfloat16), down).astype(jnp.bfloat16)
+
+    return local_call(
+        kernel,
+        [spots] + sources + pieces,
+        [SMEM] + [VMEM] * rows + [ANY] * len(pieces),
+        [(half, width)] * rows,
+        [pltpu.VMEM((width, weight[0].shape[1]), jnp.bfloat16) for weight in weights]
+        + [pltpu.SemaphoreType.DMA((8,))] * parts,
+    )
+
+
+def merge(spots, base, blocks, pieces):
+    count, width = blocks.shape
+    half = width // 2
+
+    def kernel(spots_ref, blocks_ref, *refs):
         piece_refs = refs[: len(pieces)]
         keep, send, weight, sems = refs[len(pieces) :]
-        for copy in load_weight(spots_ref, piece_refs, weight, sems):
+        for copy in load_weight(spots_ref, base, piece_refs, weight, sems):
             copy.wait()
-        for source, target in ((others_ref, send), (mine_ref, keep)):
-            hidden = jnp.dot(
-                source[...], weight[:, :units], preferred_element_type=jnp.float32
-            )
-            hidden = 0.5 * hidden * (1.0 + lax.erf(hidden * 0.5**0.5))
-            target[...] = dot_t(hidden.astype(jnp.bfloat16), weight[:, units:]).astype(jnp.bfloat16)
+        core = spots_ref[24]
+        source = blocks_ref[...]
+        for side, target in ((core, keep), (1 - core, send)):
+            rows = weight[pl.ds(pl.multiple_of(side * half, 16), half), :]
+            target[...] = dot_t(source, rows).astype(jnp.bfloat16)
 
     return local_call(
         kernel,
-        [spots, mine, others] + pieces,
-        [SMEM, VMEM, VMEM] + [ANY] * len(pieces),
-        [(half, width)] * 2,
+        [spots, blocks] + pieces,
+        [SMEM, VMEM] + [ANY] * len(pieces),
+        [(count, half)] * 2,
         [pltpu.VMEM((width, width), jnp.bfloat16), pltpu.SemaphoreType.DMA((8,))],
     )
 
@@ -274,8 +302,8 @@
     return jnp.concatenate([first, second], axis=axis)
 
 
-def exchange_blocks(blocks):
-    z, y, _, _ = place()
+def exchange_y(blocks):
+    _, y, _, _ = place()
     groups = blocks.shape[1]
     if groups > 1:
         members = [[i * groups + g for g in range(groups)] for i in range(8)]
@@ -283,9 +311,11 @@
             blocks, "req", split_axis=1, concat_axis=1, tiled=True, axis_index_groups=members
         )
     blocks = blocks.reshape((4, 2) + blocks.shape[1:])
-    kept = pick(blocks, y, 1)
-    other = swap_y(pick(blocks, 1 - y, 1))
-    both = jnp.stack([kept, other], axis=1)
+    return jnp.stack([pick(blocks, y, 1), swap_y(pick(blocks, 1 - y, 1))], axis=1)
+
+
+def exchange_z(both):
+    z, _, _, _ = place()
     mixed = [pick(both, z, 0)] + [swap_z(pick(both, z ^ k, 0), k) for k in (1, 2, 3)]
     return jnp.concatenate(mixed, axis=0)
 
@@ -317,13 +347,26 @@
     half_width = model_width // 2
     spots = block_places()
 
-    enc_attn = Same(own_rows(jnp.concatenate([enc_qkv, enc_out_t], axis=1)))
+    enc_attn = own_rows(jnp.concatenate([enc_qkv, enc_out_t], axis=1))
     enc_up, enc_down_t = own_rows(enc_up), own_rows(enc_down_t)
+    merge_t = own_rows(merge_t)
+    dec_attn = own_rows(jnp.concatenate([dec_qkv, dec_out_t], axis=1))
     dec_up, dec_down_t = own_rows(dec_up), own_rows(dec_down_t)
-    enc_attn.second, enc_up, enc_down_t = together(enc_attn.second, enc_up, enc_down_t)
-    enc_attn.forward()
-    enc_ff = Halved(enc_up, enc_down_t)
-    enc_attn_pieces = enc_attn.pieces()
+
+    first, second, y_own = swap_z(enc_attn, 1), swap_z(enc_attn, 2), swap_y(enc_attn)
+    first, second, y_own, enc_up, enc_down_t = together(first, second, y_own, enc_up, enc_down_t)
+    third = swap_z(second, 1)
+    y_early = swap_y(jnp.concatenate([first, second], axis=0))
+
+    up, down = halves_by_z(enc_up), halves_by_z(enc_down_t)
+    mine, others = [jnp.concatenate(pair, axis=1) for pair in zip(up, down)]
+    third, near = together(third, others)
+    enc_ff = Halved(mine, others, near)
+    enc_attn = [enc_attn, first, second, third, y_own, y_early, swap_y(third)]
+    enc_ff.third, merge_t = together(enc_ff.third, merge_t)
+    enc_ff = enc_ff.pieces()
+
+    merge_second = swap_z(merge_t, 2)
 
     cell_index = jnp.arange(cells, dtype=jnp.int32)
     slot_valid = ((cell_index // HALF)[None, :] < half_grid[:, 0:1]) & (
@@ -337,39 +380,37 @@
     allowed = (image_of[:, None] == image_of[None, :]) & jnp.tile(slot_valid, 4)[None, :]
     allowed = allowed.astype(jnp.float32)
 
-    rows, enc_ff.first, merge_t, dec_qkv, dec_out_t = together(
-        rows, enc_ff.first, merge_t, dec_qkv, dec_out_t
-    )
-    w_merge = all_rows(merge_t)
-    w_dec_attn = all_rows(jnp.concatenate([dec_qkv, dec_out_t], axis=1))
-    keep, send = attention(spots, rows, allowed, enc_attn_pieces, qkv_width)
+    keep, send = attention(spots, DIRECT, rows, allowed, enc_attn, qkv_width)
     mine = add_short(keep, swap_core(send)).astype(jnp.bfloat16)
-    mine, enc_ff.second = together(mine, enc_ff.second)
-    enc_ff.forward()
     mid, normed = middle(spots, rows, mine, swap_x(mine))
-    normed, enc_ff.third = together(normed, enc_ff.third)
-    enc_ff_pieces = enc_ff.pieces()
+    normed, merge_second = together(normed, merge_second)
     normed_pair = swap_z(normed, 1)
-    own_keep, own_send = feed_forward(spots, normed, swap_core(normed), enc_ff_pieces)
-    pair_keep, pair_send = feed_forward(spots, normed_pair, swap_core(normed_pair), enc_ff_pieces)
+    sources = [normed, swap_core(normed), normed_pair, swap_core(normed_pair)]
+    merge_two = jnp.concatenate([merge_t, merge_second], axis=0)
+    merge_pair = swap_z(merge_two, 1)
+    merge_two_y = swap_y(merge_two)
+    own_keep, own_send, pair_keep, pair_send = feed_forward(spots, sources, [enc_ff], [DIRECT])
     pair_sum = add_short(pair_keep, swap_core(pair_send)).astype(jnp.bfloat16)
+    pair_sum, merge_pair, merge_two_y, dec_attn = together(
+        pair_sum, merge_pair, merge_two_y, dec_attn
+    )
     arrived = swap_z(pair_sum, 1)
+    attn_second = swap_z(dec_attn, 2)
+    merge_all = [merge_two, merge_two_y, merge_pair, swap_y(merge_pair)]
     own_sum = add_short(own_keep, swap_core(own_send))
-    arrived, dec_up, dec_down_t = together(arrived, dec_up, dec_down_t)
-    dec_ff = Halved(dec_up, dec_down_t)
     total = (own_sum + arrived.astype(jnp.float32)).astype(jnp.bfloat16)
     total = total.reshape(2, slot_count, model_width)
     total = add_short(pick(total, x, 0), swap_x(pick(total, 1 - x, 0)))
     kept = pick(mid.reshape(2, slot_count, model_width), x, 0)
     encoded = (kept.astype(jnp.float32) + total).astype(jnp.bfloat16)
 
-    encoded, dec_ff.first = together(encoded, dec_ff.first)
-    partial_merge = dot_t(encoded, w_merge).astype(jnp.bfloat16)
-    partial_merge = partial_merge.reshape(slot_count, 2, half_width)
-    merged = add_short(pick(partial_merge, c, 1), swap_core(pick(partial_merge, 1 - c, 1)))
+    encoded, attn_second = together(encoded, attn_second)
+    attn_two = jnp.concatenate([dec_attn, attn_second], axis=0)
+    attn_pair = swap_z(attn_two, 1)
+    attn_two_y = swap_y(attn_two)
+    keep, send = merge(spots, WHOLE, encoded, merge_all)
+    merged = add_short(keep, swap_core(send))
     merged = merged.astype(jnp.bfloat16)
-    merged, dec_ff.second = together(merged, dec_ff.second)
-    dec_ff.forward()
     merged = add_short(merged, swap_x(merged)).astype(jnp.bfloat16)
 
     even_share = slot_count // senders
@@ -387,9 +428,19 @@
         jnp.concatenate([merged, digits], axis=1),
         preferred_element_type=jnp.float32,
     ).astype(jnp.bfloat16)
-    outgoing, dec_ff.third = together(outgoing, dec_ff.third)
-    dec_ff_pieces = dec_ff.pieces()
-    incoming = exchange_blocks(outgoing.reshape(8, senders // 8, padded, -1))
+    outgoing, attn_pair, attn_two_y, dec_up = together(outgoing, attn_pair, attn_two_y, dec_up)
+    mine, others = halves_by_z(dec_up)
+    dec_up = Halved(mine, others, others)
+    both = exchange_y(outgoing.reshape(8, senders // 8, padded, -1))
+    both, attn_pair = together(both, attn_pair)
+    both, dec_up.first, dec_up.second, dec_up.third = together(
+        both, dec_up.first, dec_up.second, dec_up.third
+    )
+    dec_up = dec_up.pieces()
+    dec_attn = [attn_two, attn_two_y, attn_pair, swap_y(attn_pair)]
+    incoming = exchange_z(both)
+    incoming, dec_down_t = together(incoming, dec_down_t)
+    dec_down = halved_column(dec_down_t)
     incoming = incoming.reshape(senders * padded, -1)
 
     seq_len = text_embed.shape[0]
@@ -404,14 +455,14 @@
     text_half = lax.dynamic_slice_in_dim(text_embed, c * half_width, half_width, 1)
     dec_half = jnp.where(jnp.any(hits, axis=1)[:, None], placed, text_half)
     rows = join_core(dec_half, 1)
-
     causal = (positions[:, None] >= positions[None, :]).astype(jnp.float32)
-    keep, send = attention(spots, rows, causal, [w_dec_attn], qkv_width)
+    keep, send = attention(spots, WHOLE, rows, causal, dec_attn, qkv_width)
     mine = add_short(keep, swap_core(send)).astype(jnp.bfloat16)
+    mine, *dec_up = together(mine, *dec_up)
     mid, normed = middle(spots, rows, mine, swap_x(mine))
     normed_pair = swap_z(normed, 1)
-    own_keep, own_send = feed_forward(spots, normed, swap_core(normed), dec_ff_pieces)
-    pair_keep, pair_send = feed_forward(spots, normed_pair, swap_core(normed_pair), dec_ff_pieces)
+    sources = [normed, swap_core(normed), normed_pair, swap_core(normed_pair)]
+    own_keep, own_send, pair_keep, pair_send = feed_forward(spots, sources, [dec_up, dec_down], [DIRECT, COLUMNS])
     pair_sum = add_short(pair_keep, swap_core(pair_send)).astype(jnp.bfloat16)
     arrived = swap_z(pair_sum, 1)
     own_sum = add_short(own_keep, swap_core(own_send))

time: 395 us -> 272 us (0.69)
  waiting for transfers between devices: 280 us -> 145 us
  starting transfers between devices: 48.9 us -> 63.6 us
  between operations: 14.7 us -> 1.66 us
  other arithmetic: 10.2 us -> 16.8 us
  Pallas kernels: 29.8 us -> 34.3 us
    ppermute x16 -> x20, waiting for transfers between devices: 175 us -> 81.7 us  [swap_z(): return lax.ppermute(part, AXES, routes(lambda z, y, x, c: (z ^ k, y, x, c)))]
    ppermute x10 -> x13, waiting for transfers between devices: 71.1 us -> 32.9 us  [swap_y(): return lax.ppermute(part, AXES, routes(lambda z, y, x, c: (z, 1 - y, x, c)))]
    ppermute x10 -> x13, starting transfers between devices: 12 us -> 24.9 us  [swap_y(): return lax.ppermute(part, AXES, routes(lambda z, y, x, c: (z, 1 - y, x, c)))]
    ppermute x16 -> x20, starting transfers between devices: 30.4 us -> 25.8 us  [swap_z(): return lax.ppermute(part, AXES, routes(lambda z, y, x, c: (z ^ k, y, x, c)))]
    pallas_call x8 -> x7, Pallas kernels: 29.8 us -> 34.3 us  [local_call(): pl.pallas_call(kernel, in_specs=in_specs, out_specs=[VMEM] * len(outs), o...]
    ppermute x5, starting transfers between devices: 3.79 us -> 7.74 us  [swap_x(): return lax.ppermute(part, AXES, routes(lambda z, y, x, c: (z, y, 1 - x, c)))]
  transfers between devices with their start and end apart: 46 -> 52, of which waited for: 31 -> 29; matrix products, arithmetic and copies ran while one was open for 3% -> 7% of each run, Pallas kernels for 6% -> 10%
where the time goes in v4:
time: 272 us
  waiting for transfers between devices  145 us (53%)
  starting transfers between devices  63.6 us (23%)
  Pallas kernels  34.3 us (13%)
  other arithmetic  16.8 us (6%)
  local copies, waits for them, and re-layouts  8.53 us (3%)
    ppermute x20, waiting for transfers between devices, swap_z(): return lax.ppermute(part, AXES, routes(lambda z, y, x, c: (z ^ k, y, x, c)))  81.7 us
    pallas_call x7, Pallas kernels, local_call(): pl.pallas_call(kernel, in_specs=in_specs, out_specs=[VMEM] * len(outs), o...  34.3 us
    ppermute x13, waiting for transfers between devices, swap_y(): return lax.ppermute(part, AXES, routes(lambda z, y, x, c: (z, 1 - y, x, c)))  32.9 us
    ppermute x20, starting transfers between devices, swap_z(): return lax.ppermute(part, AXES, routes(lambda z, y, x, c: (z ^ k, y, x, c)))  25.8 us
    ppermute x5, waiting for transfers between devices, swap_x(): return lax.ppermute(part, AXES, routes(lambda z, y, x, c: (z, y, 1 - x, c)))  25.4 us
    ppermute x13, starting transfers between devices, swap_y(): return lax.ppermute(part, AXES, routes(lambda z, y, x, c: (z, 1 - y, x, c)))  24.9 us
    ppermute x5, starting transfers between devices, swap_x(): return lax.ppermute(part, AXES, routes(lambda z, y, x, c: (z, y, 1 - x, c)))  7.74 us
    ppermute x13, waiting for transfers between devices, swap_core(): return lax.ppermute(part, AXES, routes(lambda z, y, x, c: (z, y, x, 1 - c)))  5.46 us
  transfers between devices with their start and end apart: 52, of which 29 were waited for; matrix products, arithmetic and copies ran while one was open for 7% of the time, Pallas kernels for 10%

profile of v4, /device:TPU:0, one launch (start us, length us, event | category | flops | bytes accessed | tf_op | source)
XLA Modules:
  0.0 271.7 jit_solution(12563126751897425652)
XLA Ops:
  0.0 1.2 pad_maximum_fusion.6.refs_0_
  1.2 3.1 %collective-permute-start = (bf16[160,1280]{1,0:T(8,128)(2,1)S(1)}, bf16[160,1280]{1,0:T(8,128)(2,1)S(1)}, u32[]{:S(2)}, u32[]{:S(2)}) collective-permute-start(bf16[160,1280]{1,0:T(8,128)(2,1)S(1)} %pad_maximum_fusion.6.refs_0_), channel_id=1, source_target_pairs={{0,8},{1,9},{2,10},{3,11},{4,12},{5,13},{6,14},{7,15},{8,0},{9,1},... | collective-permute-start | bytes 1228808 | tf_op jit(solution)/shard_map/ppermute | solution.py:43
  4.3 2.6 collective-permute-start.1
  6.9 1.5 collective-permute-start.2
  8.4 1.3 fusion.26
  9.8 12.7 %collective-permute-done.refs_1_ = bf16[160,1280]{1,0:T(8,128)(2,1)S(1)} collective-permute-done((bf16[160,1280]{1,0:T(8,128)(2,1)S(1)}, bf16[160,1280]{1,0:T(8,128)(2,1)S(1)}, u32[]{:S(2)}, u32[]{:S(2)}) %collective-permute-start) | collective-permute-done | bytes 409632 | tf_op jit(solution)/shard_map/ppermute | solution.py:43
  22.5 2.5 collective-permute-done.1.refs_2_
  25.5 1.6 collective-permute-start.4
  28.1 2.1 collective-permute-start.8
  31.2 4.7 %collective-permute-done.3.refs_3_ = bf16[160,1280]{1,0:T(8,128)(2,1)} collective-permute-done((bf16[160,1280]{1,0:T(8,128)(2,1)S(1)}, bf16[160,1280]{1,0:T(8,128)(2,1)}, u32[]{:S(2)}, u32[]{:S(2)}) %collective-permute-start.3) | collective-permute-done | bytes 409632 | tf_op jit(solution)/shard_map/ppermute | solution.py:43
  35.9 7.0 %collective-permute-start.5 = (bf16[160,1280]{1,0:T(8,128)(2,1)}, bf16[160,1280]{1,0:T(8,128)(2,1)}, u32[]{:S(2)}, u32[]{:S(2)}) collective-permute-start(bf16[160,1280]{1,0:T(8,128)(2,1)} %collective-permute-done.3.refs_3_), channel_id=1, source_target_pairs={{0,4},{1,5},{2,6},{3,7},{4,0},{5,1},{6,2},{7,3},{8,12},{9,13},{10,... | collective-permute-start | bytes 1228808 | tf_op jit(solution)/shard_map/ppermute | solution.py:39
  43.1 1.2 compare_and_fusion
  44.4 2.5 collective-permute-done.4.refs_5_
  46.9 1.5 collective-permute-start.15
  51.0 4.6 %collective-permute-done.5.refs_6_ = bf16[160,1280]{1,0:T(8,128)(2,1)} collective-permute-done((bf16[160,1280]{1,0:T(8,128)(2,1)}, bf16[160,1280]{1,0:T(8,128)(2,1)}, u32[]{:S(2)}, u32[]{:S(2)}) %collective-permute-start.5) | collective-permute-done | bytes 409632 | tf_op jit(solution)/shard_map/ppermute | solution.py:39
  55.7 7.0 %shard_map.145 = (bf16[128,1280]{1,0:T(8,128)(2,1)}, bf16[128,1280]{1,0:T(8,128)(2,1)}) custom-call(s32[25]{0:T(128)} %stack.110.spots_ref, bf16[256,1280]{1,0:T(8,128)(2,1)} %bitcast.59, f32[256,256]{1,0:T(8,128)} %and_convert_fusion.allowed_ref, bf16[160,1280]{1,0:T(8,128)(2,1)} %copy-done.14, bf16[160,1280]{1,0:T(8,128)(2,1)} %copy-done.11, ...), custom_call_target="tpu_custom_call" | custom-call | tf_op jit(solution)/shard_map/pallas_call | solution.py:147
  62.8 2.4 collective-permute-start.9
  65.2 1.2 pad_maximum_fusion.refs_5_
  66.4 1.6 collective-permute-start.16
  68.1 1.6 collective-permute-start.7
  69.6 8.0 %collective-permute-done.7.right_ref = bf16[128,1280]{1,0:T(8,128)(2,1)S(1)} collective-permute-done((bf16[128,1280]{1,0:T(8,128)(2,1)S(1)}, bf16[128,1280]{1,0:T(8,128)(2,1)S(1)}, u32[]{:S(2)}, u32[]{:S(2)}) %collective-permute-start.7) | collective-permute-done | bytes 327712 | tf_op jit(solution)/shard_map/ppermute | solution.py:35
  78.6 5.8 %collective-permute-done.9 = bf16[160,1280]{1,0:T(8,128)(2,1)S(1)} collective-permute-done((bf16[160,1280]{1,0:T(8,128)(2,1)S(1)}, bf16[160,1280]{1,0:T(8,128)(2,1)S(1)}, u32[]{:S(2)}, u32[]{:S(2)}) %collective-permute-start.9) | collective-permute-done | bytes 409632 | tf_op jit(solution)/shard_map/ppermute | solution.py:43
  84.9 8.7 %collective-permute-done.11.refs_2_ = bf16[128,1280]{1,0:T(8,128)(2,1)S(1)} collective-permute-done((bf16[128,1280]{1,0:T(8,128)(2,1)S(1)}, bf16[128,1280]{1,0:T(8,128)(2,1)S(1)}, u32[]{:S(2)}, u32[]{:S(2)}) %collective-permute-start.11) | collective-permute-done | bytes 327712 | tf_op jit(solution)/shard_map/ppermute | solution.py:43
  94.6 1.5 collective-permute-start.20
  98.0 7.1 %shard_map.147 = (bf16[128,1280]{1,0:T(8,128)(2,1)}, bf16[128,1280]{1,0:T(8,128)(2,1)}, bf16[128,1280]{1,0:T(8,128)(2,1)}, bf16[128,1280]{1,0:T(8,128)(2,1)}) custom-call(s32[25]{0:T(128)} %stack.110.spots_ref, bf16[128,1280]{1,0:T(8,128)(2,1)} %copy-done.2, bf16[128,1280]{1,0:T(8,128)(2,1)} %copy-done.33, bf16[128,1280]{1,0:T(8,128)(2,1)} %copy-done.32, ...), custom_call_target="tpu_custom_call" | custom-call | tf_op jit(solution)/shard_map/pallas_call | solution.py:147
  108.1 6.5 %collective-permute-done.19.refs_2_ = bf16[320,1280]{1,0:T(8,128)(2,1)} collective-permute-done((bf16[320,1280]{1,0:T(8,128)(2,1)S(1)}, bf16[320,1280]{1,0:T(8,128)(2,1)}, u32[]{:S(2)}, u32[]{:S(2)}) %collective-permute-start.19) | collective-permute-done | bytes 819232 | tf_op jit(solution)/shard_map/ppermute | solution.py:43
  115.0 1.2 collective-permute-start.21
  116.4 2.6 collective-permute-start.23
  119.0 1.5 collective-permute-start.24
  120.5 11.2 %collective-permute-done.21 = bf16[128,1280]{1,0:T(8,128)(2,1)S(1)} collective-permute-done((bf16[128,1280]{1,0:T(8,128)(2,1)S(1)}, bf16[128,1280]{1,0:T(8,128)(2,1)S(1)}, u32[]{:S(2)}, u32[]{:S(2)}) %collective-permute-start.21) | collective-permute-done | bytes 327712 | tf_op jit(solution)/shard_map/ppermute | solution.py:43
  131.8 1.6 collective-permute-start.22
  133.4 3.8 %collective-permute-done.22 = bf16[64,1280]{1,0:T(8,128)(2,1)S(1)} collective-permute-done((bf16[64,1280]{1,0:T(8,128)(2,1)S(1)}, bf16[64,1280]{1,0:T(8,128)(2,1)S(1)}, u32[]{:S(2)}, u32[]{:S(2)}) %collective-permute-start.22) | collective-permute-done | bytes 163872 | tf_op jit(solution)/shard_map/ppermute | solution.py:35
  138.1 1.6 collective-permute-start.28
  140.6 4.6 %shard_map.148 = (bf16[64,640]{1,0:T(8,128)(2,1)}, bf16[64,640]{1,0:T(8,128)(2,1)}) custom-call(s32[25]{0:T(128)} %stack.110.spots_ref, bf16[64,1280]{1,0:T(8,128)(2,1)} %fusion.2.blocks_ref, bf16[320,1280]{1,0:T(8,128)(2,1)} %copy-done.10, bf16[320,1280]{1,0:T(8,128)(2,1)} %copy-done.18, bf16[320,1280]{1,0:T(8,128)(2,1)} %collective-permute-done.19.refs_2_, ...), custom_call_target="tpu_custom_call" | custom-call | tf_op jit(solution)/shard_map/pallas_call | solution.py:147
  145.3 1.2 fusion.20
  147.7 1.6 collective-permute-start.26
  149.4 3.0 %collective-permute-done.26 = bf16[64,640]{1,0:T(8,128)(2,1)S(1)} collective-permute-done((bf16[64,640]{1,0:T(8,128)(2,1)S(1)}, bf16[64,640]{1,0:T(8,128)(2,1)S(1)}, u32[]{:S(2)}, u32[]{:S(2)}) %collective-permute-start.26) | collective-permute-done | bytes 81952 | tf_op jit(solution)/shard_map/ppermute | solution.py:35
  152.6 3.7 %collective-permute-done.27.refs_2_ = bf16[320,1280]{1,0:T(8,128)(2,1)S(1)} collective-permute-done((bf16[320,1280]{1,0:T(8,128)(2,1)S(1)}, bf16[320,1280]{1,0:T(8,128)(2,1)S(1)}, u32[]{:S(2)}, u32[]{:S(2)}) %collective-permute-start.27) | collective-permute-done | bytes 819232 | tf_op jit(solution)/shard_map/ppermute | solution.py:43
  156.3 1.5 collective-permute-start.30
  157.9 2.8 %collective-permute-start.32 = (bf16[160,640]{1,0:T(8,128)(2,1)S(1)}, bf16[160,640]{1,0:T(8,128)(2,1)S(1)}, u32[]{:S(2)}, u32[]{:S(2)}) collective-permute-start(bf16[160,640]{1,0:T(8,128)(2,1)S(1)} %get-tuple-element.124), channel_id=1, source_target_pairs={{0,24},{1,25},{2,26},{3,27},{4,28},{5,29},{6,30},{7,31},{8,16},{9,... | collective-permute-start | bytes 614408 | tf_op jit(solution)/shard_map/ppermute | solution.py:43
  160.7 1.6 collective-permute-start.29
  162.3 3.1 %collective-permute-done.29 = bf16[4,1,16,768]{3,2,0,1:T(8,128)(2,1)S(1)} collective-permute-done((bf16[4,1,16,768]{3,2,0,1:T(8,128)(2,1)S(1)}, bf16[4,1,16,768]{3,2,0,1:T(8,128)(2,1)S(1)}, u32[]{:S(2)}, u32[]{:S(2)}) %collective-permute-start.29) | collective-permute-done | bytes 98336 | tf_op jit(solution)/shard_map/ppermute | solution.py:39
  165.4 11.0 %collective-permute-done.31 = bf16[160,640]{1,0:T(8,128)(2,1)S(1)} collective-permute-done((bf16[160,640]{1,0:T(8,128)(2,1)S(1)}, bf16[160,640]{1,0:T(8,128)(2,1)S(1)}, u32[]{:S(2)}, u32[]{:S(2)}) %collective-permute-start.31) | collective-permute-done | bytes 204832 | tf_op jit(solution)/shard_map/ppermute | solution.py:43
  176.4 1.9 collective-permute-start.35
  178.3 2.5 collective-permute-start.33
  180.9 1.8 collective-permute-start.37
  185.9 3.5 %all-to-all-start = ((bf16[4,160,640]{2,1,0:T(8,128)(2,1)}), bf16[4,160,640]{2,1,0:T(8,128)(2,1)S(1)}, u32[]{:S(2)}, u32[]{:S(2)}) async-start(bf16[4,160,640]{2,1,0:T(8,128)(2,1)} %pad_maximum_fusion.2), calls=%async_computation | async-start | bytes 1638400 | tf_op jit(solution)/shard_map/all_to_all | solution.py:92
  189.4 1.2 fusion
  191.3 1.6 collective-permute-start.39
  193.8 6.4 %collective-permute-done.37.refs_3_ = bf16[320,1280]{1,0:T(8,128)(2,1)S(1)} collective-permute-done((bf16[320,1280]{1,0:T(8,128)(2,1)S(1)}, bf16[320,1280]{1,0:T(8,128)(2,1)S(1)}, u32[]{:S(2)}, u32[]{:S(2)}) %collective-permute-start.37) | collective-permute-done | bytes 819232 | tf_op jit(solution)/shard_map/ppermute | solution.py:39
  201.0 6.7 %shard_map.149 = (bf16[96,1280]{1,0:T(8,128)(2,1)}, bf16[96,1280]{1,0:T(8,128)(2,1)}) custom-call(s32[25]{0:T(128)} %stack.110.spots_ref, bf16[192,1280]{1,0:T(8,128)(2,1)} %pad_maximum_fusion.4.rows_ref, f32[192,192]{1,0:T(8,128)} %fusion.4.allowed_ref, bf16[320,1280]{1,0:T(8,128)(2,1)} %copy-done.9, bf16[320,1280]{1,0:T(8,128)(2,1)} %copy-done.17, ...), custom_call_target="tpu_custom_call" | custom-call | tf_op jit(solution)/shard_map/pallas_call | solution.py:147
  208.0 1.2 collective-permute-start.40
  210.1 14.5 %collective-permute-done.40.refs_7_ = bf16[480,640]{1,0:T(8,128)(2,1)S(1)} collective-permute-done((bf16[480,640]{1,0:T(8,128)(2,1)S(1)}, bf16[480,640]{1,0:T(8,128)(2,1)S(1)}, u32[]{:S(2)}, u32[]{:S(2)}) %collective-permute-start.40) | collective-permute-done | bytes 614432 | tf_op jit(solution)/shard_map/ppermute | solution.py:39
  224.7 1.5 collective-permute-start.41
  226.2 5.6 %collective-permute-done.41.right_ref = bf16[96,1280]{1,0:T(8,128)(2,1)S(1)} collective-permute-done((bf16[96,1280]{1,0:T(8,128)(2,1)S(1)}, bf16[96,1280]{1,0:T(8,128)(2,1)S(1)}, u32[]{:S(2)}, u32[]{:S(2)}) %collective-permute-start.41) | collective-permute-done | bytes 245792 | tf_op jit(solution)/shard_map/ppermute | solution.py:35
  232.8 6.1 %collective-permute-done.43.refs_2_ = bf16[96,1280]{1,0:T(8,128)(2,1)S(1)} collective-permute-done((bf16[96,1280]{1,0:T(8,128)(2,1)S(1)}, bf16[96,1280]{1,0:T(8,128)(2,1)S(1)}, u32[]{:S(2)}, u32[]{:S(2)}) %collective-permute-start.43) | collective-permute-done | bytes 245792 | tf_op jit(solution)/shard_map/ppermute | solution.py:43
  239.0 1.5 collective-permute-done.44.refs_3_
  240.5 1.3 collective-permute-done.45.refs_9_
  242.8 7.2 %shard_map.151 = (bf16[96,1280]{1,0:T(8,128)(2,1)}, bf16[96,1280]{1,0:T(8,128)(2,1)}, bf16[96,1280]{1,0:T(8,128)(2,1)}, bf16[96,1280]{1,0:T(8,128)(2,1)}) custom-call(s32[25]{0:T(128)} %stack.110.spots_ref, bf16[96,1280]{1,0:T(8,128)(2,1)} %copy-done.3, bf16[96,1280]{1,0:T(8,128)(2,1)} %copy-done.40, bf16[96,1280]{1,0:T(8,128)(2,1)} %copy-done.39, ...), custom_call_target="tpu_custom_call" | custom-call | tf_op jit(solution)/shard_map/pallas_call | solution.py:147
  250.6 1.2 collective-permute-done.47
  252.9 8.0 %collective-permute-done.48 = bf16[96,1280]{1,0:T(8,128)(2,1)S(1)} collective-permute-done((bf16[96,1280]{1,0:T(8,128)(2,1)S(1)}, bf16[96,1280]{1,0:T(8,128)(2,1)S(1)}, u32[]{:S(2)}, u32[]{:S(2)}) %collective-permute-start.48) | collective-permute-done | bytes 245792 | tf_op jit(solution)/shard_map/ppermute | solution.py:43
  261.9 1.6 collective-permute-start.49
  264.2 5.0 %collective-permute-done.49 = bf16[96,1280]{1,0:T(8,128)(2,1)S(1)} collective-permute-done((bf16[96,1280]{1,0:T(8,128)(2,1)S(1)}, bf16[96,1280]{1,0:T(8,128)(2,1)S(1)}, u32[]{:S(2)}, u32[]{:S(2)}) %collective-permute-start.49) | collective-permute-done | bytes 245792 | tf_op jit(solution)/shard_map/ppermute | solution.py:35
  269.4 1.5 collective-permute-done.50
  (213 shorter events, 29.3 us)
Async XLA Ops:
  0.0 27.1 %copy-start.28 = (bf16[160,1280]{1,0:T(8,128)(2,1)S(1)}, bf16[160,1280]{1,0:T(8,128)(2,1)}, u32[]{:S(2)}) copy-start(bf16[160,1280]{1,0:T(8,128)(2,1)} %param.23) | copy-start | bytes 1228804
  0.0 27.1 %copy-start.27 = (bf16[160,1280]{1,0:T(8,128)(2,1)S(1)}, bf16[160,1280]{1,0:T(8,128)(2,1)}, u32[]{:S(2)}) copy-start(bf16[160,1280]{1,0:T(8,128)(2,1)} %param.24) | copy-start | bytes 1228804
  1.2 21.2 %collective-permute-start = (bf16[160,1280]{1,0:T(8,128)(2,1)S(1)}, bf16[160,1280]{1,0:T(8,128)(2,1)S(1)}, u32[]{:S(2)}, u32[]{:S(2)}) collective-permute-start(bf16[160,1280]{1,0:T(8,128)(2,1)S(1)} %pad_maximum_fusion.6.refs_0_), channel_id=1, source_target_pairs={{0,8},{1,9},{2,10},{3,11},{4,12},{5,13},{6,14},{7,15},{8,0},{9,1},... | collective-permute-start | bytes 1228808 | tf_op jit(solution)/shard_map/ppermute | solution.py:43
  4.3 20.7 %collective-permute-start.1 = (bf16[160,1280]{1,0:T(8,128)(2,1)S(1)}, bf16[160,1280]{1,0:T(8,128)(2,1)S(1)}, u32[]{:S(2)}, u32[]{:S(2)}) collective-permute-start(bf16[160,1280]{1,0:T(8,128)(2,1)S(1)} %pad_maximum_fusion.6.refs_0_), channel_id=1, source_target_pairs={{0,16},{1,17},{2,18},{3,19},{4,20},{5,21},{6,22},{7,23},{8,24},{9,... | collective-permute-start | bytes 1228808 | tf_op jit(solution)/shard_map/ppermute | solution.py:43
  6.9 18.1 %collective-permute-start.2 = (bf16[160,1280]{1,0:T(8,128)(2,1)S(1)}, bf16[160,1280]{1,0:T(8,128)(2,1)S(1)}, u32[]{:S(2)}, u32[]{:S(2)}) collective-permute-start(bf16[160,1280]{1,0:T(8,128)(2,1)S(1)} %pad_maximum_fusion.6.refs_0_), channel_id=1, source_target_pairs={{0,4},{1,5},{2,6},{3,7},{4,0},{5,1},{6,2},{7,3},{8,12},{9,13},{10,... | collective-permute-start | bytes 1228808 | tf_op jit(solution)/shard_map/ppermute | solution.py:39
  25.0 11.0 %collective-permute-start.3 = (bf16[160,1280]{1,0:T(8,128)(2,1)S(1)}, bf16[160,1280]{1,0:T(8,128)(2,1)}, u32[]{:S(2)}, u32[]{:S(2)}) collective-permute-start(bf16[160,1280]{1,0:T(8,128)(2,1)S(1)} %collective-permute-done.1.refs_2_), channel_id=1, source_target_pairs={{0,8},{1,9},{2,10},{3,11},{4,12},{5,13},{6,14},{7,15},{8,0},{9,1},... | collective-permute-start | bytes 1228808 | tf_op jit(solution)/shard_map/ppermute | solution.py:43
  25.5 21.4 %collective-permute-start.4 = (bf16[320,1280]{1,0:T(8,128)(2,1)S(1)}, bf16[320,1280]{1,0:T(8,128)(2,1)}, u32[]{:S(2)}, u32[]{:S(2)}) collective-permute-start(bf16[320,1280]{1,0:T(8,128)(2,1)S(1)} %pad_maximum_fusion.1), channel_id=1, source_target_pairs={{0,4},{1,5},{2,6},{3,7},{4,0},{5,1},{6,2},{7,3},{8,12},{9,13},{10,... | collective-permute-start | bytes 2457608 | tf_op jit(solution)/shard_map/ppermute | solution.py:39
  28.1 34.7 %collective-permute-start.8 = (bf16[160,1280]{1,0:T(8,128)(2,1)}, bf16[160,1280]{1,0:T(8,128)(2,1)S(1)}, u32[]{:S(2)}, u32[]{:S(2)}) collective-permute-start(bf16[160,1280]{1,0:T(8,128)(2,1)} %pad_maximum_fusion.7), channel_id=1, source_target_pairs={{0,24},{1,25},{2,26},{3,27},{4,28},{5,29},{6,30},{7,31},{8,16},{9,... | collective-permute-start | bytes 1228808 | tf_op jit(solution)/shard_map/ppermute | solution.py:43
  30.2 34.9 %collective-permute-start.14 = (bf16[160,1280]{1,0:T(8,128)(2,1)S(1)}, bf16[160,1280]{1,0:T(8,128)(2,1)}, u32[]{:S(2)}, u32[]{:S(2)}) collective-permute-start(bf16[160,1280]{1,0:T(8,128)(2,1)S(1)} %pad_maximum_fusion.8.refs_4_), channel_id=1, source_target_pairs={{0,16},{1,17},{2,18},{3,19},{4,20},{5,21},{6,22},{7,23},{8,24},{9,... | collective-permute-start | bytes 1228808 | tf_op jit(solution)/shard_map/ppermute | solution.py:43
  35.9 19.7 %collective-permute-start.5 = (bf16[160,1280]{1,0:T(8,128)(2,1)}, bf16[160,1280]{1,0:T(8,128)(2,1)}, u32[]{:S(2)}, u32[]{:S(2)}) collective-permute-start(bf16[160,1280]{1,0:T(8,128)(2,1)} %collective-permute-done.3.refs_3_), channel_id=1, source_target_pairs={{0,4},{1,5},{2,6},{3,7},{4,0},{5,1},{6,2},{7,3},{8,12},{9,13},{10,... | collective-permute-start | bytes 1228808 | tf_op jit(solution)/shard_map/ppermute | solution.py:39
  43.0 22.2 %collective-permute-start.13 = (bf16[160,1280]{1,0:T(8,128)(2,1)}, bf16[160,1280]{1,0:T(8,128)(2,1)}, u32[]{:S(2)}, u32[]{:S(2)}) collective-permute-start(bf16[160,1280]{1,0:T(8,128)(2,1)} %pad_maximum_fusion.7), channel_id=1, source_target_pairs={{0,8},{1,9},{2,10},{3,11},{4,12},{5,13},{6,14},{7,15},{8,0},{9,1},... | collective-permute-start | bytes 1228808 | tf_op jit(solution)/shard_map/ppermute | solution.py:43
  46.9 19.5 %collective-permute-start.15 = (bf16[160,1280]{1,0:T(8,128)(2,1)S(1)}, bf16[160,1280]{1,0:T(8,128)(2,1)S(1)}, u32[]{:S(2)}, u32[]{:S(2)}) collective-permute-start(bf16[160,1280]{1,0:T(8,128)(2,1)S(1)} %pad_maximum_fusion.8.refs_4_), channel_id=1, source_target_pairs={{0,4},{1,5},{2,6},{3,7},{4,0},{5,1},{6,2},{7,3},{8,12},{9,13},{10,... | collective-permute-start | bytes 1228808 | tf_op jit(solution)/shard_map/ppermute | solution.py:39
  62.7 5.3 %collective-permute-start.6 = (bf16[128,1280]{1,0:T(8,128)(2,1)}, bf16[128,1280]{1,0:T(8,128)(2,1)S(1)}, u32[]{:S(2)}, u32[]{:S(2)}) collective-permute-start(bf16[128,1280]{1,0:T(8,128)(2,1)} %get-tuple-element.68), channel_id=1, source_target_pairs={{0,1},{1,0},{2,3},{3,2},{4,5},{5,4},{6,7},{7,6},{8,9},{9,8},{10,11... | collective-permute-start | bytes 983048 | tf_op jit(solution)/shard_map/ppermute | solution.py:31
  62.8 21.5 %collective-permute-start.9 = (bf16[160,1280]{1,0:T(8,128)(2,1)S(1)}, bf16[160,1280]{1,0:T(8,128)(2,1)S(1)}, u32[]{:S(2)}, u32[]{:S(2)}) collective-permute-start(bf16[160,1280]{1,0:T(8,128)(2,1)S(1)} %copy-done.29), channel_id=1, source_target_pairs={{0,16},{1,17},{2,18},{3,19},{4,20},{5,21},{6,22},{7,23},{8,24},{9,... | collective-permute-start | bytes 1228808 | tf_op jit(solution)/shard_map/ppermute | solution.py:43
  66.4 27.3 %copy-start.6 = (bf16[480,1280]{1,0:T(8,128)(2,1)}, bf16[480,1280]{1,0:T(8,128)(2,1)S(1)}, u32[]{:S(2)}) copy-start(bf16[480,1280]{1,0:T(8,128)(2,1)S(1)} %pad_maximum_fusion.refs_5_) | copy-start | bytes 3686404
  66.4 27.2 %copy-start.26 = (bf16[160,1280]{1,0:T(8,128)(2,1)}, bf16[160,1280]{1,0:T(8,128)(2,1)S(1)}, u32[]{:S(2)}) copy-start(bf16[160,1280]{1,0:T(8,128)(2,1)S(1)} %collective-permute-done.15.refs_6_) | copy-start | bytes 1228804
  66.4 29.7 %collective-permute-start.16 = (bf16[480,1280]{1,0:T(8,128)(2,1)S(1)}, bf16[480,1280]{1,0:T(8,128)(2,1)S(1)}, u32[]{:S(2)}, u32[]{:S(2)}) collective-permute-start(bf16[480,1280]{1,0:T(8,128)(2,1)S(1)} %pad_maximum_fusion.refs_5_), channel_id=1, source_target_pairs={{0,4},{1,5},{2,6},{3,7},{4,0},{5,1},{6,2},{7,3},{8,12},{9,13},{10,... | collective-permute-start | bytes 3686408 | tf_op jit(solution)/shard_map/ppermute | solution.py:39
  68.1 9.6 %collective-permute-start.7 = (bf16[128,1280]{1,0:T(8,128)(2,1)S(1)}, bf16[128,1280]{1,0:T(8,128)(2,1)S(1)}, u32[]{:S(2)}, u32[]{:S(2)}) collective-permute-start(bf16[128,1280]{1,0:T(8,128)(2,1)S(1)} %add_convert_fusion.2.left_ref), channel_id=1, source_target_pairs={{0,2},{1,3},{2,0},{3,1},{4,6},{5,7},{6,4},{7,5},{8,10},{9,11},{10,... | collective-permute-start | bytes 983048 | tf_op jit(solution)/shard_map/ppermute | solution.py:35
  84.3 9.3 %collective-permute-start.11 = (bf16[128,1280]{1,0:T(8,128)(2,1)S(1)}, bf16[128,1280]{1,0:T(8,128)(2,1)S(1)}, u32[]{:S(2)}, u32[]{:S(2)}) collective-permute-start(bf16[128,1280]{1,0:T(8,128)(2,1)S(1)} %get-tuple-element.72.refs_0_), channel_id=1, source_target_pairs={{0,8},{1,9},{2,10},{3,11},{4,12},{5,13},{6,14},{7,15},{8,0},{9,1},... | collective-permute-start | bytes 983048 | tf_op jit(solution)/shard_map/ppermute | solution.py:43
  84.8 11.3 %collective-permute-start.10 = (bf16[128,1280]{1,0:T(8,128)(2,1)S(1)}, bf16[128,1280]{1,0:T(8,128)(2,1)S(1)}, u32[]{:S(2)}, u32[]{:S(2)}) collective-permute-start(bf16[128,1280]{1,0:T(8,128)(2,1)S(1)} %get-tuple-element.72.refs_0_), channel_id=1, source_target_pairs={{0,1},{1,0},{2,3},{3,2},{4,5},{5,4},{6,7},{7,6},{8,9},{9,8},{10,11... | collective-permute-start | bytes 983048 | tf_op jit(solution)/shard_map/ppermute | solution.py:31
  93.6 2.6 collective-permute-start.12
  93.7 20.8 %collective-permute-start.19 = (bf16[320,1280]{1,0:T(8,128)(2,1)S(1)}, bf16[320,1280]{1,0:T(8,128)(2,1)}, u32[]{:S(2)}, u32[]{:S(2)}) collective-permute-start(bf16[320,1280]{1,0:T(8,128)(2,1)S(1)} %constant_dynamic-update-slice_fusion.refs_0_), channel_id=1, source_target_pairs={{0,8},{1,9},{2,10},{3,11},{4,12},{5,13},{6,14},{7,15},{8,0},{9,1},... | collective-permute-start | bytes 2457608 | tf_op jit(solution)/shard_map/ppermute | solution.py:43
  94.6 20.4 %collective-permute-start.20 = (bf16[320,1280]{1,0:T(8,128)(2,1)S(1)}, bf16[320,1280]{1,0:T(8,128)(2,1)S(1)}, u32[]{:S(2)}, u32[]{:S(2)}) collective-permute-start(bf16[320,1280]{1,0:T(8,128)(2,1)S(1)} %constant_dynamic-update-slice_fusion.refs_0_), channel_id=1, source_target_pairs={{0,4},{1,5},{2,6},{3,7},{4,0},{5,1},{6,2},{7,3},{8,12},{9,13},{10,... | collective-permute-start | bytes 2457608 | tf_op jit(solution)/shard_map/ppermute | solution.py:39
  105.1 26.6 %copy-start.35 = (bf16[128,1280]{1,0:T(8,128)(2,1)S(1)}, bf16[128,1280]{1,0:T(8,128)(2,1)}, u32[]{:S(2)}) copy-start(bf16[128,1280]{1,0:T(8,128)(2,1)} %get-tuple-element.77) | copy-start | bytes 983044
  105.1 1.9 collective-permute-start.18
  105.5 15.0 %collective-permute-start.17 = (bf16[128,1280]{1,0:T(8,128)(2,1)}, bf16[128,1280]{1,0:T(8,128)(2,1)S(1)}, u32[]{:S(2)}, u32[]{:S(2)}) collective-permute-start(bf16[128,1280]{1,0:T(8,128)(2,1)} %get-tuple-element.78), channel_id=1, source_target_pairs={{0,1},{1,0},{2,3},{3,2},{4,5},{5,4},{6,7},{7,6},{8,9},{9,8},{10,11... | collective-permute-start | bytes 983048 | tf_op jit(solution)/shard_map/ppermute | solution.py:31
  115.0 16.7 %collective-permute-start.21 = (bf16[128,1280]{1,0:T(8,128)(2,1)S(1)}, bf16[128,1280]{1,0:T(8,128)(2,1)S(1)}, u32[]{:S(2)}, u32[]{:S(2)}) collective-permute-start(bf16[128,1280]{1,0:T(8,128)(2,1)S(1)} %add_convert_fusion.1), channel_id=1, source_target_pairs={{0,8},{1,9},{2,10},{3,11},{4,12},{5,13},{6,14},{7,15},{8,0},{9,1},... | collective-permute-start | bytes 983048 | tf_op jit(solution)/shard_map/ppermute | solution.py:43
  116.4 21.6 %collective-permute-start.23 = (bf16[160,1280]{1,0:T(8,128)(2,1)S(1)}, bf16[160,1280]{1,0:T(8,128)(2,1)S(1)}, u32[]{:S(2)}, u32[]{:S(2)}) collective-permute-start(bf16[160,1280]{1,0:T(8,128)(2,1)S(1)} %pad_maximum_fusion.9), channel_id=1, source_target_pairs={{0,16},{1,17},{2,18},{3,19},{4,20},{5,21},{6,22},{7,23},{8,24},{9,... | collective-permute-start | bytes 1228808 | tf_op jit(solution)/shard_map/ppermute | solution.py:43
  119.0 20.7 %collective-permute-start.24 = (bf16[320,1280]{1,0:T(8,128)(2,1)}, bf16[320,1280]{1,0:T(8,128)(2,1)S(1)}, u32[]{:S(2)}, u32[]{:S(2)}) collective-permute-start(bf16[320,1280]{1,0:T(8,128)(2,1)} %collective-permute-done.19.refs_2_), channel_id=1, source_target_pairs={{0,4},{1,5},{2,6},{3,7},{4,0},{5,1},{6,2},{7,3},{8,12},{9,13},{10,... | collective-permute-start | bytes 2457608 | tf_op jit(solution)/shard_map/ppermute | solution.py:39
  131.8 5.4 %collective-permute-start.22 = (bf16[64,1280]{1,0:T(8,128)(2,1)S(1)}, bf16[64,1280]{1,0:T(8,128)(2,1)S(1)}, u32[]{:S(2)}, u32[]{:S(2)}) collective-permute-start(bf16[64,1280]{1,0:T(8,128)(2,1)S(1)} %dynamic-slice_bitcast_fusion), channel_id=1, source_target_pairs={{0,2},{1,3},{2,0},{3,1},{4,6},{5,7},{6,4},{7,5},{8,10},{9,11},{10,... | collective-permute-start | bytes 491528 | tf_op jit(solution)/shard_map/ppermute | solution.py:35
  138.0 18.2 %collective-permute-start.27 = (bf16[320,1280]{1,0:T(8,128)(2,1)S(1)}, bf16[320,1280]{1,0:T(8,128)(2,1)S(1)}, u32[]{:S(2)}, u32[]{:S(2)}) collective-permute-start(bf16[320,1280]{1,0:T(8,128)(2,1)S(1)} %constant_dynamic-update-slice_fusion.2.refs_0_), channel_id=1, source_target_pairs={{0,8},{1,9},{2,10},{3,11},{4,12},{5,13},{6,14},{7,15},{8,0},{9,1},... | collective-permute-start | bytes 2457608 | tf_op jit(solution)/shard_map/ppermute | solution.py:43
  138.1 18.2 %collective-permute-start.28 = (bf16[320,1280]{1,0:T(8,128)(2,1)S(1)}, bf16[320,1280]{1,0:T(8,128)(2,1)S(1)}, u32[]{:S(2)}, u32[]{:S(2)}) collective-permute-start(bf16[320,1280]{1,0:T(8,128)(2,1)S(1)} %constant_dynamic-update-slice_fusion.2.refs_0_), channel_id=1, source_target_pairs={{0,4},{1,5},{2,6},{3,7},{4,0},{5,1},{6,2},{7,3},{8,12},{9,13},{10,... | collective-permute-start | bytes 2457608 | tf_op jit(solution)/shard_map/ppermute | solution.py:39
  145.2 1.6 collective-permute-start.25
  147.7 4.7 %collective-permute-start.26 = (bf16[64,640]{1,0:T(8,128)(2,1)S(1)}, bf16[64,640]{1,0:T(8,128)(2,1)S(1)}, u32[]{:S(2)}, u32[]{:S(2)}) collective-permute-start(bf16[64,640]{1,0:T(8,128)(2,1)S(1)} %add_convert_fusion.8), channel_id=1, source_target_pairs={{0,2},{1,3},{2,0},{3,1},{4,6},{5,7},{6,4},{7,5},{8,10},{9,11},{10,... | collective-permute-start | bytes 245768 | tf_op jit(solution)/shard_map/ppermute | solution.py:35
  152.6 32.2 %copy-start.31 = (bf16[160,1280]{1,0:T(8,128)(2,1)S(1)}, bf16[160,1280]{1,0:T(8,128)(2,1)}, u32[]{:S(2)}) copy-start(bf16[160,1280]{1,0:T(8,128)(2,1)} %param.29) | copy-start | bytes 1228804
  156.3 28.2 %copy-start.16 = (bf16[320,1280]{1,0:T(8,128)(2,1)}, bf16[320,1280]{1,0:T(8,128)(2,1)S(1)}, u32[]{:S(2)}) copy-start(bf16[320,1280]{1,0:T(8,128)(2,1)S(1)} %collective-permute-done.27.refs_2_) | copy-start | bytes 2457604
  156.3 28.2 %copy-start.17 = (bf16[320,1280]{1,0:T(8,128)(2,1)}, bf16[320,1280]{1,0:T(8,128)(2,1)S(1)}, u32[]{:S(2)}) copy-start(bf16[320,1280]{1,0:T(8,128)(2,1)S(1)} %collective-permute-done.28.refs_1_) | copy-start | bytes 2457604
  156.3 35.0 %copy-start.22 = (bf16[160,640]{1,0:T(8,128)(2,1)}, bf16[160,640]{1,0:T(8,128)(2,1)S(1)}, u32[]{:S(2)}) copy-start(bf16[160,640]{1,0:T(8,128)(2,1)S(1)} %get-tuple-element.108.refs_4_) | copy-start | bytes 614404
  156.3 9.1 %collective-permute-start.30 = (bf16[160,640]{1,0:T(8,128)(2,1)S(1)}, bf16[160,640]{1,0:T(8,128)(2,1)S(1)}, u32[]{:S(2)}, u32[]{:S(2)}) collective-permute-start(bf16[160,640]{1,0:T(8,128)(2,1)S(1)} %get-tuple-element.124), channel_id=1, source_target_pairs={{0,8},{1,9},{2,10},{3,11},{4,12},{5,13},{6,14},{7,15},{8,0},{9,1},... | collective-permute-start | bytes 614408 | tf_op jit(solution)/shard_map/ppermute | solution.py:43
  157.9 18.5 %collective-permute-start.32 = (bf16[160,640]{1,0:T(8,128)(2,1)S(1)}, bf16[160,640]{1,0:T(8,128)(2,1)S(1)}, u32[]{:S(2)}, u32[]{:S(2)}) collective-permute-start(bf16[160,640]{1,0:T(8,128)(2,1)S(1)} %get-tuple-element.124), channel_id=1, source_target_pairs={{0,24},{1,25},{2,26},{3,27},{4,28},{5,29},{6,30},{7,31},{8,16},{9,... | collective-permute-start | bytes 614408 | tf_op jit(solution)/shard_map/ppermute | solution.py:43
  160.7 4.7 %collective-permute-start.29 = (bf16[4,1,16,768]{3,2,0,1:T(8,128)(2,1)S(1)}, bf16[4,1,16,768]{3,2,0,1:T(8,128)(2,1)S(1)}, u32[]{:S(2)}, u32[]{:S(2)}) collective-permute-start(bf16[4,1,16,768]{3,2,0,1:T(8,128)(2,1)S(1)} %dynamic-slice_bitcast_fusion.1), channel_id=1, source_target_pairs={{0,4},{1,5},{2,6},{3,7},{4,0},{5,1},{6,2},{7,3},{8,12},{9,13},{10,... | collective-permute-start | bytes 294920 | tf_op jit(solution)/shard_map/ppermute | solution.py:39
  162.3 14.1 %collective-permute-start.31 = (bf16[160,640]{1,0:T(8,128)(2,1)S(1)}, bf16[160,640]{1,0:T(8,128)(2,1)S(1)}, u32[]{:S(2)}, u32[]{:S(2)}) collective-permute-start(bf16[160,640]{1,0:T(8,128)(2,1)S(1)} %get-tuple-element.108.refs_4_), channel_id=1, source_target_pairs={{0,16},{1,17},{2,18},{3,19},{4,20},{5,21},{6,22},{7,23},{8,24},{9,... | collective-permute-start | bytes 614408 | tf_op jit(solution)/shard_map/ppermute | solution.py:43
  176.4 6.3 %collective-permute-start.35 = (bf16[2,1,16,768]{3,2,0,1:T(8,128)(2,1)S(1)}, bf16[2,1,16,768]{3,2,0,1:T(8,128)(2,1)S(1)}, u32[]{:S(2)}, u32[]{:S(2)}) collective-permute-start(bf16[2,1,16,768]{3,2,0,1:T(8,128)(2,1)S(1)} %get-tuple-element.130), channel_id=1, source_target_pairs={{0,24},{1,25},{2,26},{3,27},{4,28},{5,29},{6,30},{7,31},{8,16},{9,... | collective-permute-start | bytes 147464 | tf_op jit(solution)/shard_map/ppermute | solution.py:43
  178.3 5.2 %collective-permute-start.34 = (bf16[2,1,16,768]{3,2,0,1:T(8,128)(2,1)S(1)}, bf16[2,1,16,768]{3,2,0,1:T(8,128)(2,1)}, u32[]{:S(2)}, u32[]{:S(2)}) collective-permute-start(bf16[2,1,16,768]{3,2,0,1:T(8,128)(2,1)S(1)} %get-tuple-element.131), channel_id=1, source_target_pairs={{0,16},{1,17},{2,18},{3,19},{4,20},{5,21},{6,22},{7,23},{8,24},{9,... | collective-permute-start | bytes 147464 | tf_op jit(solution)/shard_map/ppermute | solution.py:43
  178.3 5.2 %collective-permute-start.33 = (bf16[2,1,16,768]{3,2,0,1:T(8,128)(2,1)S(1)}, bf16[2,1,16,768]{3,2,0,1:T(8,128)(2,1)}, u32[]{:S(2)}, u32[]{:S(2)}) collective-permute-start(bf16[2,1,16,768]{3,2,0,1:T(8,128)(2,1)S(1)} %get-tuple-element.132), channel_id=1, source_target_pairs={{0,8},{1,9},{2,10},{3,11},{4,12},{5,13},{6,14},{7,15},{8,0},{9,1},... | collective-permute-start | bytes 147464 | tf_op jit(solution)/shard_map/ppermute | solution.py:43
  180.9 19.2 %collective-permute-start.37 = (bf16[320,1280]{1,0:T(8,128)(2,1)S(1)}, bf16[320,1280]{1,0:T(8,128)(2,1)S(1)}, u32[]{:S(2)}, u32[]{:S(2)}) collective-permute-start(bf16[320,1280]{1,0:T(8,128)(2,1)S(1)} %collective-permute-done.27.refs_2_), channel_id=1, source_target_pairs={{0,4},{1,5},{2,6},{3,7},{4,0},{5,1},{6,2},{7,3},{8,12},{9,13},{10,... | collective-permute-start | bytes 2457608 | tf_op jit(solution)/shard_map/ppermute | solution.py:39
  185.9 23.3 %all-to-all-start = ((bf16[4,160,640]{2,1,0:T(8,128)(2,1)}), bf16[4,160,640]{2,1,0:T(8,128)(2,1)S(1)}, u32[]{:S(2)}, u32[]{:S(2)}) async-start(bf16[4,160,640]{2,1,0:T(8,128)(2,1)} %pad_maximum_fusion.2), calls=%async_computation | async-start | bytes 1638400 | tf_op jit(solution)/shard_map/all_to_all | solution.py:92
  190.5 2.3 collective-permute-start.36
  191.3 16.6 %collective-permute-start.39 = (bf16[160,640]{1,0:T(8,128)(2,1)S(1)}, bf16[160,640]{1,0:T(8,128)(2,1)S(1)}, u32[]{:S(2)}, u32[]{:S(2)}) collective-permute-start(bf16[160,640]{1,0:T(8,128)(2,1)S(1)} %get-tuple-element.108.refs_4_), channel_id=1, source_target_pairs={{0,4},{1,5},{2,6},{3,7},{4,0},{5,1},{6,2},{7,3},{8,12},{9,13},{10,... | collective-permute-start | bytes 614408 | tf_op jit(solution)/shard_map/ppermute | solution.py:39
  207.8 2.3 collective-permute-start.38
  207.9 33.9 %copy-start.8 = (bf16[480,640]{1,0:T(8,128)(2,1)}, bf16[480,640]{1,0:T(8,128)(2,1)S(1)}, u32[]{:S(2)}) copy-start(bf16[480,640]{1,0:T(8,128)(2,1)S(1)} %pad_maximum_fusion.3.refs_5_) | copy-start | bytes 1843204
  207.9 33.9 %copy-start.48 = (bf16[160,640]{1,0:T(8,128)(2,1)}, bf16[160,640]{1,0:T(8,128)(2,1)S(1)}, u32[]{:S(2)}) copy-start(bf16[160,640]{1,0:T(8,128)(2,1)S(1)} %collective-permute-done.39.refs_6_) | copy-start | bytes 614404
  208.0 16.7 %collective-permute-start.40 = (bf16[480,640]{1,0:T(8,128)(2,1)S(1)}, bf16[480,640]{1,0:T(8,128)(2,1)S(1)}, u32[]{:S(2)}, u32[]{:S(2)}) collective-permute-start(bf16[480,640]{1,0:T(8,128)(2,1)S(1)} %pad_maximum_fusion.3.refs_5_), channel_id=1, source_target_pairs={{0,4},{1,5},{2,6},{3,7},{4,0},{5,1},{6,2},{7,3},{8,12},{9,13},{10,... | collective-permute-start | bytes 1843208 | tf_op jit(solution)/shard_map/ppermute | solution.py:39
  209.2 32.7 %copy-start.7 = (bf16[4,160,640]{2,1,0:T(8,128)(2,1)}, bf16[4,160,640]{2,1,0:T(8,128)(2,1)S(1)}, u32[]{:S(2)}) copy-start(bf16[4,160,640]{2,1,0:T(8,128)(2,1)S(1)} %all-to-all-done) | copy-start | bytes 2457604
  209.2 32.6 %collective-permute-start.45 = (bf16[640,640]{1,0:T(8,128)(2,1)S(1)}, bf16[640,640]{1,0:T(8,128)(2,1)S(1)}, u32[]{:S(2)}, u32[]{:S(2)}) collective-permute-start(bf16[640,640]{1,0:T(8,128)(2,1)S(1)} %bitcast.62), channel_id=1, source_target_pairs={{0,4},{1,5},{2,6},{3,7},{4,0},{5,1},{6,2},{7,3},{8,12},{9,13},{10,... | collective-permute-start | bytes 2457608 | tf_op jit(solution)/shard_map/ppermute | solution.py:39
  224.7 7.1 %collective-permute-start.41 = (bf16[96,1280]{1,0:T(8,128)(2,1)S(1)}, bf16[96,1280]{1,0:T(8,128)(2,1)S(1)}, u32[]{:S(2)}, u32[]{:S(2)}) collective-permute-start(bf16[96,1280]{1,0:T(8,128)(2,1)S(1)} %add_convert_fusion.6.left_ref), channel_id=1, source_target_pairs={{0,2},{1,3},{2,0},{3,1},{4,6},{5,7},{6,4},{7,5},{8,10},{9,11},{10,... | collective-permute-start | bytes 737288 | tf_op jit(solution)/shard_map/ppermute | solution.py:35
  232.7 6.3 %collective-permute-start.43 = (bf16[96,1280]{1,0:T(8,128)(2,1)S(1)}, bf16[96,1280]{1,0:T(8,128)(2,1)S(1)}, u32[]{:S(2)}, u32[]{:S(2)}) collective-permute-start(bf16[96,1280]{1,0:T(8,128)(2,1)S(1)} %get-tuple-element.107.refs_0_), channel_id=1, source_target_pairs={{0,8},{1,9},{2,10},{3,11},{4,12},{5,13},{6,14},{7,15},{8,0},{9,1},... | collective-permute-start | bytes 737288 | tf_op jit(solution)/shard_map/ppermute | solution.py:43
  232.8 6.2 %collective-permute-start.42 = (bf16[96,1280]{1,0:T(8,128)(2,1)S(1)}, bf16[96,1280]{1,0:T(8,128)(2,1)S(1)}, u32[]{:S(2)}, u32[]{:S(2)}) collective-permute-start(bf16[96,1280]{1,0:T(8,128)(2,1)S(1)} %get-tuple-element.107.refs_0_), channel_id=1, source_target_pairs={{0,1},{1,0},{2,3},{3,2},{4,5},{5,4},{6,7},{7,6},{8,9},{9,8},{10,11... | collective-permute-start | bytes 737288 | tf_op jit(solution)/shard_map/ppermute | solution.py:31
  238.9 1.5 collective-permute-start.44
  250.0 1.8 collective-permute-start.47
  250.1 2.8 %collective-permute-start.46 = (bf16[96,1280]{1,0:T(8,128)(2,1)}, bf16[96,1280]{1,0:T(8,128)(2,1)S(1)}, u32[]{:S(2)}, u32[]{:S(2)}) collective-permute-start(bf16[96,1280]{1,0:T(8,128)(2,1)} %get-tuple-element.114), channel_id=1, source_target_pairs={{0,1},{1,0},{2,3},{3,2},{4,5},{5,4},{6,7},{7,6},{8,9},{9,8},{10,11... | collective-permute-start | bytes 737288 | tf_op jit(solution)/shard_map/ppermute | solution.py:31
  252.8 8.1 %collective-permute-start.48 = (bf16[96,1280]{1,0:T(8,128)(2,1)S(1)}, bf16[96,1280]{1,0:T(8,128)(2,1)S(1)}, u32[]{:S(2)}, u32[]{:S(2)}) collective-permute-start(bf16[96,1280]{1,0:T(8,128)(2,1)S(1)} %add_convert_fusion.5), channel_id=1, source_target_pairs={{0,8},{1,9},{2,10},{3,11},{4,12},{5,13},{6,14},{7,15},{8,0},{9,1},... | collective-permute-start | bytes 737288 | tf_op jit(solution)/shard_map/ppermute | solution.py:43
  261.9 7.2 %collective-permute-start.49 = (bf16[96,1280]{1,0:T(8,128)(2,1)S(1)}, bf16[96,1280]{1,0:T(8,128)(2,1)S(1)}, u32[]{:S(2)}, u32[]{:S(2)}) collective-permute-start(bf16[96,1280]{1,0:T(8,128)(2,1)S(1)} %add_convert_fusion.4), channel_id=1, source_target_pairs={{0,2},{1,3},{2,0},{3,1},{4,6},{5,7},{6,4},{7,5},{8,10},{9,11},{10,... | collective-permute-start | bytes 737288 | tf_op jit(solution)/shard_map/ppermute | solution.py:35
  269.3 1.6 collective-permute-start.50
  (40 other events, 403.0 us)

commit v5 on v4

--- a/solution.py
+++ b/solution.py
@@ -437,9 +437,10 @@
         both, dec_up.first, dec_up.second, dec_up.third
     )
     dec_up = dec_up.pieces()
-    dec_attn = [attn_two, attn_two_y, attn_pair, swap_y(attn_pair)]
+    attn_pair_y = swap_y(attn_pair)
     incoming = exchange_z(both)
-    incoming, dec_down_t = together(incoming, dec_down_t)
+    incoming, attn_pair_y, dec_down_t = together(incoming, attn_pair_y, dec_down_t)
+    dec_attn = [attn_two, attn_two_y, attn_pair, attn_pair_y]
     dec_down = halved_column(dec_down_t)
     incoming = incoming.reshape(senders * padded, -1)
 
@@ -454,11 +455,11 @@
     ).astype(jnp.bfloat16)
     text_half = lax.dynamic_slice_in_dim(text_embed, c * half_width, half_width, 1)
     dec_half = jnp.where(jnp.any(hits, axis=1)[:, None], placed, text_half)
+    dec_half, *dec_up = together(dec_half, *dec_up)
     rows = join_core(dec_half, 1)
     causal = (positions[:, None] >= positions[None, :]).astype(jnp.float32)
     keep, send = attention(spots, WHOLE, rows, causal, dec_attn, qkv_width)
     mine = add_short(keep, swap_core(send)).astype(jnp.bfloat16)
-    mine, *dec_up = together(mine, *dec_up)
     mid, normed = middle(spots, rows, mine, swap_x(mine))
     normed_pair = swap_z(normed, 1)
     sources = [normed, swap_core(normed), normed_pair, swap_core(normed_pair)]

time: 272 us -> 260 us (0.956)
  waiting for transfers between devices: 145 us -> 132 us
    ppermute x13, waiting for transfers between devices: 32.9 us -> 14.3 us  [swap_y(): return lax.ppermute(part, AXES, routes(lambda z, y, x, c: (z, 1 - y, x, c)))]
    all_to_all x1, waiting for transfers between devices: 0.01 us -> 4.78 us  [halved_column(): lax.all_to_all(jnp.stack([weight[:, :half], weight[:, half:]] * 2), 'req'...]
  transfers between devices with their start and end apart: 52 -> 52, of which waited for: 29 -> 34; matrix products, arithmetic and copies ran while one was open for 7% -> 8% of each run, Pallas kernels for 10% -> 10%
where the time goes in v5:
time: 260 us; the launch traced here: 259 us
  waiting for transfers between devices  132 us (51%)
  starting transfers between devices  62.6 us (24%)
  Pallas kernels  34.4 us (13%)
  other arithmetic  17.3 us (7%)
  local copies, waits for them, and re-layouts  9.56 us (4%)
    ppermute x20, waiting for transfers between devices, swap_z(): return lax.ppermute(part, AXES, routes(lambda z, y, x, c: (z ^ k, y, x, c)))  82.6 us
    pallas_call x7, Pallas kernels, local_call(): pl.pallas_call(kernel, in_specs=in_specs, out_specs=[VMEM] * len(outs), o...  34.4 us
    ppermute x20, starting transfers between devices, swap_z(): return lax.ppermute(part, AXES, routes(lambda z, y, x, c: (z ^ k, y, x, c)))  26.5 us
    ppermute x5, waiting for transfers between devices, swap_x(): return lax.ppermute(part, AXES, routes(lambda z, y, x, c: (z, y, 1 - x, c)))  24.6 us
    ppermute x13, starting transfers between devices, swap_y(): return lax.ppermute(part, AXES, routes(lambda z, y, x, c: (z, 1 - y, x, c)))  22.6 us
    ppermute x13, waiting for transfers between devices, swap_y(): return lax.ppermute(part, AXES, routes(lambda z, y, x, c: (z, 1 - y, x, c)))  14.3 us
    ppermute x5, starting transfers between devices, swap_x(): return lax.ppermute(part, AXES, routes(lambda z, y, x, c: (z, y, 1 - x, c)))  7.81 us
    ppermute x13, waiting for transfers between devices, swap_core(): return lax.ppermute(part, AXES, routes(lambda z, y, x, c: (z, y, x, 1 - c)))  6.1 us
  transfers between devices with their start and end apart: 52, of which 34 were waited for; matrix products, arithmetic and copies ran while one was open for 8% of the time, Pallas kernels for 10%

profile of v5, /device:TPU:0, one launch (start us, length us, event | category | flops | bytes accessed | tf_op | source)
XLA Modules:
  0.0 259.0 jit_solution(11925831367054180317)
XLA Ops:
  0.0 1.2 pad_maximum_fusion.6.refs_0_
  1.2 3.1 %collective-permute-start = (bf16[160,1280]{1,0:T(8,128)(2,1)S(1)}, bf16[160,1280]{1,0:T(8,128)(2,1)S(1)}, u32[]{:S(2)}, u32[]{:S(2)}) collective-permute-start(bf16[160,1280]{1,0:T(8,128)(2,1)S(1)} %pad_maximum_fusion.6.refs_0_), channel_id=1, source_target_pairs={{0,8},{1,9},{2,10},{3,11},{4,12},{5,13},{6,14},{7,15},{8,0},{9,1},... | collective-permute-start | bytes 1228808 | tf_op jit(solution)/shard_map/ppermute | solution.py:43
  4.3 2.6 collective-permute-start.1
  6.9 1.5 collective-permute-start.2
  8.4 1.4 fusion.26
  9.8 12.6 %collective-permute-done.refs_1_ = bf16[160,1280]{1,0:T(8,128)(2,1)S(1)} collective-permute-done((bf16[160,1280]{1,0:T(8,128)(2,1)S(1)}, bf16[160,1280]{1,0:T(8,128)(2,1)S(1)}, u32[]{:S(2)}, u32[]{:S(2)}) %collective-permute-start) | collective-permute-done | bytes 409632 | tf_op jit(solution)/shard_map/ppermute | solution.py:43
  22.5 2.5 collective-permute-done.1.refs_2_
  25.5 1.6 collective-permute-start.4
  28.1 2.1 collective-permute-start.8
  31.2 4.7 %collective-permute-done.3.refs_3_ = bf16[160,1280]{1,0:T(8,128)(2,1)} collective-permute-done((bf16[160,1280]{1,0:T(8,128)(2,1)S(1)}, bf16[160,1280]{1,0:T(8,128)(2,1)}, u32[]{:S(2)}, u32[]{:S(2)}) %collective-permute-start.3) | collective-permute-done | bytes 409632 | tf_op jit(solution)/shard_map/ppermute | solution.py:43
  35.9 7.0 %collective-permute-start.5 = (bf16[160,1280]{1,0:T(8,128)(2,1)}, bf16[160,1280]{1,0:T(8,128)(2,1)}, u32[]{:S(2)}, u32[]{:S(2)}) collective-permute-start(bf16[160,1280]{1,0:T(8,128)(2,1)} %collective-permute-done.3.refs_3_), channel_id=1, source_target_pairs={{0,4},{1,5},{2,6},{3,7},{4,0},{5,1},{6,2},{7,3},{8,12},{9,13},{10,... | collective-permute-start | bytes 1228808 | tf_op jit(solution)/shard_map/ppermute | solution.py:39
  43.1 1.3 compare_and_fusion
  44.5 2.4 collective-permute-done.4.refs_5_
  46.9 1.5 collective-permute-start.15
  51.0 4.7 %collective-permute-done.5.refs_6_ = bf16[160,1280]{1,0:T(8,128)(2,1)} collective-permute-done((bf16[160,1280]{1,0:T(8,128)(2,1)}, bf16[160,1280]{1,0:T(8,128)(2,1)}, u32[]{:S(2)}, u32[]{:S(2)}) %collective-permute-start.5) | collective-permute-done | bytes 409632 | tf_op jit(solution)/shard_map/ppermute | solution.py:39
  55.7 7.0 %shard_map.145 = (bf16[128,1280]{1,0:T(8,128)(2,1)}, bf16[128,1280]{1,0:T(8,128)(2,1)}) custom-call(s32[25]{0:T(128)} %stack.110.spots_ref, bf16[256,1280]{1,0:T(8,128)(2,1)} %bitcast.59, f32[256,256]{1,0:T(8,128)} %and_convert_fusion.allowed_ref, bf16[160,1280]{1,0:T(8,128)(2,1)} %copy-done.14, bf16[160,1280]{1,0:T(8,128)(2,1)} %copy-done.11, ...), custom_call_target="tpu_custom_call" | custom-call | tf_op jit(solution)/shard_map/pallas_call | solution.py:147
  62.8 2.4 collective-permute-start.9
  65.2 1.2 pad_maximum_fusion.refs_5_
  66.4 1.6 collective-permute-start.16
  68.1 1.6 collective-permute-start.7
  69.6 8.0 %collective-permute-done.7.right_ref = bf16[128,1280]{1,0:T(8,128)(2,1)S(1)} collective-permute-done((bf16[128,1280]{1,0:T(8,128)(2,1)S(1)}, bf16[128,1280]{1,0:T(8,128)(2,1)S(1)}, u32[]{:S(2)}, u32[]{:S(2)}) %collective-permute-start.7) | collective-permute-done | bytes 327712 | tf_op jit(solution)/shard_map/ppermute | solution.py:35
  78.6 5.8 %collective-permute-done.9 = bf16[160,1280]{1,0:T(8,128)(2,1)S(1)} collective-permute-done((bf16[160,1280]{1,0:T(8,128)(2,1)S(1)}, bf16[160,1280]{1,0:T(8,128)(2,1)S(1)}, u32[]{:S(2)}, u32[]{:S(2)}) %collective-permute-start.9) | collective-permute-done | bytes 409632 | tf_op jit(solution)/shard_map/ppermute | solution.py:43
  84.9 8.7 %collective-permute-done.11.refs_2_ = bf16[128,1280]{1,0:T(8,128)(2,1)S(1)} collective-permute-done((bf16[128,1280]{1,0:T(8,128)(2,1)S(1)}, bf16[128,1280]{1,0:T(8,128)(2,1)S(1)}, u32[]{:S(2)}, u32[]{:S(2)}) %collective-permute-start.11) | collective-permute-done | bytes 327712 | tf_op jit(solution)/shard_map/ppermute | solution.py:43
  94.6 1.5 collective-permute-start.20
  98.0 7.1 %shard_map.147 = (bf16[128,1280]{1,0:T(8,128)(2,1)}, bf16[128,1280]{1,0:T(8,128)(2,1)}, bf16[128,1280]{1,0:T(8,128)(2,1)}, bf16[128,1280]{1,0:T(8,128)(2,1)}) custom-call(s32[25]{0:T(128)} %stack.110.spots_ref, bf16[128,1280]{1,0:T(8,128)(2,1)} %copy-done.2, bf16[128,1280]{1,0:T(8,128)(2,1)} %copy-done.32, bf16[128,1280]{1,0:T(8,128)(2,1)} %copy-done.31, ...), custom_call_target="tpu_custom_call" | custom-call | tf_op jit(solution)/shard_map/pallas_call | solution.py:147
  108.1 6.5 %collective-permute-done.19.refs_2_ = bf16[320,1280]{1,0:T(8,128)(2,1)} collective-permute-done((bf16[320,1280]{1,0:T(8,128)(2,1)S(1)}, bf16[320,1280]{1,0:T(8,128)(2,1)}, u32[]{:S(2)}, u32[]{:S(2)}) %collective-permute-start.19) | collective-permute-done | bytes 819232 | tf_op jit(solution)/shard_map/ppermute | solution.py:43
  115.0 1.2 collective-permute-start.21
  116.4 2.6 %collective-permute-start.23 = (bf16[160,1280]{1,0:T(8,128)(2,1)S(1)}, bf16[160,1280]{1,0:T(8,128)(2,1)S(1)}, u32[]{:S(2)}, u32[]{:S(2)}) collective-permute-start(bf16[160,1280]{1,0:T(8,128)(2,1)S(1)} %pad_maximum_fusion.9), channel_id=1, source_target_pairs={{0,16},{1,17},{2,18},{3,19},{4,20},{5,21},{6,22},{7,23},{8,24},{9,... | collective-permute-start | bytes 1228808 | tf_op jit(solution)/shard_map/ppermute | solution.py:43
  119.0 1.5 collective-permute-start.24
  120.5 11.2 %collective-permute-done.21 = bf16[128,1280]{1,0:T(8,128)(2,1)S(1)} collective-permute-done((bf16[128,1280]{1,0:T(8,128)(2,1)S(1)}, bf16[128,1280]{1,0:T(8,128)(2,1)S(1)}, u32[]{:S(2)}, u32[]{:S(2)}) %collective-permute-start.21) | collective-permute-done | bytes 327712 | tf_op jit(solution)/shard_map/ppermute | solution.py:43
  131.8 1.6 collective-permute-start.22
  133.4 3.8 %collective-permute-done.22 = bf16[64,1280]{1,0:T(8,128)(2,1)S(1)} collective-permute-done((bf16[64,1280]{1,0:T(8,128)(2,1)S(1)}, bf16[64,1280]{1,0:T(8,128)(2,1)S(1)}, u32[]{:S(2)}, u32[]{:S(2)}) %collective-permute-start.22) | collective-permute-done | bytes 163872 | tf_op jit(solution)/shard_map/ppermute | solution.py:35
  138.1 1.6 collective-permute-start.28
  140.6 4.6 %shard_map.148 = (bf16[64,640]{1,0:T(8,128)(2,1)}, bf16[64,640]{1,0:T(8,128)(2,1)}) custom-call(s32[25]{0:T(128)} %stack.110.spots_ref, bf16[64,1280]{1,0:T(8,128)(2,1)} %fusion.2.blocks_ref, bf16[320,1280]{1,0:T(8,128)(2,1)} %copy-done.10, bf16[320,1280]{1,0:T(8,128)(2,1)} %copy-done.19, bf16[320,1280]{1,0:T(8,128)(2,1)} %collective-permute-done.19.refs_2_, ...), custom_call_target="tpu_custom_call" | custom-call | tf_op jit(solution)/shard_map/pallas_call | solution.py:147
  145.3 1.4 fusion.20
  147.7 1.6 collective-permute-start.26
  149.4 3.1 %collective-permute-done.26 = bf16[64,640]{1,0:T(8,128)(2,1)S(1)} collective-permute-done((bf16[64,640]{1,0:T(8,128)(2,1)S(1)}, bf16[64,640]{1,0:T(8,128)(2,1)S(1)}, u32[]{:S(2)}, u32[]{:S(2)}) %collective-permute-start.26) | collective-permute-done | bytes 81952 | tf_op jit(solution)/shard_map/ppermute | solution.py:35
  152.7 3.3 %collective-permute-done.27.refs_2_ = bf16[320,1280]{1,0:T(8,128)(2,1)S(1)} collective-permute-done((bf16[320,1280]{1,0:T(8,128)(2,1)S(1)}, bf16[320,1280]{1,0:T(8,128)(2,1)S(1)}, u32[]{:S(2)}, u32[]{:S(2)}) %collective-permute-start.27) | collective-permute-done | bytes 819232 | tf_op jit(solution)/shard_map/ppermute | solution.py:43
  156.5 1.6 collective-permute-start.29
  158.1 4.1 %collective-permute-done.29 = bf16[4,1,16,768]{3,2,0,1:T(8,128)(2,1)S(1)} collective-permute-done((bf16[4,1,16,768]{3,2,0,1:T(8,128)(2,1)S(1)}, bf16[4,1,16,768]{3,2,0,1:T(8,128)(2,1)S(1)}, u32[]{:S(2)}, u32[]{:S(2)}) %collective-permute-start.29) | collective-permute-done | bytes 98336 | tf_op jit(solution)/shard_map/ppermute | solution.py:39
  162.2 1.6 collective-permute-start.36
  164.5 2.0 collective-permute-start.30
  167.5 1.3 collective-permute-start.32
  169.4 4.3 %collective-permute-done.30 = bf16[160,640]{1,0:T(8,128)(2,1)S(1)} collective-permute-done((bf16[160,640]{1,0:T(8,128)(2,1)}, bf16[160,640]{1,0:T(8,128)(2,1)S(1)}, u32[]{:S(2)}, u32[]{:S(2)}) %collective-permute-start.30) | collective-permute-done | bytes 204832 | tf_op jit(solution)/shard_map/ppermute | solution.py:43
  173.7 6.1 %collective-permute-done.31 = bf16[160,640]{1,0:T(8,128)(2,1)S(1)} collective-permute-done((bf16[160,640]{1,0:T(8,128)(2,1)S(1)}, bf16[160,640]{1,0:T(8,128)(2,1)S(1)}, u32[]{:S(2)}, u32[]{:S(2)}) %collective-permute-start.31) | collective-permute-done | bytes 204832 | tf_op jit(solution)/shard_map/ppermute | solution.py:43
  179.8 2.9 %collective-permute-start.35 = (bf16[2,1,16,768]{3,2,0,1:T(8,128)(2,1)S(1)}, bf16[2,1,16,768]{3,2,0,1:T(8,128)(2,1)S(1)}, u32[]{:S(2)}, u32[]{:S(2)}) collective-permute-start(bf16[2,1,16,768]{3,2,0,1:T(8,128)(2,1)S(1)} %get-tuple-element.132), channel_id=1, source_target_pairs={{0,24},{1,25},{2,26},{3,27},{4,28},{5,29},{6,30},{7,31},{8,16},{9,... | collective-permute-start | bytes 147464 | tf_op jit(solution)/shard_map/ppermute | solution.py:43
  182.7 1.6 collective-permute-start.34
  186.3 1.4 collective-permute-done.34
  188.4 1.4 slice_bitcast_fusion.1
  190.8 3.9 %all-to-all-start = ((bf16[4,160,640]{2,1,0:T(8,128)(2,1)}), bf16[4,160,640]{2,1,0:T(8,128)(2,1)S(1)}, u32[]{:S(2)}, u32[]{:S(2)}) async-start(bf16[4,160,640]{2,1,0:T(8,128)(2,1)} %pad_maximum_fusion.2), calls=%async_computation | async-start | bytes 1638400 | tf_op jit(solution)/shard_map/all_to_all | solution.py:92
  195.1 1.2 fusion
  196.2 1.6 collective-permute-done.38.refs_7_
  200.2 6.8 %shard_map.149 = (bf16[96,1280]{1,0:T(8,128)(2,1)}, bf16[96,1280]{1,0:T(8,128)(2,1)}) custom-call(s32[25]{0:T(128)} %stack.110.spots_ref, bf16[192,1280]{1,0:T(8,128)(2,1)} %pad_maximum_fusion.4.rows_ref, f32[192,192]{1,0:T(8,128)} %fusion.4.allowed_ref, bf16[320,1280]{1,0:T(8,128)(2,1)} %copy-done.9, bf16[320,1280]{1,0:T(8,128)(2,1)} %copy-done.17, ...), custom_call_target="tpu_custom_call" | custom-call | tf_op jit(solution)/shard_map/pallas_call | solution.py:147
  207.2 4.8 %all-to-all-done = bf16[4,160,640]{2,1,0:T(8,128)(2,1)S(1)} async-done(((bf16[4,160,640]{2,1,0:T(8,128)(2,1)}), bf16[4,160,640]{2,1,0:T(8,128)(2,1)S(1)}, u32[]{:S(2)}, u32[]{:S(2)}) %all-to-all-start) | async-done | bytes 819232 | tf_op jit(solution)/shard_map/all_to_all | solution.py:92
  213.5 1.6 collective-permute-start.41
  215.0 4.7 %collective-permute-done.41.right_ref = bf16[96,1280]{1,0:T(8,128)(2,1)S(1)} collective-permute-done((bf16[96,1280]{1,0:T(8,128)(2,1)S(1)}, bf16[96,1280]{1,0:T(8,128)(2,1)S(1)}, u32[]{:S(2)}, u32[]{:S(2)}) %collective-permute-start.41) | collective-permute-done | bytes 245792 | tf_op jit(solution)/shard_map/ppermute | solution.py:35
  220.8 6.1 %collective-permute-done.43.refs_2_ = bf16[96,1280]{1,0:T(8,128)(2,1)S(1)} collective-permute-done((bf16[96,1280]{1,0:T(8,128)(2,1)S(1)}, bf16[96,1280]{1,0:T(8,128)(2,1)S(1)}, u32[]{:S(2)}, u32[]{:S(2)}) %collective-permute-start.43) | collective-permute-done | bytes 245792 | tf_op jit(solution)/shard_map/ppermute | solution.py:43
  226.9 1.5 collective-permute-done.44.refs_3_
  230.0 7.2 %shard_map.151 = (bf16[96,1280]{1,0:T(8,128)(2,1)}, bf16[96,1280]{1,0:T(8,128)(2,1)}, bf16[96,1280]{1,0:T(8,128)(2,1)}, bf16[96,1280]{1,0:T(8,128)(2,1)}) custom-call(s32[25]{0:T(128)} %stack.110.spots_ref, bf16[96,1280]{1,0:T(8,128)(2,1)} %copy-done.3, bf16[96,1280]{1,0:T(8,128)(2,1)} %copy-done.38, bf16[96,1280]{1,0:T(8,128)(2,1)} %copy-done.37, ...), custom_call_target="tpu_custom_call" | custom-call | tf_op jit(solution)/shard_map/pallas_call | solution.py:147
  237.8 1.2 collective-permute-done.47
  240.5 7.6 %collective-permute-done.48 = bf16[96,1280]{1,0:T(8,128)(2,1)S(1)} collective-permute-done((bf16[96,1280]{1,0:T(8,128)(2,1)S(1)}, bf16[96,1280]{1,0:T(8,128)(2,1)S(1)}, u32[]{:S(2)}, u32[]{:S(2)}) %collective-permute-start.48) | collective-permute-done | bytes 245792 | tf_op jit(solution)/shard_map/ppermute | solution.py:43
  249.2 1.6 collective-permute-start.49
  251.4 5.0 %collective-permute-done.49 = bf16[96,1280]{1,0:T(8,128)(2,1)S(1)} collective-permute-done((bf16[96,1280]{1,0:T(8,128)(2,1)S(1)}, bf16[96,1280]{1,0:T(8,128)(2,1)S(1)}, u32[]{:S(2)}, u32[]{:S(2)}) %collective-permute-start.49) | collective-permute-done | bytes 245792 | tf_op jit(solution)/shard_map/ppermute | solution.py:35
  256.6 1.5 collective-permute-done.50
  (197 shorter events, 34.2 us)
Async XLA Ops:
  0.0 27.1 %copy-start.28 = (bf16[160,1280]{1,0:T(8,128)(2,1)S(1)}, bf16[160,1280]{1,0:T(8,128)(2,1)}, u32[]{:S(2)}) copy-start(bf16[160,1280]{1,0:T(8,128)(2,1)} %param.23) | copy-start | bytes 1228804
  0.0 27.1 %copy-start.27 = (bf16[160,1280]{1,0:T(8,128)(2,1)S(1)}, bf16[160,1280]{1,0:T(8,128)(2,1)}, u32[]{:S(2)}) copy-start(bf16[160,1280]{1,0:T(8,128)(2,1)} %param.24) | copy-start | bytes 1228804
  1.2 26.0 %copy-start.14 = (bf16[160,1280]{1,0:T(8,128)(2,1)}, bf16[160,1280]{1,0:T(8,128)(2,1)S(1)}, u32[]{:S(2)}) copy-start(bf16[160,1280]{1,0:T(8,128)(2,1)S(1)} %pad_maximum_fusion.6.refs_0_) | copy-start | bytes 1228804
  1.2 21.2 %collective-permute-start = (bf16[160,1280]{1,0:T(8,128)(2,1)S(1)}, bf16[160,1280]{1,0:T(8,128)(2,1)S(1)}, u32[]{:S(2)}, u32[]{:S(2)}) collective-permute-start(bf16[160,1280]{1,0:T(8,128)(2,1)S(1)} %pad_maximum_fusion.6.refs_0_), channel_id=1, source_target_pairs={{0,8},{1,9},{2,10},{3,11},{4,12},{5,13},{6,14},{7,15},{8,0},{9,1},... | collective-permute-start | bytes 1228808 | tf_op jit(solution)/shard_map/ppermute | solution.py:43
  4.3 20.7 %collective-permute-start.1 = (bf16[160,1280]{1,0:T(8,128)(2,1)S(1)}, bf16[160,1280]{1,0:T(8,128)(2,1)S(1)}, u32[]{:S(2)}, u32[]{:S(2)}) collective-permute-start(bf16[160,1280]{1,0:T(8,128)(2,1)S(1)} %pad_maximum_fusion.6.refs_0_), channel_id=1, source_target_pairs={{0,16},{1,17},{2,18},{3,19},{4,20},{5,21},{6,22},{7,23},{8,24},{9,... | collective-permute-start | bytes 1228808 | tf_op jit(solution)/shard_map/ppermute | solution.py:43
  6.9 18.1 %collective-permute-start.2 = (bf16[160,1280]{1,0:T(8,128)(2,1)S(1)}, bf16[160,1280]{1,0:T(8,128)(2,1)S(1)}, u32[]{:S(2)}, u32[]{:S(2)}) collective-permute-start(bf16[160,1280]{1,0:T(8,128)(2,1)S(1)} %pad_maximum_fusion.6.refs_0_), channel_id=1, source_target_pairs={{0,4},{1,5},{2,6},{3,7},{4,0},{5,1},{6,2},{7,3},{8,12},{9,13},{10,... | collective-permute-start | bytes 1228808 | tf_op jit(solution)/shard_map/ppermute | solution.py:39
  25.0 11.0 %collective-permute-start.3 = (bf16[160,1280]{1,0:T(8,128)(2,1)S(1)}, bf16[160,1280]{1,0:T(8,128)(2,1)}, u32[]{:S(2)}, u32[]{:S(2)}) collective-permute-start(bf16[160,1280]{1,0:T(8,128)(2,1)S(1)} %collective-permute-done.1.refs_2_), channel_id=1, source_target_pairs={{0,8},{1,9},{2,10},{3,11},{4,12},{5,13},{6,14},{7,15},{8,0},{9,1},... | collective-permute-start | bytes 1228808 | tf_op jit(solution)/shard_map/ppermute | solution.py:43
  25.5 21.4 %collective-permute-start.4 = (bf16[320,1280]{1,0:T(8,128)(2,1)S(1)}, bf16[320,1280]{1,0:T(8,128)(2,1)}, u32[]{:S(2)}, u32[]{:S(2)}) collective-permute-start(bf16[320,1280]{1,0:T(8,128)(2,1)S(1)} %pad_maximum_fusion.1), channel_id=1, source_target_pairs={{0,4},{1,5},{2,6},{3,7},{4,0},{5,1},{6,2},{7,3},{8,12},{9,13},{10,... | collective-permute-start | bytes 2457608 | tf_op jit(solution)/shard_map/ppermute | solution.py:39
  27.3 22.0 %copy-start.23 = (bf16[256,1280]{1,0:T(8,128)(2,1)S(1)}, bf16[256,1280]{1,0:T(8,128)(2,1)}, u32[]{:S(2)}) copy-start(bf16[256,1280]{1,0:T(8,128)(2,1)} %param.15) | copy-start | bytes 1966084
  28.1 34.7 %collective-permute-start.8 = (bf16[160,1280]{1,0:T(8,128)(2,1)}, bf16[160,1280]{1,0:T(8,128)(2,1)S(1)}, u32[]{:S(2)}, u32[]{:S(2)}) collective-permute-start(bf16[160,1280]{1,0:T(8,128)(2,1)} %pad_maximum_fusion.7), channel_id=1, source_target_pairs={{0,24},{1,25},{2,26},{3,27},{4,28},{5,29},{6,30},{7,31},{8,16},{9,... | collective-permute-start | bytes 1228808 | tf_op jit(solution)/shard_map/ppermute | solution.py:43
  30.2 20.2 %copy-start.13 = (bf16[160,1280]{1,0:T(8,128)(2,1)}, bf16[160,1280]{1,0:T(8,128)(2,1)S(1)}, u32[]{:S(2)}) copy-start(bf16[160,1280]{1,0:T(8,128)(2,1)S(1)} %pad_maximum_fusion.8.refs_4_) | copy-start | bytes 1228804
  30.2 34.9 %collective-permute-start.14 = (bf16[160,1280]{1,0:T(8,128)(2,1)S(1)}, bf16[160,1280]{1,0:T(8,128)(2,1)}, u32[]{:S(2)}, u32[]{:S(2)}) collective-permute-start(bf16[160,1280]{1,0:T(8,128)(2,1)S(1)} %pad_maximum_fusion.8.refs_4_), channel_id=1, source_target_pairs={{0,16},{1,17},{2,18},{3,19},{4,20},{5,21},{6,22},{7,23},{8,24},{9,... | collective-permute-start | bytes 1228808 | tf_op jit(solution)/shard_map/ppermute | solution.py:43
  35.9 19.7 %collective-permute-start.5 = (bf16[160,1280]{1,0:T(8,128)(2,1)}, bf16[160,1280]{1,0:T(8,128)(2,1)}, u32[]{:S(2)}, u32[]{:S(2)}) collective-permute-start(bf16[160,1280]{1,0:T(8,128)(2,1)} %collective-permute-done.3.refs_3_), channel_id=1, source_target_pairs={{0,4},{1,5},{2,6},{3,7},{4,0},{5,1},{6,2},{7,3},{8,12},{9,13},{10,... | collective-permute-start | bytes 1228808 | tf_op jit(solution)/shard_map/ppermute | solution.py:39
  43.0 22.2 %collective-permute-start.13 = (bf16[160,1280]{1,0:T(8,128)(2,1)}, bf16[160,1280]{1,0:T(8,128)(2,1)}, u32[]{:S(2)}, u32[]{:S(2)}) collective-permute-start(bf16[160,1280]{1,0:T(8,128)(2,1)} %pad_maximum_fusion.7), channel_id=1, source_target_pairs={{0,8},{1,9},{2,10},{3,11},{4,12},{5,13},{6,14},{7,15},{8,0},{9,1},... | collective-permute-start | bytes 1228808 | tf_op jit(solution)/shard_map/ppermute | solution.py:43
  46.9 19.5 %collective-permute-start.15 = (bf16[160,1280]{1,0:T(8,128)(2,1)S(1)}, bf16[160,1280]{1,0:T(8,128)(2,1)S(1)}, u32[]{:S(2)}, u32[]{:S(2)}) collective-permute-start(bf16[160,1280]{1,0:T(8,128)(2,1)S(1)} %pad_maximum_fusion.8.refs_4_), channel_id=1, source_target_pairs={{0,4},{1,5},{2,6},{3,7},{4,0},{5,1},{6,2},{7,3},{8,12},{9,13},{10,... | collective-permute-start | bytes 1228808 | tf_op jit(solution)/shard_map/ppermute | solution.py:39
  62.7 5.3 %collective-permute-start.6 = (bf16[128,1280]{1,0:T(8,128)(2,1)}, bf16[128,1280]{1,0:T(8,128)(2,1)S(1)}, u32[]{:S(2)}, u32[]{:S(2)}) collective-permute-start(bf16[128,1280]{1,0:T(8,128)(2,1)} %get-tuple-element.69), channel_id=1, source_target_pairs={{0,1},{1,0},{2,3},{3,2},{4,5},{5,4},{6,7},{7,6},{8,9},{9,8},{10,11... | collective-permute-start | bytes 983048 | tf_op jit(solution)/shard_map/ppermute | solution.py:31
  62.8 21.5 %collective-permute-start.9 = (bf16[160,1280]{1,0:T(8,128)(2,1)S(1)}, bf16[160,1280]{1,0:T(8,128)(2,1)S(1)}, u32[]{:S(2)}, u32[]{:S(2)}) collective-permute-start(bf16[160,1280]{1,0:T(8,128)(2,1)S(1)} %copy-done.29), channel_id=1, source_target_pairs={{0,16},{1,17},{2,18},{3,19},{4,20},{5,21},{6,22},{7,23},{8,24},{9,... | collective-permute-start | bytes 1228808 | tf_op jit(solution)/shard_map/ppermute | solution.py:43
  66.4 27.3 %copy-start.6 = (bf16[480,1280]{1,0:T(8,128)(2,1)}, bf16[480,1280]{1,0:T(8,128)(2,1)S(1)}, u32[]{:S(2)}) copy-start(bf16[480,1280]{1,0:T(8,128)(2,1)S(1)} %pad_maximum_fusion.refs_5_) | copy-start | bytes 3686404
  66.4 27.2 %copy-start.26 = (bf16[160,1280]{1,0:T(8,128)(2,1)}, bf16[160,1280]{1,0:T(8,128)(2,1)S(1)}, u32[]{:S(2)}) copy-start(bf16[160,1280]{1,0:T(8,128)(2,1)S(1)} %collective-permute-done.15.refs_6_) | copy-start | bytes 1228804
  66.4 29.7 %collective-permute-start.16 = (bf16[480,1280]{1,0:T(8,128)(2,1)S(1)}, bf16[480,1280]{1,0:T(8,128)(2,1)S(1)}, u32[]{:S(2)}, u32[]{:S(2)}) collective-permute-start(bf16[480,1280]{1,0:T(8,128)(2,1)S(1)} %pad_maximum_fusion.refs_5_), channel_id=1, source_target_pairs={{0,4},{1,5},{2,6},{3,7},{4,0},{5,1},{6,2},{7,3},{8,12},{9,13},{10,... | collective-permute-start | bytes 3686408 | tf_op jit(solution)/shard_map/ppermute | solution.py:39
  68.1 9.6 %collective-permute-start.7 = (bf16[128,1280]{1,0:T(8,128)(2,1)S(1)}, bf16[128,1280]{1,0:T(8,128)(2,1)S(1)}, u32[]{:S(2)}, u32[]{:S(2)}) collective-permute-start(bf16[128,1280]{1,0:T(8,128)(2,1)S(1)} %add_convert_fusion.2.left_ref), channel_id=1, source_target_pairs={{0,2},{1,3},{2,0},{3,1},{4,6},{5,7},{6,4},{7,5},{8,10},{9,11},{10,... | collective-permute-start | bytes 983048 | tf_op jit(solution)/shard_map/ppermute | solution.py:35
  84.3 9.3 %collective-permute-start.11 = (bf16[128,1280]{1,0:T(8,128)(2,1)S(1)}, bf16[128,1280]{1,0:T(8,128)(2,1)S(1)}, u32[]{:S(2)}, u32[]{:S(2)}) collective-permute-start(bf16[128,1280]{1,0:T(8,128)(2,1)S(1)} %get-tuple-element.73.refs_0_), channel_id=1, source_target_pairs={{0,8},{1,9},{2,10},{3,11},{4,12},{5,13},{6,14},{7,15},{8,0},{9,1},... | collective-permute-start | bytes 983048 | tf_op jit(solution)/shard_map/ppermute | solution.py:43
  84.8 11.3 %collective-permute-start.10 = (bf16[128,1280]{1,0:T(8,128)(2,1)S(1)}, bf16[128,1280]{1,0:T(8,128)(2,1)S(1)}, u32[]{:S(2)}, u32[]{:S(2)}) collective-permute-start(bf16[128,1280]{1,0:T(8,128)(2,1)S(1)} %get-tuple-element.73.refs_0_), channel_id=1, source_target_pairs={{0,1},{1,0},{2,3},{3,2},{4,5},{5,4},{6,7},{7,6},{8,9},{9,8},{10,11... | collective-permute-start | bytes 983048 | tf_op jit(solution)/shard_map/ppermute | solution.py:31
  93.6 2.6 collective-permute-start.12
  93.7 20.8 %collective-permute-start.19 = (bf16[320,1280]{1,0:T(8,128)(2,1)S(1)}, bf16[320,1280]{1,0:T(8,128)(2,1)}, u32[]{:S(2)}, u32[]{:S(2)}) collective-permute-start(bf16[320,1280]{1,0:T(8,128)(2,1)S(1)} %constant_dynamic-update-slice_fusion.refs_0_), channel_id=1, source_target_pairs={{0,8},{1,9},{2,10},{3,11},{4,12},{5,13},{6,14},{7,15},{8,0},{9,1},... | collective-permute-start | bytes 2457608 | tf_op jit(solution)/shard_map/ppermute | solution.py:43
  94.6 20.4 %collective-permute-start.20 = (bf16[320,1280]{1,0:T(8,128)(2,1)S(1)}, bf16[320,1280]{1,0:T(8,128)(2,1)S(1)}, u32[]{:S(2)}, u32[]{:S(2)}) collective-permute-start(bf16[320,1280]{1,0:T(8,128)(2,1)S(1)} %constant_dynamic-update-slice_fusion.refs_0_), channel_id=1, source_target_pairs={{0,4},{1,5},{2,6},{3,7},{4,0},{5,1},{6,2},{7,3},{8,12},{9,13},{10,... | collective-permute-start | bytes 2457608 | tf_op jit(solution)/shard_map/ppermute | solution.py:39
  105.1 26.6 %copy-start.34 = (bf16[128,1280]{1,0:T(8,128)(2,1)S(1)}, bf16[128,1280]{1,0:T(8,128)(2,1)}, u32[]{:S(2)}) copy-start(bf16[128,1280]{1,0:T(8,128)(2,1)} %get-tuple-element.78) | copy-start | bytes 983044
  105.1 1.9 collective-permute-start.18
  105.5 15.0 %collective-permute-start.17 = (bf16[128,1280]{1,0:T(8,128)(2,1)}, bf16[128,1280]{1,0:T(8,128)(2,1)S(1)}, u32[]{:S(2)}, u32[]{:S(2)}) collective-permute-start(bf16[128,1280]{1,0:T(8,128)(2,1)} %get-tuple-element.79), channel_id=1, source_target_pairs={{0,1},{1,0},{2,3},{3,2},{4,5},{5,4},{6,7},{7,6},{8,9},{9,8},{10,11... | collective-permute-start | bytes 983048 | tf_op jit(solution)/shard_map/ppermute | solution.py:31
  115.0 16.7 %collective-permute-start.21 = (bf16[128,1280]{1,0:T(8,128)(2,1)S(1)}, bf16[128,1280]{1,0:T(8,128)(2,1)S(1)}, u32[]{:S(2)}, u32[]{:S(2)}) collective-permute-start(bf16[128,1280]{1,0:T(8,128)(2,1)S(1)} %add_convert_fusion.1), channel_id=1, source_target_pairs={{0,8},{1,9},{2,10},{3,11},{4,12},{5,13},{6,14},{7,15},{8,0},{9,1},... | collective-permute-start | bytes 983048 | tf_op jit(solution)/shard_map/ppermute | solution.py:43
  116.4 21.6 %collective-permute-start.23 = (bf16[160,1280]{1,0:T(8,128)(2,1)S(1)}, bf16[160,1280]{1,0:T(8,128)(2,1)S(1)}, u32[]{:S(2)}, u32[]{:S(2)}) collective-permute-start(bf16[160,1280]{1,0:T(8,128)(2,1)S(1)} %pad_maximum_fusion.9), channel_id=1, source_target_pairs={{0,16},{1,17},{2,18},{3,19},{4,20},{5,21},{6,22},{7,23},{8,24},{9,... | collective-permute-start | bytes 1228808 | tf_op jit(solution)/shard_map/ppermute | solution.py:43
  119.0 20.7 %collective-permute-start.24 = (bf16[320,1280]{1,0:T(8,128)(2,1)}, bf16[320,1280]{1,0:T(8,128)(2,1)S(1)}, u32[]{:S(2)}, u32[]{:S(2)}) collective-permute-start(bf16[320,1280]{1,0:T(8,128)(2,1)} %collective-permute-done.19.refs_2_), channel_id=1, source_target_pairs={{0,4},{1,5},{2,6},{3,7},{4,0},{5,1},{6,2},{7,3},{8,12},{9,13},{10,... | collective-permute-start | bytes 2457608 | tf_op jit(solution)/shard_map/ppermute | solution.py:39
  131.8 5.4 %collective-permute-start.22 = (bf16[64,1280]{1,0:T(8,128)(2,1)S(1)}, bf16[64,1280]{1,0:T(8,128)(2,1)S(1)}, u32[]{:S(2)}, u32[]{:S(2)}) collective-permute-start(bf16[64,1280]{1,0:T(8,128)(2,1)S(1)} %dynamic-slice_bitcast_fusion), channel_id=1, source_target_pairs={{0,2},{1,3},{2,0},{3,1},{4,6},{5,7},{6,4},{7,5},{8,10},{9,11},{10,... | collective-permute-start | bytes 491528 | tf_op jit(solution)/shard_map/ppermute | solution.py:35
  138.0 18.0 %collective-permute-start.27 = (bf16[320,1280]{1,0:T(8,128)(2,1)S(1)}, bf16[320,1280]{1,0:T(8,128)(2,1)S(1)}, u32[]{:S(2)}, u32[]{:S(2)}) collective-permute-start(bf16[320,1280]{1,0:T(8,128)(2,1)S(1)} %constant_dynamic-update-slice_fusion.2.refs_0_), channel_id=1, source_target_pairs={{0,8},{1,9},{2,10},{3,11},{4,12},{5,13},{6,14},{7,15},{8,0},{9,1},... | collective-permute-start | bytes 2457608 | tf_op jit(solution)/shard_map/ppermute | solution.py:43
  138.1 18.4 %collective-permute-start.28 = (bf16[320,1280]{1,0:T(8,128)(2,1)S(1)}, bf16[320,1280]{1,0:T(8,128)(2,1)S(1)}, u32[]{:S(2)}, u32[]{:S(2)}) collective-permute-start(bf16[320,1280]{1,0:T(8,128)(2,1)S(1)} %constant_dynamic-update-slice_fusion.2.refs_0_), channel_id=1, source_target_pairs={{0,4},{1,5},{2,6},{3,7},{4,0},{5,1},{6,2},{7,3},{8,12},{9,13},{10,... | collective-permute-start | bytes 2457608 | tf_op jit(solution)/shard_map/ppermute | solution.py:39
  145.2 1.6 collective-permute-start.25
  147.7 4.8 %collective-permute-start.26 = (bf16[64,640]{1,0:T(8,128)(2,1)S(1)}, bf16[64,640]{1,0:T(8,128)(2,1)S(1)}, u32[]{:S(2)}, u32[]{:S(2)}) collective-permute-start(bf16[64,640]{1,0:T(8,128)(2,1)S(1)} %add_convert_fusion.8), channel_id=1, source_target_pairs={{0,2},{1,3},{2,0},{3,1},{4,6},{5,7},{6,4},{7,5},{8,10},{9,11},{10,... | collective-permute-start | bytes 245768 | tf_op jit(solution)/shard_map/ppermute | solution.py:35
  156.0 28.7 %copy-start.16 = (bf16[320,1280]{1,0:T(8,128)(2,1)}, bf16[320,1280]{1,0:T(8,128)(2,1)S(1)}, u32[]{:S(2)}) copy-start(bf16[320,1280]{1,0:T(8,128)(2,1)S(1)} %collective-permute-done.27.refs_2_) | copy-start | bytes 2457604
  156.5 27.8 %copy-start.17 = (bf16[320,1280]{1,0:T(8,128)(2,1)}, bf16[320,1280]{1,0:T(8,128)(2,1)S(1)}, u32[]{:S(2)}) copy-start(bf16[320,1280]{1,0:T(8,128)(2,1)S(1)} %collective-permute-done.28.refs_1_) | copy-start | bytes 2457604
  156.5 5.7 %collective-permute-start.29 = (bf16[4,1,16,768]{3,2,0,1:T(8,128)(2,1)S(1)}, bf16[4,1,16,768]{3,2,0,1:T(8,128)(2,1)S(1)}, u32[]{:S(2)}, u32[]{:S(2)}) collective-permute-start(bf16[4,1,16,768]{3,2,0,1:T(8,128)(2,1)S(1)} %dynamic-slice_bitcast_fusion.1), channel_id=1, source_target_pairs={{0,4},{1,5},{2,6},{3,7},{4,0},{5,1},{6,2},{7,3},{8,12},{9,13},{10,... | collective-permute-start | bytes 294920 | tf_op jit(solution)/shard_map/ppermute | solution.py:39
  162.2 26.2 %collective-permute-start.36 = (bf16[320,1280]{1,0:T(8,128)(2,1)S(1)}, bf16[320,1280]{1,0:T(8,128)(2,1)S(1)}, u32[]{:S(2)}, u32[]{:S(2)}) collective-permute-start(bf16[320,1280]{1,0:T(8,128)(2,1)S(1)} %collective-permute-done.27.refs_2_), channel_id=1, source_target_pairs={{0,4},{1,5},{2,6},{3,7},{4,0},{5,1},{6,2},{7,3},{8,12},{9,13},{10,... | collective-permute-start | bytes 2457608 | tf_op jit(solution)/shard_map/ppermute | solution.py:39
  164.5 25.3 %copy-start.22 = (bf16[160,640]{1,0:T(8,128)(2,1)}, bf16[160,640]{1,0:T(8,128)(2,1)S(1)}, u32[]{:S(2)}) copy-start(bf16[160,640]{1,0:T(8,128)(2,1)S(1)} %get-tuple-element.110.refs_4_) | copy-start | bytes 614404
  164.5 9.2 %collective-permute-start.30 = (bf16[160,640]{1,0:T(8,128)(2,1)}, bf16[160,640]{1,0:T(8,128)(2,1)S(1)}, u32[]{:S(2)}, u32[]{:S(2)}) collective-permute-start(bf16[160,640]{1,0:T(8,128)(2,1)} %get-tuple-element.126), channel_id=1, source_target_pairs={{0,8},{1,9},{2,10},{3,11},{4,12},{5,13},{6,14},{7,15},{8,0},{9,1},... | collective-permute-start | bytes 614408 | tf_op jit(solution)/shard_map/ppermute | solution.py:43
  166.5 13.3 %collective-permute-start.31 = (bf16[160,640]{1,0:T(8,128)(2,1)S(1)}, bf16[160,640]{1,0:T(8,128)(2,1)S(1)}, u32[]{:S(2)}, u32[]{:S(2)}) collective-permute-start(bf16[160,640]{1,0:T(8,128)(2,1)S(1)} %get-tuple-element.110.refs_4_), channel_id=1, source_target_pairs={{0,16},{1,17},{2,18},{3,19},{4,20},{5,21},{6,22},{7,23},{8,24},{9,... | collective-permute-start | bytes 614408 | tf_op jit(solution)/shard_map/ppermute | solution.py:43
  167.5 12.3 %collective-permute-start.32 = (bf16[160,640]{1,0:T(8,128)(2,1)}, bf16[160,640]{1,0:T(8,128)(2,1)S(1)}, u32[]{:S(2)}, u32[]{:S(2)}) collective-permute-start(bf16[160,640]{1,0:T(8,128)(2,1)} %get-tuple-element.126), channel_id=1, source_target_pairs={{0,24},{1,25},{2,26},{3,27},{4,28},{5,29},{6,30},{7,31},{8,16},{9,... | collective-permute-start | bytes 614408 | tf_op jit(solution)/shard_map/ppermute | solution.py:43
  168.9 15.8 %collective-permute-start.37 = (bf16[160,640]{1,0:T(8,128)(2,1)S(1)}, bf16[160,640]{1,0:T(8,128)(2,1)S(1)}, u32[]{:S(2)}, u32[]{:S(2)}) collective-permute-start(bf16[160,640]{1,0:T(8,128)(2,1)S(1)} %get-tuple-element.110.refs_4_), channel_id=1, source_target_pairs={{0,4},{1,5},{2,6},{3,7},{4,0},{5,1},{6,2},{7,3},{8,12},{9,13},{10,... | collective-permute-start | bytes 614408 | tf_op jit(solution)/shard_map/ppermute | solution.py:39
  179.8 6.5 %collective-permute-start.35 = (bf16[2,1,16,768]{3,2,0,1:T(8,128)(2,1)S(1)}, bf16[2,1,16,768]{3,2,0,1:T(8,128)(2,1)S(1)}, u32[]{:S(2)}, u32[]{:S(2)}) collective-permute-start(bf16[2,1,16,768]{3,2,0,1:T(8,128)(2,1)S(1)} %get-tuple-element.132), channel_id=1, source_target_pairs={{0,24},{1,25},{2,26},{3,27},{4,28},{5,29},{6,30},{7,31},{8,16},{9,... | collective-permute-start | bytes 147464 | tf_op jit(solution)/shard_map/ppermute | solution.py:43
  182.7 5.0 %collective-permute-start.34 = (bf16[2,1,16,768]{3,2,0,1:T(8,128)(2,1)S(1)}, bf16[2,1,16,768]{3,2,0,1:T(8,128)(2,1)S(1)}, u32[]{:S(2)}, u32[]{:S(2)}) collective-permute-start(bf16[2,1,16,768]{3,2,0,1:T(8,128)(2,1)S(1)} %get-tuple-element.133), channel_id=1, source_target_pairs={{0,16},{1,17},{2,18},{3,19},{4,20},{5,21},{6,22},{7,23},{8,24},{9,... | collective-permute-start | bytes 147464 | tf_op jit(solution)/shard_map/ppermute | solution.py:43
  184.3 4.1 %collective-permute-start.33 = (bf16[2,1,16,768]{3,2,0,1:T(8,128)(2,1)S(1)}, bf16[2,1,16,768]{3,2,0,1:T(8,128)(2,1)S(1)}, u32[]{:S(2)}, u32[]{:S(2)}) collective-permute-start(bf16[2,1,16,768]{3,2,0,1:T(8,128)(2,1)S(1)} %get-tuple-element.134), channel_id=1, source_target_pairs={{0,8},{1,9},{2,10},{3,11},{4,12},{5,13},{6,14},{7,15},{8,0},{9,1},... | collective-permute-start | bytes 147464 | tf_op jit(solution)/shard_map/ppermute | solution.py:43
  184.7 13.1 %collective-permute-start.38 = (bf16[480,640]{1,0:T(8,128)(2,1)S(1)}, bf16[480,640]{1,0:T(8,128)(2,1)S(1)}, u32[]{:S(2)}, u32[]{:S(2)}) collective-permute-start(bf16[480,640]{1,0:T(8,128)(2,1)S(1)} %pad_maximum_fusion.3.refs_5_), channel_id=1, source_target_pairs={{0,4},{1,5},{2,6},{3,7},{4,0},{5,1},{6,2},{7,3},{8,12},{9,13},{10,... | collective-permute-start | bytes 1843208 | tf_op jit(solution)/shard_map/ppermute | solution.py:39
  190.8 21.2 %all-to-all-start = ((bf16[4,160,640]{2,1,0:T(8,128)(2,1)}), bf16[4,160,640]{2,1,0:T(8,128)(2,1)S(1)}, u32[]{:S(2)}, u32[]{:S(2)}) async-start(bf16[4,160,640]{2,1,0:T(8,128)(2,1)} %pad_maximum_fusion.2), calls=%async_computation | async-start | bytes 1638400 | tf_op jit(solution)/shard_map/all_to_all | solution.py:92
  197.8 1.5 collective-permute-start.39
  200.2 19.6 %copy-start.5 = (s32[25]{0:T(128)S(1)}, s32[25]{0:T(128)}, u32[]{:S(2)}) copy-start(s32[25]{0:T(128)} %stack.110.spots_ref) | copy-start | bytes 304
  207.0 5.5 %collective-permute-start.40 = (bf16[96,1280]{1,0:T(8,128)(2,1)}, bf16[96,1280]{1,0:T(8,128)(2,1)S(1)}, u32[]{:S(2)}, u32[]{:S(2)}) collective-permute-start(bf16[96,1280]{1,0:T(8,128)(2,1)} %get-tuple-element.107), channel_id=1, source_target_pairs={{0,1},{1,0},{2,3},{3,2},{4,5},{5,4},{6,7},{7,6},{8,9},{9,8},{10,11... | collective-permute-start | bytes 737288 | tf_op jit(solution)/shard_map/ppermute | solution.py:31
  212.0 17.1 %collective-permute-start.45 = (bf16[640,640]{1,0:T(8,128)(2,1)S(1)}, bf16[640,640]{1,0:T(8,128)(2,1)S(1)}, u32[]{:S(2)}, u32[]{:S(2)}) collective-permute-start(bf16[640,640]{1,0:T(8,128)(2,1)S(1)} %bitcast.62), channel_id=1, source_target_pairs={{0,4},{1,5},{2,6},{3,7},{4,0},{5,1},{6,2},{7,3},{8,12},{9,13},{10,... | collective-permute-start | bytes 2457608 | tf_op jit(solution)/shard_map/ppermute | solution.py:39
  213.5 6.3 %collective-permute-start.41 = (bf16[96,1280]{1,0:T(8,128)(2,1)S(1)}, bf16[96,1280]{1,0:T(8,128)(2,1)S(1)}, u32[]{:S(2)}, u32[]{:S(2)}) collective-permute-start(bf16[96,1280]{1,0:T(8,128)(2,1)S(1)} %add_convert_fusion.6.left_ref), channel_id=1, source_target_pairs={{0,2},{1,3},{2,0},{3,1},{4,6},{5,7},{6,4},{7,5},{8,10},{9,11},{10,... | collective-permute-start | bytes 737288 | tf_op jit(solution)/shard_map/ppermute | solution.py:35
  220.6 6.3 %collective-permute-start.43 = (bf16[96,1280]{1,0:T(8,128)(2,1)S(1)}, bf16[96,1280]{1,0:T(8,128)(2,1)S(1)}, u32[]{:S(2)}, u32[]{:S(2)}) collective-permute-start(bf16[96,1280]{1,0:T(8,128)(2,1)S(1)} %get-tuple-element.109.refs_0_), channel_id=1, source_target_pairs={{0,8},{1,9},{2,10},{3,11},{4,12},{5,13},{6,14},{7,15},{8,0},{9,1},... | collective-permute-start | bytes 737288 | tf_op jit(solution)/shard_map/ppermute | solution.py:43
  220.7 6.2 %collective-permute-start.42 = (bf16[96,1280]{1,0:T(8,128)(2,1)S(1)}, bf16[96,1280]{1,0:T(8,128)(2,1)S(1)}, u32[]{:S(2)}, u32[]{:S(2)}) collective-permute-start(bf16[96,1280]{1,0:T(8,128)(2,1)S(1)} %get-tuple-element.109.refs_0_), channel_id=1, source_target_pairs={{0,1},{1,0},{2,3},{3,2},{4,5},{5,4},{6,7},{7,6},{8,9},{9,8},{10,11... | collective-permute-start | bytes 737288 | tf_op jit(solution)/shard_map/ppermute | solution.py:31
  226.9 1.5 collective-permute-start.44
  237.2 1.8 collective-permute-start.47
  237.4 3.0 %collective-permute-start.46 = (bf16[96,1280]{1,0:T(8,128)(2,1)}, bf16[96,1280]{1,0:T(8,128)(2,1)S(1)}, u32[]{:S(2)}, u32[]{:S(2)}) collective-permute-start(bf16[96,1280]{1,0:T(8,128)(2,1)} %get-tuple-element.116), channel_id=1, source_target_pairs={{0,1},{1,0},{2,3},{3,2},{4,5},{5,4},{6,7},{7,6},{8,9},{9,8},{10,11... | collective-permute-start | bytes 737288 | tf_op jit(solution)/shard_map/ppermute | solution.py:31
  240.0 8.1 %collective-permute-start.48 = (bf16[96,1280]{1,0:T(8,128)(2,1)S(1)}, bf16[96,1280]{1,0:T(8,128)(2,1)S(1)}, u32[]{:S(2)}, u32[]{:S(2)}) collective-permute-start(bf16[96,1280]{1,0:T(8,128)(2,1)S(1)} %add_convert_fusion.5), channel_id=1, source_target_pairs={{0,8},{1,9},{2,10},{3,11},{4,12},{5,13},{6,14},{7,15},{8,0},{9,1},... | collective-permute-start | bytes 737288 | tf_op jit(solution)/shard_map/ppermute | solution.py:43
  249.2 7.2 %collective-permute-start.49 = (bf16[96,1280]{1,0:T(8,128)(2,1)S(1)}, bf16[96,1280]{1,0:T(8,128)(2,1)S(1)}, u32[]{:S(2)}, u32[]{:S(2)}) collective-permute-start(bf16[96,1280]{1,0:T(8,128)(2,1)S(1)} %add_convert_fusion.4), channel_id=1, source_target_pairs={{0,2},{1,3},{2,0},{3,1},{4,6},{5,7},{6,4},{7,5},{8,10},{9,11},{10,... | collective-permute-start | bytes 737288 | tf_op jit(solution)/shard_map/ppermute | solution.py:35
  256.5 1.6 collective-permute-start.50
  (32 other events, 255.0 us)

commit v6 on v5

--- a/solution.py
+++ b/solution.py
@@ -143,7 +143,7 @@
 ANY = pl.BlockSpec(memory_space=pl.ANY)
 
 
-def local_call(kernel, ins, in_specs, outs, scratch, limit=56):
+def local_call(kernel, ins, in_specs, outs, scratch, limit=28):
     return pl.pallas_call(
         kernel,
         in_specs=in_specs,
@@ -160,7 +160,16 @@
     heads = qkv_width // (3 * HEAD_DIM)
     half = length // 2
 
-    def kernel(spots_ref, rows_ref, allowed_ref, *refs):
+    masks = [] if allowed is None else [allowed]
+
+    def kernel(spots_ref, rows_ref, *refs):
+        if allowed is None:
+            seen = lax.broadcasted_iota(jnp.int32, (length, length), 0) >= lax.broadcasted_iota(
+                jnp.int32, (length, length), 1
+            )
+        else:
+            seen = refs[0][...] > 0
+            refs = refs[1:]
         piece_refs = refs[: len(pieces)]
         keep, send, weight, projected, mixed, sems = refs[len(pieces) :]
         copies = load_weight(spots_ref, base, piece_refs, weight, sems)
@@ -179,7 +188,7 @@
             key = projected[:, at + HEAD_DIM : at + 2 * HEAD_DIM].astype(jnp.bfloat16)
             value = projected[:, at + 2 * HEAD_DIM : at + 3 * HEAD_DIM].astype(jnp.bfloat16)
             scores = dot_t(query, key) * HEAD_DIM ** (-0.5)
-            scores = jnp.where(allowed_ref[...] > 0, scores, -1e30)
+            scores = jnp.where(seen, scores, -1e30)
             exponent = jnp.exp(scores - jnp.max(scores, axis=-1, keepdims=True))
             soft = (exponent / jnp.sum(exponent, axis=-1, keepdims=True)).astype(jnp.bfloat16)
             out_at = qkv_width + head * HEAD_DIM
@@ -195,8 +204,8 @@
 
     return local_call(
         kernel,
-        [spots, rows, allowed] + pieces,
-        [SMEM, VMEM, VMEM] + [ANY] * len(pieces),
+        [spots, rows] + masks + pieces,
+        [SMEM, VMEM] + [VMEM] * len(masks) + [ANY] * len(pieces),
         [(half, width)] * 2,
         [
             pltpu.VMEM((width, width), jnp.bfloat16),
@@ -433,9 +442,6 @@
     dec_up = Halved(mine, others, others)
     both = exchange_y(outgoing.reshape(8, senders // 8, padded, -1))
     both, attn_pair = together(both, attn_pair)
-    both, dec_up.first, dec_up.second, dec_up.third = together(
-        both, dec_up.first, dec_up.second, dec_up.third
-    )
     dec_up = dec_up.pieces()
     attn_pair_y = swap_y(attn_pair)
     incoming = exchange_z(both)
@@ -455,10 +461,10 @@
     ).astype(jnp.bfloat16)
     text_half = lax.dynamic_slice_in_dim(text_embed, c * half_width, half_width, 1)
     dec_half = jnp.where(jnp.any(hits, axis=1)[:, None], placed, text_half)
-    dec_half, *dec_up = together(dec_half, *dec_up)
     rows = join_core(dec_half, 1)
-    causal = (positions[:, None] >= positions[None, :]).astype(jnp.float32)
+    causal = None
     keep, send = attention(spots, WHOLE, rows, causal, dec_attn, qkv_width)
+    send, *dec_up = together(send, *dec_up)
     mine = add_short(keep, swap_core(send)).astype(jnp.bfloat16)
     mid, normed = middle(spots, rows, mine, swap_x(mine))
     normed_pair = swap_z(normed, 1)

time: 260 us -> 255 us (0.981)
  other arithmetic: 17.3 us -> 12.9 us
  Pallas kernels: 34.4 us -> 31.1 us
  starting transfers between devices: 62.6 us -> 65.2 us
    ppermute x13, waiting for transfers between devices: 14.3 us -> 20.8 us  [swap_y(): return lax.ppermute(part, AXES, routes(lambda z, y, x, c: (z, 1 - y, x, c)))]
    all_to_all x1, waiting for transfers between devices: 4.78 us -> 0.01 us  [halved_column(): lax.all_to_all(jnp.stack([weight[:, :half], weight[:, half:]] * 2), 'req'...]
    pallas_call x7, Pallas kernels: 34.4 us -> 31.1 us  [local_call(): pl.pallas_call(kernel, in_specs=in_specs, out_specs=[VMEM] * len(outs), o...]
    ppermute x20, starting transfers between devices: 26.5 us -> 29.7 us  [swap_z(): return lax.ppermute(part, AXES, routes(lambda z, y, x, c: (z ^ k, y, x, c)))]
    reshape x2, local copies, waits for them, and re-layouts: 1.16 us -> 3.81 us  [on_device(): rows = patches.reshape(image_count, HALF, 2, HALF, 2, model_width)]
  transfers between devices with their start and end apart: 52 -> 52, of which waited for: 34 -> 30; matrix products, arithmetic and copies ran while one was open for 8% -> 7% of each run, Pallas kernels for 10% -> 9%
where the time goes in v6:
time: 255 us; the launch traced here: 254 us
  waiting for transfers between devices  134 us (53%)
  starting transfers between devices  65.2 us (26%)
  Pallas kernels  31.1 us (12%)
  other arithmetic  12.9 us (5%)
  local copies, waits for them, and re-layouts  8.82 us (3%)
    ppermute x20, waiting for transfers between devices, swap_z(): return lax.ppermute(part, AXES, routes(lambda z, y, x, c: (z ^ k, y, x, c)))  80.5 us
    pallas_call x7, Pallas kernels, local_call(): pl.pallas_call(kernel, in_specs=in_specs, out_specs=[VMEM] * len(outs), o...  31.1 us
    ppermute x20, starting transfers between devices, swap_z(): return lax.ppermute(part, AXES, routes(lambda z, y, x, c: (z ^ k, y, x, c)))  29.7 us
    ppermute x5, waiting for transfers between devices, swap_x(): return lax.ppermute(part, AXES, routes(lambda z, y, x, c: (z, y, 1 - x, c)))  26.7 us
    ppermute x13, starting transfers between devices, swap_y(): return lax.ppermute(part, AXES, routes(lambda z, y, x, c: (z, 1 - y, x, c)))  21.9 us
    ppermute x13, waiting for transfers between devices, swap_y(): return lax.ppermute(part, AXES, routes(lambda z, y, x, c: (z, 1 - y, x, c)))  20.8 us
    ppermute x5, starting transfers between devices, swap_x(): return lax.ppermute(part, AXES, routes(lambda z, y, x, c: (z, y, 1 - x, c)))  7.77 us
    ppermute x13, waiting for transfers between devices, swap_core(): return lax.ppermute(part, AXES, routes(lambda z, y, x, c: (z, y, x, 1 - c)))  5.77 us
  transfers between devices with their start and end apart: 52, of which 30 were waited for; matrix products, arithmetic and copies ran while one was open for 7% of the time, Pallas kernels for 9%

profile of v6, /device:TPU:0, one launch (start us, length us, event | category | flops | bytes accessed | tf_op | source)
XLA Modules:
  0.0 254.4 jit_solution(6639159834919028564)
XLA Ops:
  1.1 3.1 %collective-permute-start = (bf16[160,1280]{1,0:T(8,128)(2,1)S(1)}, bf16[160,1280]{1,0:T(8,128)(2,1)S(1)}, u32[]{:S(2)}, u32[]{:S(2)}) collective-permute-start(bf16[160,1280]{1,0:T(8,128)(2,1)S(1)} %pad_maximum_fusion.6.refs_1_), channel_id=1, source_target_pairs={{0,8},{1,9},{2,10},{3,11},{4,12},{5,13},{6,14},{7,15},{8,0},{9,1},... | collective-permute-start | bytes 1228808 | tf_op jit(solution)/shard_map/ppermute | solution.py:43
  4.2 2.6 %collective-permute-start.1 = (bf16[160,1280]{1,0:T(8,128)(2,1)S(1)}, bf16[160,1280]{1,0:T(8,128)(2,1)S(1)}, u32[]{:S(2)}, u32[]{:S(2)}) collective-permute-start(bf16[160,1280]{1,0:T(8,128)(2,1)S(1)} %pad_maximum_fusion.6.refs_1_), channel_id=1, source_target_pairs={{0,16},{1,17},{2,18},{3,19},{4,20},{5,21},{6,22},{7,23},{8,24},{9,... | collective-permute-start | bytes 1228808 | tf_op jit(solution)/shard_map/ppermute | solution.py:43
  6.8 1.5 collective-permute-start.2
  8.4 1.4 fusion.25
  9.7 12.6 %collective-permute-done.refs_2_ = bf16[160,1280]{1,0:T(8,128)(2,1)S(1)} collective-permute-done((bf16[160,1280]{1,0:T(8,128)(2,1)S(1)}, bf16[160,1280]{1,0:T(8,128)(2,1)S(1)}, u32[]{:S(2)}, u32[]{:S(2)}) %collective-permute-start) | collective-permute-done | bytes 409632 | tf_op jit(solution)/shard_map/ppermute | solution.py:43
  22.4 2.5 collective-permute-done.1.refs_3_
  25.4 1.6 collective-permute-start.4
  27.9 2.1 collective-permute-start.8
  31.0 4.8 %collective-permute-done.3.refs_4_ = bf16[160,1280]{1,0:T(8,128)(2,1)} collective-permute-done((bf16[160,1280]{1,0:T(8,128)(2,1)S(1)}, bf16[160,1280]{1,0:T(8,128)(2,1)}, u32[]{:S(2)}, u32[]{:S(2)}) %collective-permute-start.3) | collective-permute-done | bytes 409632 | tf_op jit(solution)/shard_map/ppermute | solution.py:43
  35.8 7.3 %collective-permute-start.5 = (bf16[160,1280]{1,0:T(8,128)(2,1)}, bf16[160,1280]{1,0:T(8,128)(2,1)}, u32[]{:S(2)}, u32[]{:S(2)}) collective-permute-start(bf16[160,1280]{1,0:T(8,128)(2,1)} %collective-permute-done.3.refs_4_), channel_id=1, source_target_pairs={{0,4},{1,5},{2,6},{3,7},{4,0},{5,1},{6,2},{7,3},{8,12},{9,13},{10,... | collective-permute-start | bytes 1228808 | tf_op jit(solution)/shard_map/ppermute | solution.py:39
  43.2 1.3 compare_and_fusion
  44.7 2.0 collective-permute-done.4.refs_6_
  46.6 1.5 collective-permute-start.15
  48.3 2.7 %reshape.162 = bf16[1,8,2,8,2,1280]{5,4,3,2,1,0:T(2,128)(2,1)} reshape(bf16[256,1280]{1,0:T(8,128)(2,1)} %param.15) | data formatting | bytes 1310720 | tf_op jit(solution)/shard_map/reshape | solution.py:386
  51.0 1.2 copy.30
  52.2 3.3 %collective-permute-done.5.refs_7_ = bf16[160,1280]{1,0:T(8,128)(2,1)} collective-permute-done((bf16[160,1280]{1,0:T(8,128)(2,1)}, bf16[160,1280]{1,0:T(8,128)(2,1)}, u32[]{:S(2)}, u32[]{:S(2)}) %collective-permute-start.5) | collective-permute-done | bytes 409632 | tf_op jit(solution)/shard_map/ppermute | solution.py:39
  56.5 6.0 %shard_map.145 = (bf16[128,1280]{1,0:T(8,128)(2,1)S(1)}, bf16[128,1280]{1,0:T(8,128)(2,1)S(1)}) custom-call(s32[25]{0:T(128)S(1)} %stack.110.spots_ref, bf16[256,1280]{1,0:T(8,128)(2,1)S(1)} %bitcast.59, f32[256,256]{1,0:T(8,128)S(1)} %and_convert_fusion.refs_0_, bf16[160,1280]{1,0:T(8,128)(2,1)S(1)} %pad_maximum_fusion.6.refs_1_, ...), custom_call_target="tpu_custom_call" | custom-call | tf_op jit(solution)/shard_map/pallas_call | solution.py:147
  62.7 2.4 collective-permute-start.9
  65.1 1.3 pad_maximum_fusion.refs_5_
  66.4 1.6 collective-permute-start.16
  68.1 1.6 collective-permute-start.7
  69.7 8.0 %collective-permute-done.7.right_ref = bf16[128,1280]{1,0:T(8,128)(2,1)S(1)} collective-permute-done((bf16[128,1280]{1,0:T(8,128)(2,1)S(1)}, bf16[128,1280]{1,0:T(8,128)(2,1)S(1)}, u32[]{:S(2)}, u32[]{:S(2)}) %collective-permute-start.7) | collective-permute-done | bytes 327712 | tf_op jit(solution)/shard_map/ppermute | solution.py:35
  78.6 5.6 %collective-permute-done.9 = bf16[160,1280]{1,0:T(8,128)(2,1)S(1)} collective-permute-done((bf16[160,1280]{1,0:T(8,128)(2,1)S(1)}, bf16[160,1280]{1,0:T(8,128)(2,1)S(1)}, u32[]{:S(2)}, u32[]{:S(2)}) %collective-permute-start.9) | collective-permute-done | bytes 409632 | tf_op jit(solution)/shard_map/ppermute | solution.py:43
  84.8 8.7 %collective-permute-done.11.refs_2_ = bf16[128,1280]{1,0:T(8,128)(2,1)S(1)} collective-permute-done((bf16[128,1280]{1,0:T(8,128)(2,1)S(1)}, bf16[128,1280]{1,0:T(8,128)(2,1)S(1)}, u32[]{:S(2)}, u32[]{:S(2)}) %collective-permute-start.11) | collective-permute-done | bytes 327712 | tf_op jit(solution)/shard_map/ppermute | solution.py:43
  94.5 1.5 collective-permute-start.20
  96.0 6.3 %shard_map.147 = (bf16[128,1280]{1,0:T(8,128)(2,1)S(1)}, bf16[128,1280]{1,0:T(8,128)(2,1)S(1)}, bf16[128,1280]{1,0:T(8,128)(2,1)S(1)}, bf16[128,1280]{1,0:T(8,128)(2,1)}) custom-call(s32[25]{0:T(128)S(1)} %stack.110.spots_ref, bf16[128,1280]{1,0:T(8,128)(2,1)S(1)} %get-tuple-element.69.refs_0_, bf16[128,1280]{1,0:T(8,128)(2,1)S(1)} %collective-permute-done.10.refs_1_, ...), custom_call_target="tpu_custom_call" | custom-call | tf_op jit(solution)/shard_map/pallas_call | solution.py:147
  102.6 1.1 pad_maximum_fusion.9
  105.5 8.9 %collective-permute-done.19.refs_2_ = bf16[320,1280]{1,0:T(8,128)(2,1)} collective-permute-done((bf16[320,1280]{1,0:T(8,128)(2,1)S(1)}, bf16[320,1280]{1,0:T(8,128)(2,1)}, u32[]{:S(2)}, u32[]{:S(2)}) %collective-permute-start.19) | collective-permute-done | bytes 819232 | tf_op jit(solution)/shard_map/ppermute | solution.py:43
  114.8 1.2 collective-permute-start.21
  116.2 2.7 %collective-permute-start.23 = (bf16[160,1280]{1,0:T(8,128)(2,1)S(1)}, bf16[160,1280]{1,0:T(8,128)(2,1)S(1)}, u32[]{:S(2)}, u32[]{:S(2)}) collective-permute-start(bf16[160,1280]{1,0:T(8,128)(2,1)S(1)} %pad_maximum_fusion.9), channel_id=1, source_target_pairs={{0,16},{1,17},{2,18},{3,19},{4,20},{5,21},{6,22},{7,23},{8,24},{9,... | collective-permute-start | bytes 1228808 | tf_op jit(solution)/shard_map/ppermute | solution.py:43
  118.9 1.5 collective-permute-start.24
  120.4 11.2 %collective-permute-done.21 = bf16[128,1280]{1,0:T(8,128)(2,1)S(1)} collective-permute-done((bf16[128,1280]{1,0:T(8,128)(2,1)S(1)}, bf16[128,1280]{1,0:T(8,128)(2,1)S(1)}, u32[]{:S(2)}, u32[]{:S(2)}) %collective-permute-start.21) | collective-permute-done | bytes 327712 | tf_op jit(solution)/shard_map/ppermute | solution.py:43
  131.7 1.6 collective-permute-start.22
  133.3 3.8 %collective-permute-done.22 = bf16[64,1280]{1,0:T(8,128)(2,1)S(1)} collective-permute-done((bf16[64,1280]{1,0:T(8,128)(2,1)S(1)}, bf16[64,1280]{1,0:T(8,128)(2,1)S(1)}, u32[]{:S(2)}, u32[]{:S(2)}) %collective-permute-start.22) | collective-permute-done | bytes 163872 | tf_op jit(solution)/shard_map/ppermute | solution.py:35
  137.4 1.5 collective-permute-start.28
  139.0 3.7 %shard_map.148 = (bf16[64,640]{1,0:T(8,128)(2,1)S(1)}, bf16[64,640]{1,0:T(8,128)(2,1)S(1)}) custom-call(s32[25]{0:T(128)S(1)} %stack.110.spots_ref, bf16[64,1280]{1,0:T(8,128)(2,1)S(1)} %fusion.2.blocks_ref, bf16[320,1280]{1,0:T(8,128)(2,1)S(1)} %constant_dynamic-update-slice_fusion.refs_0_, bf16[320,1280]{1,0:T(8,128)(2,1)S(1)} %copy-done.1, ...), custom_call_target="tpu_custom_call" | custom-call | tf_op jit(solution)/shard_map/pallas_call | solution.py:147
  142.7 1.4 fusion.19
  144.2 1.6 collective-permute-start.26
  145.8 3.2 %collective-permute-done.26 = bf16[64,640]{1,0:T(8,128)(2,1)S(1)} collective-permute-done((bf16[64,640]{1,0:T(8,128)(2,1)S(1)}, bf16[64,640]{1,0:T(8,128)(2,1)S(1)}, u32[]{:S(2)}, u32[]{:S(2)}) %collective-permute-start.26) | collective-permute-done | bytes 81952 | tf_op jit(solution)/shard_map/ppermute | solution.py:35
  149.3 6.0 %collective-permute-done.27.refs_2_ = bf16[320,1280]{1,0:T(8,128)(2,1)} collective-permute-done((bf16[320,1280]{1,0:T(8,128)(2,1)S(1)}, bf16[320,1280]{1,0:T(8,128)(2,1)}, u32[]{:S(2)}, u32[]{:S(2)}) %collective-permute-start.27) | collective-permute-done | bytes 819232 | tf_op jit(solution)/shard_map/ppermute | solution.py:43
  156.1 1.6 collective-permute-start.29
  157.7 3.9 %collective-permute-done.29 = bf16[4,1,16,768]{3,2,0,1:T(8,128)(2,1)S(1)} collective-permute-done((bf16[4,1,16,768]{3,2,0,1:T(8,128)(2,1)S(1)}, bf16[4,1,16,768]{3,2,0,1:T(8,128)(2,1)S(1)}, u32[]{:S(2)}, u32[]{:S(2)}) %collective-permute-start.29) | collective-permute-done | bytes 98336 | tf_op jit(solution)/shard_map/ppermute | solution.py:39
  161.6 1.6 collective-permute-start.33
  163.2 3.0 %collective-permute-start.32 = (bf16[2,1,16,768]{3,2,0,1:T(8,128)(2,1)S(1)}, bf16[2,1,16,768]{3,2,0,1:T(8,128)(2,1)S(1)}, u32[]{:S(2)}, u32[]{:S(2)}) collective-permute-start(bf16[2,1,16,768]{3,2,0,1:T(8,128)(2,1)S(1)} %get-tuple-element.124), channel_id=1, source_target_pairs={{0,24},{1,25},{2,26},{3,27},{4,28},{5,29},{6,30},{7,31},{8,16},{9,... | collective-permute-start | bytes 147464 | tf_op jit(solution)/shard_map/ppermute | solution.py:43
  168.4 2.9 %collective-permute-start.37 = (bf16[160,640]{1,0:T(8,128)(2,1)}, bf16[160,640]{1,0:T(8,128)(2,1)}, u32[]{:S(2)}, u32[]{:S(2)}) collective-permute-start(bf16[160,640]{1,0:T(8,128)(2,1)} %get-tuple-element.117), channel_id=1, source_target_pairs={{0,24},{1,25},{2,26},{3,27},{4,28},{5,29},{6,30},{7,31},{8,16},{9,... | collective-permute-start | bytes 614408 | tf_op jit(solution)/shard_map/ppermute | solution.py:43
  174.1 6.4 %collective-permute-done.33.refs_3_ = bf16[320,1280]{1,0:T(8,128)(2,1)S(1)} collective-permute-done((bf16[320,1280]{1,0:T(8,128)(2,1)}, bf16[320,1280]{1,0:T(8,128)(2,1)S(1)}, u32[]{:S(2)}, u32[]{:S(2)}) %collective-permute-start.33) | collective-permute-done | bytes 819232 | tf_op jit(solution)/shard_map/ppermute | solution.py:39
  181.8 4.3 %all-to-all-start = ((bf16[4,160,640]{2,1,0:T(8,128)(2,1)}), bf16[4,160,640]{2,1,0:T(8,128)(2,1)S(1)}, u32[]{:S(2)}, u32[]{:S(2)}) async-start(bf16[4,160,640]{2,1,0:T(8,128)(2,1)} %pad_maximum_fusion.2), calls=%async_computation | async-start | bytes 1638400 | tf_op jit(solution)/shard_map/all_to_all | solution.py:92
  186.2 1.2 fusion
  187.4 7.5 %collective-permute-done.36 = bf16[160,640]{1,0:T(8,128)(2,1)} collective-permute-done((bf16[160,640]{1,0:T(8,128)(2,1)S(1)}, bf16[160,640]{1,0:T(8,128)(2,1)}, u32[]{:S(2)}, u32[]{:S(2)}) %collective-permute-start.36) | collective-permute-done | bytes 204832 | tf_op jit(solution)/shard_map/ppermute | solution.py:43
  195.0 1.2 pad_maximum_fusion.3.refs_5_
  197.5 6.0 %shard_map.149 = (bf16[96,1280]{1,0:T(8,128)(2,1)S(1)}, bf16[96,1280]{1,0:T(8,128)(2,1)}) custom-call(s32[25]{0:T(128)S(1)} %stack.110.spots_ref, bf16[192,1280]{1,0:T(8,128)(2,1)S(1)} %pad_maximum_fusion.4.rows_ref, bf16[320,1280]{1,0:T(8,128)(2,1)S(1)} %constant_dynamic-update-slice_fusion.2.refs_0_, bf16[320,1280]{1,0:T(8,128)(2,1)} %collective-permute-done.28.refs_1_, ...), custom_call_target="tpu_custom_call" | custom-call | tf_op jit(solution)/shard_map/pallas_call | solution.py:147
  203.6 2.9 %collective-permute-done.39.refs_7_ = bf16[480,640]{1,0:T(8,128)(2,1)} collective-permute-done((bf16[480,640]{1,0:T(8,128)(2,1)S(1)}, bf16[480,640]{1,0:T(8,128)(2,1)}, u32[]{:S(2)}, u32[]{:S(2)}) %collective-permute-start.39) | collective-permute-done | bytes 614432 | tf_op jit(solution)/shard_map/ppermute | solution.py:39
  206.6 1.6 collective-permute-done.40
  208.3 1.6 collective-permute-start.41
  209.9 6.5 %collective-permute-done.41.right_ref = bf16[96,1280]{1,0:T(8,128)(2,1)S(1)} collective-permute-done((bf16[96,1280]{1,0:T(8,128)(2,1)S(1)}, bf16[96,1280]{1,0:T(8,128)(2,1)S(1)}, u32[]{:S(2)}, u32[]{:S(2)}) %collective-permute-start.41) | collective-permute-done | bytes 245792 | tf_op jit(solution)/shard_map/ppermute | solution.py:35
  217.2 2.0 collective-permute-start.43
  219.2 5.4 %collective-permute-done.43.refs_2_ = bf16[96,1280]{1,0:T(8,128)(2,1)S(1)} collective-permute-done((bf16[96,1280]{1,0:T(8,128)(2,1)S(1)}, bf16[96,1280]{1,0:T(8,128)(2,1)S(1)}, u32[]{:S(2)}, u32[]{:S(2)}) %collective-permute-start.43) | collective-permute-done | bytes 245792 | tf_op jit(solution)/shard_map/ppermute | solution.py:43
  224.6 1.5 collective-permute-done.44.refs_3_
  227.2 7.3 %shard_map.151 = (bf16[96,1280]{1,0:T(8,128)(2,1)S(1)}, bf16[96,1280]{1,0:T(8,128)(2,1)S(1)}, bf16[96,1280]{1,0:T(8,128)(2,1)S(1)}, bf16[96,1280]{1,0:T(8,128)(2,1)S(1)}) custom-call(s32[25]{0:T(128)S(1)} %stack.110.spots_ref, bf16[96,1280]{1,0:T(8,128)(2,1)S(1)} %get-tuple-element.101.refs_0_, bf16[96,1280]{1,0:T(8,128)(2,1)S(1)} %collective-permute-done.42.refs_1_, ...), custom_call_target="tpu_custom_call" | custom-call | tf_op jit(solution)/shard_map/pallas_call | solution.py:147
  236.1 2.0 collective-permute-start.48
  238.1 6.3 %collective-permute-done.48 = bf16[96,1280]{1,0:T(8,128)(2,1)S(1)} collective-permute-done((bf16[96,1280]{1,0:T(8,128)(2,1)S(1)}, bf16[96,1280]{1,0:T(8,128)(2,1)S(1)}, u32[]{:S(2)}, u32[]{:S(2)}) %collective-permute-start.48) | collective-permute-done | bytes 245792 | tf_op jit(solution)/shard_map/ppermute | solution.py:43
  244.4 1.5 collective-permute-start.49
  246.7 5.2 %collective-permute-done.49 = bf16[96,1280]{1,0:T(8,128)(2,1)S(1)} collective-permute-done((bf16[96,1280]{1,0:T(8,128)(2,1)S(1)}, bf16[96,1280]{1,0:T(8,128)(2,1)S(1)}, u32[]{:S(2)}, u32[]{:S(2)}) %collective-permute-start.49) | collective-permute-done | bytes 245792 | tf_op jit(solution)/shard_map/ppermute | solution.py:35
  252.0 1.5 collective-permute-done.50
  (134 shorter events, 24.6 us)
Async XLA Ops:
  1.1 21.2 %collective-permute-start = (bf16[160,1280]{1,0:T(8,128)(2,1)S(1)}, bf16[160,1280]{1,0:T(8,128)(2,1)S(1)}, u32[]{:S(2)}, u32[]{:S(2)}) collective-permute-start(bf16[160,1280]{1,0:T(8,128)(2,1)S(1)} %pad_maximum_fusion.6.refs_1_), channel_id=1, source_target_pairs={{0,8},{1,9},{2,10},{3,11},{4,12},{5,13},{6,14},{7,15},{8,0},{9,1},... | collective-permute-start | bytes 1228808 | tf_op jit(solution)/shard_map/ppermute | solution.py:43
  4.2 20.7 %collective-permute-start.1 = (bf16[160,1280]{1,0:T(8,128)(2,1)S(1)}, bf16[160,1280]{1,0:T(8,128)(2,1)S(1)}, u32[]{:S(2)}, u32[]{:S(2)}) collective-permute-start(bf16[160,1280]{1,0:T(8,128)(2,1)S(1)} %pad_maximum_fusion.6.refs_1_), channel_id=1, source_target_pairs={{0,16},{1,17},{2,18},{3,19},{4,20},{5,21},{6,22},{7,23},{8,24},{9,... | collective-permute-start | bytes 1228808 | tf_op jit(solution)/shard_map/ppermute | solution.py:43
  6.8 18.1 %collective-permute-start.2 = (bf16[160,1280]{1,0:T(8,128)(2,1)S(1)}, bf16[160,1280]{1,0:T(8,128)(2,1)S(1)}, u32[]{:S(2)}, u32[]{:S(2)}) collective-permute-start(bf16[160,1280]{1,0:T(8,128)(2,1)S(1)} %pad_maximum_fusion.6.refs_1_), channel_id=1, source_target_pairs={{0,4},{1,5},{2,6},{3,7},{4,0},{5,1},{6,2},{7,3},{8,12},{9,13},{10,... | collective-permute-start | bytes 1228808 | tf_op jit(solution)/shard_map/ppermute | solution.py:39
  8.3 18.6 %copy-start.6 = (bf16[160,1280]{1,0:T(8,128)(2,1)S(1)}, bf16[160,1280]{1,0:T(8,128)(2,1)}, u32[]{:S(2)}) copy-start(bf16[160,1280]{1,0:T(8,128)(2,1)} %param.24) | copy-start | bytes 1228804
  8.3 18.6 %copy-start.7 = (bf16[160,1280]{1,0:T(8,128)(2,1)S(1)}, bf16[160,1280]{1,0:T(8,128)(2,1)}, u32[]{:S(2)}) copy-start(bf16[160,1280]{1,0:T(8,128)(2,1)} %param.23) | copy-start | bytes 1228804
  24.9 2.2 copy-start.4
  24.9 10.9 %collective-permute-start.3 = (bf16[160,1280]{1,0:T(8,128)(2,1)S(1)}, bf16[160,1280]{1,0:T(8,128)(2,1)}, u32[]{:S(2)}, u32[]{:S(2)}) collective-permute-start(bf16[160,1280]{1,0:T(8,128)(2,1)S(1)} %collective-permute-done.1.refs_3_), channel_id=1, source_target_pairs={{0,8},{1,9},{2,10},{3,11},{4,12},{5,13},{6,14},{7,15},{8,0},{9,1},... | collective-permute-start | bytes 1228808 | tf_op jit(solution)/shard_map/ppermute | solution.py:43
  25.4 21.2 %collective-permute-start.4 = (bf16[320,1280]{1,0:T(8,128)(2,1)S(1)}, bf16[320,1280]{1,0:T(8,128)(2,1)S(1)}, u32[]{:S(2)}, u32[]{:S(2)}) collective-permute-start(bf16[320,1280]{1,0:T(8,128)(2,1)S(1)} %pad_maximum_fusion.1), channel_id=1, source_target_pairs={{0,4},{1,5},{2,6},{3,7},{4,0},{5,1},{6,2},{7,3},{8,12},{9,13},{10,... | collective-permute-start | bytes 2457608 | tf_op jit(solution)/shard_map/ppermute | solution.py:39
  27.9 34.8 %collective-permute-start.8 = (bf16[160,1280]{1,0:T(8,128)(2,1)}, bf16[160,1280]{1,0:T(8,128)(2,1)}, u32[]{:S(2)}, u32[]{:S(2)}) collective-permute-start(bf16[160,1280]{1,0:T(8,128)(2,1)} %pad_maximum_fusion.7), channel_id=1, source_target_pairs={{0,24},{1,25},{2,26},{3,27},{4,28},{5,29},{6,30},{7,31},{8,16},{9,... | collective-permute-start | bytes 1228808 | tf_op jit(solution)/shard_map/ppermute | solution.py:43
  30.0 35.1 %collective-permute-start.14 = (bf16[160,1280]{1,0:T(8,128)(2,1)S(1)}, bf16[160,1280]{1,0:T(8,128)(2,1)}, u32[]{:S(2)}, u32[]{:S(2)}) collective-permute-start(bf16[160,1280]{1,0:T(8,128)(2,1)S(1)} %pad_maximum_fusion.8.refs_4_), channel_id=1, source_target_pairs={{0,16},{1,17},{2,18},{3,19},{4,20},{5,21},{6,22},{7,23},{8,24},{9,... | collective-permute-start | bytes 1228808 | tf_op jit(solution)/shard_map/ppermute | solution.py:43
  35.8 19.7 %collective-permute-start.5 = (bf16[160,1280]{1,0:T(8,128)(2,1)}, bf16[160,1280]{1,0:T(8,128)(2,1)}, u32[]{:S(2)}, u32[]{:S(2)}) collective-permute-start(bf16[160,1280]{1,0:T(8,128)(2,1)} %collective-permute-done.3.refs_4_), channel_id=1, source_target_pairs={{0,4},{1,5},{2,6},{3,7},{4,0},{5,1},{6,2},{7,3},{8,12},{9,13},{10,... | collective-permute-start | bytes 1228808 | tf_op jit(solution)/shard_map/ppermute | solution.py:39
  43.1 21.9 %collective-permute-start.13 = (bf16[160,1280]{1,0:T(8,128)(2,1)}, bf16[160,1280]{1,0:T(8,128)(2,1)}, u32[]{:S(2)}, u32[]{:S(2)}) collective-permute-start(bf16[160,1280]{1,0:T(8,128)(2,1)} %pad_maximum_fusion.7), channel_id=1, source_target_pairs={{0,8},{1,9},{2,10},{3,11},{4,12},{5,13},{6,14},{7,15},{8,0},{9,1},... | collective-permute-start | bytes 1228808 | tf_op jit(solution)/shard_map/ppermute | solution.py:43
  46.6 19.8 %collective-permute-start.15 = (bf16[160,1280]{1,0:T(8,128)(2,1)S(1)}, bf16[160,1280]{1,0:T(8,128)(2,1)}, u32[]{:S(2)}, u32[]{:S(2)}) collective-permute-start(bf16[160,1280]{1,0:T(8,128)(2,1)S(1)} %pad_maximum_fusion.8.refs_4_), channel_id=1, source_target_pairs={{0,4},{1,5},{2,6},{3,7},{4,0},{5,1},{6,2},{7,3},{8,12},{9,13},{10,... | collective-permute-start | bytes 1228808 | tf_op jit(solution)/shard_map/ppermute | solution.py:39
  56.5 6.1 %copy-start.8 = (bf16[160,1280]{1,0:T(8,128)(2,1)S(1)}, bf16[160,1280]{1,0:T(8,128)(2,1)}, u32[]{:S(2)}) copy-start(bf16[160,1280]{1,0:T(8,128)(2,1)} %param.25) | copy-start | bytes 1228804
  62.6 5.5 %collective-permute-start.6 = (bf16[128,1280]{1,0:T(8,128)(2,1)S(1)}, bf16[128,1280]{1,0:T(8,128)(2,1)S(1)}, u32[]{:S(2)}, u32[]{:S(2)}) collective-permute-start(bf16[128,1280]{1,0:T(8,128)(2,1)S(1)} %get-tuple-element.65), channel_id=1, source_target_pairs={{0,1},{1,0},{2,3},{3,2},{4,5},{5,4},{6,7},{7,6},{8,9},{9,8},{10,11... | collective-permute-start | bytes 983048 | tf_op jit(solution)/shard_map/ppermute | solution.py:31
  62.7 21.5 %collective-permute-start.9 = (bf16[160,1280]{1,0:T(8,128)(2,1)S(1)}, bf16[160,1280]{1,0:T(8,128)(2,1)S(1)}, u32[]{:S(2)}, u32[]{:S(2)}) collective-permute-start(bf16[160,1280]{1,0:T(8,128)(2,1)S(1)} %copy-done.8), channel_id=1, source_target_pairs={{0,16},{1,17},{2,18},{3,19},{4,20},{5,21},{6,22},{7,23},{8,24},{9,... | collective-permute-start | bytes 1228808 | tf_op jit(solution)/shard_map/ppermute | solution.py:43
  66.4 18.2 %copy-start.11 = (s32[64]{0:T(128)S(1)}, s32[64]{0:T(128)}, u32[]{:S(2)}) copy-start(s32[64]{0:T(128)} %param.18) | copy-start | bytes 772
  66.4 29.6 %collective-permute-start.16 = (bf16[480,1280]{1,0:T(8,128)(2,1)S(1)}, bf16[480,1280]{1,0:T(8,128)(2,1)S(1)}, u32[]{:S(2)}, u32[]{:S(2)}) collective-permute-start(bf16[480,1280]{1,0:T(8,128)(2,1)S(1)} %pad_maximum_fusion.refs_5_), channel_id=1, source_target_pairs={{0,4},{1,5},{2,6},{3,7},{4,0},{5,1},{6,2},{7,3},{8,12},{9,13},{10,... | collective-permute-start | bytes 3686408 | tf_op jit(solution)/shard_map/ppermute | solution.py:39
  68.1 9.6 %collective-permute-start.7 = (bf16[128,1280]{1,0:T(8,128)(2,1)S(1)}, bf16[128,1280]{1,0:T(8,128)(2,1)S(1)}, u32[]{:S(2)}, u32[]{:S(2)}) collective-permute-start(bf16[128,1280]{1,0:T(8,128)(2,1)S(1)} %add_convert_fusion.2.left_ref), channel_id=1, source_target_pairs={{0,2},{1,3},{2,0},{3,1},{4,6},{5,7},{6,4},{7,5},{8,10},{9,11},{10,... | collective-permute-start | bytes 983048 | tf_op jit(solution)/shard_map/ppermute | solution.py:35
  84.2 9.3 %collective-permute-start.11 = (bf16[128,1280]{1,0:T(8,128)(2,1)S(1)}, bf16[128,1280]{1,0:T(8,128)(2,1)S(1)}, u32[]{:S(2)}, u32[]{:S(2)}) collective-permute-start(bf16[128,1280]{1,0:T(8,128)(2,1)S(1)} %get-tuple-element.69.refs_0_), channel_id=1, source_target_pairs={{0,8},{1,9},{2,10},{3,11},{4,12},{5,13},{6,14},{7,15},{8,0},{9,1},... | collective-permute-start | bytes 983048 | tf_op jit(solution)/shard_map/ppermute | solution.py:43
  84.7 11.3 %collective-permute-start.10 = (bf16[128,1280]{1,0:T(8,128)(2,1)S(1)}, bf16[128,1280]{1,0:T(8,128)(2,1)S(1)}, u32[]{:S(2)}, u32[]{:S(2)}) collective-permute-start(bf16[128,1280]{1,0:T(8,128)(2,1)S(1)} %get-tuple-element.69.refs_0_), channel_id=1, source_target_pairs={{0,1},{1,0},{2,3},{3,2},{4,5},{5,4},{6,7},{7,6},{8,9},{9,8},{10,11... | collective-permute-start | bytes 983048 | tf_op jit(solution)/shard_map/ppermute | solution.py:31
  93.5 2.5 %collective-permute-start.12 = (bf16[128,1280]{1,0:T(8,128)(2,1)S(1)}, bf16[128,1280]{1,0:T(8,128)(2,1)S(1)}, u32[]{:S(2)}, u32[]{:S(2)}) collective-permute-start(bf16[128,1280]{1,0:T(8,128)(2,1)S(1)} %collective-permute-done.11.refs_2_), channel_id=1, source_target_pairs={{0,1},{1,0},{2,3},{3,2},{4,5},{5,4},{6,7},{7,6},{8,9},{9,8},{10,11... | collective-permute-start | bytes 983048 | tf_op jit(solution)/shard_map/ppermute | solution.py:31
  93.5 8.9 %copy-start.12 = (s32[64]{0:T(128)S(1)}, s32[64]{0:T(128)}, u32[]{:S(2)}) copy-start(s32[64]{0:T(128)} %param.19) | copy-start | bytes 772
  93.5 20.8 %collective-permute-start.19 = (bf16[320,1280]{1,0:T(8,128)(2,1)S(1)}, bf16[320,1280]{1,0:T(8,128)(2,1)}, u32[]{:S(2)}, u32[]{:S(2)}) collective-permute-start(bf16[320,1280]{1,0:T(8,128)(2,1)S(1)} %constant_dynamic-update-slice_fusion.refs_0_), channel_id=1, source_target_pairs={{0,8},{1,9},{2,10},{3,11},{4,12},{5,13},{6,14},{7,15},{8,0},{9,1},... | collective-permute-start | bytes 2457608 | tf_op jit(solution)/shard_map/ppermute | solution.py:43
  94.5 20.4 %collective-permute-start.20 = (bf16[320,1280]{1,0:T(8,128)(2,1)S(1)}, bf16[320,1280]{1,0:T(8,128)(2,1)S(1)}, u32[]{:S(2)}, u32[]{:S(2)}) collective-permute-start(bf16[320,1280]{1,0:T(8,128)(2,1)S(1)} %constant_dynamic-update-slice_fusion.refs_0_), channel_id=1, source_target_pairs={{0,4},{1,5},{2,6},{3,7},{4,0},{5,1},{6,2},{7,3},{8,12},{9,13},{10,... | collective-permute-start | bytes 2457608 | tf_op jit(solution)/shard_map/ppermute | solution.py:39
  102.3 2.0 collective-permute-start.18
  103.7 16.7 %collective-permute-start.17 = (bf16[128,1280]{1,0:T(8,128)(2,1)S(1)}, bf16[128,1280]{1,0:T(8,128)(2,1)S(1)}, u32[]{:S(2)}, u32[]{:S(2)}) collective-permute-start(bf16[128,1280]{1,0:T(8,128)(2,1)S(1)} %get-tuple-element.75), channel_id=1, source_target_pairs={{0,1},{1,0},{2,3},{3,2},{4,5},{5,4},{6,7},{7,6},{8,9},{9,8},{10,11... | collective-permute-start | bytes 983048 | tf_op jit(solution)/shard_map/ppermute | solution.py:31
  114.8 16.9 %copy-start = (bf16[320,1280]{1,0:T(8,128)(2,1)}, bf16[320,1280]{1,0:T(8,128)(2,1)S(1)}, u32[]{:S(2)}) copy-start(bf16[320,1280]{1,0:T(8,128)(2,1)S(1)} %collective-permute-done.20.refs_1_) | copy-start | bytes 2457604
  114.8 16.7 %collective-permute-start.21 = (bf16[128,1280]{1,0:T(8,128)(2,1)S(1)}, bf16[128,1280]{1,0:T(8,128)(2,1)S(1)}, u32[]{:S(2)}, u32[]{:S(2)}) collective-permute-start(bf16[128,1280]{1,0:T(8,128)(2,1)S(1)} %add_convert_fusion.1), channel_id=1, source_target_pairs={{0,8},{1,9},{2,10},{3,11},{4,12},{5,13},{6,14},{7,15},{8,0},{9,1},... | collective-permute-start | bytes 983048 | tf_op jit(solution)/shard_map/ppermute | solution.py:43
  116.2 21.0 %collective-permute-start.23 = (bf16[160,1280]{1,0:T(8,128)(2,1)S(1)}, bf16[160,1280]{1,0:T(8,128)(2,1)S(1)}, u32[]{:S(2)}, u32[]{:S(2)}) collective-permute-start(bf16[160,1280]{1,0:T(8,128)(2,1)S(1)} %pad_maximum_fusion.9), channel_id=1, source_target_pairs={{0,16},{1,17},{2,18},{3,19},{4,20},{5,21},{6,22},{7,23},{8,24},{9,... | collective-permute-start | bytes 1228808 | tf_op jit(solution)/shard_map/ppermute | solution.py:43
  118.9 20.1 %collective-permute-start.24 = (bf16[320,1280]{1,0:T(8,128)(2,1)}, bf16[320,1280]{1,0:T(8,128)(2,1)S(1)}, u32[]{:S(2)}, u32[]{:S(2)}) collective-permute-start(bf16[320,1280]{1,0:T(8,128)(2,1)} %collective-permute-done.19.refs_2_), channel_id=1, source_target_pairs={{0,4},{1,5},{2,6},{3,7},{4,0},{5,1},{6,2},{7,3},{8,12},{9,13},{10,... | collective-permute-start | bytes 2457608 | tf_op jit(solution)/shard_map/ppermute | solution.py:39
  131.7 5.4 %collective-permute-start.22 = (bf16[64,1280]{1,0:T(8,128)(2,1)S(1)}, bf16[64,1280]{1,0:T(8,128)(2,1)S(1)}, u32[]{:S(2)}, u32[]{:S(2)}) collective-permute-start(bf16[64,1280]{1,0:T(8,128)(2,1)S(1)} %dynamic-slice_bitcast_fusion), channel_id=1, source_target_pairs={{0,2},{1,3},{2,0},{3,1},{4,6},{5,7},{6,4},{7,5},{8,10},{9,11},{10,... | collective-permute-start | bytes 491528 | tf_op jit(solution)/shard_map/ppermute | solution.py:35
  133.3 5.7 %copy-start.1 = (bf16[320,1280]{1,0:T(8,128)(2,1)S(1)}, bf16[320,1280]{1,0:T(8,128)(2,1)}, u32[]{:S(2)}) copy-start(bf16[320,1280]{1,0:T(8,128)(2,1)} %copy-done) | copy-start | bytes 2457604
  137.2 18.1 %collective-permute-start.27 = (bf16[320,1280]{1,0:T(8,128)(2,1)S(1)}, bf16[320,1280]{1,0:T(8,128)(2,1)}, u32[]{:S(2)}, u32[]{:S(2)}) collective-permute-start(bf16[320,1280]{1,0:T(8,128)(2,1)S(1)} %constant_dynamic-update-slice_fusion.2.refs_0_), channel_id=1, source_target_pairs={{0,8},{1,9},{2,10},{3,11},{4,12},{5,13},{6,14},{7,15},{8,0},{9,1},... | collective-permute-start | bytes 2457608 | tf_op jit(solution)/shard_map/ppermute | solution.py:43
  137.4 18.6 %collective-permute-start.28 = (bf16[320,1280]{1,0:T(8,128)(2,1)S(1)}, bf16[320,1280]{1,0:T(8,128)(2,1)}, u32[]{:S(2)}, u32[]{:S(2)}) collective-permute-start(bf16[320,1280]{1,0:T(8,128)(2,1)S(1)} %constant_dynamic-update-slice_fusion.2.refs_0_), channel_id=1, source_target_pairs={{0,4},{1,5},{2,6},{3,7},{4,0},{5,1},{6,2},{7,3},{8,12},{9,13},{10,... | collective-permute-start | bytes 2457608 | tf_op jit(solution)/shard_map/ppermute | solution.py:39
  142.7 25.0 %copy-start.9 = (bf16[160,1280]{1,0:T(8,128)(2,1)S(1)}, bf16[160,1280]{1,0:T(8,128)(2,1)}, u32[]{:S(2)}) copy-start(bf16[160,1280]{1,0:T(8,128)(2,1)} %param.28) | copy-start | bytes 1228804
  142.7 1.4 collective-permute-start.25
  144.2 4.9 %collective-permute-start.26 = (bf16[64,640]{1,0:T(8,128)(2,1)S(1)}, bf16[64,640]{1,0:T(8,128)(2,1)S(1)}, u32[]{:S(2)}, u32[]{:S(2)}) collective-permute-start(bf16[64,640]{1,0:T(8,128)(2,1)S(1)} %add_convert_fusion.8), channel_id=1, source_target_pairs={{0,2},{1,3},{2,0},{3,1},{4,6},{5,7},{6,4},{7,5},{8,10},{9,11},{10,... | collective-permute-start | bytes 245768 | tf_op jit(solution)/shard_map/ppermute | solution.py:35
  156.1 5.5 %collective-permute-start.29 = (bf16[4,1,16,768]{3,2,0,1:T(8,128)(2,1)S(1)}, bf16[4,1,16,768]{3,2,0,1:T(8,128)(2,1)S(1)}, u32[]{:S(2)}, u32[]{:S(2)}) collective-permute-start(bf16[4,1,16,768]{3,2,0,1:T(8,128)(2,1)S(1)} %dynamic-slice_bitcast_fusion.1), channel_id=1, source_target_pairs={{0,4},{1,5},{2,6},{3,7},{4,0},{5,1},{6,2},{7,3},{8,12},{9,13},{10,... | collective-permute-start | bytes 294920 | tf_op jit(solution)/shard_map/ppermute | solution.py:39
  157.7 23.0 %copy-start.10 = (bf16[160,1280]{1,0:T(8,128)(2,1)S(1)}, bf16[160,1280]{1,0:T(8,128)(2,1)}, u32[]{:S(2)}) copy-start(bf16[160,1280]{1,0:T(8,128)(2,1)} %param.29) | copy-start | bytes 1228804
  161.6 18.9 %collective-permute-start.33 = (bf16[320,1280]{1,0:T(8,128)(2,1)}, bf16[320,1280]{1,0:T(8,128)(2,1)S(1)}, u32[]{:S(2)}, u32[]{:S(2)}) collective-permute-start(bf16[320,1280]{1,0:T(8,128)(2,1)} %collective-permute-done.27.refs_2_), channel_id=1, source_target_pairs={{0,4},{1,5},{2,6},{3,7},{4,0},{5,1},{6,2},{7,3},{8,12},{9,13},{10,... | collective-permute-start | bytes 2457608 | tf_op jit(solution)/shard_map/ppermute | solution.py:39
  163.2 8.1 %collective-permute-start.32 = (bf16[2,1,16,768]{3,2,0,1:T(8,128)(2,1)S(1)}, bf16[2,1,16,768]{3,2,0,1:T(8,128)(2,1)S(1)}, u32[]{:S(2)}, u32[]{:S(2)}) collective-permute-start(bf16[2,1,16,768]{3,2,0,1:T(8,128)(2,1)S(1)} %get-tuple-element.124), channel_id=1, source_target_pairs={{0,24},{1,25},{2,26},{3,27},{4,28},{5,29},{6,30},{7,31},{8,16},{9,... | collective-permute-start | bytes 147464 | tf_op jit(solution)/shard_map/ppermute | solution.py:43
  166.2 6.8 %collective-permute-start.31 = (bf16[2,1,16,768]{3,2,0,1:T(8,128)(2,1)S(1)}, bf16[2,1,16,768]{3,2,0,1:T(8,128)(2,1)S(1)}, u32[]{:S(2)}, u32[]{:S(2)}) collective-permute-start(bf16[2,1,16,768]{3,2,0,1:T(8,128)(2,1)S(1)} %get-tuple-element.125), channel_id=1, source_target_pairs={{0,16},{1,17},{2,18},{3,19},{4,20},{5,21},{6,22},{7,23},{8,24},{9,... | collective-permute-start | bytes 147464 | tf_op jit(solution)/shard_map/ppermute | solution.py:43
  166.7 6.9 %collective-permute-start.30 = (bf16[2,1,16,768]{3,2,0,1:T(8,128)(2,1)S(1)}, bf16[2,1,16,768]{3,2,0,1:T(8,128)(2,1)S(1)}, u32[]{:S(2)}, u32[]{:S(2)}) collective-permute-start(bf16[2,1,16,768]{3,2,0,1:T(8,128)(2,1)S(1)} %get-tuple-element.126), channel_id=1, source_target_pairs={{0,8},{1,9},{2,10},{3,11},{4,12},{5,13},{6,14},{7,15},{8,0},{9,1},... | collective-permute-start | bytes 147464 | tf_op jit(solution)/shard_map/ppermute | solution.py:43
  168.4 19.1 %collective-permute-start.37 = (bf16[160,640]{1,0:T(8,128)(2,1)}, bf16[160,640]{1,0:T(8,128)(2,1)}, u32[]{:S(2)}, u32[]{:S(2)}) collective-permute-start(bf16[160,640]{1,0:T(8,128)(2,1)} %get-tuple-element.117), channel_id=1, source_target_pairs={{0,24},{1,25},{2,26},{3,27},{4,28},{5,29},{6,30},{7,31},{8,16},{9,... | collective-permute-start | bytes 614408 | tf_op jit(solution)/shard_map/ppermute | solution.py:43
  171.3 23.7 %collective-permute-start.35 = (bf16[160,640]{1,0:T(8,128)(2,1)}, bf16[160,640]{1,0:T(8,128)(2,1)}, u32[]{:S(2)}, u32[]{:S(2)}) collective-permute-start(bf16[160,640]{1,0:T(8,128)(2,1)} %get-tuple-element.117), channel_id=1, source_target_pairs={{0,8},{1,9},{2,10},{3,11},{4,12},{5,13},{6,14},{7,15},{8,0},{9,1},... | collective-permute-start | bytes 614408 | tf_op jit(solution)/shard_map/ppermute | solution.py:43
  172.9 22.1 %collective-permute-start.36 = (bf16[160,640]{1,0:T(8,128)(2,1)S(1)}, bf16[160,640]{1,0:T(8,128)(2,1)}, u32[]{:S(2)}, u32[]{:S(2)}) collective-permute-start(bf16[160,640]{1,0:T(8,128)(2,1)S(1)} %get-tuple-element.102.refs_4_), channel_id=1, source_target_pairs={{0,16},{1,17},{2,18},{3,19},{4,20},{5,21},{6,22},{7,23},{8,24},{9,... | collective-permute-start | bytes 614408 | tf_op jit(solution)/shard_map/ppermute | solution.py:43
  173.6 22.6 %collective-permute-start.38 = (bf16[160,640]{1,0:T(8,128)(2,1)S(1)}, bf16[160,640]{1,0:T(8,128)(2,1)S(1)}, u32[]{:S(2)}, u32[]{:S(2)}) collective-permute-start(bf16[160,640]{1,0:T(8,128)(2,1)S(1)} %get-tuple-element.102.refs_4_), channel_id=1, source_target_pairs={{0,4},{1,5},{2,6},{3,7},{4,0},{5,1},{6,2},{7,3},{8,12},{9,13},{10,... | collective-permute-start | bytes 614408 | tf_op jit(solution)/shard_map/ppermute | solution.py:39
  180.5 1.3 copy-start.2
  181.8 24.7 %all-to-all-start = ((bf16[4,160,640]{2,1,0:T(8,128)(2,1)}), bf16[4,160,640]{2,1,0:T(8,128)(2,1)S(1)}, u32[]{:S(2)}, u32[]{:S(2)}) async-start(bf16[4,160,640]{2,1,0:T(8,128)(2,1)} %pad_maximum_fusion.2), calls=%async_computation | async-start | bytes 1638400 | tf_op jit(solution)/shard_map/all_to_all | solution.py:92
  187.4 8.9 %collective-permute-start.34 = (bf16[192,640]{1,0:T(8,128)(2,1)S(1)}, bf16[192,640]{1,0:T(8,128)(2,1)S(1)}, u32[]{:S(2)}, u32[]{:S(2)}) collective-permute-start(bf16[192,640]{1,0:T(8,128)(2,1)S(1)} %fusion), channel_id=1, source_target_pairs={{0,1},{1,0},{2,3},{3,2},{4,5},{5,4},{6,7},{7,6},{8,9},{9,8},{10,11... | collective-permute-start | bytes 737288 | tf_op jit(solution)/shard_map/ppermute | solution.py:31
  196.2 10.3 %collective-permute-start.39 = (bf16[480,640]{1,0:T(8,128)(2,1)S(1)}, bf16[480,640]{1,0:T(8,128)(2,1)}, u32[]{:S(2)}, u32[]{:S(2)}) collective-permute-start(bf16[480,640]{1,0:T(8,128)(2,1)S(1)} %pad_maximum_fusion.3.refs_5_), channel_id=1, source_target_pairs={{0,4},{1,5},{2,6},{3,7},{4,0},{5,1},{6,2},{7,3},{8,12},{9,13},{10,... | collective-permute-start | bytes 1843208 | tf_op jit(solution)/shard_map/ppermute | solution.py:39
  196.4 1.1 copy-start.3
  206.5 1.7 collective-permute-start.40
  206.5 20.7 %collective-permute-start.45 = (bf16[640,640]{1,0:T(8,128)(2,1)S(1)}, bf16[640,640]{1,0:T(8,128)(2,1)S(1)}, u32[]{:S(2)}, u32[]{:S(2)}) collective-permute-start(bf16[640,640]{1,0:T(8,128)(2,1)S(1)} %bitcast.61), channel_id=1, source_target_pairs={{0,4},{1,5},{2,6},{3,7},{4,0},{5,1},{6,2},{7,3},{8,12},{9,13},{10,... | collective-permute-start | bytes 2457608 | tf_op jit(solution)/shard_map/ppermute | solution.py:39
  208.3 8.1 %collective-permute-start.41 = (bf16[96,1280]{1,0:T(8,128)(2,1)S(1)}, bf16[96,1280]{1,0:T(8,128)(2,1)S(1)}, u32[]{:S(2)}, u32[]{:S(2)}) collective-permute-start(bf16[96,1280]{1,0:T(8,128)(2,1)S(1)} %add_convert_fusion.6.left_ref), channel_id=1, source_target_pairs={{0,2},{1,3},{2,0},{3,1},{4,6},{5,7},{6,4},{7,5},{8,10},{9,11},{10,... | collective-permute-start | bytes 737288 | tf_op jit(solution)/shard_map/ppermute | solution.py:35
  217.2 7.4 %collective-permute-start.43 = (bf16[96,1280]{1,0:T(8,128)(2,1)S(1)}, bf16[96,1280]{1,0:T(8,128)(2,1)S(1)}, u32[]{:S(2)}, u32[]{:S(2)}) collective-permute-start(bf16[96,1280]{1,0:T(8,128)(2,1)S(1)} %get-tuple-element.101.refs_0_), channel_id=1, source_target_pairs={{0,8},{1,9},{2,10},{3,11},{4,12},{5,13},{6,14},{7,15},{8,0},{9,1},... | collective-permute-start | bytes 737288 | tf_op jit(solution)/shard_map/ppermute | solution.py:43
  219.2 5.4 %collective-permute-start.42 = (bf16[96,1280]{1,0:T(8,128)(2,1)S(1)}, bf16[96,1280]{1,0:T(8,128)(2,1)S(1)}, u32[]{:S(2)}, u32[]{:S(2)}) collective-permute-start(bf16[96,1280]{1,0:T(8,128)(2,1)S(1)} %get-tuple-element.101.refs_0_), channel_id=1, source_target_pairs={{0,1},{1,0},{2,3},{3,2},{4,5},{5,4},{6,7},{7,6},{8,9},{9,8},{10,11... | collective-permute-start | bytes 737288 | tf_op jit(solution)/shard_map/ppermute | solution.py:31
  224.6 1.5 collective-permute-start.44
  234.5 1.6 collective-permute-start.47
  234.5 3.5 %collective-permute-start.46 = (bf16[96,1280]{1,0:T(8,128)(2,1)S(1)}, bf16[96,1280]{1,0:T(8,128)(2,1)S(1)}, u32[]{:S(2)}, u32[]{:S(2)}) collective-permute-start(bf16[96,1280]{1,0:T(8,128)(2,1)S(1)} %get-tuple-element.108), channel_id=1, source_target_pairs={{0,1},{1,0},{2,3},{3,2},{4,5},{5,4},{6,7},{7,6},{8,9},{9,8},{10,11... | collective-permute-start | bytes 737288 | tf_op jit(solution)/shard_map/ppermute | solution.py:31
  236.1 8.2 %collective-permute-start.48 = (bf16[96,1280]{1,0:T(8,128)(2,1)S(1)}, bf16[96,1280]{1,0:T(8,128)(2,1)S(1)}, u32[]{:S(2)}, u32[]{:S(2)}) collective-permute-start(bf16[96,1280]{1,0:T(8,128)(2,1)S(1)} %add_convert_fusion.5), channel_id=1, source_target_pairs={{0,8},{1,9},{2,10},{3,11},{4,12},{5,13},{6,14},{7,15},{8,0},{9,1},... | collective-permute-start | bytes 737288 | tf_op jit(solution)/shard_map/ppermute | solution.py:43
  244.4 7.4 %collective-permute-start.49 = (bf16[96,1280]{1,0:T(8,128)(2,1)S(1)}, bf16[96,1280]{1,0:T(8,128)(2,1)S(1)}, u32[]{:S(2)}, u32[]{:S(2)}) collective-permute-start(bf16[96,1280]{1,0:T(8,128)(2,1)S(1)} %add_convert_fusion.4), channel_id=1, source_target_pairs={{0,2},{1,3},{2,0},{3,1},{4,6},{5,7},{6,4},{7,5},{8,10},{9,11},{10,... | collective-permute-start | bytes 737288 | tf_op jit(solution)/shard_map/ppermute | solution.py:35
  252.0 1.6 collective-permute-start.50
  (1 other events, 1.0 us)

commit v7 on v6

--- a/solution.py
+++ b/solution.py
@@ -256,10 +256,12 @@
             up, down = scratch[0][:, :units], scratch[0][:, units:]
         else:
             up, down = scratch[0][...], scratch[1][...]
-        for source, target in zip(source_refs, targets):
-            hidden = jnp.dot(source[...], up, preferred_element_type=jnp.float32)
-            hidden = 0.5 * hidden * (1.0 + lax.erf(hidden * 0.5**0.5))
-            target[...] = dot_t(hidden.astype(jnp.bfloat16), down).astype(jnp.bfloat16)
+        hidden = jnp.concatenate([source[...] for source in source_refs], axis=0)
+        hidden = jnp.dot(hidden, up, preferred_element_type=jnp.float32)
+        hidden = 0.5 * hidden * (1.0 + lax.erf(hidden * 0.5**0.5))
+        result = dot_t(hidden.astype(jnp.bfloat16), down).astype(jnp.bfloat16)
+        for at, target in enumerate(targets):
+            target[...] = result[at * half : (at + 1) * half]
 
     return local_call(
         kernel,
@@ -392,8 +394,8 @@
     keep, send = attention(spots, DIRECT, rows, allowed, enc_attn, qkv_width)
     mine = add_short(keep, swap_core(send)).astype(jnp.bfloat16)
     mid, normed = middle(spots, rows, mine, swap_x(mine))
-    normed, merge_second = together(normed, merge_second)
     normed_pair = swap_z(normed, 1)
+    normed_pair, merge_second = together(normed_pair, merge_second)
     sources = [normed, swap_core(normed), normed_pair, swap_core(normed_pair)]
     merge_two = jnp.concatenate([merge_t, merge_second], axis=0)
     merge_pair = swap_z(merge_two, 1)

time: 255 us -> 253 us (level)
  waiting for transfers between devices: 134 us -> 131 us
  starting transfers between devices: 65.2 us -> 68 us
  transfers between devices with their start and end apart: 52 -> 52, of which waited for: 30 -> 32; matrix products, arithmetic and copies ran while one was open for 7% -> 7% of each run, Pallas kernels for 9% -> 9%
where the time goes in v7:
time: 253 us
  waiting for transfers between devices  131 us (52%)
  starting transfers between devices  68 us (27%)
  Pallas kernels  29 us (11%)
  other arithmetic  12.9 us (5%)
  local copies, waits for them, and re-layouts  8.83 us (3%)
    ppermute x20, waiting for transfers between devices, swap_z(): return lax.ppermute(part, AXES, routes(lambda z, y, x, c: (z ^ k, y, x, c)))  82.9 us
    ppermute x20, starting transfers between devices, swap_z(): return lax.ppermute(part, AXES, routes(lambda z, y, x, c: (z ^ k, y, x, c)))  30.8 us
    pallas_call x7, Pallas kernels, local_call(): pl.pallas_call(kernel, in_specs=in_specs, out_specs=[VMEM] * len(outs), o...  29 us
    ppermute x5, waiting for transfers between devices, swap_x(): return lax.ppermute(part, AXES, routes(lambda z, y, x, c: (z, y, 1 - x, c)))  24.5 us
    ppermute x13, starting transfers between devices, swap_y(): return lax.ppermute(part, AXES, routes(lambda z, y, x, c: (z, 1 - y, x, c)))  23.9 us
    ppermute x13, waiting for transfers between devices, swap_y(): return lax.ppermute(part, AXES, routes(lambda z, y, x, c: (z, 1 - y, x, c)))  18.7 us
    ppermute x5, starting transfers between devices, swap_x(): return lax.ppermute(part, AXES, routes(lambda z, y, x, c: (z, y, 1 - x, c)))  7.77 us
  transfers between devices with their start and end apart: 52, of which 32 were waited for; matrix products, arithmetic and copies ran while one was open for 7% of the time, Pallas kernels for 9%

profile of v7, /device:TPU:0, one launch (start us, length us, event | category | flops | bytes accessed | tf_op | source)
XLA Modules:
  0.0 252.5 jit_solution(17740992093670415627)
XLA Ops:
  0.0 1.1 pad_maximum_fusion.6.refs_1_
  1.1 3.1 %collective-permute-start = (bf16[160,1280]{1,0:T(8,128)(2,1)S(1)}, bf16[160,1280]{1,0:T(8,128)(2,1)S(1)}, u32[]{:S(2)}, u32[]{:S(2)}) collective-permute-start(bf16[160,1280]{1,0:T(8,128)(2,1)S(1)} %pad_maximum_fusion.6.refs_1_), channel_id=1, source_target_pairs={{0,8},{1,9},{2,10},{3,11},{4,12},{5,13},{6,14},{7,15},{8,0},{9,1},... | collective-permute-start | bytes 1228808 | tf_op jit(solution)/shard_map/ppermute | solution.py:43
  4.2 2.6 %collective-permute-start.1 = (bf16[160,1280]{1,0:T(8,128)(2,1)S(1)}, bf16[160,1280]{1,0:T(8,128)(2,1)S(1)}, u32[]{:S(2)}, u32[]{:S(2)}) collective-permute-start(bf16[160,1280]{1,0:T(8,128)(2,1)S(1)} %pad_maximum_fusion.6.refs_1_), channel_id=1, source_target_pairs={{0,16},{1,17},{2,18},{3,19},{4,20},{5,21},{6,22},{7,23},{8,24},{9,... | collective-permute-start | bytes 1228808 | tf_op jit(solution)/shard_map/ppermute | solution.py:43
  6.8 1.5 collective-permute-start.2
  8.4 1.4 fusion.25
  9.7 12.6 %collective-permute-done.refs_2_ = bf16[160,1280]{1,0:T(8,128)(2,1)S(1)} collective-permute-done((bf16[160,1280]{1,0:T(8,128)(2,1)S(1)}, bf16[160,1280]{1,0:T(8,128)(2,1)S(1)}, u32[]{:S(2)}, u32[]{:S(2)}) %collective-permute-start) | collective-permute-done | bytes 409632 | tf_op jit(solution)/shard_map/ppermute | solution.py:43
  22.4 2.5 collective-permute-done.1.refs_3_
  25.4 1.6 collective-permute-start.4
  27.9 2.1 collective-permute-start.10
  31.0 4.8 %collective-permute-done.3.refs_4_ = bf16[160,1280]{1,0:T(8,128)(2,1)} collective-permute-done((bf16[160,1280]{1,0:T(8,128)(2,1)S(1)}, bf16[160,1280]{1,0:T(8,128)(2,1)}, u32[]{:S(2)}, u32[]{:S(2)}) %collective-permute-start.3) | collective-permute-done | bytes 409632 | tf_op jit(solution)/shard_map/ppermute | solution.py:43
  35.8 7.3 %collective-permute-start.5 = (bf16[160,1280]{1,0:T(8,128)(2,1)}, bf16[160,1280]{1,0:T(8,128)(2,1)}, u32[]{:S(2)}, u32[]{:S(2)}) collective-permute-start(bf16[160,1280]{1,0:T(8,128)(2,1)} %collective-permute-done.3.refs_4_), channel_id=1, source_target_pairs={{0,4},{1,5},{2,6},{3,7},{4,0},{5,1},{6,2},{7,3},{8,12},{9,13},{10,... | collective-permute-start | bytes 1228808 | tf_op jit(solution)/shard_map/ppermute | solution.py:39
  43.2 1.3 compare_and_fusion
  44.7 2.0 collective-permute-done.4.refs_6_
  46.6 1.5 collective-permute-start.15
  48.3 2.7 %reshape.162 = bf16[1,8,2,8,2,1280]{5,4,3,2,1,0:T(2,128)(2,1)} reshape(bf16[256,1280]{1,0:T(8,128)(2,1)} %param.15) | data formatting | bytes 1310720 | tf_op jit(solution)/shard_map/reshape | solution.py:388
  51.0 1.2 copy.30
  52.2 3.3 %collective-permute-done.5.refs_7_ = bf16[160,1280]{1,0:T(8,128)(2,1)} collective-permute-done((bf16[160,1280]{1,0:T(8,128)(2,1)}, bf16[160,1280]{1,0:T(8,128)(2,1)}, u32[]{:S(2)}, u32[]{:S(2)}) %collective-permute-start.5) | collective-permute-done | bytes 409632 | tf_op jit(solution)/shard_map/ppermute | solution.py:39
  56.5 6.0 %shard_map.145 = (bf16[128,1280]{1,0:T(8,128)(2,1)S(1)}, bf16[128,1280]{1,0:T(8,128)(2,1)S(1)}) custom-call(s32[25]{0:T(128)S(1)} %stack.110.spots_ref, bf16[256,1280]{1,0:T(8,128)(2,1)S(1)} %bitcast.59, f32[256,256]{1,0:T(8,128)S(1)} %and_convert_fusion.refs_0_, bf16[160,1280]{1,0:T(8,128)(2,1)S(1)} %pad_maximum_fusion.6.refs_1_, ...), custom_call_target="tpu_custom_call" | custom-call | tf_op jit(solution)/shard_map/pallas_call | solution.py:147
  62.7 1.3 collective-permute-done.14
  64.0 1.3 pad_maximum_fusion.refs_5_
  66.3 1.6 collective-permute-start.7
  67.8 1.8 collective-permute-start.11
  69.6 5.9 %collective-permute-done.7.right_ref = bf16[128,1280]{1,0:T(8,128)(2,1)S(1)} collective-permute-done((bf16[128,1280]{1,0:T(8,128)(2,1)S(1)}, bf16[128,1280]{1,0:T(8,128)(2,1)S(1)}, u32[]{:S(2)}, u32[]{:S(2)}) %collective-permute-start.7) | collective-permute-done | bytes 327712 | tf_op jit(solution)/shard_map/ppermute | solution.py:35
  76.5 1.6 collective-permute-start.9
  78.3 10.1 %collective-permute-done.11 = bf16[160,1280]{1,0:T(8,128)(2,1)S(1)} collective-permute-done((bf16[160,1280]{1,0:T(8,128)(2,1)S(1)}, bf16[160,1280]{1,0:T(8,128)(2,1)S(1)}, u32[]{:S(2)}, u32[]{:S(2)}) %collective-permute-start.11) | collective-permute-done | bytes 409632 | tf_op jit(solution)/shard_map/ppermute | solution.py:43
  88.3 4.7 %collective-permute-done.9.refs_2_ = bf16[128,1280]{1,0:T(8,128)(2,1)S(1)} collective-permute-done((bf16[128,1280]{1,0:T(8,128)(2,1)S(1)}, bf16[128,1280]{1,0:T(8,128)(2,1)S(1)}, u32[]{:S(2)}, u32[]{:S(2)}) %collective-permute-start.9) | collective-permute-done | bytes 327712 | tf_op jit(solution)/shard_map/ppermute | solution.py:43
  94.6 5.5 %shard_map.147 = (bf16[128,1280]{1,0:T(8,128)(2,1)S(1)}, bf16[128,1280]{1,0:T(8,128)(2,1)S(1)}, bf16[128,1280]{1,0:T(8,128)(2,1)S(1)}, bf16[128,1280]{1,0:T(8,128)(2,1)}) custom-call(s32[25]{0:T(128)S(1)} %stack.110.spots_ref, bf16[128,1280]{1,0:T(8,128)(2,1)S(1)} %get-tuple-element.67.refs_0_, bf16[128,1280]{1,0:T(8,128)(2,1)S(1)} %collective-permute-done.8.refs_1_, ...), custom_call_target="tpu_custom_call" | custom-call | tf_op jit(solution)/shard_map/pallas_call | solution.py:147
  100.5 1.1 pad_maximum_fusion.9
  103.3 10.6 %collective-permute-done.19.refs_2_ = bf16[320,1280]{1,0:T(8,128)(2,1)} collective-permute-done((bf16[320,1280]{1,0:T(8,128)(2,1)S(1)}, bf16[320,1280]{1,0:T(8,128)(2,1)}, u32[]{:S(2)}, u32[]{:S(2)}) %collective-permute-start.19) | collective-permute-done | bytes 819232 | tf_op jit(solution)/shard_map/ppermute | solution.py:43
  113.9 1.6 collective-permute-start.21
  115.7 3.5 %collective-permute-start.23 = (bf16[160,1280]{1,0:T(8,128)(2,1)S(1)}, bf16[160,1280]{1,0:T(8,128)(2,1)S(1)}, u32[]{:S(2)}, u32[]{:S(2)}) collective-permute-start(bf16[160,1280]{1,0:T(8,128)(2,1)S(1)} %pad_maximum_fusion.9), channel_id=1, source_target_pairs={{0,16},{1,17},{2,18},{3,19},{4,20},{5,21},{6,22},{7,23},{8,24},{9,... | collective-permute-start | bytes 1228808 | tf_op jit(solution)/shard_map/ppermute | solution.py:43
  119.8 11.1 %collective-permute-done.21 = bf16[128,1280]{1,0:T(8,128)(2,1)S(1)} collective-permute-done((bf16[128,1280]{1,0:T(8,128)(2,1)S(1)}, bf16[128,1280]{1,0:T(8,128)(2,1)S(1)}, u32[]{:S(2)}, u32[]{:S(2)}) %collective-permute-start.21) | collective-permute-done | bytes 327712 | tf_op jit(solution)/shard_map/ppermute | solution.py:43
  131.0 1.6 collective-permute-start.22
  132.6 3.8 %collective-permute-done.22 = bf16[64,1280]{1,0:T(8,128)(2,1)S(1)} collective-permute-done((bf16[64,1280]{1,0:T(8,128)(2,1)S(1)}, bf16[64,1280]{1,0:T(8,128)(2,1)S(1)}, u32[]{:S(2)}, u32[]{:S(2)}) %collective-permute-start.22) | collective-permute-done | bytes 163872 | tf_op jit(solution)/shard_map/ppermute | solution.py:35
  138.8 3.7 %shard_map.148 = (bf16[64,640]{1,0:T(8,128)(2,1)S(1)}, bf16[64,640]{1,0:T(8,128)(2,1)S(1)}) custom-call(s32[25]{0:T(128)S(1)} %stack.110.spots_ref, bf16[64,1280]{1,0:T(8,128)(2,1)S(1)} %fusion.2.blocks_ref, bf16[320,1280]{1,0:T(8,128)(2,1)S(1)} %constant_dynamic-update-slice_fusion.refs_0_, bf16[320,1280]{1,0:T(8,128)(2,1)S(1)} %copy-done.1, ...), custom_call_target="tpu_custom_call" | custom-call | tf_op jit(solution)/shard_map/pallas_call | solution.py:147
  142.6 1.4 fusion.19
  144.0 1.6 collective-permute-start.26
  145.7 3.2 %collective-permute-done.26 = bf16[64,640]{1,0:T(8,128)(2,1)S(1)} collective-permute-done((bf16[64,640]{1,0:T(8,128)(2,1)S(1)}, bf16[64,640]{1,0:T(8,128)(2,1)S(1)}, u32[]{:S(2)}, u32[]{:S(2)}) %collective-permute-start.26) | collective-permute-done | bytes 81952 | tf_op jit(solution)/shard_map/ppermute | solution.py:35
  149.1 7.4 %collective-permute-done.27.refs_2_ = bf16[320,1280]{1,0:T(8,128)(2,1)} collective-permute-done((bf16[320,1280]{1,0:T(8,128)(2,1)S(1)}, bf16[320,1280]{1,0:T(8,128)(2,1)}, u32[]{:S(2)}, u32[]{:S(2)}) %collective-permute-start.27) | collective-permute-done | bytes 819232 | tf_op jit(solution)/shard_map/ppermute | solution.py:43
  157.2 4.4 %collective-permute-done.29 = bf16[4,1,16,768]{3,2,0,1:T(8,128)(2,1)S(1)} collective-permute-done((bf16[4,1,16,768]{3,2,0,1:T(8,128)(2,1)S(1)}, bf16[4,1,16,768]{3,2,0,1:T(8,128)(2,1)S(1)}, u32[]{:S(2)}, u32[]{:S(2)}) %collective-permute-start.29) | collective-permute-done | bytes 98336 | tf_op jit(solution)/shard_map/ppermute | solution.py:39
  162.2 3.3 %collective-permute-start.32 = (bf16[2,1,16,768]{3,2,0,1:T(8,128)(2,1)S(1)}, bf16[2,1,16,768]{3,2,0,1:T(8,128)(2,1)S(1)}, u32[]{:S(2)}, u32[]{:S(2)}) collective-permute-start(bf16[2,1,16,768]{3,2,0,1:T(8,128)(2,1)S(1)} %get-tuple-element.124), channel_id=1, source_target_pairs={{0,24},{1,25},{2,26},{3,27},{4,28},{5,29},{6,30},{7,31},{8,16},{9,... | collective-permute-start | bytes 147464 | tf_op jit(solution)/shard_map/ppermute | solution.py:43
  167.4 3.2 %collective-permute-start.37 = (bf16[160,640]{1,0:T(8,128)(2,1)}, bf16[160,640]{1,0:T(8,128)(2,1)}, u32[]{:S(2)}, u32[]{:S(2)}) collective-permute-start(bf16[160,640]{1,0:T(8,128)(2,1)} %get-tuple-element.117), channel_id=1, source_target_pairs={{0,24},{1,25},{2,26},{3,27},{4,28},{5,29},{6,30},{7,31},{8,16},{9,... | collective-permute-start | bytes 614408 | tf_op jit(solution)/shard_map/ppermute | solution.py:43
  170.6 1.8 collective-permute-start.35
  173.0 1.5 collective-permute-start.38
  174.6 6.5 %collective-permute-done.33.refs_3_ = bf16[320,1280]{1,0:T(8,128)(2,1)S(1)} collective-permute-done((bf16[320,1280]{1,0:T(8,128)(2,1)}, bf16[320,1280]{1,0:T(8,128)(2,1)S(1)}, u32[]{:S(2)}, u32[]{:S(2)}) %collective-permute-start.33) | collective-permute-done | bytes 819232 | tf_op jit(solution)/shard_map/ppermute | solution.py:39
  182.4 4.1 %all-to-all-start = ((bf16[4,160,640]{2,1,0:T(8,128)(2,1)}), bf16[4,160,640]{2,1,0:T(8,128)(2,1)S(1)}, u32[]{:S(2)}, u32[]{:S(2)}) async-start(bf16[4,160,640]{2,1,0:T(8,128)(2,1)} %pad_maximum_fusion.2), calls=%async_computation | async-start | bytes 1638400 | tf_op jit(solution)/shard_map/all_to_all | solution.py:92
  186.6 1.2 fusion
  187.8 3.9 %collective-permute-done.36 = bf16[160,640]{1,0:T(8,128)(2,1)} collective-permute-done((bf16[160,640]{1,0:T(8,128)(2,1)S(1)}, bf16[160,640]{1,0:T(8,128)(2,1)}, u32[]{:S(2)}, u32[]{:S(2)}) %collective-permute-start.36) | collective-permute-done | bytes 204832 | tf_op jit(solution)/shard_map/ppermute | solution.py:43
  191.7 1.2 pad_maximum_fusion.3.refs_5_
  192.9 4.8 %collective-permute-start.39 = (bf16[480,640]{1,0:T(8,128)(2,1)S(1)}, bf16[480,640]{1,0:T(8,128)(2,1)}, u32[]{:S(2)}, u32[]{:S(2)}) collective-permute-start(bf16[480,640]{1,0:T(8,128)(2,1)S(1)} %pad_maximum_fusion.3.refs_5_), channel_id=1, source_target_pairs={{0,4},{1,5},{2,6},{3,7},{4,0},{5,1},{6,2},{7,3},{8,12},{9,13},{10,... | collective-permute-start | bytes 1843208 | tf_op jit(solution)/shard_map/ppermute | solution.py:39
  197.8 1.1 copy-done.3
  199.0 6.0 %shard_map.149 = (bf16[96,1280]{1,0:T(8,128)(2,1)S(1)}, bf16[96,1280]{1,0:T(8,128)(2,1)}) custom-call(s32[25]{0:T(128)S(1)} %stack.110.spots_ref, bf16[192,1280]{1,0:T(8,128)(2,1)S(1)} %pad_maximum_fusion.4.rows_ref, bf16[320,1280]{1,0:T(8,128)(2,1)S(1)} %constant_dynamic-update-slice_fusion.2.refs_0_, bf16[320,1280]{1,0:T(8,128)(2,1)} %collective-permute-done.28.refs_1_, ...), custom_call_target="tpu_custom_call" | custom-call | tf_op jit(solution)/shard_map/pallas_call | solution.py:147
  206.0 2.0 collective-permute-start.45
  208.0 1.5 collective-permute-start.41
  209.6 6.6 %collective-permute-done.41.right_ref = bf16[96,1280]{1,0:T(8,128)(2,1)S(1)} collective-permute-done((bf16[96,1280]{1,0:T(8,128)(2,1)S(1)}, bf16[96,1280]{1,0:T(8,128)(2,1)S(1)}, u32[]{:S(2)}, u32[]{:S(2)}) %collective-permute-start.41) | collective-permute-done | bytes 245792 | tf_op jit(solution)/shard_map/ppermute | solution.py:35
  217.0 1.4 collective-permute-start.43
  218.5 5.9 %collective-permute-done.43.refs_2_ = bf16[96,1280]{1,0:T(8,128)(2,1)S(1)} collective-permute-done((bf16[96,1280]{1,0:T(8,128)(2,1)S(1)}, bf16[96,1280]{1,0:T(8,128)(2,1)S(1)}, u32[]{:S(2)}, u32[]{:S(2)}) %collective-permute-start.43) | collective-permute-done | bytes 245792 | tf_op jit(solution)/shard_map/ppermute | solution.py:43
  224.4 1.5 collective-permute-done.44.refs_3_
  226.9 6.0 %shard_map.151 = (bf16[96,1280]{1,0:T(8,128)(2,1)S(1)}, bf16[96,1280]{1,0:T(8,128)(2,1)S(1)}, bf16[96,1280]{1,0:T(8,128)(2,1)S(1)}, bf16[96,1280]{1,0:T(8,128)(2,1)S(1)}) custom-call(s32[25]{0:T(128)S(1)} %stack.110.spots_ref, bf16[96,1280]{1,0:T(8,128)(2,1)S(1)} %get-tuple-element.101.refs_0_, bf16[96,1280]{1,0:T(8,128)(2,1)S(1)} %collective-permute-done.42.refs_1_, ...), custom_call_target="tpu_custom_call" | custom-call | tf_op jit(solution)/shard_map/pallas_call | solution.py:147
  234.6 1.4 collective-permute-start.48
  236.0 6.6 %collective-permute-done.48 = bf16[96,1280]{1,0:T(8,128)(2,1)S(1)} collective-permute-done((bf16[96,1280]{1,0:T(8,128)(2,1)S(1)}, bf16[96,1280]{1,0:T(8,128)(2,1)S(1)}, u32[]{:S(2)}, u32[]{:S(2)}) %collective-permute-start.48) | collective-permute-done | bytes 245792 | tf_op jit(solution)/shard_map/ppermute | solution.py:43
  242.7 1.5 collective-permute-start.49
  244.9 5.0 %collective-permute-done.49 = bf16[96,1280]{1,0:T(8,128)(2,1)S(1)} collective-permute-done((bf16[96,1280]{1,0:T(8,128)(2,1)S(1)}, bf16[96,1280]{1,0:T(8,128)(2,1)S(1)}, u32[]{:S(2)}, u32[]{:S(2)}) %collective-permute-start.49) | collective-permute-done | bytes 245792 | tf_op jit(solution)/shard_map/ppermute | solution.py:35
  250.1 1.5 collective-permute-done.50
  (134 shorter events, 24.2 us)
Async XLA Ops:
  1.1 21.2 %collective-permute-start = (bf16[160,1280]{1,0:T(8,128)(2,1)S(1)}, bf16[160,1280]{1,0:T(8,128)(2,1)S(1)}, u32[]{:S(2)}, u32[]{:S(2)}) collective-permute-start(bf16[160,1280]{1,0:T(8,128)(2,1)S(1)} %pad_maximum_fusion.6.refs_1_), channel_id=1, source_target_pairs={{0,8},{1,9},{2,10},{3,11},{4,12},{5,13},{6,14},{7,15},{8,0},{9,1},... | collective-permute-start | bytes 1228808 | tf_op jit(solution)/shard_map/ppermute | solution.py:43
  4.2 20.7 %collective-permute-start.1 = (bf16[160,1280]{1,0:T(8,128)(2,1)S(1)}, bf16[160,1280]{1,0:T(8,128)(2,1)S(1)}, u32[]{:S(2)}, u32[]{:S(2)}) collective-permute-start(bf16[160,1280]{1,0:T(8,128)(2,1)S(1)} %pad_maximum_fusion.6.refs_1_), channel_id=1, source_target_pairs={{0,16},{1,17},{2,18},{3,19},{4,20},{5,21},{6,22},{7,23},{8,24},{9,... | collective-permute-start | bytes 1228808 | tf_op jit(solution)/shard_map/ppermute | solution.py:43
  6.8 18.1 %collective-permute-start.2 = (bf16[160,1280]{1,0:T(8,128)(2,1)S(1)}, bf16[160,1280]{1,0:T(8,128)(2,1)S(1)}, u32[]{:S(2)}, u32[]{:S(2)}) collective-permute-start(bf16[160,1280]{1,0:T(8,128)(2,1)S(1)} %pad_maximum_fusion.6.refs_1_), channel_id=1, source_target_pairs={{0,4},{1,5},{2,6},{3,7},{4,0},{5,1},{6,2},{7,3},{8,12},{9,13},{10,... | collective-permute-start | bytes 1228808 | tf_op jit(solution)/shard_map/ppermute | solution.py:39
  8.3 18.6 %copy-start.6 = (bf16[160,1280]{1,0:T(8,128)(2,1)S(1)}, bf16[160,1280]{1,0:T(8,128)(2,1)}, u32[]{:S(2)}) copy-start(bf16[160,1280]{1,0:T(8,128)(2,1)} %param.24) | copy-start | bytes 1228804
  8.3 18.6 %copy-start.7 = (bf16[160,1280]{1,0:T(8,128)(2,1)S(1)}, bf16[160,1280]{1,0:T(8,128)(2,1)}, u32[]{:S(2)}) copy-start(bf16[160,1280]{1,0:T(8,128)(2,1)} %param.23) | copy-start | bytes 1228804
  24.9 2.2 copy-start.4
  24.9 10.9 %collective-permute-start.3 = (bf16[160,1280]{1,0:T(8,128)(2,1)S(1)}, bf16[160,1280]{1,0:T(8,128)(2,1)}, u32[]{:S(2)}, u32[]{:S(2)}) collective-permute-start(bf16[160,1280]{1,0:T(8,128)(2,1)S(1)} %collective-permute-done.1.refs_3_), channel_id=1, source_target_pairs={{0,8},{1,9},{2,10},{3,11},{4,12},{5,13},{6,14},{7,15},{8,0},{9,1},... | collective-permute-start | bytes 1228808 | tf_op jit(solution)/shard_map/ppermute | solution.py:43
  25.4 21.2 %collective-permute-start.4 = (bf16[320,1280]{1,0:T(8,128)(2,1)S(1)}, bf16[320,1280]{1,0:T(8,128)(2,1)S(1)}, u32[]{:S(2)}, u32[]{:S(2)}) collective-permute-start(bf16[320,1280]{1,0:T(8,128)(2,1)S(1)} %pad_maximum_fusion.1), channel_id=1, source_target_pairs={{0,4},{1,5},{2,6},{3,7},{4,0},{5,1},{6,2},{7,3},{8,12},{9,13},{10,... | collective-permute-start | bytes 2457608 | tf_op jit(solution)/shard_map/ppermute | solution.py:39
  27.9 34.8 %collective-permute-start.10 = (bf16[160,1280]{1,0:T(8,128)(2,1)}, bf16[160,1280]{1,0:T(8,128)(2,1)}, u32[]{:S(2)}, u32[]{:S(2)}) collective-permute-start(bf16[160,1280]{1,0:T(8,128)(2,1)} %pad_maximum_fusion.7), channel_id=1, source_target_pairs={{0,24},{1,25},{2,26},{3,27},{4,28},{5,29},{6,30},{7,31},{8,16},{9,... | collective-permute-start | bytes 1228808 | tf_op jit(solution)/shard_map/ppermute | solution.py:43
  30.0 33.9 %collective-permute-start.14 = (bf16[160,1280]{1,0:T(8,128)(2,1)S(1)}, bf16[160,1280]{1,0:T(8,128)(2,1)}, u32[]{:S(2)}, u32[]{:S(2)}) collective-permute-start(bf16[160,1280]{1,0:T(8,128)(2,1)S(1)} %pad_maximum_fusion.8.refs_4_), channel_id=1, source_target_pairs={{0,16},{1,17},{2,18},{3,19},{4,20},{5,21},{6,22},{7,23},{8,24},{9,... | collective-permute-start | bytes 1228808 | tf_op jit(solution)/shard_map/ppermute | solution.py:43
  35.8 19.7 %collective-permute-start.5 = (bf16[160,1280]{1,0:T(8,128)(2,1)}, bf16[160,1280]{1,0:T(8,128)(2,1)}, u32[]{:S(2)}, u32[]{:S(2)}) collective-permute-start(bf16[160,1280]{1,0:T(8,128)(2,1)} %collective-permute-done.3.refs_4_), channel_id=1, source_target_pairs={{0,4},{1,5},{2,6},{3,7},{4,0},{5,1},{6,2},{7,3},{8,12},{9,13},{10,... | collective-permute-start | bytes 1228808 | tf_op jit(solution)/shard_map/ppermute | solution.py:39
  43.1 20.8 %collective-permute-start.13 = (bf16[160,1280]{1,0:T(8,128)(2,1)}, bf16[160,1280]{1,0:T(8,128)(2,1)}, u32[]{:S(2)}, u32[]{:S(2)}) collective-permute-start(bf16[160,1280]{1,0:T(8,128)(2,1)} %pad_maximum_fusion.7), channel_id=1, source_target_pairs={{0,8},{1,9},{2,10},{3,11},{4,12},{5,13},{6,14},{7,15},{8,0},{9,1},... | collective-permute-start | bytes 1228808 | tf_op jit(solution)/shard_map/ppermute | solution.py:43
  46.6 18.7 %collective-permute-start.15 = (bf16[160,1280]{1,0:T(8,128)(2,1)S(1)}, bf16[160,1280]{1,0:T(8,128)(2,1)}, u32[]{:S(2)}, u32[]{:S(2)}) collective-permute-start(bf16[160,1280]{1,0:T(8,128)(2,1)S(1)} %pad_maximum_fusion.8.refs_4_), channel_id=1, source_target_pairs={{0,4},{1,5},{2,6},{3,7},{4,0},{5,1},{6,2},{7,3},{8,12},{9,13},{10,... | collective-permute-start | bytes 1228808 | tf_op jit(solution)/shard_map/ppermute | solution.py:39
  62.6 5.3 %copy-start.8 = (bf16[160,1280]{1,0:T(8,128)(2,1)S(1)}, bf16[160,1280]{1,0:T(8,128)(2,1)}, u32[]{:S(2)}) copy-start(bf16[160,1280]{1,0:T(8,128)(2,1)} %param.25) | copy-start | bytes 1228804
  62.6 3.6 %collective-permute-start.6 = (bf16[128,1280]{1,0:T(8,128)(2,1)S(1)}, bf16[128,1280]{1,0:T(8,128)(2,1)S(1)}, u32[]{:S(2)}, u32[]{:S(2)}) collective-permute-start(bf16[128,1280]{1,0:T(8,128)(2,1)S(1)} %get-tuple-element.65), channel_id=1, source_target_pairs={{0,1},{1,0},{2,3},{3,2},{4,5},{5,4},{6,7},{7,6},{8,9},{9,8},{10,11... | collective-permute-start | bytes 983048 | tf_op jit(solution)/shard_map/ppermute | solution.py:31
  65.3 12.8 %copy-start.11 = (s32[64]{0:T(128)S(1)}, s32[64]{0:T(128)}, u32[]{:S(2)}) copy-start(s32[64]{0:T(128)} %param.18) | copy-start | bytes 772
  65.3 28.4 %collective-permute-start.16 = (bf16[480,1280]{1,0:T(8,128)(2,1)S(1)}, bf16[480,1280]{1,0:T(8,128)(2,1)S(1)}, u32[]{:S(2)}, u32[]{:S(2)}) collective-permute-start(bf16[480,1280]{1,0:T(8,128)(2,1)S(1)} %pad_maximum_fusion.refs_5_), channel_id=1, source_target_pairs={{0,4},{1,5},{2,6},{3,7},{4,0},{5,1},{6,2},{7,3},{8,12},{9,13},{10,... | collective-permute-start | bytes 3686408 | tf_op jit(solution)/shard_map/ppermute | solution.py:39
  66.3 9.3 %collective-permute-start.7 = (bf16[128,1280]{1,0:T(8,128)(2,1)S(1)}, bf16[128,1280]{1,0:T(8,128)(2,1)S(1)}, u32[]{:S(2)}, u32[]{:S(2)}) collective-permute-start(bf16[128,1280]{1,0:T(8,128)(2,1)S(1)} %add_convert_fusion.2.left_ref), channel_id=1, source_target_pairs={{0,2},{1,3},{2,0},{3,1},{4,6},{5,7},{6,4},{7,5},{8,10},{9,11},{10,... | collective-permute-start | bytes 983048 | tf_op jit(solution)/shard_map/ppermute | solution.py:35
  67.8 20.5 %collective-permute-start.11 = (bf16[160,1280]{1,0:T(8,128)(2,1)S(1)}, bf16[160,1280]{1,0:T(8,128)(2,1)S(1)}, u32[]{:S(2)}, u32[]{:S(2)}) collective-permute-start(bf16[160,1280]{1,0:T(8,128)(2,1)S(1)} %copy-done.8), channel_id=1, source_target_pairs={{0,16},{1,17},{2,18},{3,19},{4,20},{5,21},{6,22},{7,23},{8,24},{9,... | collective-permute-start | bytes 1228808 | tf_op jit(solution)/shard_map/ppermute | solution.py:43
  76.5 16.5 %collective-permute-start.9 = (bf16[128,1280]{1,0:T(8,128)(2,1)S(1)}, bf16[128,1280]{1,0:T(8,128)(2,1)S(1)}, u32[]{:S(2)}, u32[]{:S(2)}) collective-permute-start(bf16[128,1280]{1,0:T(8,128)(2,1)S(1)} %get-tuple-element.67.refs_0_), channel_id=1, source_target_pairs={{0,8},{1,9},{2,10},{3,11},{4,12},{5,13},{6,14},{7,15},{8,0},{9,1},... | collective-permute-start | bytes 983048 | tf_op jit(solution)/shard_map/ppermute | solution.py:43
  78.2 15.5 %collective-permute-start.8 = (bf16[128,1280]{1,0:T(8,128)(2,1)S(1)}, bf16[128,1280]{1,0:T(8,128)(2,1)S(1)}, u32[]{:S(2)}, u32[]{:S(2)}) collective-permute-start(bf16[128,1280]{1,0:T(8,128)(2,1)S(1)} %get-tuple-element.67.refs_0_), channel_id=1, source_target_pairs={{0,1},{1,0},{2,3},{3,2},{4,5},{5,4},{6,7},{7,6},{8,9},{9,8},{10,11... | collective-permute-start | bytes 983048 | tf_op jit(solution)/shard_map/ppermute | solution.py:31
  93.0 1.6 collective-permute-start.12
  93.1 7.3 %copy-start.12 = (s32[64]{0:T(128)S(1)}, s32[64]{0:T(128)}, u32[]{:S(2)}) copy-start(s32[64]{0:T(128)} %param.19) | copy-start | bytes 772
  93.1 20.8 %collective-permute-start.19 = (bf16[320,1280]{1,0:T(8,128)(2,1)S(1)}, bf16[320,1280]{1,0:T(8,128)(2,1)}, u32[]{:S(2)}, u32[]{:S(2)}) collective-permute-start(bf16[320,1280]{1,0:T(8,128)(2,1)S(1)} %constant_dynamic-update-slice_fusion.refs_0_), channel_id=1, source_target_pairs={{0,8},{1,9},{2,10},{3,11},{4,12},{5,13},{6,14},{7,15},{8,0},{9,1},... | collective-permute-start | bytes 2457608 | tf_op jit(solution)/shard_map/ppermute | solution.py:43
  93.2 20.7 %collective-permute-start.20 = (bf16[320,1280]{1,0:T(8,128)(2,1)S(1)}, bf16[320,1280]{1,0:T(8,128)(2,1)S(1)}, u32[]{:S(2)}, u32[]{:S(2)}) collective-permute-start(bf16[320,1280]{1,0:T(8,128)(2,1)S(1)} %constant_dynamic-update-slice_fusion.refs_0_), channel_id=1, source_target_pairs={{0,4},{1,5},{2,6},{3,7},{4,0},{5,1},{6,2},{7,3},{8,12},{9,13},{10,... | collective-permute-start | bytes 2457608 | tf_op jit(solution)/shard_map/ppermute | solution.py:39
  100.2 2.0 collective-permute-start.18
  101.7 18.1 %collective-permute-start.17 = (bf16[128,1280]{1,0:T(8,128)(2,1)S(1)}, bf16[128,1280]{1,0:T(8,128)(2,1)S(1)}, u32[]{:S(2)}, u32[]{:S(2)}) collective-permute-start(bf16[128,1280]{1,0:T(8,128)(2,1)S(1)} %get-tuple-element.75), channel_id=1, source_target_pairs={{0,1},{1,0},{2,3},{3,2},{4,5},{5,4},{6,7},{7,6},{8,9},{9,8},{10,11... | collective-permute-start | bytes 983048 | tf_op jit(solution)/shard_map/ppermute | solution.py:31
  113.9 17.1 %copy-start = (bf16[320,1280]{1,0:T(8,128)(2,1)}, bf16[320,1280]{1,0:T(8,128)(2,1)S(1)}, u32[]{:S(2)}) copy-start(bf16[320,1280]{1,0:T(8,128)(2,1)S(1)} %collective-permute-done.20.refs_1_) | copy-start | bytes 2457604
  113.9 16.9 %collective-permute-start.21 = (bf16[128,1280]{1,0:T(8,128)(2,1)S(1)}, bf16[128,1280]{1,0:T(8,128)(2,1)S(1)}, u32[]{:S(2)}, u32[]{:S(2)}) collective-permute-start(bf16[128,1280]{1,0:T(8,128)(2,1)S(1)} %add_convert_fusion.1), channel_id=1, source_target_pairs={{0,8},{1,9},{2,10},{3,11},{4,12},{5,13},{6,14},{7,15},{8,0},{9,1},... | collective-permute-start | bytes 983048 | tf_op jit(solution)/shard_map/ppermute | solution.py:43
  115.7 21.5 %collective-permute-start.23 = (bf16[160,1280]{1,0:T(8,128)(2,1)S(1)}, bf16[160,1280]{1,0:T(8,128)(2,1)S(1)}, u32[]{:S(2)}, u32[]{:S(2)}) collective-permute-start(bf16[160,1280]{1,0:T(8,128)(2,1)S(1)} %pad_maximum_fusion.9), channel_id=1, source_target_pairs={{0,16},{1,17},{2,18},{3,19},{4,20},{5,21},{6,22},{7,23},{8,24},{9,... | collective-permute-start | bytes 1228808 | tf_op jit(solution)/shard_map/ppermute | solution.py:43
  119.2 19.6 %collective-permute-start.24 = (bf16[320,1280]{1,0:T(8,128)(2,1)}, bf16[320,1280]{1,0:T(8,128)(2,1)S(1)}, u32[]{:S(2)}, u32[]{:S(2)}) collective-permute-start(bf16[320,1280]{1,0:T(8,128)(2,1)} %collective-permute-done.19.refs_2_), channel_id=1, source_target_pairs={{0,4},{1,5},{2,6},{3,7},{4,0},{5,1},{6,2},{7,3},{8,12},{9,13},{10,... | collective-permute-start | bytes 2457608 | tf_op jit(solution)/shard_map/ppermute | solution.py:39
  131.0 5.4 %collective-permute-start.22 = (bf16[64,1280]{1,0:T(8,128)(2,1)S(1)}, bf16[64,1280]{1,0:T(8,128)(2,1)S(1)}, u32[]{:S(2)}, u32[]{:S(2)}) collective-permute-start(bf16[64,1280]{1,0:T(8,128)(2,1)S(1)} %dynamic-slice_bitcast_fusion), channel_id=1, source_target_pairs={{0,2},{1,3},{2,0},{3,1},{4,6},{5,7},{6,4},{7,5},{8,10},{9,11},{10,... | collective-permute-start | bytes 491528 | tf_op jit(solution)/shard_map/ppermute | solution.py:35
  132.6 6.3 %copy-start.1 = (bf16[320,1280]{1,0:T(8,128)(2,1)S(1)}, bf16[320,1280]{1,0:T(8,128)(2,1)}, u32[]{:S(2)}) copy-start(bf16[320,1280]{1,0:T(8,128)(2,1)} %copy-done) | copy-start | bytes 2457604
  137.2 19.3 %collective-permute-start.27 = (bf16[320,1280]{1,0:T(8,128)(2,1)S(1)}, bf16[320,1280]{1,0:T(8,128)(2,1)}, u32[]{:S(2)}, u32[]{:S(2)}) collective-permute-start(bf16[320,1280]{1,0:T(8,128)(2,1)S(1)} %constant_dynamic-update-slice_fusion.2.refs_0_), channel_id=1, source_target_pairs={{0,8},{1,9},{2,10},{3,11},{4,12},{5,13},{6,14},{7,15},{8,0},{9,1},... | collective-permute-start | bytes 2457608 | tf_op jit(solution)/shard_map/ppermute | solution.py:43
  137.8 18.8 %collective-permute-start.28 = (bf16[320,1280]{1,0:T(8,128)(2,1)S(1)}, bf16[320,1280]{1,0:T(8,128)(2,1)}, u32[]{:S(2)}, u32[]{:S(2)}) collective-permute-start(bf16[320,1280]{1,0:T(8,128)(2,1)S(1)} %constant_dynamic-update-slice_fusion.2.refs_0_), channel_id=1, source_target_pairs={{0,4},{1,5},{2,6},{3,7},{4,0},{5,1},{6,2},{7,3},{8,12},{9,13},{10,... | collective-permute-start | bytes 2457608 | tf_op jit(solution)/shard_map/ppermute | solution.py:39
  142.5 24.2 %copy-start.9 = (bf16[160,1280]{1,0:T(8,128)(2,1)S(1)}, bf16[160,1280]{1,0:T(8,128)(2,1)}, u32[]{:S(2)}) copy-start(bf16[160,1280]{1,0:T(8,128)(2,1)} %param.28) | copy-start | bytes 1228804
  142.5 1.4 collective-permute-start.25
  144.0 4.9 %collective-permute-start.26 = (bf16[64,640]{1,0:T(8,128)(2,1)S(1)}, bf16[64,640]{1,0:T(8,128)(2,1)S(1)}, u32[]{:S(2)}, u32[]{:S(2)}) collective-permute-start(bf16[64,640]{1,0:T(8,128)(2,1)S(1)} %add_convert_fusion.8), channel_id=1, source_target_pairs={{0,2},{1,3},{2,0},{3,1},{4,6},{5,7},{6,4},{7,5},{8,10},{9,11},{10,... | collective-permute-start | bytes 245768 | tf_op jit(solution)/shard_map/ppermute | solution.py:35
  156.6 5.0 %collective-permute-start.29 = (bf16[4,1,16,768]{3,2,0,1:T(8,128)(2,1)S(1)}, bf16[4,1,16,768]{3,2,0,1:T(8,128)(2,1)S(1)}, u32[]{:S(2)}, u32[]{:S(2)}) collective-permute-start(bf16[4,1,16,768]{3,2,0,1:T(8,128)(2,1)S(1)} %dynamic-slice_bitcast_fusion.1), channel_id=1, source_target_pairs={{0,4},{1,5},{2,6},{3,7},{4,0},{5,1},{6,2},{7,3},{8,12},{9,13},{10,... | collective-permute-start | bytes 294920 | tf_op jit(solution)/shard_map/ppermute | solution.py:39
  157.2 24.1 %copy-start.10 = (bf16[160,1280]{1,0:T(8,128)(2,1)S(1)}, bf16[160,1280]{1,0:T(8,128)(2,1)}, u32[]{:S(2)}) copy-start(bf16[160,1280]{1,0:T(8,128)(2,1)} %param.29) | copy-start | bytes 1228804
  161.7 19.4 %collective-permute-start.33 = (bf16[320,1280]{1,0:T(8,128)(2,1)}, bf16[320,1280]{1,0:T(8,128)(2,1)S(1)}, u32[]{:S(2)}, u32[]{:S(2)}) collective-permute-start(bf16[320,1280]{1,0:T(8,128)(2,1)} %collective-permute-done.27.refs_2_), channel_id=1, source_target_pairs={{0,4},{1,5},{2,6},{3,7},{4,0},{5,1},{6,2},{7,3},{8,12},{9,13},{10,... | collective-permute-start | bytes 2457608 | tf_op jit(solution)/shard_map/ppermute | solution.py:39
  162.2 8.4 %collective-permute-start.32 = (bf16[2,1,16,768]{3,2,0,1:T(8,128)(2,1)S(1)}, bf16[2,1,16,768]{3,2,0,1:T(8,128)(2,1)S(1)}, u32[]{:S(2)}, u32[]{:S(2)}) collective-permute-start(bf16[2,1,16,768]{3,2,0,1:T(8,128)(2,1)S(1)} %get-tuple-element.124), channel_id=1, source_target_pairs={{0,24},{1,25},{2,26},{3,27},{4,28},{5,29},{6,30},{7,31},{8,16},{9,... | collective-permute-start | bytes 147464 | tf_op jit(solution)/shard_map/ppermute | solution.py:43
  165.5 7.5 %collective-permute-start.31 = (bf16[2,1,16,768]{3,2,0,1:T(8,128)(2,1)S(1)}, bf16[2,1,16,768]{3,2,0,1:T(8,128)(2,1)S(1)}, u32[]{:S(2)}, u32[]{:S(2)}) collective-permute-start(bf16[2,1,16,768]{3,2,0,1:T(8,128)(2,1)S(1)} %get-tuple-element.125), channel_id=1, source_target_pairs={{0,16},{1,17},{2,18},{3,19},{4,20},{5,21},{6,22},{7,23},{8,24},{9,... | collective-permute-start | bytes 147464 | tf_op jit(solution)/shard_map/ppermute | solution.py:43
  166.0 7.0 %collective-permute-start.30 = (bf16[2,1,16,768]{3,2,0,1:T(8,128)(2,1)S(1)}, bf16[2,1,16,768]{3,2,0,1:T(8,128)(2,1)S(1)}, u32[]{:S(2)}, u32[]{:S(2)}) collective-permute-start(bf16[2,1,16,768]{3,2,0,1:T(8,128)(2,1)S(1)} %get-tuple-element.126), channel_id=1, source_target_pairs={{0,8},{1,9},{2,10},{3,11},{4,12},{5,13},{6,14},{7,15},{8,0},{9,1},... | collective-permute-start | bytes 147464 | tf_op jit(solution)/shard_map/ppermute | solution.py:43
  167.4 20.4 %collective-permute-start.37 = (bf16[160,640]{1,0:T(8,128)(2,1)}, bf16[160,640]{1,0:T(8,128)(2,1)}, u32[]{:S(2)}, u32[]{:S(2)}) collective-permute-start(bf16[160,640]{1,0:T(8,128)(2,1)} %get-tuple-element.117), channel_id=1, source_target_pairs={{0,24},{1,25},{2,26},{3,27},{4,28},{5,29},{6,30},{7,31},{8,16},{9,... | collective-permute-start | bytes 614408 | tf_op jit(solution)/shard_map/ppermute | solution.py:43
  170.6 21.1 %collective-permute-start.35 = (bf16[160,640]{1,0:T(8,128)(2,1)}, bf16[160,640]{1,0:T(8,128)(2,1)}, u32[]{:S(2)}, u32[]{:S(2)}) collective-permute-start(bf16[160,640]{1,0:T(8,128)(2,1)} %get-tuple-element.117), channel_id=1, source_target_pairs={{0,8},{1,9},{2,10},{3,11},{4,12},{5,13},{6,14},{7,15},{8,0},{9,1},... | collective-permute-start | bytes 614408 | tf_op jit(solution)/shard_map/ppermute | solution.py:43
  173.0 18.7 %collective-permute-start.36 = (bf16[160,640]{1,0:T(8,128)(2,1)S(1)}, bf16[160,640]{1,0:T(8,128)(2,1)}, u32[]{:S(2)}, u32[]{:S(2)}) collective-permute-start(bf16[160,640]{1,0:T(8,128)(2,1)S(1)} %get-tuple-element.102.refs_4_), channel_id=1, source_target_pairs={{0,16},{1,17},{2,18},{3,19},{4,20},{5,21},{6,22},{7,23},{8,24},{9,... | collective-permute-start | bytes 614408 | tf_op jit(solution)/shard_map/ppermute | solution.py:43
  173.0 19.9 %collective-permute-start.38 = (bf16[160,640]{1,0:T(8,128)(2,1)S(1)}, bf16[160,640]{1,0:T(8,128)(2,1)S(1)}, u32[]{:S(2)}, u32[]{:S(2)}) collective-permute-start(bf16[160,640]{1,0:T(8,128)(2,1)S(1)} %get-tuple-element.102.refs_4_), channel_id=1, source_target_pairs={{0,4},{1,5},{2,6},{3,7},{4,0},{5,1},{6,2},{7,3},{8,12},{9,13},{10,... | collective-permute-start | bytes 614408 | tf_op jit(solution)/shard_map/ppermute | solution.py:39
  181.1 1.3 copy-start.2
  182.4 23.6 %all-to-all-start = ((bf16[4,160,640]{2,1,0:T(8,128)(2,1)}), bf16[4,160,640]{2,1,0:T(8,128)(2,1)S(1)}, u32[]{:S(2)}, u32[]{:S(2)}) async-start(bf16[4,160,640]{2,1,0:T(8,128)(2,1)} %pad_maximum_fusion.2), calls=%async_computation | async-start | bytes 1638400 | tf_op jit(solution)/shard_map/all_to_all | solution.py:92
  187.7 10.0 %collective-permute-start.34 = (bf16[192,640]{1,0:T(8,128)(2,1)S(1)}, bf16[192,640]{1,0:T(8,128)(2,1)S(1)}, u32[]{:S(2)}, u32[]{:S(2)}) collective-permute-start(bf16[192,640]{1,0:T(8,128)(2,1)S(1)} %fusion), channel_id=1, source_target_pairs={{0,1},{1,0},{2,3},{3,2},{4,5},{5,4},{6,7},{7,6},{8,9},{9,8},{10,11... | collective-permute-start | bytes 737288 | tf_op jit(solution)/shard_map/ppermute | solution.py:31
  192.9 13.0 %collective-permute-start.39 = (bf16[480,640]{1,0:T(8,128)(2,1)S(1)}, bf16[480,640]{1,0:T(8,128)(2,1)}, u32[]{:S(2)}, u32[]{:S(2)}) collective-permute-start(bf16[480,640]{1,0:T(8,128)(2,1)S(1)} %pad_maximum_fusion.3.refs_5_), channel_id=1, source_target_pairs={{0,4},{1,5},{2,6},{3,7},{4,0},{5,1},{6,2},{7,3},{8,12},{9,13},{10,... | collective-permute-start | bytes 1843208 | tf_op jit(solution)/shard_map/ppermute | solution.py:39
  197.8 1.1 copy-start.3
  205.9 2.0 collective-permute-start.40
  206.0 20.9 %collective-permute-start.45 = (bf16[640,640]{1,0:T(8,128)(2,1)S(1)}, bf16[640,640]{1,0:T(8,128)(2,1)S(1)}, u32[]{:S(2)}, u32[]{:S(2)}) collective-permute-start(bf16[640,640]{1,0:T(8,128)(2,1)S(1)} %bitcast.61), channel_id=1, source_target_pairs={{0,4},{1,5},{2,6},{3,7},{4,0},{5,1},{6,2},{7,3},{8,12},{9,13},{10,... | collective-permute-start | bytes 2457608 | tf_op jit(solution)/shard_map/ppermute | solution.py:39
  208.0 8.2 %collective-permute-start.41 = (bf16[96,1280]{1,0:T(8,128)(2,1)S(1)}, bf16[96,1280]{1,0:T(8,128)(2,1)S(1)}, u32[]{:S(2)}, u32[]{:S(2)}) collective-permute-start(bf16[96,1280]{1,0:T(8,128)(2,1)S(1)} %add_convert_fusion.6.left_ref), channel_id=1, source_target_pairs={{0,2},{1,3},{2,0},{3,1},{4,6},{5,7},{6,4},{7,5},{8,10},{9,11},{10,... | collective-permute-start | bytes 737288 | tf_op jit(solution)/shard_map/ppermute | solution.py:35
  217.0 7.3 %collective-permute-start.43 = (bf16[96,1280]{1,0:T(8,128)(2,1)S(1)}, bf16[96,1280]{1,0:T(8,128)(2,1)S(1)}, u32[]{:S(2)}, u32[]{:S(2)}) collective-permute-start(bf16[96,1280]{1,0:T(8,128)(2,1)S(1)} %get-tuple-element.101.refs_0_), channel_id=1, source_target_pairs={{0,8},{1,9},{2,10},{3,11},{4,12},{5,13},{6,14},{7,15},{8,0},{9,1},... | collective-permute-start | bytes 737288 | tf_op jit(solution)/shard_map/ppermute | solution.py:43
  218.5 5.9 %collective-permute-start.42 = (bf16[96,1280]{1,0:T(8,128)(2,1)S(1)}, bf16[96,1280]{1,0:T(8,128)(2,1)S(1)}, u32[]{:S(2)}, u32[]{:S(2)}) collective-permute-start(bf16[96,1280]{1,0:T(8,128)(2,1)S(1)} %get-tuple-element.101.refs_0_), channel_id=1, source_target_pairs={{0,1},{1,0},{2,3},{3,2},{4,5},{5,4},{6,7},{7,6},{8,9},{9,8},{10,11... | collective-permute-start | bytes 737288 | tf_op jit(solution)/shard_map/ppermute | solution.py:31
  224.4 1.5 collective-permute-start.44
  232.9 1.6 collective-permute-start.47
  233.0 3.0 %collective-permute-start.46 = (bf16[96,1280]{1,0:T(8,128)(2,1)S(1)}, bf16[96,1280]{1,0:T(8,128)(2,1)S(1)}, u32[]{:S(2)}, u32[]{:S(2)}) collective-permute-start(bf16[96,1280]{1,0:T(8,128)(2,1)S(1)} %get-tuple-element.108), channel_id=1, source_target_pairs={{0,1},{1,0},{2,3},{3,2},{4,5},{5,4},{6,7},{7,6},{8,9},{9,8},{10,11... | collective-permute-start | bytes 737288 | tf_op jit(solution)/shard_map/ppermute | solution.py:31
  234.6 8.1 %collective-permute-start.48 = (bf16[96,1280]{1,0:T(8,128)(2,1)S(1)}, bf16[96,1280]{1,0:T(8,128)(2,1)S(1)}, u32[]{:S(2)}, u32[]{:S(2)}) collective-permute-start(bf16[96,1280]{1,0:T(8,128)(2,1)S(1)} %add_convert_fusion.5), channel_id=1, source_target_pairs={{0,8},{1,9},{2,10},{3,11},{4,12},{5,13},{6,14},{7,15},{8,0},{9,1},... | collective-permute-start | bytes 737288 | tf_op jit(solution)/shard_map/ppermute | solution.py:43
  242.7 7.2 %collective-permute-start.49 = (bf16[96,1280]{1,0:T(8,128)(2,1)S(1)}, bf16[96,1280]{1,0:T(8,128)(2,1)S(1)}, u32[]{:S(2)}, u32[]{:S(2)}) collective-permute-start(bf16[96,1280]{1,0:T(8,128)(2,1)S(1)} %add_convert_fusion.4), channel_id=1, source_target_pairs={{0,2},{1,3},{2,0},{3,1},{4,6},{5,7},{6,4},{7,5},{8,10},{9,11},{10,... | collective-permute-start | bytes 737288 | tf_op jit(solution)/shard_map/ppermute | solution.py:35
  250.1 1.6 collective-permute-start.50
  (1 other events, 1.0 us)

commit v8 on v7

--- a/solution.py
+++ b/solution.py
@@ -159,6 +159,7 @@
     length, width = rows.shape
     heads = qkv_width // (3 * HEAD_DIM)
     half = length // 2
+    qkv_end, out_start = -(-qkv_width // 128) * 128, qkv_width // 128 * 128
 
     masks = [] if allowed is None else [allowed]
 
@@ -177,8 +178,8 @@
         mixed[...] = jnp.zeros_like(mixed)
         for copy in copies:
             copy.wait()
-        projected[...] = (
-            jnp.dot(normed, weight[...], preferred_element_type=jnp.float32)
+        projected[:, :qkv_end] = (
+            jnp.dot(normed, weight[:, :qkv_end], preferred_element_type=jnp.float32)
             .astype(jnp.bfloat16)
             .astype(jnp.float32)
         )
@@ -195,7 +196,7 @@
             mixed[:, out_at : out_at + HEAD_DIM] = jnp.dot(
                 soft, value, preferred_element_type=jnp.float32
             )
-        projected[...] = dot_t(mixed[...].astype(jnp.bfloat16), weight[...])
+        projected[...] = dot_t(mixed[:, out_start:].astype(jnp.bfloat16), weight[:, out_start:])
         core = spots_ref[24]
         keep[...] = projected[pl.ds(pl.multiple_of(core * half, 16), half), :].astype(jnp.bfloat16)
         send[...] = projected[pl.ds(pl.multiple_of((1 - core) * half, 16), half), :].astype(

time: 253 us -> 253 us (level)
  no operation moved by 1% of the time
where the time goes in v8:
time: 253 us; the launch traced here: 252 us
  waiting for transfers between devices  132 us (52%)
  starting transfers between devices  67.8 us (27%)
  Pallas kernels  28.1 us (11%)
  other arithmetic  12.9 us (5%)
  local copies, waits for them, and re-layouts  8.83 us (3%)
    ppermute x20, waiting for transfers between devices, swap_z(): return lax.ppermute(part, AXES, routes(lambda z, y, x, c: (z ^ k, y, x, c)))  83.1 us
    ppermute x20, starting transfers between devices, swap_z(): return lax.ppermute(part, AXES, routes(lambda z, y, x, c: (z ^ k, y, x, c)))  30.5 us
    pallas_call x7, Pallas kernels, local_call(): pl.pallas_call(kernel, in_specs=in_specs, out_specs=[VMEM] * len(outs), o...  28.1 us
    ppermute x5, waiting for transfers between devices, swap_x(): return lax.ppermute(part, AXES, routes(lambda z, y, x, c: (z, y, 1 - x, c)))  24.5 us
    ppermute x13, starting transfers between devices, swap_y(): return lax.ppermute(part, AXES, routes(lambda z, y, x, c: (z, 1 - y, x, c)))  23.9 us
    ppermute x13, waiting for transfers between devices, swap_y(): return lax.ppermute(part, AXES, routes(lambda z, y, x, c: (z, 1 - y, x, c)))  19.4 us
    ppermute x5, starting transfers between devices, swap_x(): return lax.ppermute(part, AXES, routes(lambda z, y, x, c: (z, y, 1 - x, c)))  7.75 us
  transfers between devices with their start and end apart: 52, of which 32 were waited for; matrix products, arithmetic and copies ran while one was open for 7% of the time, Pallas kernels for 9%

profile of v8, /device:TPU:0, one launch (start us, length us, event | category | flops | bytes accessed | tf_op | source)
XLA Modules:
  0.0 252.3 jit_solution(17862024258578975990)
XLA Ops:
  0.0 1.1 pad_maximum_fusion.6.refs_1_
  1.1 3.1 %collective-permute-start = (bf16[160,1280]{1,0:T(8,128)(2,1)S(1)}, bf16[160,1280]{1,0:T(8,128)(2,1)S(1)}, u32[]{:S(2)}, u32[]{:S(2)}) collective-permute-start(bf16[160,1280]{1,0:T(8,128)(2,1)S(1)} %pad_maximum_fusion.6.refs_1_), channel_id=1, source_target_pairs={{0,8},{1,9},{2,10},{3,11},{4,12},{5,13},{6,14},{7,15},{8,0},{9,1},... | collective-permute-start | bytes 1228808 | tf_op jit(solution)/shard_map/ppermute | solution.py:43
  4.2 2.6 %collective-permute-start.1 = (bf16[160,1280]{1,0:T(8,128)(2,1)S(1)}, bf16[160,1280]{1,0:T(8,128)(2,1)S(1)}, u32[]{:S(2)}, u32[]{:S(2)}) collective-permute-start(bf16[160,1280]{1,0:T(8,128)(2,1)S(1)} %pad_maximum_fusion.6.refs_1_), channel_id=1, source_target_pairs={{0,16},{1,17},{2,18},{3,19},{4,20},{5,21},{6,22},{7,23},{8,24},{9,... | collective-permute-start | bytes 1228808 | tf_op jit(solution)/shard_map/ppermute | solution.py:43
  6.8 1.5 collective-permute-start.2
  8.4 1.4 fusion.25
  9.7 12.6 %collective-permute-done.refs_2_ = bf16[160,1280]{1,0:T(8,128)(2,1)S(1)} collective-permute-done((bf16[160,1280]{1,0:T(8,128)(2,1)S(1)}, bf16[160,1280]{1,0:T(8,128)(2,1)S(1)}, u32[]{:S(2)}, u32[]{:S(2)}) %collective-permute-start) | collective-permute-done | bytes 409632 | tf_op jit(solution)/shard_map/ppermute | solution.py:43
  22.4 2.5 collective-permute-done.1.refs_3_
  25.4 1.6 collective-permute-start.4
  27.9 2.1 collective-permute-start.10
  31.0 4.8 %collective-permute-done.3.refs_4_ = bf16[160,1280]{1,0:T(8,128)(2,1)} collective-permute-done((bf16[160,1280]{1,0:T(8,128)(2,1)S(1)}, bf16[160,1280]{1,0:T(8,128)(2,1)}, u32[]{:S(2)}, u32[]{:S(2)}) %collective-permute-start.3) | collective-permute-done | bytes 409632 | tf_op jit(solution)/shard_map/ppermute | solution.py:43
  35.8 7.3 %collective-permute-start.5 = (bf16[160,1280]{1,0:T(8,128)(2,1)}, bf16[160,1280]{1,0:T(8,128)(2,1)}, u32[]{:S(2)}, u32[]{:S(2)}) collective-permute-start(bf16[160,1280]{1,0:T(8,128)(2,1)} %collective-permute-done.3.refs_4_), channel_id=1, source_target_pairs={{0,4},{1,5},{2,6},{3,7},{4,0},{5,1},{6,2},{7,3},{8,12},{9,13},{10,... | collective-permute-start | bytes 1228808 | tf_op jit(solution)/shard_map/ppermute | solution.py:39
  43.2 1.3 compare_and_fusion
  44.7 2.0 collective-permute-done.4.refs_6_
  46.6 1.5 collective-permute-start.15
  48.3 2.7 %reshape.162 = bf16[1,8,2,8,2,1280]{5,4,3,2,1,0:T(2,128)(2,1)} reshape(bf16[256,1280]{1,0:T(8,128)(2,1)} %param.15) | data formatting | bytes 1310720 | tf_op jit(solution)/shard_map/reshape | solution.py:389
  51.0 1.2 copy.30
  52.2 3.3 %collective-permute-done.5.refs_7_ = bf16[160,1280]{1,0:T(8,128)(2,1)} collective-permute-done((bf16[160,1280]{1,0:T(8,128)(2,1)}, bf16[160,1280]{1,0:T(8,128)(2,1)}, u32[]{:S(2)}, u32[]{:S(2)}) %collective-permute-start.5) | collective-permute-done | bytes 409632 | tf_op jit(solution)/shard_map/ppermute | solution.py:39
  56.5 5.8 %shard_map.145 = (bf16[128,1280]{1,0:T(8,128)(2,1)S(1)}, bf16[128,1280]{1,0:T(8,128)(2,1)S(1)}) custom-call(s32[25]{0:T(128)S(1)} %stack.110.spots_ref, bf16[256,1280]{1,0:T(8,128)(2,1)S(1)} %bitcast.59, f32[256,256]{1,0:T(8,128)S(1)} %and_convert_fusion.refs_0_, bf16[160,1280]{1,0:T(8,128)(2,1)S(1)} %pad_maximum_fusion.6.refs_1_, ...), custom_call_target="tpu_custom_call" | custom-call | tf_op jit(solution)/shard_map/pallas_call | solution.py:147
  62.4 1.5 collective-permute-done.14
  64.0 1.3 pad_maximum_fusion.refs_5_
  66.3 1.6 collective-permute-start.7
  67.8 1.6 collective-permute-start.11
  69.4 5.9 %collective-permute-done.7.right_ref = bf16[128,1280]{1,0:T(8,128)(2,1)S(1)} collective-permute-done((bf16[128,1280]{1,0:T(8,128)(2,1)S(1)}, bf16[128,1280]{1,0:T(8,128)(2,1)S(1)}, u32[]{:S(2)}, u32[]{:S(2)}) %collective-permute-start.7) | collective-permute-done | bytes 327712 | tf_op jit(solution)/shard_map/ppermute | solution.py:35
  76.2 1.6 collective-permute-start.9
  78.0 10.1 %collective-permute-done.11 = bf16[160,1280]{1,0:T(8,128)(2,1)S(1)} collective-permute-done((bf16[160,1280]{1,0:T(8,128)(2,1)S(1)}, bf16[160,1280]{1,0:T(8,128)(2,1)S(1)}, u32[]{:S(2)}, u32[]{:S(2)}) %collective-permute-start.11) | collective-permute-done | bytes 409632 | tf_op jit(solution)/shard_map/ppermute | solution.py:43
  88.1 4.7 %collective-permute-done.9.refs_2_ = bf16[128,1280]{1,0:T(8,128)(2,1)S(1)} collective-permute-done((bf16[128,1280]{1,0:T(8,128)(2,1)S(1)}, bf16[128,1280]{1,0:T(8,128)(2,1)S(1)}, u32[]{:S(2)}, u32[]{:S(2)}) %collective-permute-start.9) | collective-permute-done | bytes 327712 | tf_op jit(solution)/shard_map/ppermute | solution.py:43
  94.4 5.5 %shard_map.147 = (bf16[128,1280]{1,0:T(8,128)(2,1)S(1)}, bf16[128,1280]{1,0:T(8,128)(2,1)S(1)}, bf16[128,1280]{1,0:T(8,128)(2,1)S(1)}, bf16[128,1280]{1,0:T(8,128)(2,1)}) custom-call(s32[25]{0:T(128)S(1)} %stack.110.spots_ref, bf16[128,1280]{1,0:T(8,128)(2,1)S(1)} %get-tuple-element.67.refs_0_, bf16[128,1280]{1,0:T(8,128)(2,1)S(1)} %collective-permute-done.8.refs_1_, ...), custom_call_target="tpu_custom_call" | custom-call | tf_op jit(solution)/shard_map/pallas_call | solution.py:147
  100.3 1.1 pad_maximum_fusion.9
  103.0 10.6 %collective-permute-done.19.refs_2_ = bf16[320,1280]{1,0:T(8,128)(2,1)} collective-permute-done((bf16[320,1280]{1,0:T(8,128)(2,1)S(1)}, bf16[320,1280]{1,0:T(8,128)(2,1)}, u32[]{:S(2)}, u32[]{:S(2)}) %collective-permute-start.19) | collective-permute-done | bytes 819232 | tf_op jit(solution)/shard_map/ppermute | solution.py:43
  113.7 1.6 collective-permute-start.21
  115.5 3.5 %collective-permute-start.23 = (bf16[160,1280]{1,0:T(8,128)(2,1)S(1)}, bf16[160,1280]{1,0:T(8,128)(2,1)S(1)}, u32[]{:S(2)}, u32[]{:S(2)}) collective-permute-start(bf16[160,1280]{1,0:T(8,128)(2,1)S(1)} %pad_maximum_fusion.9), channel_id=1, source_target_pairs={{0,16},{1,17},{2,18},{3,19},{4,20},{5,21},{6,22},{7,23},{8,24},{9,... | collective-permute-start | bytes 1228808 | tf_op jit(solution)/shard_map/ppermute | solution.py:43
  119.5 11.1 %collective-permute-done.21 = bf16[128,1280]{1,0:T(8,128)(2,1)S(1)} collective-permute-done((bf16[128,1280]{1,0:T(8,128)(2,1)S(1)}, bf16[128,1280]{1,0:T(8,128)(2,1)S(1)}, u32[]{:S(2)}, u32[]{:S(2)}) %collective-permute-start.21) | collective-permute-done | bytes 327712 | tf_op jit(solution)/shard_map/ppermute | solution.py:43
  130.8 1.6 collective-permute-start.22
  132.4 3.8 %collective-permute-done.22 = bf16[64,1280]{1,0:T(8,128)(2,1)S(1)} collective-permute-done((bf16[64,1280]{1,0:T(8,128)(2,1)S(1)}, bf16[64,1280]{1,0:T(8,128)(2,1)S(1)}, u32[]{:S(2)}, u32[]{:S(2)}) %collective-permute-start.22) | collective-permute-done | bytes 163872 | tf_op jit(solution)/shard_map/ppermute | solution.py:35
  138.6 3.7 %shard_map.148 = (bf16[64,640]{1,0:T(8,128)(2,1)S(1)}, bf16[64,640]{1,0:T(8,128)(2,1)S(1)}) custom-call(s32[25]{0:T(128)S(1)} %stack.110.spots_ref, bf16[64,1280]{1,0:T(8,128)(2,1)S(1)} %fusion.2.blocks_ref, bf16[320,1280]{1,0:T(8,128)(2,1)S(1)} %constant_dynamic-update-slice_fusion.refs_0_, bf16[320,1280]{1,0:T(8,128)(2,1)S(1)} %copy-done.1, ...), custom_call_target="tpu_custom_call" | custom-call | tf_op jit(solution)/shard_map/pallas_call | solution.py:147
  142.4 1.4 fusion.19
  143.8 1.5 collective-permute-start.26
  145.5 3.2 %collective-permute-done.26 = bf16[64,640]{1,0:T(8,128)(2,1)S(1)} collective-permute-done((bf16[64,640]{1,0:T(8,128)(2,1)S(1)}, bf16[64,640]{1,0:T(8,128)(2,1)S(1)}, u32[]{:S(2)}, u32[]{:S(2)}) %collective-permute-start.26) | collective-permute-done | bytes 81952 | tf_op jit(solution)/shard_map/ppermute | solution.py:35
  148.9 7.4 %collective-permute-done.27.refs_2_ = bf16[320,1280]{1,0:T(8,128)(2,1)} collective-permute-done((bf16[320,1280]{1,0:T(8,128)(2,1)S(1)}, bf16[320,1280]{1,0:T(8,128)(2,1)}, u32[]{:S(2)}, u32[]{:S(2)}) %collective-permute-start.27) | collective-permute-done | bytes 819232 | tf_op jit(solution)/shard_map/ppermute | solution.py:43
  157.0 4.4 %collective-permute-done.29 = bf16[4,1,16,768]{3,2,0,1:T(8,128)(2,1)S(1)} collective-permute-done((bf16[4,1,16,768]{3,2,0,1:T(8,128)(2,1)S(1)}, bf16[4,1,16,768]{3,2,0,1:T(8,128)(2,1)S(1)}, u32[]{:S(2)}, u32[]{:S(2)}) %collective-permute-start.29) | collective-permute-done | bytes 98336 | tf_op jit(solution)/shard_map/ppermute | solution.py:39
  162.0 3.3 %collective-permute-start.32 = (bf16[2,1,16,768]{3,2,0,1:T(8,128)(2,1)S(1)}, bf16[2,1,16,768]{3,2,0,1:T(8,128)(2,1)S(1)}, u32[]{:S(2)}, u32[]{:S(2)}) collective-permute-start(bf16[2,1,16,768]{3,2,0,1:T(8,128)(2,1)S(1)} %get-tuple-element.124), channel_id=1, source_target_pairs={{0,24},{1,25},{2,26},{3,27},{4,28},{5,29},{6,30},{7,31},{8,16},{9,... | collective-permute-start | bytes 147464 | tf_op jit(solution)/shard_map/ppermute | solution.py:43
  167.2 3.2 %collective-permute-start.37 = (bf16[160,640]{1,0:T(8,128)(2,1)}, bf16[160,640]{1,0:T(8,128)(2,1)}, u32[]{:S(2)}, u32[]{:S(2)}) collective-permute-start(bf16[160,640]{1,0:T(8,128)(2,1)} %get-tuple-element.117), channel_id=1, source_target_pairs={{0,24},{1,25},{2,26},{3,27},{4,28},{5,29},{6,30},{7,31},{8,16},{9,... | collective-permute-start | bytes 614408 | tf_op jit(solution)/shard_map/ppermute | solution.py:43
  170.4 1.8 collective-permute-start.35
  172.8 1.5 collective-permute-start.38
  174.3 6.5 %collective-permute-done.33.refs_3_ = bf16[320,1280]{1,0:T(8,128)(2,1)S(1)} collective-permute-done((bf16[320,1280]{1,0:T(8,128)(2,1)}, bf16[320,1280]{1,0:T(8,128)(2,1)S(1)}, u32[]{:S(2)}, u32[]{:S(2)}) %collective-permute-start.33) | collective-permute-done | bytes 819232 | tf_op jit(solution)/shard_map/ppermute | solution.py:39
  182.1 4.1 %all-to-all-start = ((bf16[4,160,640]{2,1,0:T(8,128)(2,1)}), bf16[4,160,640]{2,1,0:T(8,128)(2,1)S(1)}, u32[]{:S(2)}, u32[]{:S(2)}) async-start(bf16[4,160,640]{2,1,0:T(8,128)(2,1)} %pad_maximum_fusion.2), calls=%async_computation | async-start | bytes 1638400 | tf_op jit(solution)/shard_map/all_to_all | solution.py:92
  186.4 1.2 fusion
  187.6 3.9 %collective-permute-done.36 = bf16[160,640]{1,0:T(8,128)(2,1)} collective-permute-done((bf16[160,640]{1,0:T(8,128)(2,1)S(1)}, bf16[160,640]{1,0:T(8,128)(2,1)}, u32[]{:S(2)}, u32[]{:S(2)}) %collective-permute-start.36) | collective-permute-done | bytes 204832 | tf_op jit(solution)/shard_map/ppermute | solution.py:43
  191.5 1.2 pad_maximum_fusion.3.refs_5_
  192.7 4.8 %collective-permute-start.39 = (bf16[480,640]{1,0:T(8,128)(2,1)S(1)}, bf16[480,640]{1,0:T(8,128)(2,1)}, u32[]{:S(2)}, u32[]{:S(2)}) collective-permute-start(bf16[480,640]{1,0:T(8,128)(2,1)S(1)} %pad_maximum_fusion.3.refs_5_), channel_id=1, source_target_pairs={{0,4},{1,5},{2,6},{3,7},{4,0},{5,1},{6,2},{7,3},{8,12},{9,13},{10,... | collective-permute-start | bytes 1843208 | tf_op jit(solution)/shard_map/ppermute | solution.py:39
  198.7 5.3 %shard_map.149 = (bf16[96,1280]{1,0:T(8,128)(2,1)S(1)}, bf16[96,1280]{1,0:T(8,128)(2,1)}) custom-call(s32[25]{0:T(128)S(1)} %stack.110.spots_ref, bf16[192,1280]{1,0:T(8,128)(2,1)S(1)} %pad_maximum_fusion.4.rows_ref, bf16[320,1280]{1,0:T(8,128)(2,1)S(1)} %constant_dynamic-update-slice_fusion.2.refs_0_, bf16[320,1280]{1,0:T(8,128)(2,1)} %collective-permute-done.28.refs_1_, ...), custom_call_target="tpu_custom_call" | custom-call | tf_op jit(solution)/shard_map/pallas_call | solution.py:147
  204.1 1.6 collective-permute-done.39.refs_7_
  205.7 2.0 collective-permute-start.45
  207.8 1.5 collective-permute-start.41
  209.4 6.6 %collective-permute-done.41.right_ref = bf16[96,1280]{1,0:T(8,128)(2,1)S(1)} collective-permute-done((bf16[96,1280]{1,0:T(8,128)(2,1)S(1)}, bf16[96,1280]{1,0:T(8,128)(2,1)S(1)}, u32[]{:S(2)}, u32[]{:S(2)}) %collective-permute-start.41) | collective-permute-done | bytes 245792 | tf_op jit(solution)/shard_map/ppermute | solution.py:35
  216.8 1.4 collective-permute-start.43
  218.3 5.9 %collective-permute-done.43.refs_2_ = bf16[96,1280]{1,0:T(8,128)(2,1)S(1)} collective-permute-done((bf16[96,1280]{1,0:T(8,128)(2,1)S(1)}, bf16[96,1280]{1,0:T(8,128)(2,1)S(1)}, u32[]{:S(2)}, u32[]{:S(2)}) %collective-permute-start.43) | collective-permute-done | bytes 245792 | tf_op jit(solution)/shard_map/ppermute | solution.py:43
  224.2 1.5 collective-permute-done.44.refs_3_
  226.7 6.0 %shard_map.151 = (bf16[96,1280]{1,0:T(8,128)(2,1)S(1)}, bf16[96,1280]{1,0:T(8,128)(2,1)S(1)}, bf16[96,1280]{1,0:T(8,128)(2,1)S(1)}, bf16[96,1280]{1,0:T(8,128)(2,1)S(1)}) custom-call(s32[25]{0:T(128)S(1)} %stack.110.spots_ref, bf16[96,1280]{1,0:T(8,128)(2,1)S(1)} %get-tuple-element.101.refs_0_, bf16[96,1280]{1,0:T(8,128)(2,1)S(1)} %collective-permute-done.42.refs_1_, ...), custom_call_target="tpu_custom_call" | custom-call | tf_op jit(solution)/shard_map/pallas_call | solution.py:147
  234.3 1.4 collective-permute-start.48
  235.8 6.6 %collective-permute-done.48 = bf16[96,1280]{1,0:T(8,128)(2,1)S(1)} collective-permute-done((bf16[96,1280]{1,0:T(8,128)(2,1)S(1)}, bf16[96,1280]{1,0:T(8,128)(2,1)S(1)}, u32[]{:S(2)}, u32[]{:S(2)}) %collective-permute-start.48) | collective-permute-done | bytes 245792 | tf_op jit(solution)/shard_map/ppermute | solution.py:43
  242.5 1.5 collective-permute-start.49
  244.7 5.0 %collective-permute-done.49 = bf16[96,1280]{1,0:T(8,128)(2,1)S(1)} collective-permute-done((bf16[96,1280]{1,0:T(8,128)(2,1)S(1)}, bf16[96,1280]{1,0:T(8,128)(2,1)S(1)}, u32[]{:S(2)}, u32[]{:S(2)}) %collective-permute-start.49) | collective-permute-done | bytes 245792 | tf_op jit(solution)/shard_map/ppermute | solution.py:35
  249.9 1.5 collective-permute-done.50
  (134 shorter events, 24.4 us)
Async XLA Ops:
  1.1 21.2 %collective-permute-start = (bf16[160,1280]{1,0:T(8,128)(2,1)S(1)}, bf16[160,1280]{1,0:T(8,128)(2,1)S(1)}, u32[]{:S(2)}, u32[]{:S(2)}) collective-permute-start(bf16[160,1280]{1,0:T(8,128)(2,1)S(1)} %pad_maximum_fusion.6.refs_1_), channel_id=1, source_target_pairs={{0,8},{1,9},{2,10},{3,11},{4,12},{5,13},{6,14},{7,15},{8,0},{9,1},... | collective-permute-start | bytes 1228808 | tf_op jit(solution)/shard_map/ppermute | solution.py:43
  4.2 20.7 %collective-permute-start.1 = (bf16[160,1280]{1,0:T(8,128)(2,1)S(1)}, bf16[160,1280]{1,0:T(8,128)(2,1)S(1)}, u32[]{:S(2)}, u32[]{:S(2)}) collective-permute-start(bf16[160,1280]{1,0:T(8,128)(2,1)S(1)} %pad_maximum_fusion.6.refs_1_), channel_id=1, source_target_pairs={{0,16},{1,17},{2,18},{3,19},{4,20},{5,21},{6,22},{7,23},{8,24},{9,... | collective-permute-start | bytes 1228808 | tf_op jit(solution)/shard_map/ppermute | solution.py:43
  6.8 18.1 %collective-permute-start.2 = (bf16[160,1280]{1,0:T(8,128)(2,1)S(1)}, bf16[160,1280]{1,0:T(8,128)(2,1)S(1)}, u32[]{:S(2)}, u32[]{:S(2)}) collective-permute-start(bf16[160,1280]{1,0:T(8,128)(2,1)S(1)} %pad_maximum_fusion.6.refs_1_), channel_id=1, source_target_pairs={{0,4},{1,5},{2,6},{3,7},{4,0},{5,1},{6,2},{7,3},{8,12},{9,13},{10,... | collective-permute-start | bytes 1228808 | tf_op jit(solution)/shard_map/ppermute | solution.py:39
  8.3 18.6 %copy-start.6 = (bf16[160,1280]{1,0:T(8,128)(2,1)S(1)}, bf16[160,1280]{1,0:T(8,128)(2,1)}, u32[]{:S(2)}) copy-start(bf16[160,1280]{1,0:T(8,128)(2,1)} %param.24) | copy-start | bytes 1228804
  8.3 18.6 %copy-start.7 = (bf16[160,1280]{1,0:T(8,128)(2,1)S(1)}, bf16[160,1280]{1,0:T(8,128)(2,1)}, u32[]{:S(2)}) copy-start(bf16[160,1280]{1,0:T(8,128)(2,1)} %param.23) | copy-start | bytes 1228804
  24.9 2.2 copy-start.4
  24.9 10.9 %collective-permute-start.3 = (bf16[160,1280]{1,0:T(8,128)(2,1)S(1)}, bf16[160,1280]{1,0:T(8,128)(2,1)}, u32[]{:S(2)}, u32[]{:S(2)}) collective-permute-start(bf16[160,1280]{1,0:T(8,128)(2,1)S(1)} %collective-permute-done.1.refs_3_), channel_id=1, source_target_pairs={{0,8},{1,9},{2,10},{3,11},{4,12},{5,13},{6,14},{7,15},{8,0},{9,1},... | collective-permute-start | bytes 1228808 | tf_op jit(solution)/shard_map/ppermute | solution.py:43
  25.4 21.2 %collective-permute-start.4 = (bf16[320,1280]{1,0:T(8,128)(2,1)S(1)}, bf16[320,1280]{1,0:T(8,128)(2,1)S(1)}, u32[]{:S(2)}, u32[]{:S(2)}) collective-permute-start(bf16[320,1280]{1,0:T(8,128)(2,1)S(1)} %pad_maximum_fusion.1), channel_id=1, source_target_pairs={{0,4},{1,5},{2,6},{3,7},{4,0},{5,1},{6,2},{7,3},{8,12},{9,13},{10,... | collective-permute-start | bytes 2457608 | tf_op jit(solution)/shard_map/ppermute | solution.py:39
  27.9 34.5 %collective-permute-start.10 = (bf16[160,1280]{1,0:T(8,128)(2,1)}, bf16[160,1280]{1,0:T(8,128)(2,1)}, u32[]{:S(2)}, u32[]{:S(2)}) collective-permute-start(bf16[160,1280]{1,0:T(8,128)(2,1)} %pad_maximum_fusion.7), channel_id=1, source_target_pairs={{0,24},{1,25},{2,26},{3,27},{4,28},{5,29},{6,30},{7,31},{8,16},{9,... | collective-permute-start | bytes 1228808 | tf_op jit(solution)/shard_map/ppermute | solution.py:43
  30.0 33.9 %collective-permute-start.14 = (bf16[160,1280]{1,0:T(8,128)(2,1)S(1)}, bf16[160,1280]{1,0:T(8,128)(2,1)}, u32[]{:S(2)}, u32[]{:S(2)}) collective-permute-start(bf16[160,1280]{1,0:T(8,128)(2,1)S(1)} %pad_maximum_fusion.8.refs_4_), channel_id=1, source_target_pairs={{0,16},{1,17},{2,18},{3,19},{4,20},{5,21},{6,22},{7,23},{8,24},{9,... | collective-permute-start | bytes 1228808 | tf_op jit(solution)/shard_map/ppermute | solution.py:43
  35.8 19.7 %collective-permute-start.5 = (bf16[160,1280]{1,0:T(8,128)(2,1)}, bf16[160,1280]{1,0:T(8,128)(2,1)}, u32[]{:S(2)}, u32[]{:S(2)}) collective-permute-start(bf16[160,1280]{1,0:T(8,128)(2,1)} %collective-permute-done.3.refs_4_), channel_id=1, source_target_pairs={{0,4},{1,5},{2,6},{3,7},{4,0},{5,1},{6,2},{7,3},{8,12},{9,13},{10,... | collective-permute-start | bytes 1228808 | tf_op jit(solution)/shard_map/ppermute | solution.py:39
  43.1 20.8 %collective-permute-start.13 = (bf16[160,1280]{1,0:T(8,128)(2,1)}, bf16[160,1280]{1,0:T(8,128)(2,1)}, u32[]{:S(2)}, u32[]{:S(2)}) collective-permute-start(bf16[160,1280]{1,0:T(8,128)(2,1)} %pad_maximum_fusion.7), channel_id=1, source_target_pairs={{0,8},{1,9},{2,10},{3,11},{4,12},{5,13},{6,14},{7,15},{8,0},{9,1},... | collective-permute-start | bytes 1228808 | tf_op jit(solution)/shard_map/ppermute | solution.py:43
  46.6 18.7 %collective-permute-start.15 = (bf16[160,1280]{1,0:T(8,128)(2,1)S(1)}, bf16[160,1280]{1,0:T(8,128)(2,1)}, u32[]{:S(2)}, u32[]{:S(2)}) collective-permute-start(bf16[160,1280]{1,0:T(8,128)(2,1)S(1)} %pad_maximum_fusion.8.refs_4_), channel_id=1, source_target_pairs={{0,4},{1,5},{2,6},{3,7},{4,0},{5,1},{6,2},{7,3},{8,12},{9,13},{10,... | collective-permute-start | bytes 1228808 | tf_op jit(solution)/shard_map/ppermute | solution.py:39
  62.3 5.5 %copy-start.8 = (bf16[160,1280]{1,0:T(8,128)(2,1)S(1)}, bf16[160,1280]{1,0:T(8,128)(2,1)}, u32[]{:S(2)}) copy-start(bf16[160,1280]{1,0:T(8,128)(2,1)} %param.25) | copy-start | bytes 1228804
  62.3 3.9 %collective-permute-start.6 = (bf16[128,1280]{1,0:T(8,128)(2,1)S(1)}, bf16[128,1280]{1,0:T(8,128)(2,1)S(1)}, u32[]{:S(2)}, u32[]{:S(2)}) collective-permute-start(bf16[128,1280]{1,0:T(8,128)(2,1)S(1)} %get-tuple-element.65), channel_id=1, source_target_pairs={{0,1},{1,0},{2,3},{3,2},{4,5},{5,4},{6,7},{7,6},{8,9},{9,8},{10,11... | collective-permute-start | bytes 983048 | tf_op jit(solution)/shard_map/ppermute | solution.py:31
  65.3 12.6 %copy-start.11 = (s32[64]{0:T(128)S(1)}, s32[64]{0:T(128)}, u32[]{:S(2)}) copy-start(s32[64]{0:T(128)} %param.18) | copy-start | bytes 772
  65.3 28.2 %collective-permute-start.16 = (bf16[480,1280]{1,0:T(8,128)(2,1)S(1)}, bf16[480,1280]{1,0:T(8,128)(2,1)S(1)}, u32[]{:S(2)}, u32[]{:S(2)}) collective-permute-start(bf16[480,1280]{1,0:T(8,128)(2,1)S(1)} %pad_maximum_fusion.refs_5_), channel_id=1, source_target_pairs={{0,4},{1,5},{2,6},{3,7},{4,0},{5,1},{6,2},{7,3},{8,12},{9,13},{10,... | collective-permute-start | bytes 3686408 | tf_op jit(solution)/shard_map/ppermute | solution.py:39
  66.3 9.1 %collective-permute-start.7 = (bf16[128,1280]{1,0:T(8,128)(2,1)S(1)}, bf16[128,1280]{1,0:T(8,128)(2,1)S(1)}, u32[]{:S(2)}, u32[]{:S(2)}) collective-permute-start(bf16[128,1280]{1,0:T(8,128)(2,1)S(1)} %add_convert_fusion.2.left_ref), channel_id=1, source_target_pairs={{0,2},{1,3},{2,0},{3,1},{4,6},{5,7},{6,4},{7,5},{8,10},{9,11},{10,... | collective-permute-start | bytes 983048 | tf_op jit(solution)/shard_map/ppermute | solution.py:35
  67.8 20.3 %collective-permute-start.11 = (bf16[160,1280]{1,0:T(8,128)(2,1)S(1)}, bf16[160,1280]{1,0:T(8,128)(2,1)S(1)}, u32[]{:S(2)}, u32[]{:S(2)}) collective-permute-start(bf16[160,1280]{1,0:T(8,128)(2,1)S(1)} %copy-done.8), channel_id=1, source_target_pairs={{0,16},{1,17},{2,18},{3,19},{4,20},{5,21},{6,22},{7,23},{8,24},{9,... | collective-permute-start | bytes 1228808 | tf_op jit(solution)/shard_map/ppermute | solution.py:43
  76.2 16.5 %collective-permute-start.9 = (bf16[128,1280]{1,0:T(8,128)(2,1)S(1)}, bf16[128,1280]{1,0:T(8,128)(2,1)S(1)}, u32[]{:S(2)}, u32[]{:S(2)}) collective-permute-start(bf16[128,1280]{1,0:T(8,128)(2,1)S(1)} %get-tuple-element.67.refs_0_), channel_id=1, source_target_pairs={{0,8},{1,9},{2,10},{3,11},{4,12},{5,13},{6,14},{7,15},{8,0},{9,1},... | collective-permute-start | bytes 983048 | tf_op jit(solution)/shard_map/ppermute | solution.py:43
  78.0 15.5 %collective-permute-start.8 = (bf16[128,1280]{1,0:T(8,128)(2,1)S(1)}, bf16[128,1280]{1,0:T(8,128)(2,1)S(1)}, u32[]{:S(2)}, u32[]{:S(2)}) collective-permute-start(bf16[128,1280]{1,0:T(8,128)(2,1)S(1)} %get-tuple-element.67.refs_0_), channel_id=1, source_target_pairs={{0,1},{1,0},{2,3},{3,2},{4,5},{5,4},{6,7},{7,6},{8,9},{9,8},{10,11... | collective-permute-start | bytes 983048 | tf_op jit(solution)/shard_map/ppermute | solution.py:31
  92.8 1.6 collective-permute-start.12
  92.8 7.3 %copy-start.12 = (s32[64]{0:T(128)S(1)}, s32[64]{0:T(128)}, u32[]{:S(2)}) copy-start(s32[64]{0:T(128)} %param.19) | copy-start | bytes 772
  92.8 20.8 %collective-permute-start.19 = (bf16[320,1280]{1,0:T(8,128)(2,1)S(1)}, bf16[320,1280]{1,0:T(8,128)(2,1)}, u32[]{:S(2)}, u32[]{:S(2)}) collective-permute-start(bf16[320,1280]{1,0:T(8,128)(2,1)S(1)} %constant_dynamic-update-slice_fusion.refs_0_), channel_id=1, source_target_pairs={{0,8},{1,9},{2,10},{3,11},{4,12},{5,13},{6,14},{7,15},{8,0},{9,1},... | collective-permute-start | bytes 2457608 | tf_op jit(solution)/shard_map/ppermute | solution.py:43
  92.9 20.7 %collective-permute-start.20 = (bf16[320,1280]{1,0:T(8,128)(2,1)S(1)}, bf16[320,1280]{1,0:T(8,128)(2,1)S(1)}, u32[]{:S(2)}, u32[]{:S(2)}) collective-permute-start(bf16[320,1280]{1,0:T(8,128)(2,1)S(1)} %constant_dynamic-update-slice_fusion.refs_0_), channel_id=1, source_target_pairs={{0,4},{1,5},{2,6},{3,7},{4,0},{5,1},{6,2},{7,3},{8,12},{9,13},{10,... | collective-permute-start | bytes 2457608 | tf_op jit(solution)/shard_map/ppermute | solution.py:39
  99.9 2.0 collective-permute-start.18
  101.4 18.1 %collective-permute-start.17 = (bf16[128,1280]{1,0:T(8,128)(2,1)S(1)}, bf16[128,1280]{1,0:T(8,128)(2,1)S(1)}, u32[]{:S(2)}, u32[]{:S(2)}) collective-permute-start(bf16[128,1280]{1,0:T(8,128)(2,1)S(1)} %get-tuple-element.75), channel_id=1, source_target_pairs={{0,1},{1,0},{2,3},{3,2},{4,5},{5,4},{6,7},{7,6},{8,9},{9,8},{10,11... | collective-permute-start | bytes 983048 | tf_op jit(solution)/shard_map/ppermute | solution.py:31
  113.7 17.1 %copy-start = (bf16[320,1280]{1,0:T(8,128)(2,1)}, bf16[320,1280]{1,0:T(8,128)(2,1)S(1)}, u32[]{:S(2)}) copy-start(bf16[320,1280]{1,0:T(8,128)(2,1)S(1)} %collective-permute-done.20.refs_1_) | copy-start | bytes 2457604
  113.7 16.9 %collective-permute-start.21 = (bf16[128,1280]{1,0:T(8,128)(2,1)S(1)}, bf16[128,1280]{1,0:T(8,128)(2,1)S(1)}, u32[]{:S(2)}, u32[]{:S(2)}) collective-permute-start(bf16[128,1280]{1,0:T(8,128)(2,1)S(1)} %add_convert_fusion.1), channel_id=1, source_target_pairs={{0,8},{1,9},{2,10},{3,11},{4,12},{5,13},{6,14},{7,15},{8,0},{9,1},... | collective-permute-start | bytes 983048 | tf_op jit(solution)/shard_map/ppermute | solution.py:43
  115.5 21.5 %collective-permute-start.23 = (bf16[160,1280]{1,0:T(8,128)(2,1)S(1)}, bf16[160,1280]{1,0:T(8,128)(2,1)S(1)}, u32[]{:S(2)}, u32[]{:S(2)}) collective-permute-start(bf16[160,1280]{1,0:T(8,128)(2,1)S(1)} %pad_maximum_fusion.9), channel_id=1, source_target_pairs={{0,16},{1,17},{2,18},{3,19},{4,20},{5,21},{6,22},{7,23},{8,24},{9,... | collective-permute-start | bytes 1228808 | tf_op jit(solution)/shard_map/ppermute | solution.py:43
  119.0 19.6 %collective-permute-start.24 = (bf16[320,1280]{1,0:T(8,128)(2,1)}, bf16[320,1280]{1,0:T(8,128)(2,1)S(1)}, u32[]{:S(2)}, u32[]{:S(2)}) collective-permute-start(bf16[320,1280]{1,0:T(8,128)(2,1)} %collective-permute-done.19.refs_2_), channel_id=1, source_target_pairs={{0,4},{1,5},{2,6},{3,7},{4,0},{5,1},{6,2},{7,3},{8,12},{9,13},{10,... | collective-permute-start | bytes 2457608 | tf_op jit(solution)/shard_map/ppermute | solution.py:39
  130.8 5.4 %collective-permute-start.22 = (bf16[64,1280]{1,0:T(8,128)(2,1)S(1)}, bf16[64,1280]{1,0:T(8,128)(2,1)S(1)}, u32[]{:S(2)}, u32[]{:S(2)}) collective-permute-start(bf16[64,1280]{1,0:T(8,128)(2,1)S(1)} %dynamic-slice_bitcast_fusion), channel_id=1, source_target_pairs={{0,2},{1,3},{2,0},{3,1},{4,6},{5,7},{6,4},{7,5},{8,10},{9,11},{10,... | collective-permute-start | bytes 491528 | tf_op jit(solution)/shard_map/ppermute | solution.py:35
  132.3 6.3 %copy-start.1 = (bf16[320,1280]{1,0:T(8,128)(2,1)S(1)}, bf16[320,1280]{1,0:T(8,128)(2,1)}, u32[]{:S(2)}) copy-start(bf16[320,1280]{1,0:T(8,128)(2,1)} %copy-done) | copy-start | bytes 2457604
  137.0 19.3 %collective-permute-start.27 = (bf16[320,1280]{1,0:T(8,128)(2,1)S(1)}, bf16[320,1280]{1,0:T(8,128)(2,1)}, u32[]{:S(2)}, u32[]{:S(2)}) collective-permute-start(bf16[320,1280]{1,0:T(8,128)(2,1)S(1)} %constant_dynamic-update-slice_fusion.2.refs_0_), channel_id=1, source_target_pairs={{0,8},{1,9},{2,10},{3,11},{4,12},{5,13},{6,14},{7,15},{8,0},{9,1},... | collective-permute-start | bytes 2457608 | tf_op jit(solution)/shard_map/ppermute | solution.py:43
  137.6 18.8 %collective-permute-start.28 = (bf16[320,1280]{1,0:T(8,128)(2,1)S(1)}, bf16[320,1280]{1,0:T(8,128)(2,1)}, u32[]{:S(2)}, u32[]{:S(2)}) collective-permute-start(bf16[320,1280]{1,0:T(8,128)(2,1)S(1)} %constant_dynamic-update-slice_fusion.2.refs_0_), channel_id=1, source_target_pairs={{0,4},{1,5},{2,6},{3,7},{4,0},{5,1},{6,2},{7,3},{8,12},{9,13},{10,... | collective-permute-start | bytes 2457608 | tf_op jit(solution)/shard_map/ppermute | solution.py:39
  142.3 24.2 %copy-start.9 = (bf16[160,1280]{1,0:T(8,128)(2,1)S(1)}, bf16[160,1280]{1,0:T(8,128)(2,1)}, u32[]{:S(2)}) copy-start(bf16[160,1280]{1,0:T(8,128)(2,1)} %param.28) | copy-start | bytes 1228804
  142.3 1.4 collective-permute-start.25
  143.8 4.9 %collective-permute-start.26 = (bf16[64,640]{1,0:T(8,128)(2,1)S(1)}, bf16[64,640]{1,0:T(8,128)(2,1)S(1)}, u32[]{:S(2)}, u32[]{:S(2)}) collective-permute-start(bf16[64,640]{1,0:T(8,128)(2,1)S(1)} %add_convert_fusion.8), channel_id=1, source_target_pairs={{0,2},{1,3},{2,0},{3,1},{4,6},{5,7},{6,4},{7,5},{8,10},{9,11},{10,... | collective-permute-start | bytes 245768 | tf_op jit(solution)/shard_map/ppermute | solution.py:35
  156.4 5.0 %collective-permute-start.29 = (bf16[4,1,16,768]{3,2,0,1:T(8,128)(2,1)S(1)}, bf16[4,1,16,768]{3,2,0,1:T(8,128)(2,1)S(1)}, u32[]{:S(2)}, u32[]{:S(2)}) collective-permute-start(bf16[4,1,16,768]{3,2,0,1:T(8,128)(2,1)S(1)} %dynamic-slice_bitcast_fusion.1), channel_id=1, source_target_pairs={{0,4},{1,5},{2,6},{3,7},{4,0},{5,1},{6,2},{7,3},{8,12},{9,13},{10,... | collective-permute-start | bytes 294920 | tf_op jit(solution)/shard_map/ppermute | solution.py:39
  157.0 24.1 %copy-start.10 = (bf16[160,1280]{1,0:T(8,128)(2,1)S(1)}, bf16[160,1280]{1,0:T(8,128)(2,1)}, u32[]{:S(2)}) copy-start(bf16[160,1280]{1,0:T(8,128)(2,1)} %param.29) | copy-start | bytes 1228804
  161.4 19.4 %collective-permute-start.33 = (bf16[320,1280]{1,0:T(8,128)(2,1)}, bf16[320,1280]{1,0:T(8,128)(2,1)S(1)}, u32[]{:S(2)}, u32[]{:S(2)}) collective-permute-start(bf16[320,1280]{1,0:T(8,128)(2,1)} %collective-permute-done.27.refs_2_), channel_id=1, source_target_pairs={{0,4},{1,5},{2,6},{3,7},{4,0},{5,1},{6,2},{7,3},{8,12},{9,13},{10,... | collective-permute-start | bytes 2457608 | tf_op jit(solution)/shard_map/ppermute | solution.py:39
  162.0 8.4 %collective-permute-start.32 = (bf16[2,1,16,768]{3,2,0,1:T(8,128)(2,1)S(1)}, bf16[2,1,16,768]{3,2,0,1:T(8,128)(2,1)S(1)}, u32[]{:S(2)}, u32[]{:S(2)}) collective-permute-start(bf16[2,1,16,768]{3,2,0,1:T(8,128)(2,1)S(1)} %get-tuple-element.124), channel_id=1, source_target_pairs={{0,24},{1,25},{2,26},{3,27},{4,28},{5,29},{6,30},{7,31},{8,16},{9,... | collective-permute-start | bytes 147464 | tf_op jit(solution)/shard_map/ppermute | solution.py:43
  165.3 7.5 %collective-permute-start.31 = (bf16[2,1,16,768]{3,2,0,1:T(8,128)(2,1)S(1)}, bf16[2,1,16,768]{3,2,0,1:T(8,128)(2,1)S(1)}, u32[]{:S(2)}, u32[]{:S(2)}) collective-permute-start(bf16[2,1,16,768]{3,2,0,1:T(8,128)(2,1)S(1)} %get-tuple-element.125), channel_id=1, source_target_pairs={{0,16},{1,17},{2,18},{3,19},{4,20},{5,21},{6,22},{7,23},{8,24},{9,... | collective-permute-start | bytes 147464 | tf_op jit(solution)/shard_map/ppermute | solution.py:43
  165.8 7.0 %collective-permute-start.30 = (bf16[2,1,16,768]{3,2,0,1:T(8,128)(2,1)S(1)}, bf16[2,1,16,768]{3,2,0,1:T(8,128)(2,1)S(1)}, u32[]{:S(2)}, u32[]{:S(2)}) collective-permute-start(bf16[2,1,16,768]{3,2,0,1:T(8,128)(2,1)S(1)} %get-tuple-element.126), channel_id=1, source_target_pairs={{0,8},{1,9},{2,10},{3,11},{4,12},{5,13},{6,14},{7,15},{8,0},{9,1},... | collective-permute-start | bytes 147464 | tf_op jit(solution)/shard_map/ppermute | solution.py:43
  167.2 20.4 %collective-permute-start.37 = (bf16[160,640]{1,0:T(8,128)(2,1)}, bf16[160,640]{1,0:T(8,128)(2,1)}, u32[]{:S(2)}, u32[]{:S(2)}) collective-permute-start(bf16[160,640]{1,0:T(8,128)(2,1)} %get-tuple-element.117), channel_id=1, source_target_pairs={{0,24},{1,25},{2,26},{3,27},{4,28},{5,29},{6,30},{7,31},{8,16},{9,... | collective-permute-start | bytes 614408 | tf_op jit(solution)/shard_map/ppermute | solution.py:43
  170.4 21.1 %collective-permute-start.35 = (bf16[160,640]{1,0:T(8,128)(2,1)}, bf16[160,640]{1,0:T(8,128)(2,1)}, u32[]{:S(2)}, u32[]{:S(2)}) collective-permute-start(bf16[160,640]{1,0:T(8,128)(2,1)} %get-tuple-element.117), channel_id=1, source_target_pairs={{0,8},{1,9},{2,10},{3,11},{4,12},{5,13},{6,14},{7,15},{8,0},{9,1},... | collective-permute-start | bytes 614408 | tf_op jit(solution)/shard_map/ppermute | solution.py:43
  172.8 18.7 %collective-permute-start.36 = (bf16[160,640]{1,0:T(8,128)(2,1)S(1)}, bf16[160,640]{1,0:T(8,128)(2,1)}, u32[]{:S(2)}, u32[]{:S(2)}) collective-permute-start(bf16[160,640]{1,0:T(8,128)(2,1)S(1)} %get-tuple-element.102.refs_4_), channel_id=1, source_target_pairs={{0,16},{1,17},{2,18},{3,19},{4,20},{5,21},{6,22},{7,23},{8,24},{9,... | collective-permute-start | bytes 614408 | tf_op jit(solution)/shard_map/ppermute | solution.py:43
  172.8 19.9 %collective-permute-start.38 = (bf16[160,640]{1,0:T(8,128)(2,1)S(1)}, bf16[160,640]{1,0:T(8,128)(2,1)S(1)}, u32[]{:S(2)}, u32[]{:S(2)}) collective-permute-start(bf16[160,640]{1,0:T(8,128)(2,1)S(1)} %get-tuple-element.102.refs_4_), channel_id=1, source_target_pairs={{0,4},{1,5},{2,6},{3,7},{4,0},{5,1},{6,2},{7,3},{8,12},{9,13},{10,... | collective-permute-start | bytes 614408 | tf_op jit(solution)/shard_map/ppermute | solution.py:39
  180.8 1.3 copy-start.2
  182.1 23.6 %all-to-all-start = ((bf16[4,160,640]{2,1,0:T(8,128)(2,1)}), bf16[4,160,640]{2,1,0:T(8,128)(2,1)S(1)}, u32[]{:S(2)}, u32[]{:S(2)}) async-start(bf16[4,160,640]{2,1,0:T(8,128)(2,1)} %pad_maximum_fusion.2), calls=%async_computation | async-start | bytes 1638400 | tf_op jit(solution)/shard_map/all_to_all | solution.py:92
  187.5 10.0 %collective-permute-start.34 = (bf16[192,640]{1,0:T(8,128)(2,1)S(1)}, bf16[192,640]{1,0:T(8,128)(2,1)S(1)}, u32[]{:S(2)}, u32[]{:S(2)}) collective-permute-start(bf16[192,640]{1,0:T(8,128)(2,1)S(1)} %fusion), channel_id=1, source_target_pairs={{0,1},{1,0},{2,3},{3,2},{4,5},{5,4},{6,7},{7,6},{8,9},{9,8},{10,11... | collective-permute-start | bytes 737288 | tf_op jit(solution)/shard_map/ppermute | solution.py:31
  192.7 13.0 %collective-permute-start.39 = (bf16[480,640]{1,0:T(8,128)(2,1)S(1)}, bf16[480,640]{1,0:T(8,128)(2,1)}, u32[]{:S(2)}, u32[]{:S(2)}) collective-permute-start(bf16[480,640]{1,0:T(8,128)(2,1)S(1)} %pad_maximum_fusion.3.refs_5_), channel_id=1, source_target_pairs={{0,4},{1,5},{2,6},{3,7},{4,0},{5,1},{6,2},{7,3},{8,12},{9,13},{10,... | collective-permute-start | bytes 1843208 | tf_op jit(solution)/shard_map/ppermute | solution.py:39
  197.6 1.1 copy-start.3
  205.7 2.0 collective-permute-start.40
  205.7 20.9 %collective-permute-start.45 = (bf16[640,640]{1,0:T(8,128)(2,1)S(1)}, bf16[640,640]{1,0:T(8,128)(2,1)S(1)}, u32[]{:S(2)}, u32[]{:S(2)}) collective-permute-start(bf16[640,640]{1,0:T(8,128)(2,1)S(1)} %bitcast.61), channel_id=1, source_target_pairs={{0,4},{1,5},{2,6},{3,7},{4,0},{5,1},{6,2},{7,3},{8,12},{9,13},{10,... | collective-permute-start | bytes 2457608 | tf_op jit(solution)/shard_map/ppermute | solution.py:39
  207.8 8.2 %collective-permute-start.41 = (bf16[96,1280]{1,0:T(8,128)(2,1)S(1)}, bf16[96,1280]{1,0:T(8,128)(2,1)S(1)}, u32[]{:S(2)}, u32[]{:S(2)}) collective-permute-start(bf16[96,1280]{1,0:T(8,128)(2,1)S(1)} %add_convert_fusion.6.left_ref), channel_id=1, source_target_pairs={{0,2},{1,3},{2,0},{3,1},{4,6},{5,7},{6,4},{7,5},{8,10},{9,11},{10,... | collective-permute-start | bytes 737288 | tf_op jit(solution)/shard_map/ppermute | solution.py:35
  216.8 7.3 %collective-permute-start.43 = (bf16[96,1280]{1,0:T(8,128)(2,1)S(1)}, bf16[96,1280]{1,0:T(8,128)(2,1)S(1)}, u32[]{:S(2)}, u32[]{:S(2)}) collective-permute-start(bf16[96,1280]{1,0:T(8,128)(2,1)S(1)} %get-tuple-element.101.refs_0_), channel_id=1, source_target_pairs={{0,8},{1,9},{2,10},{3,11},{4,12},{5,13},{6,14},{7,15},{8,0},{9,1},... | collective-permute-start | bytes 737288 | tf_op jit(solution)/shard_map/ppermute | solution.py:43
  218.3 5.9 %collective-permute-start.42 = (bf16[96,1280]{1,0:T(8,128)(2,1)S(1)}, bf16[96,1280]{1,0:T(8,128)(2,1)S(1)}, u32[]{:S(2)}, u32[]{:S(2)}) collective-permute-start(bf16[96,1280]{1,0:T(8,128)(2,1)S(1)} %get-tuple-element.101.refs_0_), channel_id=1, source_target_pairs={{0,1},{1,0},{2,3},{3,2},{4,5},{5,4},{6,7},{7,6},{8,9},{9,8},{10,11... | collective-permute-start | bytes 737288 | tf_op jit(solution)/shard_map/ppermute | solution.py:31
  224.2 1.5 collective-permute-start.44
  232.7 1.6 collective-permute-start.47
  232.8 3.0 %collective-permute-start.46 = (bf16[96,1280]{1,0:T(8,128)(2,1)S(1)}, bf16[96,1280]{1,0:T(8,128)(2,1)S(1)}, u32[]{:S(2)}, u32[]{:S(2)}) collective-permute-start(bf16[96,1280]{1,0:T(8,128)(2,1)S(1)} %get-tuple-element.108), channel_id=1, source_target_pairs={{0,1},{1,0},{2,3},{3,2},{4,5},{5,4},{6,7},{7,6},{8,9},{9,8},{10,11... | collective-permute-start | bytes 737288 | tf_op jit(solution)/shard_map/ppermute | solution.py:31
  234.3 8.1 %collective-permute-start.48 = (bf16[96,1280]{1,0:T(8,128)(2,1)S(1)}, bf16[96,1280]{1,0:T(8,128)(2,1)S(1)}, u32[]{:S(2)}, u32[]{:S(2)}) collective-permute-start(bf16[96,1280]{1,0:T(8,128)(2,1)S(1)} %add_convert_fusion.5), channel_id=1, source_target_pairs={{0,8},{1,9},{2,10},{3,11},{4,12},{5,13},{6,14},{7,15},{8,0},{9,1},... | collective-permute-start | bytes 737288 | tf_op jit(solution)/shard_map/ppermute | solution.py:43
  242.5 7.2 %collective-permute-start.49 = (bf16[96,1280]{1,0:T(8,128)(2,1)S(1)}, bf16[96,1280]{1,0:T(8,128)(2,1)S(1)}, u32[]{:S(2)}, u32[]{:S(2)}) collective-permute-start(bf16[96,1280]{1,0:T(8,128)(2,1)S(1)} %add_convert_fusion.4), channel_id=1, source_target_pairs={{0,2},{1,3},{2,0},{3,1},{4,6},{5,7},{6,4},{7,5},{8,10},{9,11},{10,... | collective-permute-start | bytes 737288 | tf_op jit(solution)/shard_map/ppermute | solution.py:35
  249.8 1.6 collective-permute-start.50
  (1 other events, 1.0 us)
